TPU v7x, 32 devices: a whole 2x2x4 slice. The times are simulated.
32 devices in a mesh: dom: 8 (over z, x), rep: 4 (over y, core).
Axes of the slice: x: 2, y: 2, z: 4, core: 2. Of those that a mesh axis runs over, the one named last changes fastest.
Arguments:
- entities: bfloat16 [8192, 512], P('dom'), may hold values from -60 to 60
- relations: bfloat16 [4, 512, 512], replicated, may hold values from -2 to 2
- head_local: int32 [16384], P(('dom', 'rep')), may hold values from 0 to 1023
- rel_ids: int32 [16384], P(('dom', 'rep')), may hold values from 0 to 3
- tail_part: int32 [16384, 1], P(('dom', 'rep')), may hold values from 0 to 7; in each aligned block of 512 rows (0 to 511, 512 to 1023, ...) at most 128 rows name the same one
- tail_local: int32 [16384], P(('dom', 'rep')), may hold values from 0 to 1023
- neg_local: int32 [256], P('dom'), may hold values from 0 to 1023
Outputs:
- entity_grad: float32 [8192, 512], P('dom')
- relation_grad: float32 [4, 512, 512], replicated
- edge_loss: float32 [16384], P(('dom', 'rep'))
Inputs may be any that keep to these rules, and one draw needn't show every extreme that they name: `tail_part`: in the 512 edges of one device no partition is named by more than 128 edges, a bound that some block reaches.
All inputs are finite; a program needn't handle non-finite values.
Results may differ from a plain program's by a relative error of at most 0.012.
The roundings to bfloat16 on the way count: a program that leaves them out, or rounds other values in their place, can miss the bound.
Values may be sent and summed in bfloat16 or wider, within the bound.
No kernel may reach another device: no remote copies, remote signals or barrier semaphores. Data moves between devices by JAX's collectives and lax.ppermute only.
A program may use at most 64 MiB of HBM per device.

v0:
```python
import math

import jax
import jax.numpy as jnp
from jax import lax
from jax.sharding import PartitionSpec as P

D = 512


def local(entities, relations, head_local, rel_ids, tail_part, tail_local, neg_local):
    factor = 1.0 / math.sqrt(D)
    ent_dev = entities.shape[0]
    columns = entities.shape[1]
    edge_count = head_local.shape[0]
    part_count = lax.axis_size("dom")
    capacity = 2 * edge_count // part_count
    slot_count = part_count * capacity
    relation_count = relations.shape[0]
    head_rows = jnp.take(entities, head_local, axis=0)
    selectors = [(rel_ids == relation)[:, None] for relation in range(relation_count)]
    query_sum = jnp.zeros((edge_count, columns), jnp.float32)
    for relation in range(relation_count):
        picked = jnp.where(selectors[relation], head_rows, jnp.zeros_like(head_rows))
        query_sum = query_sum + jnp.dot(
            picked, relations[relation], preferred_element_type=jnp.float32
        )
    queries = query_sum.astype(jnp.bfloat16)
    target = tail_part[:, 0]
    target_hot = (target[:, None] == jnp.arange(part_count, dtype=jnp.int32)[None, :]).astype(
        jnp.int32
    )
    earlier = jnp.cumsum(target_hot, axis=0) - target_hot
    position = jnp.sum(earlier * target_hot, axis=1)
    slot_index = target * capacity + position
    slot_match = (slot_index[None, :] == jnp.arange(slot_count, dtype=jnp.int32)[:, None]).astype(
        jnp.int32
    )
    filled = jnp.sum(slot_match, axis=1) > 0
    source = jnp.sum(slot_match * jnp.arange(edge_count, dtype=jnp.int32)[None, :], axis=1)
    send_ids = jnp.where(filled, jnp.take(tail_local, source, axis=0), 0).reshape(
        part_count, capacity
    )
    recv_ids = lax.all_to_all(send_ids, "dom", split_axis=0, concat_axis=0, tiled=True)
    looked_up = jnp.take(entities, recv_ids.reshape(-1), axis=0).reshape(
        part_count, capacity, columns
    )
    returned = lax.all_to_all(looked_up, "dom", split_axis=0, concat_axis=0, tiled=True)
    tail_embed = jnp.take(returned.reshape(slot_count, columns), slot_index, axis=0)
    own_negs = jnp.take(entities, neg_local, axis=0)
    negatives = lax.all_gather(own_negs, "dom", axis=0, tiled=True)
    positive = (
        jnp.sum(queries.astype(jnp.float32) * tail_embed.astype(jnp.float32), axis=1) * factor
    )
    scores = (
        lax.dot_general(
            queries, negatives, (((1,), (1,)), ((), ())), preferred_element_type=jnp.float32
        )
        * factor
    )
    row_max = jnp.maximum(positive, jnp.max(scores, axis=1))
    exp_pos = jnp.exp(positive - row_max)
    exp_neg = jnp.exp(scores - row_max[:, None])
    partition_sum = exp_pos + jnp.sum(exp_neg, axis=1)
    edge_loss = jnp.log(partition_sum) + row_max - positive
    prob_pos = exp_pos / partition_sum
    prob_neg = (exp_neg / partition_sum[:, None]).astype(jnp.bfloat16)
    mixed = jnp.dot(prob_neg, negatives, preferred_element_type=jnp.float32)
    query_grad = (
        factor * ((prob_pos - 1.0)[:, None] * tail_embed.astype(jnp.float32) + mixed)
    ).astype(jnp.bfloat16)
    tail_grad = factor * (prob_pos - 1.0)[:, None] * queries.astype(jnp.float32)
    neg_grad = factor * lax.dot_general(
        prob_neg, queries, (((0,), (0,)), ((), ())), preferred_element_type=jnp.float32
    )
    head_grad = jnp.zeros((edge_count, columns), jnp.float32)
    rel_terms = []
    for relation in range(relation_count):
        picked_grad = jnp.where(selectors[relation], query_grad, jnp.zeros_like(query_grad))
        head_grad = head_grad + lax.dot_general(
            picked_grad,
            relations[relation],
            (((1,), (1,)), ((), ())),
            preferred_element_type=jnp.float32,
        )
        picked_rows = jnp.where(selectors[relation], head_rows, jnp.zeros_like(head_rows))
        rel_terms.append(
            lax.dot_general(
                picked_rows,
                query_grad,
                (((0,), (0,)), ((), ())),
                preferred_element_type=jnp.float32,
            )
        )
    relation_grad = lax.psum(jnp.stack(rel_terms), ("dom", "rep"))
    grad_send = jnp.where(filled[:, None], jnp.take(tail_grad, source, axis=0), 0.0)
    grad_recv = lax.all_to_all(
        grad_send.reshape(part_count, capacity, columns),
        "dom",
        split_axis=0,
        concat_axis=0,
        tiled=True,
    )
    owned = lax.psum_scatter(neg_grad, "dom", scatter_dimension=0, tiled=True)
    target_ids = jnp.concatenate([head_local, recv_ids.reshape(-1), neg_local])
    target_rows = jnp.concatenate(
        [head_grad, grad_recv.reshape(slot_count, columns), owned], axis=0
    )
    block_rows = min(512, ent_dev)
    block_count = ent_dev // block_rows

    def add_block(start):
        hot = (
            target_ids[None, :] == (start + jnp.arange(block_rows, dtype=jnp.int32))[:, None]
        ).astype(jnp.float32)
        return jnp.dot(
            hot, target_rows, precision=lax.Precision.HIGHEST, preferred_element_type=jnp.float32
        )

    local_grad = lax.map(add_block, jnp.arange(block_count, dtype=jnp.int32) * block_rows).reshape(
        ent_dev, columns
    )
    entity_grad = lax.psum(local_grad, "rep")
    return (entity_grad, relation_grad, edge_loss)


def solution(mesh):
    return jax.shard_map(
        local,
        mesh=mesh,
        in_specs=(
            P("dom", None),
            P(),
            P(("dom", "rep")),
            P(("dom", "rep")),
            P(("dom", "rep"), None),
            P(("dom", "rep")),
            P("dom"),
        ),
        out_specs=(P("dom", None), P(), P(("dom", "rep"))),
        check_vma=False,
    )
```

profile of v0, /device:TPU:0, one launch (start us, length us, event | category | flops | bytes accessed | tf_op | source)
XLA Modules:
  0.0 350.4 jit_solution(16507864653260838199)
XLA Ops:
  8.0 0.8 fusion.55
  8.8 1.1 reduce-window.6
  9.9 0.2 slice_reduce_fusion
  10.2 0.8 fusion.54
  11.0 0.7 compare_and_fusion.2
  11.7 0.6 convert_reduce_fusion
  12.4 6.9 %gather_fusion = s32[1024]{0:T(1024)S(1)} fusion(s32[512]{0:T(512)S(1)} %copy-done.1, s32[1024]{0:T(1024)S(1)} %broadcast_clamp_fusion.1), kind=kCustom, calls=%fused_computation.2 | custom fusion | bytes 12288 | tf_op jit(solution)/shard_map/jit(_take)/gather | solution.py:41
  19.3 0.6 fusion.56
  19.9 7.3 %all-to-all-start = ((s32[8,1,128]{2,1,0:T(1,128)}), s32[8,1,128]{2,1,0:T(1,128)S(1)}, u32[]{:S(2)}, u32[]{:S(2)}) async-start(s32[8,1,128]{2,1,0:T(1,128)} %bitcast.11), calls=%async_computation | async-start | bytes 8192 | tf_op jit(solution)/shard_map/all_to_all | solution.py:44
  27.2 6.3 %all-to-all-done = s32[8,1,128]{2,1,0:T(1,128)S(1)} async-done(((s32[8,1,128]{2,1,0:T(1,128)}), s32[8,1,128]{2,1,0:T(1,128)S(1)}, u32[]{:S(2)}, u32[]{:S(2)}) %all-to-all-start) | async-done | bytes 4128 | tf_op jit(solution)/shard_map/all_to_all | solution.py:44
  33.5 4.0 %gather_fusion.1 = bf16[1024,512]{1,0:T(8,128)(2,1)S(1)} fusion(bf16[1024,512]{1,0:T(8,128)(2,1)S(1)} %copy-done, s32[1024]{0:T(1024)S(1)} %broadcast_clamp_fusion), kind=kCustom, calls=%fused_computation.3 | custom fusion | bytes 2101248 | tf_op jit(solution)/shard_map/jit(_take)/gather | solution.py:45
  37.5 1.2 broadcast_select_fusion
  38.7 3.6 %all-to-all-start.1 = ((bf16[8,128,512]{2,1,0:T(8,128)(2,1)}), bf16[8,128,512]{2,1,0:T(8,128)(2,1)S(1)}, u32[]{:S(2)}, u32[]{:S(2)}) async-start(bf16[8,128,512]{2,1,0:T(8,128)(2,1)} %broadcast_select_fusion), calls=%async_computation.1 | async-start | bytes 2097152 | tf_op jit(solution)/shard_map/all_to_all | solution.py:48
  42.3 2.0 gather_fusion.4
  44.3 0.2 copy.28
  44.5 0.6 gather_fusion.2
  45.1 0.1 broadcast_select_fusion.23
  45.2 42.2 %all_gather.3 = bf16[256,512]{1,0:T(8,128)(2,1)S(1)} all-gather(bf16[32,512]{1,0:T(8,128)(2,1)S(1)} %broadcast_select_fusion.23), channel_id=1, replica_groups=mesh['dom'=8,'rep'=4] {'dom'}, dimensions={0}, use_global_device_ids=true | all-gather | bytes 294912 | tf_op jit(solution)/shard_map/all_gather | solution.py:51
  87.4 1.5 fusion.22
  89.0 0.5 convolution_add_fusion.5
  89.5 1.5 convolution_add_fusion.4
  90.9 2.0 gather_fusion.5
  92.9 0.2 copy.29
  93.1 2.1 fusion.13
  95.3 0.3 fusion.78
  95.6 0.1 fusion.32
  95.7 0.6 broadcast_multiply_fusion
  96.3 0.0 copy-done.9
  96.4 0.1 convert_multiply_fusion.2
  96.5 0.3 copy.31
  96.9 4.9 %gather_fusion.3 = f32[1024,512]{1,0:T(8,128)} fusion(f32[512,512]{1,0:T(8,128)S(1)} %copy.31, s32[1024]{0:T(1024)S(1)} %broadcast_clamp_fusion.1), kind=kCustom, calls=%fused_computation.5 | custom fusion | bytes 4198400 | tf_op jit(solution)/shard_map/jit(_take)/gather | solution.py:96
  101.7 2.8 select_select_fusion
  104.5 3.7 %all-to-all-start.2 = ((f32[8,128,512]{2,1,0:T(8,128)}), f32[8,128,512]{2,1,0:T(8,128)S(1)}, u32[]{:S(2)}, u32[]{:S(2)}) async-start(f32[8,128,512]{2,1,0:T(8,128)} %select_select_fusion), calls=%async_computation.2 | async-start | bytes 4194304 | tf_op jit(solution)/shard_map/all_to_all | solution.py:97
  108.2 0.0 reduce-scatter.2.cloned.1.call-start
  108.3 2.3 convolution_multiply_fusion.1
  110.6 0.0 reduce-scatter.2.cloned.1.call-update
  110.7 0.0 all-reduce.5.cloned.1.call-start
  110.7 1.6 fusion.11
  112.4 0.5 convolution_bitcast_fusion
  112.9 0.5 convolution_bitcast_fusion.1
  113.3 0.5 convolution_bitcast_fusion.2
  113.8 0.5 convolution_bitcast_fusion.3
  114.3 2.5 pad_maximum_fusion
  116.7 0.0 all-reduce.5.cloned.1.call-update
  116.8 0.2 all-reduce.3.cloned.1.call-start
  117.0 1.7 fusion.20
  118.8 1.7 convolution_add_fusion.2
  120.5 0.0 copy-done.8
  120.5 0.5 convolution_add_fusion.1
  121.0 1.5 convolution_add_fusion
  122.5 79.0 %reduce-scatter.2.cloned.1.call-done = f32[32,512]{1,0:T(8,128)} async-done(((f32[256,512]{1,0:T(8,128)}), f32[32,512]{1,0:T(8,128)}) %reduce-scatter.2.cloned.1.call-update) | async-done | bytes 65552 | tf_op jit(solution)/shard_map/reduce_scatter | solution.py:104
  201.5 3.3 pad_maximum_fusion.1
  204.8 14.8 %while.10 = (s32[]{:T(128)}, f32[2,512,512]{2,1,0:T(8,128)}, s32[1568]{0:T(1024)S(1)}, s32[2]{0:T(128)S(1)}, f32[1568,512]{1,0:T(8,128)}, /*index=5*/s32[]{:T(128)}) while((s32[]{:T(128)}, f32[2,512,512]{2,1,0:T(8,128)}, s32[1568]{0:T(1024)S(1)}, s32[2]{0:T(128)S(1)}, f32[1568,512]{1,0:T(8,128)}, /*index=5*/s32[]{:T(128)}) %tuple.35), condition=%wide.region_10.12_spmd, body=%wide.region_9.11_spmd.sunk | while | flops 4933304832 | bytes 4270305 | solution.py:120
  204.8 0.6 dynamic_slice.5
  205.4 0.6 iota_add_fusion.2
  206.1 6.1 %fusion.93 = f32[2,512,512]{2,1,0:T(8,128)} fusion(f32[2,512,512]{2,1,0:T(8,128)} %get-tuple-element.99, s32[]{:T(128)S(6)} %copy.36, f32[1568,512]{1,0:T(8,128)} %get-tuple-element.108, s32[1568]{0:T(1024)S(1)} %get-tuple-element.106, s32[512]{0:T(512)S(1)} %iota_add_fusion.2), kind=kOutput, calls=%fused_computation.11.clone.1 | convolution fusion | flops 4933304320 | bytes 4268164 | tf_op jit(solution)/shard_map/while/body/eval_jaxpr/dot_general | solution.py:116
  212.2 0.6 dynamic_slice.5
  212.8 0.6 iota_add_fusion.2
  213.5 6.1 %fusion.93 = f32[2,512,512]{2,1,0:T(8,128)} fusion(f32[2,512,512]{2,1,0:T(8,128)} %get-tuple-element.99, s32[]{:T(128)S(6)} %copy.36, f32[1568,512]{1,0:T(8,128)} %get-tuple-element.108, s32[1568]{0:T(1024)S(1)} %get-tuple-element.106, s32[512]{0:T(512)S(1)} %iota_add_fusion.2), kind=kOutput, calls=%fused_computation.11.clone.1 | convolution fusion | flops 4933304320 | bytes 4268164 | tf_op jit(solution)/shard_map/while/body/eval_jaxpr/dot_general | solution.py:116
  219.6 0.0 all-reduce.3.cloned.1.call-update
  219.6 65.1 %all-reduce.5.cloned.1.call-done = f32[4,512,512]{2,1,0:T(8,128)} async-done(((f32[4,512,512]{2,1,0:T(8,128)}), f32[4,512,512]{2,1,0:T(8,128)}) %all-reduce.5.cloned.1.call-update) | async-done | bytes 4194320 | tf_op jit(solution)/shard_map/psum | solution.py:95
  284.7 53.1 %all-reduce.3.cloned.1.call-done = f32[1024,512]{1,0:T(8,128)} async-done(((f32[1024,512]{1,0:T(8,128)}), f32[1024,512]{1,0:T(8,128)}) %all-reduce.3.cloned.1.call-update) | async-done | bytes 2097168 | tf_op jit(solution)/shard_map/psum | solution.py:123
  337.7 3.2 copy.44
  341.0 2.0 copy.45
  (50 shorter events, 0.2 us)
Async XLA Ops:
  8.0 25.5 %copy-start = (bf16[1024,512]{1,0:T(8,128)(2,1)S(1)}, bf16[1024,512]{1,0:T(8,128)(2,1)}, u32[]{:S(2)}) copy-start(bf16[1024,512]{1,0:T(8,128)(2,1)} %param.11) | copy-start | bytes 3145732
  8.0 4.3 %copy-start.1 = (s32[512]{0:T(512)S(1)}, s32[512]{0:T(512)}, u32[]{:S(2)}) copy-start(s32[512]{0:T(512)} %param.16) | copy-start | bytes 6148
  12.4 14.8 %copy-start.12 = (s32[512]{0:T(512)S(1)}, s32[512]{0:T(512)}, u32[]{:S(2)}) copy-start(s32[512]{0:T(512)} %param.13) | copy-start | bytes 6148
  12.4 14.8 %copy-start.14 = (s32[32]{0:T(128)S(1)}, s32[32]{0:T(128)}, u32[]{:S(2)}) copy-start(s32[32]{0:T(128)} %param.17) | copy-start | bytes 388
  19.9 13.6 %all-to-all-start = ((s32[8,1,128]{2,1,0:T(1,128)}), s32[8,1,128]{2,1,0:T(1,128)S(1)}, u32[]{:S(2)}, u32[]{:S(2)}) async-start(s32[8,1,128]{2,1,0:T(1,128)} %bitcast.11), calls=%async_computation | async-start | bytes 8192 | tf_op jit(solution)/shard_map/all_to_all | solution.py:44
  38.7 52.2 %all-to-all-start.1 = ((bf16[8,128,512]{2,1,0:T(8,128)(2,1)}), bf16[8,128,512]{2,1,0:T(8,128)(2,1)S(1)}, u32[]{:S(2)}, u32[]{:S(2)}) async-start(bf16[8,128,512]{2,1,0:T(8,128)(2,1)} %broadcast_select_fusion), calls=%async_computation.1 | async-start | bytes 2097152 | tf_op jit(solution)/shard_map/all_to_all | solution.py:48
  42.3 45.1 %copy-start.13 = (s32[512]{0:T(512)S(1)}, s32[512]{0:T(512)}, u32[]{:S(2)}) copy-start(s32[512]{0:T(512)} %param.14) | copy-start | bytes 6148
  44.5 48.7 %copy-start.2 = (bf16[512,512]{0,1:T(8,128)(2,1)}, bf16[512,512]{0,1:T(8,128)(2,1)S(1)}, u32[]{:S(2)}) copy-start(bf16[512,512]{0,1:T(8,128)(2,1)S(1)} %copy.28) | copy-start | bytes 1572868
  45.1 43.8 %copy-start.7 = (bf16[4,512,512]{2,1,0:T(8,128)(2,1)S(1)}, bf16[4,512,512]{2,1,0:T(8,128)(2,1)}, u32[]{:S(2)}) copy-start(bf16[4,512,512]{2,1,0:T(8,128)(2,1)} %param.12) | copy-start | bytes 6291460
  93.1 2.1 copy-start.11
  95.2 1.1 copy-start.10
  95.6 0.8 copy-start.9
  104.5 97.1 %all-to-all-start.2 = ((f32[8,128,512]{2,1,0:T(8,128)}), f32[8,128,512]{2,1,0:T(8,128)S(1)}, u32[]{:S(2)}, u32[]{:S(2)}) async-start(f32[8,128,512]{2,1,0:T(8,128)} %select_select_fusion), calls=%async_computation.2 | async-start | bytes 4194304 | tf_op jit(solution)/shard_map/all_to_all | solution.py:97
  108.2 93.3 %reduce-scatter.2.cloned.1.call-start = ((), (), s32[]{:S(2)}) async-start(), calls=%async_computation.4 | async-start | bytes 589824 | tf_op jit(solution)/shard_map/reduce_scatter | solution.py:104
  110.7 174.0 %all-reduce.5.cloned.1.call-start = ((), (), s32[]{:S(2)}) async-start(), calls=%async_computation.6 | async-start | bytes 8388608 | tf_op jit(solution)/shard_map/psum | solution.py:95
  110.7 1.7 copy-start.3
  112.4 1.4 copy-start.4
  116.8 221.0 %all-reduce.3.cloned.1.call-start = ((), (), s32[]{:S(2)}) async-start(), calls=%async_computation.5 | async-start | bytes 4194304 | tf_op jit(solution)/shard_map/psum | solution.py:123
  117.0 1.8 copy-start.5
  118.8 1.8 copy-start.8
  337.7 3.2 copy-start.6
Sparse Core Ops, SparseCore 0:
  112.4 89.1 reduce-scatter.1
Sparse Core Ops, SparseCore 1:
  117.3 167.4 all-reduce.4
  287.6 50.1 all-reduce.2
where the time goes:
time: 351 us; the launch traced here: 350 us
  waiting for transfers between devices  203 us (58%)
  blocking collectives  42.2 us (12%)
  matrix products  29.4 us (8%)
  local copies, waits for them, and re-layouts  27.9 us (8%)
  other arithmetic  16.6 us (5%)
  between operations  15.9 us (5%)
  starting transfers between devices  14.8 us (4%)
    reduce_scatter x1, waiting for transfers between devices, local(): owned = lax.psum_scatter(neg_grad, 'dom', scatter_dimension=0, tiled=True)  79 us
    psum x1, waiting for transfers between devices, local(): relation_grad = lax.psum(jnp.stack(rel_terms), ('dom', 'rep'))  65.1 us
    psum x1, waiting for transfers between devices, local(): entity_grad = lax.psum(local_grad, 'rep')  53.1 us
    all_gather x1, blocking collectives, local(): negatives = lax.all_gather(own_negs, 'dom', axis=0, tiled=True)  42.2 us
    dot_general x2, matrix products, add_block(): jnp.dot(hot, target_rows, precision=lax.Precision.HIGHEST, preferred_elem...  12.3 us
    all_to_all x1, starting transfers between devices, local(): lax.all_to_all(send_ids, 'dom', split_axis=0, concat_axis=0, tiled=True)  7.25 us
  transfers between devices with their start and end apart: 6, of which 4 were waited for; matrix products, arithmetic and copies ran while one was open for 11% of the time, Pallas kernels for 0%

commit v1 on v0

v1 whole, which is shorter than its diff:
```python
import functools
import math

import jax
import jax.numpy as jnp
from jax import lax
from jax.experimental import pallas as pl
from jax.experimental.pallas import tpu as pltpu
from jax.sharding import PartitionSpec as P

BF = jnp.bfloat16
F32 = jnp.float32
VMEM = pl.BlockSpec(memory_space=pltpu.VMEM)
SMEM = pl.BlockSpec(memory_space=pltpu.SMEM)


def call(body, outs, scalars, *operands):
    return pl.pallas_call(
        body,
        out_shape=[jax.ShapeDtypeStruct(s, d) for s, d in outs],
        in_specs=[SMEM] * len(scalars) + [VMEM] * len(operands),
        out_specs=[VMEM] * len(outs),
        compiler_params=pltpu.CompilerParams(vmem_limit_bytes=40 * 1024 * 1024),
    )(*scalars, *operands)


def iota(shape, axis):
    return lax.broadcasted_iota(jnp.int32, shape, axis)


def as_column(row):
    size = row.shape[1]
    step = min(128, size)
    eye = iota((step, step), 0) == iota((step, step), 1)
    pieces = [
        jnp.sum(jnp.where(eye, row[:, at : at + step], 0), axis=1, keepdims=True)
        for at in range(0, size, step)
    ]
    return jnp.concatenate(pieces, axis=0)


def as_row(column):
    size = column.shape[0]
    step = min(128, size)
    eye = iota((step, step), 0) == iota((step, step), 1)
    pieces = [
        jnp.sum(jnp.where(eye, column[at : at + step, :], 0.0), axis=0, keepdims=True)
        for at in range(0, size, step)
    ]
    return jnp.concatenate(pieces, axis=1)


def hot_rows(row, count):
    return (as_column(row) == iota((row.shape[1], count), 1)).astype(F32).astype(BF)


def dot(a, b):
    return jnp.dot(a, b, preferred_element_type=F32)


def dot_t0(a, b):
    return lax.dot_general(a, b, (((0,), (0,)), ((), ())), preferred_element_type=F32)


def dot_t1(a, b):
    return lax.dot_general(a, b, (((1,), (1,)), ((), ())), preferred_element_type=F32)


def split(x):
    high = x.astype(BF)
    return high, (x - high.astype(F32)).astype(BF)


def slots_kernel(parts, cap, part_ref, tail_ref, neg_ref, ent_ref, ids_ref, slot_ref, negs_ref):
    edges = part_ref.shape[1]
    slots = parts * cap
    part = part_ref[...]
    tail = tail_ref[...]
    named = (iota((parts, edges), 0) == part).astype(F32)
    before = (iota((edges, edges), 0) < iota((edges, edges), 1)).astype(F32).astype(BF)
    earlier = dot(named.astype(BF), before)
    position = jnp.sum(earlier * named, axis=0, keepdims=True).astype(jnp.int32)
    slot = part * cap + position
    slot_ref[...] = slot
    placed = (iota((slots, edges), 0) == slot).astype(F32).astype(BF)
    which = iota((8, edges), 0)
    digits = jnp.where(which == 0, tail >> 7, jnp.where(which == 1, tail & 127, 0))
    found = dot_t1(digits.astype(F32).astype(BF), placed)
    ids_ref[...] = (found[0:1, :] * 128.0 + found[1:2, :]).astype(jnp.int32)
    negs_ref[...] = dot(hot_rows(neg_ref[...], ent_ref.shape[0]), ent_ref[...]).astype(BF)


def query_kernel(head_ref, rel_ref, slot_ref, ent_ref, op_ref, rows_ref, query_ref, sent_ref):
    rows = dot(hot_rows(head_ref[...], ent_ref.shape[0]), ent_ref[...]).astype(BF)
    rows_ref[...] = rows
    rel = as_column(rel_ref[...])
    total = jnp.zeros(rows.shape, F32)
    for relation in range(op_ref.shape[0]):
        picked = jnp.where(rel == relation, rows, jnp.zeros_like(rows))
        total = total + dot(picked, op_ref[relation])
    queries = total.astype(BF)
    query_ref[...] = queries
    slot = slot_ref[...]
    slots, edges = sent_ref.shape[0], slot.shape[1]
    placed = (iota((slots, edges), 0) == slot).astype(F32).astype(BF)
    sent_ref[...] = dot(placed, queries).astype(BF)


def lookup_kernel(ids_ref, ent_ref, rows_ref):
    rows_ref[...] = dot(hot_rows(ids_ref[...], ent_ref.shape[0]), ent_ref[...]).astype(BF)


def edge_kernel(
    factor,
    picks_ref,
    blocks_ref,
    query_ref,
    got_ref,
    slot_ref,
    negs_ref,
    rows_ref,
    rel_ref,
    loss_ref,
    weight_ref,
    grad_ref,
    prob_ref,
    rel_grad_ref,
):
    queries = query_ref[...]
    negatives = negs_ref[...]
    slots = got_ref.shape[0]
    edges, columns = queries.shape
    placed = as_column(slot_ref[...]) == iota((edges, slots), 1)
    tails = dot(placed.astype(F32).astype(BF), got_ref[...])
    positive = jnp.sum(queries.astype(F32) * tails, axis=1, keepdims=True) * factor
    scores = dot_t1(queries, negatives) * factor
    row_max = jnp.maximum(positive, jnp.max(scores, axis=1, keepdims=True))
    exp_pos = jnp.exp(positive - row_max)
    exp_neg = jnp.exp(scores - row_max)
    total = exp_pos + jnp.sum(exp_neg, axis=1, keepdims=True)
    loss_ref[...] = as_row(jnp.log(total) + row_max - positive)
    pull = exp_pos / total - 1.0
    prob = (exp_neg / total).astype(BF)
    prob_ref[...] = prob
    grad = (factor * (pull * tails + dot(prob, negatives))).astype(BF)
    grad_ref[...] = grad
    weight_ref[...] = jnp.sum(jnp.where(placed, factor * pull, 0.0), axis=0, keepdims=True)
    rel = as_column(rel_ref[...])
    relation_count, blocks = blocks_ref.shape[0] // 4, 4
    width = columns // blocks
    for place in range(relation_count):
        picked_grad = jnp.where(rel == picks_ref[place], grad, jnp.zeros_like(grad))
        for block in range(blocks):
            at = pl.multiple_of(blocks_ref[place * blocks + block] * width, width)
            rel_grad_ref[place, pl.ds(block * width, width), :] = dot_t0(
                rows_ref[:, pl.ds(at, width)], picked_grad
            ).astype(rel_grad_ref.dtype)


def back_kernel(factor, query_ref, prob_ref, grad_ref, rel_ref, op_ref, neg_ref, high_ref, low_ref):
    neg_ref[...] = (factor * dot_t0(prob_ref[...], query_ref[...])).astype(BF)
    rel = as_column(rel_ref[...])
    grad = grad_ref[...]
    total = jnp.zeros(grad.shape, F32)
    for relation in range(op_ref.shape[0]):
        picked = jnp.where(rel == relation, grad, jnp.zeros_like(grad))
        total = total + dot_t1(picked, op_ref[relation])
    high_ref[...], low_ref[...] = split(total)


def add_kernel(
    base_ref,
    ids_ref,
    weight_ref,
    query_ref,
    head_ref,
    high_ref,
    low_ref,
    neg_ref,
    neg_sum_ref,
    out_ref,
):
    count = out_ref.shape[0]
    base = base_ref[0]

    def hot(row):
        return (iota((count, row.shape[1]), 0) + base) == row

    tails = jnp.where(hot(ids_ref[...]), weight_ref[...], 0.0).astype(BF)
    total = dot(tails, query_ref[...])
    heads = hot(head_ref[...]).astype(F32).astype(BF)
    total = total + dot(heads, high_ref[...]) + dot(heads, low_ref[...])
    own = hot(neg_ref[...]).astype(F32).astype(BF)
    high, low = split(neg_sum_ref[...])
    out_ref[...] = (total + (dot(own, high) + dot(own, low))).astype(out_ref.dtype)


def join_kernel(core_ref, mine_ref, other_ref, out_ref):
    half = mine_ref.shape[0]
    at = pl.multiple_of(core_ref[0] * half, half)
    out_ref[pl.ds(at, half), :] = mine_ref[...]
    at = pl.multiple_of((1 - core_ref[0]) * half, half)
    out_ref[pl.ds(at, half), :] = other_ref[...]


def operator_kernel(picks_ref, blocks_ref, mine_ref, other_ref, out_ref):
    width = out_ref.shape[1] // 4
    for place in range(4):
        source = mine_ref if place < 2 else other_ref
        for block in range(4):
            at = pl.multiple_of(blocks_ref[place * 4 + block] * width, width)
            out_ref[picks_ref[place], pl.ds(at, width), :] = source[
                (place % 2) * 4 + block
            ].astype(F32)


def flip(x, axis, size, bit):
    return lax.ppermute(x, axis, [(i, i ^ bit) for i in range(size)])


def exchange(x):
    return lax.all_to_all(x, "dom", split_axis=0, concat_axis=0, tiled=True)


def local(special, entities, relations, head_local, rel_ids, tail_part, tail_local, neg_local):
    columns = entities.shape[1]
    factor = 1.0 / math.sqrt(columns)
    ent_dev = entities.shape[0]
    edges = head_local.shape[0]
    parts = lax.axis_size("dom")
    cap = 2 * edges // parts
    slots = parts * cap
    neg_dev = neg_local.shape[0]
    negs = parts * neg_dev
    count = relations.shape[0]
    head = head_local.reshape(1, edges)
    rel = rel_ids.reshape(1, edges)
    neg_own = neg_local.reshape(1, neg_dev)

    ids, slot, own_negs = call(
        functools.partial(slots_kernel, parts, cap),
        [((1, slots), jnp.int32), ((1, edges), jnp.int32), ((neg_dev, columns), BF)],
        (),
        tail_part.reshape(1, edges),
        tail_local.reshape(1, edges),
        neg_own,
        entities,
    )
    asked = exchange(ids.reshape(parts, cap)).reshape(1, slots)
    negatives = exchange(
        jnp.broadcast_to(own_negs[None], (parts, neg_dev, columns))
    ).reshape(negs, columns)
    rows, queries, sent = call(
        query_kernel,
        [((edges, columns), BF), ((edges, columns), BF), ((slots, columns), BF)],
        (),
        head,
        rel,
        slot,
        entities,
        relations,
    )
    (found,) = call(lookup_kernel, [((slots, columns), BF)], (), asked, entities)
    got = exchange(found.reshape(parts, cap, columns)).reshape(slots, columns)
    sent, got = lax.optimization_barrier((sent, got))
    tail_queries = exchange(sent.reshape(parts, cap, columns)).reshape(slots, columns)

    if special:
        dom = lax.axis_index("dom")
        rep = lax.axis_index("rep")
        z, x, y, core = dom // 2, dom % 2, rep // 2, rep % 2
        picks = jnp.stack([2 * core, 2 * core + 1, 2 - 2 * core, 3 - 2 * core])
        by_y = [(2 * y + x) ^ k for k in range(4)]
        by_x = [(2 * x + y) ^ k for k in range(4)]
        blocks = jnp.stack((by_y + by_x) * 2)
        part_type = BF
    else:
        picks = jnp.arange(count, dtype=jnp.int32)
        blocks = jnp.tile(jnp.arange(4, dtype=jnp.int32), count)
        part_type = F32
    loss, weight, grad, prob, rel_grad = call(
        functools.partial(edge_kernel, factor),
        [
            ((1, edges), F32),
            ((1, slots), F32),
            ((edges, columns), BF),
            ((edges, negs), BF),
            ((count, columns, columns), part_type),
        ],
        (picks, blocks),
        queries,
        got,
        slot,
        negatives,
        rows,
        rel,
    )
    neg_part, high, low = call(
        functools.partial(back_kernel, factor),
        [((negs, columns), BF), ((edges, columns), BF), ((edges, columns), BF)],
        (),
        queries,
        prob,
        grad,
        rel,
        relations,
    )
    weight_high, weight_low = split(weight.reshape(parts, 1, cap))
    weights = jnp.pad(
        jnp.concatenate([weight_high, weight_low], axis=1), ((0, 0), (0, 14), (0, columns - cap))
    )
    back = exchange(
        jnp.concatenate([neg_part.reshape(parts, neg_dev, columns), weights], axis=1)
    )
    neg_sum = jnp.sum(back[:, :neg_dev].astype(F32), axis=0)
    tail_weight = (
        back[:, neg_dev, :cap].astype(F32) + back[:, neg_dev + 1, :cap].astype(F32)
    ).reshape(1, slots)

    def add(base, size, kind):
        return call(
            add_kernel,
            [((size, columns), kind)],
            (base.reshape(1),),
            asked,
            tail_weight,
            tail_queries,
            head,
            high,
            low,
            neg_own,
            neg_sum,
        )[0]

    if not special:
        relation_grad = lax.psum(rel_grad, ("dom", "rep"))
        whole = add(jnp.zeros((), jnp.int32), ent_dev, F32)
        return lax.psum(whole, "rep"), relation_grad, loss.reshape(edges)

    half = columns // 2
    other = flip(rel_grad[2:], "rep", 4, 1)
    mine = rel_grad[:2].astype(F32) + other.astype(F32)
    first_y = flip(mine[0, half:].astype(BF), "rep", 4, 2)
    first_x = flip(mine[1, half:].astype(BF), "dom", 8, 1)
    half_y = mine[0, :half] + first_y.astype(F32)
    half_x = mine[1, :half] + first_x.astype(F32)
    quarter = half // 2
    second_x = flip(half_y[quarter:].astype(BF), "dom", 8, 1)
    second_y = flip(half_x[quarter:].astype(BF), "rep", 4, 2)
    piece = jnp.stack(
        [half_y[:quarter] + second_x.astype(F32), half_x[:quarter] + second_y.astype(F32)]
    ).astype(BF)
    along_z = [[0, 2, 4, 6], [1, 3, 5, 7]]
    stripe = quarter // 4
    spread = piece.reshape(2, 4, stripe, columns).swapaxes(0, 1)
    gathered = lax.all_to_all(spread, "dom", 0, 0, tiled=True, axis_index_groups=along_z)
    summed = jnp.sum(gathered.astype(F32), axis=0).astype(BF)
    everywhere = lax.all_to_all(
        jnp.broadcast_to(summed[None], (4, 2, stripe, columns)),
        "dom",
        0,
        0,
        tiled=True,
        axis_index_groups=along_z,
    )
    pair = everywhere.swapaxes(0, 1).reshape(2, quarter, columns)
    other_x = flip(pair[0], "dom", 8, 1)
    other_y = flip(pair[1], "rep", 4, 2)
    by_y_half = jnp.stack([pair[0], other_x])
    by_x_half = jnp.stack([pair[1], other_y])
    far_y = flip(by_y_half, "rep", 4, 2)
    far_x = flip(by_x_half, "dom", 8, 1)
    own_ops = jnp.concatenate([by_y_half, far_y, by_x_half, far_x], axis=0)
    other_ops = flip(own_ops, "rep", 4, 1)
    (relation_grad,) = call(
        operator_kernel,
        [((count, columns, columns), F32)],
        (picks, blocks),
        own_ops,
        other_ops,
    )

    rows_half = ent_dev // 2
    away = add((1 - core) * rows_half, rows_half, BF)
    arrived = flip(away, "rep", 4, 1)
    kept = add(core * rows_half, rows_half, F32)
    both = (kept + arrived.astype(F32)).astype(BF)
    across = flip(both, "rep", 4, 2)
    done = both.astype(F32) + across.astype(F32)
    partner = flip(done, "rep", 4, 1)
    (entity_grad,) = call(
        join_kernel, [((ent_dev, columns), F32)], (core.reshape(1),), done, partner
    )
    return entity_grad, relation_grad, loss.reshape(edges)


def solution(mesh):
    special = dict(mesh.shape) == {"dom": 8, "rep": 4}
    return jax.shard_map(
        functools.partial(local, special),
        mesh=mesh,
        in_specs=(
            P("dom", None),
            P(),
            P(("dom", "rep")),
            P(("dom", "rep")),
            P(("dom", "rep"), None),
            P(("dom", "rep")),
            P("dom"),
        ),
        out_specs=(P("dom", None), P(), P(("dom", "rep"))),
        check_vma=False,
    )
```

time: 351 us -> 181 us (0.52)
  waiting for transfers between devices: 203 us -> 62.1 us
  matrix products: 29.4 us -> 0 us
  Pallas kernels: 0 us -> 19.9 us
  local copies, waits for them, and re-layouts: 27.9 us -> 12.2 us
  starting transfers between devices: 14.8 us -> 30 us
  between operations: 15.9 us -> 1 us
  other arithmetic: 16.6 us -> 3.05 us
  blocking collectives: 42.2 us -> 51.5 us
    psum x2 -> x0, waiting for transfers between devices: 118 us -> none  [the longest x1 65.1 us: local(): relation_grad = lax.psum(jnp.stack(rel_terms), ('dom', 'rep'))]
    reduce_scatter x1 -> x0, waiting for transfers between devices: 79 us -> none  [local(): owned = lax.psum_scatter(neg_grad, 'dom', scatter_dimension=0, tiled=True)]
    all_to_all x0 -> x3, blocking collectives: none -> 51.5 us  [the longest x2 41.2 us: exchange(): return lax.all_to_all(x, 'dom', split_axis=0, concat_axis=0, tiled=True)]
    all_gather x1 -> x0, blocking collectives: 42.2 us -> none  [local(): negatives = lax.all_gather(own_negs, 'dom', axis=0, tiled=True)]
    dot_general x17 -> x0, matrix products: 29.4 us -> none  [the longest x2 12.3 us: add_block(): jnp.dot(hot, target_rows, precision=lax.Precision.HIGHEST, preferred_elem...]
    all_to_all x3 -> x4, waiting for transfers between devices: 6.32 us -> 34.4 us  [the longest x3 31.5 us: exchange(): return lax.all_to_all(x, 'dom', split_axis=0, concat_axis=0, tiled=True)]
    ppermute x0 -> x13, waiting for transfers between devices: none -> 27.7 us  [flip(): return lax.ppermute(x, axis, [(i, i ^ bit) for i in range(size)])]
    gather x8 -> x0, local copies, waits for them, and re-layouts: 20.7 us -> none  [the longest x1 6.87 us: local(): jnp.take(tail_local, source, axis=0)]
  transfers between devices with their start and end apart: 6 -> 17, of which waited for: 4 -> 12; matrix products, arithmetic and copies ran while one was open for 11% -> 2% of each run, Pallas kernels for 0% -> 7%
where the time goes in v1:
time: 181 us; the launch traced here: 180 us
  waiting for transfers between devices  62.1 us (34%)
  blocking collectives  51.5 us (28%)
  starting transfers between devices  30 us (17%)
  Pallas kernels  19.9 us (11%)
  local copies, waits for them, and re-layouts  12.2 us (7%)
  other arithmetic  3.05 us (2%)
    all_to_all x2, blocking collectives, exchange(): return lax.all_to_all(x, 'dom', split_axis=0, concat_axis=0, tiled=True)  41.2 us
    all_to_all x3, waiting for transfers between devices, exchange(): return lax.all_to_all(x, 'dom', split_axis=0, concat_axis=0, tiled=True)  31.5 us
    ppermute x13, waiting for transfers between devices, flip(): return lax.ppermute(x, axis, [(i, i ^ bit) for i in range(size)])  27.7 us
    pallas_call x9, Pallas kernels, call(): pl.pallas_call(body, out_shape=[jax.ShapeDtypeStruct(s, d) for s, d in ou...  19.9 us
    ppermute x13, starting transfers between devices, flip(): return lax.ppermute(x, axis, [(i, i ^ bit) for i in range(size)])  14.4 us
    all_to_all x3, starting transfers between devices, exchange(): return lax.all_to_all(x, 'dom', split_axis=0, concat_axis=0, tiled=True)  11.3 us
    all_to_all x1, blocking collectives, local(): lax.all_to_all(spread, 'dom', 0, 0, tiled=True, axis_index_groups=along_z)  10.3 us
    unnamed x43, local copies, waits for them, and re-layouts  9.46 us
  transfers between devices with their start and end apart: 17, of which 12 were waited for; matrix products, arithmetic and copies ran while one was open for 2% of the time, Pallas kernels for 7%

profile of v1, /device:TPU:0, one launch (start us, length us, event | category | flops | bytes accessed | tf_op | source)
XLA Modules:
  0.0 179.7 jit_solution(4826762574599839508)
XLA Ops:
  0.6 0.0 copy-start
  0.6 1.2 copy-done
  1.9 0.7 copy-done.15
  2.5 0.7 copy-done.17
  3.2 0.7 copy-done.18
  3.9 0.8 shard_map.94
  4.7 13.5 %all_to_all.39 = s32[8,1,128]{2,1,0:T(1,128)S(1)} all-to-all(s32[8,1,128]{2,1,0:T(1,128)S(1)} %bitcast.89), channel_id=1, replica_groups=mesh['dom'=8,'rep'=4] {'dom'}, dimensions={0} | all-to-all | bytes 8192 | tf_op jit(solution)/shard_map/all_to_all | solution.py:222
  18.2 1.2 copy-done.1
  19.4 1.7 shard_map.96
  21.1 27.7 %all_to_all.40 = bf16[8,128,512]{2,1,0:T(8,128)(2,1)} all-to-all(bf16[8,128,512]{2,1,0:T(8,128)(2,1)S(1)} %bitcast.74), channel_id=1, replica_groups=mesh['dom'=8,'rep'=4] {'dom'}, dimensions={0} | all-to-all | bytes 2097152 | tf_op jit(solution)/shard_map/all_to_all | solution.py:222
  48.8 0.7 broadcast_in_dim.4
  49.5 3.6 %all-to-all-start.2 = ((bf16[8,32,512]{2,1,0:T(8,128)(2,1)}), bf16[8,32,512]{2,1,0:T(8,128)(2,1)S(1)}, u32[]{:S(2)}, u32[]{:S(2)}) async-start(bf16[8,32,512]{2,1,0:T(8,128)(2,1)} %broadcast_in_dim.4), calls=%async_computation.2 | async-start | bytes 524288 | tf_op jit(solution)/shard_map/all_to_all | solution.py:222
  53.2 3.7 %shard_map.95 = (bf16[512,512]{1,0:T(8,128)(2,1)S(1)}, bf16[512,512]{1,0:T(8,128)(2,1)S(1)}, bf16[1024,512]{1,0:T(8,128)(2,1)}) custom-call(s32[1,512]{1,0:T(1,128)S(1)} %bitcast.83, s32[1,512]{1,0:T(1,128)S(1)} %bitcast.80, s32[1,512]{1,0:T(1,128)S(1)} %get-tuple-element.20.slot_ref, bf16[1024,512]{1,0:T(8,128)(2,1)S(1)} %copy-done.2, ...), custom_call_target="tpu_custom_call" | custom-call | tf_op jit(solution)/shard_map/pallas_call | solution.py:18
  56.9 0.8 copy-done.9
  57.6 0.8 copy-done.11
  58.4 0.1 stack.84.blocks_ref
  58.5 0.1 pad_add_fusion.picks_ref
  58.6 3.0 %all-to-all-done.2 = bf16[8,32,512]{2,1,0:T(8,128)(2,1)S(1)} async-done(((bf16[8,32,512]{2,1,0:T(8,128)(2,1)}), bf16[8,32,512]{2,1,0:T(8,128)(2,1)S(1)}, u32[]{:S(2)}, u32[]{:S(2)}) %all-to-all-start.2) | async-done | bytes 262176 | tf_op jit(solution)/shard_map/all_to_all | solution.py:222
  61.7 1.2 copy-done.4
  62.9 1.0 copy-done.10
  63.9 1.0 copy-done.12
  65.0 3.9 %shard_map.97 = (f32[1,512]{1,0:T(1,128)}, f32[1,1024]{1,0:T(1,128)S(1)}, bf16[512,512]{1,0:T(8,128)(2,1)S(1)}, bf16[512,256]{1,0:T(8,128)(2,1)S(1)}, bf16[4,512,512]{2,1,0:T(8,128)(2,1)S(1)}) custom-call(s32[4]{0:T(128)S(1)} %pad_add_fusion.picks_ref, s32[16]{0:T(128)S(1)} %stack.84.blocks_ref, bf16[512,512]{1,0:T(8,128)(2,1)S(1)} %copy-done.10, ...), custom_call_target="tpu_custom_call" | custom-call | tf_op jit(solution)/shard_map/pallas_call | solution.py:18
  68.8 0.1 slice.61
  68.9 0.1 collective-permute-start.3
  69.0 1.7 shard_map.98
  70.7 0.0 copy-start.5
  70.7 0.9 collective-permute-done.3
  71.6 0.4 fusion.13
  72.1 1.6 collective-permute-start.4
  73.7 1.4 collective-permute-start.6
  75.1 5.4 %collective-permute-done.4 = bf16[256,512]{1,0:T(8,128)(2,1)S(1)} collective-permute-done((bf16[256,512]{1,0:T(8,128)(2,1)S(1)}, bf16[256,512]{1,0:T(8,128)(2,1)S(1)}, u32[]{:S(2)}, u32[]{:S(2)}) %collective-permute-start.4) | collective-permute-done | bytes 262176 | tf_op jit(solution)/shard_map/ppermute | solution.py:218
  80.5 1.2 collective-permute-done.6
  81.8 0.2 fusion.1
  82.0 0.6 collective-permute-start.7
  82.5 0.8 pad_maximum_fusion
  83.3 3.5 %all-to-all-start.3 = ((bf16[8,48,512]{2,1,0:T(8,128)(2,1)}), bf16[8,48,512]{2,1,0:T(8,128)(2,1)S(1)}, u32[]{:S(2)}, u32[]{:S(2)}) async-start(bf16[8,48,512]{2,1,0:T(8,128)(2,1)} %pad_maximum_fusion), calls=%async_computation.3 | async-start | bytes 786432 | tf_op jit(solution)/shard_map/all_to_all | solution.py:222
  86.8 2.1 %collective-permute-start.5 = (bf16[128,512]{1,0:T(8,128)(2,1)S(1)}, bf16[128,512]{1,0:T(8,128)(2,1)S(1)}, u32[]{:S(2)}, u32[]{:S(2)}) collective-permute-start(bf16[128,512]{1,0:T(8,128)(2,1)S(1)} %slice.116), channel_id=1, source_target_pairs={{0,4},{4,0},{8,12},{12,8},{16,20},{20,16},{24,28},{28,24},{1,5},{5... | collective-permute-start | bytes 393224 | tf_op jit(solution)/shard_map/ppermute | solution.py:218
  88.9 5.6 %collective-permute-done.5 = bf16[128,512]{1,0:T(8,128)(2,1)S(1)} collective-permute-done((bf16[128,512]{1,0:T(8,128)(2,1)S(1)}, bf16[128,512]{1,0:T(8,128)(2,1)S(1)}, u32[]{:S(2)}, u32[]{:S(2)}) %collective-permute-start.5) | collective-permute-done | bytes 131104 | tf_op jit(solution)/shard_map/ppermute | solution.py:218
  94.6 0.0 copy-start.6
  94.6 3.0 %all-to-all-done.3 = bf16[8,48,512]{2,1,0:T(8,128)(2,1)S(1)} async-done(((bf16[8,48,512]{2,1,0:T(8,128)(2,1)}), bf16[8,48,512]{2,1,0:T(8,128)(2,1)S(1)}, u32[]{:S(2)}, u32[]{:S(2)}) %all-to-all-start.3) | async-done | bytes 393248 | tf_op jit(solution)/shard_map/all_to_all | solution.py:222
  97.6 10.3 %all_to_all.41 = bf16[4,2,32,512]{3,2,1,0:T(8,128)(2,1)S(1)} all-to-all(bf16[4,2,32,512]{3,2,1,0:T(8,128)(2,1)S(1)} %maximum_bitcast_fusion), channel_id=1, replica_groups={{0,8,16,24},{4,12,20,28},{1,9,17,25},{5,13,21,29},{2,10,18,26},{6,14,22..., dimensions={0} | all-to-all | bytes 524288 | tf_op jit(solution)/shard_map/all_to_all | solution.py:356
  107.9 4.2 %all-to-all-start.4 = ((bf16[8,128,512]{2,1,0:T(8,128)(2,1)}), bf16[8,128,512]{2,1,0:T(8,128)(2,1)S(1)}, u32[]{:S(2)}, u32[]{:S(2)}) async-start(bf16[8,128,512]{2,1,0:T(8,128)(2,1)} %bitcast.30), calls=%async_computation.4 | async-start | bytes 2097152 | tf_op jit(solution)/shard_map/all_to_all | solution.py:222
  112.3 25.4 %all-to-all-done.4 = bf16[8,128,512]{2,1,0:T(8,128)(2,1)S(1)} async-done(((bf16[8,128,512]{2,1,0:T(8,128)(2,1)}), bf16[8,128,512]{2,1,0:T(8,128)(2,1)S(1)}, u32[]{:S(2)}, u32[]{:S(2)}) %all-to-all-start.4) | async-done | bytes 1048608 | tf_op jit(solution)/shard_map/all_to_all | solution.py:222
  137.7 0.7 broadcast_in_dim.5
  138.4 4.2 %all-to-all-start.6 = ((bf16[4,2,32,512]{3,2,1,0:T(8,128)(2,1)}), bf16[4,2,32,512]{3,2,1,0:T(8,128)(2,1)}, u32[]{:S(2)}, u32[]{:S(2)}) async-start(bf16[4,2,32,512]{3,2,1,0:T(8,128)(2,1)} %broadcast_in_dim.5), calls=%async_computation.6 | async-start | bytes 524288 | tf_op jit(solution)/shard_map/all_to_all | solution.py:358
  142.7 2.3 %shard_map.100 = bf16[512,512]{1,0:T(8,128)(2,1)} custom-call(s32[1]{0:T(128)} %bitcast.32.base_ref, s32[1,1024]{1,0:T(1,128)S(1)} %bitcast.78, f32[1,1024]{1,0:T(1,128)S(1)} %fusion.11.weight_ref, bf16[1024,512]{1,0:T(8,128)(2,1)S(1)} %bitcast.71, s32[1,512]{1,0:T(1,128)S(1)} %bitcast.84, bf16[512,512]{1,0:T(8,128)(2,1)S(1)} %copy-done.6, ...), custom_call_target="tpu_custom_call" | custom-call | tf_op jit(solution)/shard_map/pallas_call | solution.py:18
  145.1 1.5 shard_map.99
  146.6 3.0 %all-to-all-done.6 = bf16[4,2,32,512]{3,2,1,0:T(8,128)(2,1)} async-done(((bf16[4,2,32,512]{3,2,1,0:T(8,128)(2,1)}), bf16[4,2,32,512]{3,2,1,0:T(8,128)(2,1)}, u32[]{:S(2)}, u32[]{:S(2)}) %all-to-all-start.6) | async-done | bytes 262176 | tf_op jit(solution)/shard_map/all_to_all | solution.py:358
  149.5 1.0 fusion.14
  150.5 2.7 %collective-permute-start.8 = (bf16[128,512]{1,0:T(8,128)(2,1)S(1)}, bf16[128,512]{1,0:T(8,128)(2,1)S(1)}, u32[]{:S(2)}, u32[]{:S(2)}) collective-permute-start(bf16[128,512]{1,0:T(8,128)(2,1)S(1)} %bitcast.95), channel_id=1, source_target_pairs={{0,4},{4,0},{8,12},{12,8},{16,20},{20,16},{24,28},{28,24},{1,5},{5... | collective-permute-start | bytes 393224 | tf_op jit(solution)/shard_map/ppermute | solution.py:218
  153.2 1.4 collective-permute-start.10
  154.6 1.2 add_convert_fusion
  155.8 0.7 collective-permute-start.1
  156.5 0.1 collective-permute-done.8
  156.6 1.9 %collective-permute-start.9 = (bf16[2,128,512]{2,1,0:T(8,128)(2,1)S(1)}, bf16[2,128,512]{2,1,0:T(8,128)(2,1)S(1)}, u32[]{:S(2)}, u32[]{:S(2)}) collective-permute-start(bf16[2,128,512]{2,1,0:T(8,128)(2,1)S(1)} %pad_maximum_fusion.1), channel_id=1, source_target_pairs={{0,2},{1,3},{2,0},{3,1},{4,6},{5,7},{6,4},{7,5},{8,10},{9,11},{10,... | collective-permute-start | bytes 786440 | tf_op jit(solution)/shard_map/ppermute | solution.py:218
  158.5 1.1 collective-permute-done.10
  159.6 1.5 collective-permute-start.11
  161.1 11.4 %collective-permute-done.9 = bf16[2,128,512]{2,1,0:T(8,128)(2,1)S(1)} collective-permute-done((bf16[2,128,512]{2,1,0:T(8,128)(2,1)S(1)}, bf16[2,128,512]{2,1,0:T(8,128)(2,1)S(1)}, u32[]{:S(2)}, u32[]{:S(2)}) %collective-permute-start.9) | collective-permute-done | bytes 262176 | tf_op jit(solution)/shard_map/ppermute | solution.py:218
  172.6 0.1 collective-permute-start.12
  172.7 0.1 convert_add_fusion.1.mine_ref
  172.9 0.6 collective-permute-start.2
  173.4 1.9 %collective-permute-done.12.other_ref = bf16[8,128,512]{2,1,0:T(8,128)(2,1)S(1)} collective-permute-done((bf16[8,128,512]{2,1,0:T(8,128)(2,1)S(1)}, bf16[8,128,512]{2,1,0:T(8,128)(2,1)S(1)}, u32[]{:S(2)}, u32[]{:S(2)}) %collective-permute-start.12) | collective-permute-done | bytes 1048608 | tf_op jit(solution)/shard_map/ppermute | solution.py:218
  175.4 2.8 %shard_map.102 = f32[4,512,512]{2,1,0:T(8,128)} custom-call(s32[4]{0:T(128)S(1)} %pad_add_fusion.picks_ref, s32[16]{0:T(128)S(1)} %stack.84.blocks_ref, bf16[8,128,512]{2,1,0:T(8,128)(2,1)S(1)} %constant_dynamic-update-slice_fusion.mine_ref, bf16[8,128,512]{2,1,0:T(8,128)(2,1)S(1)} %collective-permute-done.12.other_ref), custom_call_target="tpu_custom_call" | custom-call | tf_op jit(solution)/shard_map/pallas_call | solution.py:18
  178.2 1.5 shard_map.101
  (51 shorter events, 0.5 us)
Async XLA Ops:
  0.6 1.2 copy-start
  1.9 0.7 copy-start.15
  2.5 0.7 copy-start.17
  3.2 0.7 copy-start.18
  18.2 1.2 copy-start.1
  19.4 33.7 %copy-start.2 = (bf16[1024,512]{1,0:T(8,128)(2,1)S(1)}, bf16[1024,512]{1,0:T(8,128)(2,1)}, u32[]{:S(2)}) copy-start(bf16[1024,512]{1,0:T(8,128)(2,1)} %ent_ref.5) | copy-start | bytes 3145732
  19.4 33.7 %copy-start.3 = (bf16[4,512,512]{2,1,0:T(8,128)(2,1)S(1)}, bf16[4,512,512]{2,1,0:T(8,128)(2,1)}, u32[]{:S(2)}) copy-start(bf16[4,512,512]{2,1,0:T(8,128)(2,1)} %op_ref.3) | copy-start | bytes 6291460
  19.4 33.7 %copy-start.13 = (s32[512]{0:T(512)S(1)}, s32[512]{0:T(512)}, u32[]{:S(2)}) copy-start(s32[512]{0:T(512)} %param.10) | copy-start | bytes 6148
  19.4 33.7 %copy-start.14 = (s32[512]{0:T(512)S(1)}, s32[512]{0:T(512)}, u32[]{:S(2)}) copy-start(s32[512]{0:T(512)} %param.9) | copy-start | bytes 6148
  49.5 12.1 %all-to-all-start.2 = ((bf16[8,32,512]{2,1,0:T(8,128)(2,1)}), bf16[8,32,512]{2,1,0:T(8,128)(2,1)S(1)}, u32[]{:S(2)}, u32[]{:S(2)}) async-start(bf16[8,32,512]{2,1,0:T(8,128)(2,1)} %broadcast_in_dim.4), calls=%async_computation.2 | async-start | bytes 524288 | tf_op jit(solution)/shard_map/all_to_all | solution.py:222
  56.9 0.8 copy-start.9
  57.6 0.8 copy-start.11
  61.6 1.2 copy-start.4
  62.9 1.0 copy-start.10
  63.9 1.0 copy-start.12
  68.9 2.7 %collective-permute-start.3 = (bf16[2,512,512]{2,1,0:T(8,128)(2,1)S(1)}, bf16[2,512,512]{2,1,0:T(8,128)(2,1)S(1)}, u32[]{:S(2)}, u32[]{:S(2)}) collective-permute-start(bf16[2,512,512]{2,1,0:T(8,128)(2,1)S(1)} %slice.61), channel_id=1, source_target_pairs={{0,1},{1,0},{2,3},{3,2},{4,5},{5,4},{6,7},{7,6},{8,9},{9,8},{10,11... | collective-permute-start | bytes 3145736 | tf_op jit(solution)/shard_map/ppermute | solution.py:218
  70.7 1.4 copy-start.5
  70.7 1.4 copy-start.7
  72.1 8.4 %collective-permute-start.4 = (bf16[256,512]{1,0:T(8,128)(2,1)S(1)}, bf16[256,512]{1,0:T(8,128)(2,1)S(1)}, u32[]{:S(2)}, u32[]{:S(2)}) collective-permute-start(bf16[256,512]{1,0:T(8,128)(2,1)S(1)} %get-tuple-element.39), channel_id=1, source_target_pairs={{0,2},{1,3},{2,0},{3,1},{4,6},{5,7},{6,4},{7,5},{8,10},{9,11},{10,... | collective-permute-start | bytes 786440 | tf_op jit(solution)/shard_map/ppermute | solution.py:218
  73.7 8.1 %collective-permute-start.6 = (bf16[256,512]{1,0:T(8,128)(2,1)S(1)}, bf16[256,512]{1,0:T(8,128)(2,1)S(1)}, u32[]{:S(2)}, u32[]{:S(2)}) collective-permute-start(bf16[256,512]{1,0:T(8,128)(2,1)S(1)} %get-tuple-element.40), channel_id=1, source_target_pairs={{0,4},{4,0},{8,12},{12,8},{16,20},{20,16},{24,28},{28,24},{1,5},{5... | collective-permute-start | bytes 786440 | tf_op jit(solution)/shard_map/ppermute | solution.py:218
  82.0 6.9 %collective-permute-start.7 = (bf16[128,512]{1,0:T(8,128)(2,1)S(1)}, bf16[128,512]{1,0:T(8,128)(2,1)S(1)}, u32[]{:S(2)}, u32[]{:S(2)}) collective-permute-start(bf16[128,512]{1,0:T(8,128)(2,1)S(1)} %slice.115), channel_id=1, source_target_pairs={{0,2},{1,3},{2,0},{3,1},{4,6},{5,7},{6,4},{7,5},{8,10},{9,11},{10,... | collective-permute-start | bytes 393224 | tf_op jit(solution)/shard_map/ppermute | solution.py:218
  83.3 14.3 %all-to-all-start.3 = ((bf16[8,48,512]{2,1,0:T(8,128)(2,1)}), bf16[8,48,512]{2,1,0:T(8,128)(2,1)S(1)}, u32[]{:S(2)}, u32[]{:S(2)}) async-start(bf16[8,48,512]{2,1,0:T(8,128)(2,1)} %pad_maximum_fusion), calls=%async_computation.3 | async-start | bytes 786432 | tf_op jit(solution)/shard_map/all_to_all | solution.py:222
  86.8 7.7 %collective-permute-start.5 = (bf16[128,512]{1,0:T(8,128)(2,1)S(1)}, bf16[128,512]{1,0:T(8,128)(2,1)S(1)}, u32[]{:S(2)}, u32[]{:S(2)}) collective-permute-start(bf16[128,512]{1,0:T(8,128)(2,1)S(1)} %slice.116), channel_id=1, source_target_pairs={{0,4},{4,0},{8,12},{12,8},{16,20},{20,16},{24,28},{28,24},{1,5},{5... | collective-permute-start | bytes 393224 | tf_op jit(solution)/shard_map/ppermute | solution.py:218
  94.6 48.1 %copy-start.6 = (bf16[512,512]{1,0:T(8,128)(2,1)S(1)}, bf16[512,512]{1,0:T(8,128)(2,1)}, u32[]{:S(2)}) copy-start(bf16[512,512]{1,0:T(8,128)(2,1)} %copy-done.5) | copy-start | bytes 1572868
  94.6 48.1 %copy-start.8 = (bf16[512,512]{1,0:T(8,128)(2,1)S(1)}, bf16[512,512]{1,0:T(8,128)(2,1)}, u32[]{:S(2)}) copy-start(bf16[512,512]{1,0:T(8,128)(2,1)} %copy-done.7) | copy-start | bytes 1572868
  94.6 48.1 %copy-start.16 = (s32[32]{0:T(128)S(1)}, s32[32]{0:T(128)}, u32[]{:S(2)}) copy-start(s32[32]{0:T(128)} %param.13) | copy-start | bytes 388
  107.9 29.8 %all-to-all-start.4 = ((bf16[8,128,512]{2,1,0:T(8,128)(2,1)}), bf16[8,128,512]{2,1,0:T(8,128)(2,1)S(1)}, u32[]{:S(2)}, u32[]{:S(2)}) async-start(bf16[8,128,512]{2,1,0:T(8,128)(2,1)} %bitcast.30), calls=%async_computation.4 | async-start | bytes 2097152 | tf_op jit(solution)/shard_map/all_to_all | solution.py:222
  138.4 11.1 %all-to-all-start.6 = ((bf16[4,2,32,512]{3,2,1,0:T(8,128)(2,1)}), bf16[4,2,32,512]{3,2,1,0:T(8,128)(2,1)}, u32[]{:S(2)}, u32[]{:S(2)}) async-start(bf16[4,2,32,512]{3,2,1,0:T(8,128)(2,1)} %broadcast_in_dim.5), calls=%async_computation.6 | async-start | bytes 524288 | tf_op jit(solution)/shard_map/all_to_all | solution.py:358
  145.1 9.5 %collective-permute-start = (bf16[512,512]{1,0:T(8,128)(2,1)}, bf16[512,512]{1,0:T(8,128)(2,1)}, u32[]{:S(2)}, u32[]{:S(2)}) collective-permute-start(bf16[512,512]{1,0:T(8,128)(2,1)} %shard_map.100), channel_id=1, source_target_pairs={{0,1},{1,0},{2,3},{3,2},{4,5},{5,4},{6,7},{7,6},{8,9},{9,8},{10,11... | collective-permute-start | bytes 1572872 | tf_op jit(solution)/shard_map/ppermute | solution.py:218
  150.5 6.1 %collective-permute-start.8 = (bf16[128,512]{1,0:T(8,128)(2,1)S(1)}, bf16[128,512]{1,0:T(8,128)(2,1)S(1)}, u32[]{:S(2)}, u32[]{:S(2)}) collective-permute-start(bf16[128,512]{1,0:T(8,128)(2,1)S(1)} %bitcast.95), channel_id=1, source_target_pairs={{0,4},{4,0},{8,12},{12,8},{16,20},{20,16},{24,28},{28,24},{1,5},{5... | collective-permute-start | bytes 393224 | tf_op jit(solution)/shard_map/ppermute | solution.py:218
  153.2 6.4 %collective-permute-start.10 = (bf16[128,512]{1,0:T(8,128)(2,1)S(1)}, bf16[128,512]{1,0:T(8,128)(2,1)S(1)}, u32[]{:S(2)}, u32[]{:S(2)}) collective-permute-start(bf16[128,512]{1,0:T(8,128)(2,1)S(1)} %bitcast.92), channel_id=1, source_target_pairs={{0,2},{1,3},{2,0},{3,1},{4,6},{5,7},{6,4},{7,5},{8,10},{9,11},{10,... | collective-permute-start | bytes 393224 | tf_op jit(solution)/shard_map/ppermute | solution.py:218
  155.8 17.0 %collective-permute-start.1 = (bf16[512,512]{1,0:T(8,128)(2,1)S(1)}, bf16[512,512]{1,0:T(8,128)(2,1)S(1)}, u32[]{:S(2)}, u32[]{:S(2)}) collective-permute-start(bf16[512,512]{1,0:T(8,128)(2,1)S(1)} %add_convert_fusion), channel_id=1, source_target_pairs={{0,2},{1,3},{2,0},{3,1},{4,6},{5,7},{6,4},{7,5},{8,10},{9,11},{10,... | collective-permute-start | bytes 1572872 | tf_op jit(solution)/shard_map/ppermute | solution.py:218
  156.6 15.9 %collective-permute-start.9 = (bf16[2,128,512]{2,1,0:T(8,128)(2,1)S(1)}, bf16[2,128,512]{2,1,0:T(8,128)(2,1)S(1)}, u32[]{:S(2)}, u32[]{:S(2)}) collective-permute-start(bf16[2,128,512]{2,1,0:T(8,128)(2,1)S(1)} %pad_maximum_fusion.1), channel_id=1, source_target_pairs={{0,2},{1,3},{2,0},{3,1},{4,6},{5,7},{6,4},{7,5},{8,10},{9,11},{10,... | collective-permute-start | bytes 786440 | tf_op jit(solution)/shard_map/ppermute | solution.py:218
  159.6 13.0 %collective-permute-start.11 = (bf16[2,128,512]{2,1,0:T(8,128)(2,1)S(1)}, bf16[2,128,512]{2,1,0:T(8,128)(2,1)S(1)}, u32[]{:S(2)}, u32[]{:S(2)}) collective-permute-start(bf16[2,128,512]{2,1,0:T(8,128)(2,1)S(1)} %pad_maximum_fusion.2), channel_id=1, source_target_pairs={{0,4},{4,0},{8,12},{12,8},{16,20},{20,16},{24,28},{28,24},{1,5},{5... | collective-permute-start | bytes 786440 | tf_op jit(solution)/shard_map/ppermute | solution.py:218
  172.6 2.7 %collective-permute-start.12 = (bf16[8,128,512]{2,1,0:T(8,128)(2,1)S(1)}, bf16[8,128,512]{2,1,0:T(8,128)(2,1)S(1)}, u32[]{:S(2)}, u32[]{:S(2)}) collective-permute-start(bf16[8,128,512]{2,1,0:T(8,128)(2,1)S(1)} %constant_dynamic-update-slice_fusion.mine_ref), channel_id=1, source_target_pairs={{0,1},{1,0},{2,3},{3,2},{4,5},{5,4},{6,7},{7,6},{8,9},{9,8},{10,11... | collective-permute-start | bytes 3145736 | tf_op jit(solution)/shard_map/ppermute | solution.py:218
  172.9 5.3 %collective-permute-start.2 = (f32[512,512]{1,0:T(8,128)S(1)}, f32[512,512]{1,0:T(8,128)S(1)}, u32[]{:S(2)}, u32[]{:S(2)}) collective-permute-start(f32[512,512]{1,0:T(8,128)S(1)} %convert_add_fusion.1.mine_ref), channel_id=1, source_target_pairs={{0,1},{1,0},{2,3},{3,2},{4,5},{5,4},{6,7},{7,6},{8,9},{9,8},{10,11... | collective-permute-start | bytes 3145736 | tf_op jit(solution)/shard_map/ppermute | solution.py:218

commit v2 on v1

v2 whole, which is shorter than its diff:
```python
import functools
import math

import jax
import jax.numpy as jnp
from jax import lax
from jax.experimental import pallas as pl
from jax.experimental.pallas import tpu as pltpu
from jax.sharding import PartitionSpec as P

BF = jnp.bfloat16
F32 = jnp.float32
I32 = jnp.int32
VMEM = pl.BlockSpec(memory_space=pltpu.VMEM)
SMEM = pl.BlockSpec(memory_space=pltpu.SMEM)
FAR = pl.BlockSpec(memory_space=pl.ANY)


def call(body, outs, scalars, near, far=()):
    counts = len(scalars), len(near), len(far), len(outs)

    def kernel(*refs):
        refs = list(refs)
        groups = []
        for size in counts + (len(far),):
            groups.append(refs[:size])
            refs = refs[size:]
        scalar_refs, near_refs, far_refs, out_refs, held = groups
        copies = [
            pltpu.make_async_copy(source, target, refs[0].at[index])
            for index, (source, target) in enumerate(zip(far_refs, held))
        ]
        for copy in copies:
            copy.start()

        def take(index):
            copies[index].wait()
            return held[index]

        body(*scalar_refs, *near_refs, *([take] if far else []), *out_refs)

    scratch = [pltpu.VMEM(x.shape, x.dtype) for x in far]
    if far:
        scratch.append(pltpu.SemaphoreType.DMA((len(far),)))
    return pl.pallas_call(
        kernel,
        out_shape=[jax.ShapeDtypeStruct(s, d) for s, d in outs],
        in_specs=[SMEM] * len(scalars) + [VMEM] * len(near) + [FAR] * len(far),
        out_specs=[VMEM] * len(outs),
        scratch_shapes=scratch,
        compiler_params=pltpu.CompilerParams(vmem_limit_bytes=40 * 1024 * 1024),
    )(*scalars, *near, *far)


def iota(shape, axis):
    return lax.broadcasted_iota(I32, shape, axis)


def as_column(row):
    size = row.shape[1]
    step = min(128, size)
    eye = iota((step, step), 0) == iota((step, step), 1)
    pieces = [
        jnp.sum(jnp.where(eye, row[:, at : at + step], 0), axis=1, keepdims=True)
        for at in range(0, size, step)
    ]
    return jnp.concatenate(pieces, axis=0)


def as_row(column):
    size = column.shape[0]
    step = min(128, size)
    eye = iota((step, step), 0) == iota((step, step), 1)
    pieces = [
        jnp.sum(jnp.where(eye, column[at : at + step, :], 0.0), axis=0, keepdims=True)
        for at in range(0, size, step)
    ]
    return jnp.concatenate(pieces, axis=1)


def hot(mask):
    return mask.astype(F32).astype(BF)


def hot_rows(row, count):
    return hot(as_column(row) == iota((row.shape[1], count), 1))


def dot(a, b):
    return jnp.dot(a, b, preferred_element_type=F32)


def dot_t0(a, b):
    return lax.dot_general(a, b, (((0,), (0,)), ((), ())), preferred_element_type=F32)


def dot_t1(a, b):
    return lax.dot_general(a, b, (((1,), (1,)), ((), ())), preferred_element_type=F32)


def split(x):
    high = x.astype(BF)
    return high, (x - high.astype(F32)).astype(BF)


def slots_kernel(parts, cap, place_ref, take, slot_ref, neg_ref, request_ref):
    part = take(0)[...]
    edges = part.shape[1]
    slots = parts * cap
    named = (iota((parts, edges), 0) == part).astype(F32)
    before = hot(iota((edges, edges), 0) < iota((edges, edges), 1))
    earlier = dot(named.astype(BF), before)
    position = jnp.sum(earlier * named, axis=0, keepdims=True).astype(I32)
    slot = part * cap + position
    slot_ref[...] = slot
    placed = hot(iota((slots, edges), 0) == slot)
    which = iota((8, edges), 0)
    tail = take(1)[...]
    digits = jnp.where(which == 0, tail >> 7, jnp.where(which == 1, tail & 127, 0))
    found = dot_t1(digits.astype(F32).astype(BF), placed).astype(BF)
    neg = as_column(take(2)[...])
    negs = neg.shape[0]
    share = request_ref.shape[1]
    turned = iota((negs, negs), 0) == (iota((negs, negs), 1) ^ (place_ref[0] * share))
    ordered = jnp.sum(jnp.where(turned, neg, 0), axis=0, keepdims=True)
    neg_ref[...] = ordered
    entities = take(3)
    own = hot_rows(ordered, entities.shape[0])[:share]
    rows = dot(own, entities[...]).astype(BF)
    columns = rows.shape[1]
    for index in range(parts):
        request_ref[index, :, :columns] = rows
        ids = found[:, index * cap : (index + 1) * cap]
        if cap < 128:
            ids = jnp.concatenate([ids, jnp.zeros((share, 128 - cap), BF)], axis=1)
        request_ref[index, :, columns:] = ids


def query_kernel(slot_ref, take, rows_ref, query_ref):
    head, rel = take(0), take(1)
    entities = take(2)
    rows = dot(hot_rows(head[...], entities.shape[0]), entities[...]).astype(BF)
    rows_ref[...] = rows
    rel = as_column(rel[...])
    total = jnp.zeros(rows.shape, F32)
    operators = take(3)
    for relation in range(operators.shape[0]):
        picked = jnp.where(rel == relation, rows, jnp.zeros_like(rows))
        total = total + dot(picked, operators[relation])
    query_ref[...] = total.astype(BF)


def lookup_kernel(cap, request_ref, take, ids_ref, rows_ref, negs_ref):
    parts, share, width = request_ref.shape
    entities = take(0)
    columns = entities.shape[1]
    pieces = []
    for index in range(parts):
        digits = request_ref[index, :, columns : columns + cap].astype(F32)
        pieces.append(digits[0:1] * 128.0 + digits[1:2])
    ids = jnp.concatenate(pieces, axis=1).astype(I32)
    ids_ref[...] = ids
    rows_ref[...] = dot(hot_rows(ids, entities.shape[0]), entities[...]).astype(BF)
    negs_ref[...] = jnp.concatenate(
        [request_ref[index, :, :columns].astype(F32) for index in range(parts)], axis=0
    ).astype(BF)


def operator_terms(picks_ref, first, rows_ref, rel, grad, out_ref):
    width = out_ref.shape[1]
    for place in range(out_ref.shape[0]):
        at = pl.multiple_of(picks_ref[2 * (first + place) + 1] * width, width)
        picked = jnp.where(rel == picks_ref[2 * (first + place)], grad, jnp.zeros_like(grad))
        out_ref[place] = dot_t0(rows_ref[:, pl.ds(at, width)], picked).astype(out_ref.dtype)


def edge_kernel(
    factor,
    picks_ref,
    query_ref,
    got_ref,
    slot_ref,
    near_ref,
    core_ref,
    across_ref,
    both_ref,
    rows_ref,
    rel_ref,
    loss_ref,
    weight_ref,
    grad_ref,
    prob_ref,
    away_ref,
):
    queries = query_ref[...]
    negatives = jnp.concatenate(
        [near_ref[...], core_ref[...], across_ref[...], both_ref[...]], axis=0
    )
    slots = got_ref.shape[0]
    edges = queries.shape[0]
    scores = dot_t1(queries, negatives) * factor
    placed = as_column(slot_ref[...]) == iota((edges, slots), 1)
    tails = dot(hot(placed), got_ref[...])
    positive = jnp.sum(queries.astype(F32) * tails, axis=1, keepdims=True) * factor
    row_max = jnp.maximum(positive, jnp.max(scores, axis=1, keepdims=True))
    exp_pos = jnp.exp(positive - row_max)
    exp_neg = jnp.exp(scores - row_max)
    total = exp_pos + jnp.sum(exp_neg, axis=1, keepdims=True)
    loss_ref[...] = as_row(jnp.log(total) + row_max - positive)
    pull = exp_pos / total - 1.0
    prob = (exp_neg / total).astype(BF)
    prob_ref[...] = prob
    grad = (factor * (pull * tails + dot(prob, negatives))).astype(BF)
    grad_ref[...] = grad
    weight_ref[...] = factor * pull
    operator_terms(picks_ref, 0, rows_ref, as_column(rel_ref[...]), grad, away_ref)


def back_kernel(factor, cap, query_ref, prob_ref, weight_ref, slot_ref, back_ref):
    queries = query_ref[...]
    parts = back_ref.shape[0]
    share = prob_ref.shape[1] // parts // 4
    slots, edges = parts * cap, queries.shape[0]
    placed = hot(iota((slots, edges), 0) == slot_ref[...])
    weighted = (weight_ref[...] * queries.astype(F32)).astype(BF)
    tails = dot(placed, weighted).astype(BF)
    negs = factor * dot_t0(prob_ref[...], queries)
    for index in range(parts):
        back_ref[index, :cap] = tails[index * cap : (index + 1) * cap]
        pieces = [
            negs[(turn * parts + index) * share : (turn * parts + index + 1) * share]
            for turn in range(4)
        ]
        back_ref[index, cap:] = jnp.concatenate(pieces, axis=0).astype(BF)


def keep_kernel(picks_ref, rows_ref, rel_ref, grad_ref, op_ref, keep_ref, high_ref, low_ref):
    rel = as_column(rel_ref[...])
    grad = grad_ref[...]
    operator_terms(picks_ref, 4, rows_ref, rel, grad, keep_ref)
    total = jnp.zeros(grad.shape, F32)
    for relation in range(op_ref.shape[0]):
        picked = jnp.where(rel == relation, grad, jnp.zeros_like(grad))
        total = total + dot_t1(picked, op_ref[relation])
    high_ref[...], low_ref[...] = split(total)


def pair_kernel(keep_ref, got_ref, own_ref, *out_refs):
    own_ref[...] = keep_ref[0] + got_ref[0].astype(F32)
    for index, out_ref in enumerate(out_refs):
        out_ref[...] = (keep_ref[index + 1] + got_ref[index + 1].astype(F32)).astype(BF)


def quad_kernel(place_ref, own_ref, first_ref, second_ref, third_ref, *out_refs):
    size = out_refs[0].shape[0]
    for turn, out_ref in enumerate(out_refs):
        rows = pl.ds(pl.multiple_of((place_ref[1] ^ turn) * size, size), size)
        total = own_ref[rows, :] + first_ref[rows, :].astype(F32)
        total = total + (second_ref[rows, :].astype(F32) + third_ref[rows, :].astype(F32))
        out_ref[...] = total.astype(out_ref.dtype)


def sum_kernel(own_ref, first_ref, second_ref, third_ref, out_ref):
    total = own_ref[...] + first_ref[...].astype(F32)
    total = total + (second_ref[...].astype(F32) + third_ref[...].astype(F32))
    out_ref[...] = total.astype(BF)


def operator_kernel(picks_ref, place_ref, *refs):
    out_ref = refs[-1]
    size, width = refs[0].shape[0] // 4, refs[0].shape[0]
    for index, source in enumerate(refs[:-1]):
        pick = 2 * ((index + 4) % 8)
        for turn in range(4):
            at = picks_ref[pick + 1] * width + (place_ref[1] ^ turn) * size
            out_ref[picks_ref[pick], pl.ds(pl.multiple_of(at, size), size), :] = source[
                turn * size : (turn + 1) * size
            ].astype(F32)


def add_kernel(
    cap, base_ref, ids_ref, back_ref, head_ref, high_ref, low_ref, neg_ref, out_ref
):
    count = out_ref.shape[0]
    base = base_ref[0]
    parts = back_ref.shape[0]

    def pick(row):
        return hot((iota((count, row.shape[1]), 0) + base) == row)

    tails = jnp.concatenate([back_ref[index, :cap] for index in range(parts)], axis=0)
    total = dot(pick(ids_ref[...]), tails)
    heads = pick(head_ref[...])
    total = total + dot(heads, high_ref[...]) + dot(heads, low_ref[...])
    negs = back_ref[0, cap:].astype(F32)
    for index in range(1, parts):
        negs = negs + back_ref[index, cap:].astype(F32)
    own = pick(neg_ref[...])
    high, low = split(negs)
    out_ref[...] = (total + (dot(own, high) + dot(own, low))).astype(out_ref.dtype)


def join_kernel(place_ref, mine_ref, other_ref, out_ref):
    half = mine_ref.shape[0]
    core = place_ref[2]
    out_ref[pl.ds(pl.multiple_of(core * half, half), half), :] = mine_ref[...]
    out_ref[pl.ds(pl.multiple_of((1 - core) * half, half), half), :] = other_ref[...]


def flip(x, axis, size, bit):
    return lax.ppermute(x, axis, [(i, i ^ bit) for i in range(size)])


def exchange(x):
    return lax.all_to_all(x, "dom", split_axis=0, concat_axis=0, tiled=True)


def local(special, entities, relations, head_local, rel_ids, tail_part, tail_local, neg_local):
    columns = entities.shape[1]
    factor = 1.0 / math.sqrt(columns)
    ent_dev = entities.shape[0]
    edges = head_local.shape[0]
    parts = lax.axis_size("dom")
    reps = lax.axis_size("rep")
    cap = 2 * edges // parts
    slots = parts * cap
    neg_dev = neg_local.shape[0]
    negs = parts * neg_dev
    share = neg_dev // reps
    count = relations.shape[0]
    head = head_local.reshape(1, edges)
    rel = rel_ids.reshape(1, edges)
    dom = lax.axis_index("dom")
    rep = lax.axis_index("rep")
    z, x, y, core = dom // 2, dom % 2, rep // 2, rep % 2
    place = jnp.stack([rep, z, core])
    if special:
        quarters = [(2 * y + x) ^ k for k in range(4)]
        order = [(2 * (1 - core) + q // 2, q % 2) for q in quarters]
        order = order + [(2 * core + q // 2, q % 2) for q in quarters]
    else:
        order = [(k // 2, k % 2) for k in range(2 * count)]
    picks = jnp.stack([jnp.asarray(v, I32) for pair in order for v in pair])

    slot, neg_own, request = call(
        functools.partial(slots_kernel, parts, cap),
        [((1, edges), I32), ((1, neg_dev), I32), ((parts, share, columns + 128), BF)],
        (place,),
        (),
        (
            tail_part.reshape(1, edges),
            tail_local.reshape(1, edges),
            neg_local.reshape(1, neg_dev),
            entities,
        ),
    )
    requests = exchange(request)
    rows, queries = call(
        query_kernel,
        [((edges, columns), BF), ((edges, columns), BF)],
        (),
        (slot,),
        (head, rel, entities, relations),
    )
    requests, rows, queries = lax.optimization_barrier((requests, rows, queries))
    asked, found, neg_near = call(
        functools.partial(lookup_kernel, cap),
        [((1, slots), I32), ((slots, columns), BF), ((parts * share, columns), BF)],
        (),
        (requests,),
        (entities,),
    )
    got = exchange(found.reshape(parts, cap, columns)).reshape(slots, columns)
    neg_core, neg_across, neg_both = [flip(neg_near, "rep", reps, k) for k in (1, 2, 3)]

    terms = F32 if not special else BF
    loss, weight, grad, prob, away = call(
        functools.partial(edge_kernel, factor),
        [
            ((1, edges), F32),
            ((edges, 1), F32),
            ((edges, columns), BF),
            ((edges, negs), BF),
            ((4, columns // 2, columns), terms),
        ],
        (picks,),
        (queries, got, slot, neg_near, neg_core, neg_across, neg_both, rows, rel),
    )
    (back,) = call(
        functools.partial(back_kernel, factor, cap),
        [((parts, cap + neg_dev, columns), BF)],
        (),
        (queries, prob, weight, slot),
    )
    returned = exchange(back)
    keep, high, low = call(
        keep_kernel,
        [((4, columns // 2, columns), F32), ((edges, columns), BF), ((edges, columns), BF)],
        (picks,),
        (rows, rel, grad, relations),
    )

    def add(base, size, kind):
        return call(
            functools.partial(add_kernel, cap),
            [((size, columns), kind)],
            (base.reshape(1),),
            (asked, returned, head, high, low, neg_own),
        )[0]

    if not special:
        whole = jnp.concatenate([away, keep], axis=0).reshape(count, columns, columns)
        entity_grad = lax.psum(add(jnp.zeros((), I32), ent_dev, F32), "rep")
        return entity_grad, lax.psum(whole, ("dom", "rep")), loss.reshape(edges)

    half, quarter = columns // 2, columns // 8

    def quad(k):
        pairs = [
            (d * 4 + r, (d ^ (k & 1)) * 4 + (r ^ (k & 2))) for d in range(8) for r in range(4)
        ]
        return lambda v: lax.ppermute(v, ("dom", "rep"), pairs)

    other = flip(away, "rep", 4, 1)
    own, *sent = call(
        pair_kernel, [((half, columns), F32)] + [((half, columns), BF)] * 3, (), (keep, other)
    )
    met = [quad(k + 1)(v) for k, v in enumerate(sent)]
    own, *sent = call(
        quad_kernel,
        [((quarter, columns), F32)] + [((quarter, columns), BF)] * 3,
        (place,),
        (own, *met),
    )
    met = [flip(v, "dom", 8, 2 * (k + 1)) for k, v in enumerate(sent)]
    (own,) = call(sum_kernel, [((quarter, columns), BF)], (), (own, *met))
    stripes = [own] + [flip(own, "dom", 8, 2 * (k + 1)) for k in range(3)]
    own = jnp.concatenate(stripes, axis=0)
    mine = [own] + [quad(k)(own) for k in range(1, 4)]
    others = [flip(v, "rep", 4, 1) for v in mine]
    (relation_grad,) = call(
        operator_kernel, [((count, columns, columns), F32)], (picks, place), (*mine, *others)
    )

    rows_half = ent_dev // 2
    leaving = add((1 - core) * rows_half, rows_half, BF)
    arrived = flip(leaving, "rep", 4, 1)
    kept = add(core * rows_half, rows_half, F32)
    both = (kept + arrived.astype(F32)).astype(BF)
    across = flip(both, "rep", 4, 2)
    done = both.astype(F32) + across.astype(F32)
    partner = flip(done, "rep", 4, 1)
    (entity_grad,) = call(
        join_kernel, [((ent_dev, columns), F32)], (place,), (done, partner)
    )
    return entity_grad, relation_grad, loss.reshape(edges)


def solution(mesh):
    special = dict(mesh.shape) == {"dom": 8, "rep": 4}
    return jax.shard_map(
        functools.partial(local, special),
        mesh=mesh,
        in_specs=(
            P("dom", None),
            P(),
            P(("dom", "rep")),
            P(("dom", "rep")),
            P(("dom", "rep"), None),
            P(("dom", "rep")),
            P("dom"),
        ),
        out_specs=(P("dom", None), P(), P(("dom", "rep"))),
        check_vma=False,
    )
```

time: 181 us -> 170 us (0.939)
  blocking collectives: 51.5 us -> 0 us
  waiting for transfers between devices: 62.1 us -> 88.3 us
  starting transfers between devices: 30 us -> 37.4 us
  local copies, waits for them, and re-layouts: 12.2 us -> 18.5 us
  Pallas kernels: 19.9 us -> 23.2 us
  other arithmetic: 3.05 us -> 0.4 us
    all_to_all x3 -> x0, blocking collectives: 51.5 us -> none  [the longest x2 41.2 us: exchange(): return lax.all_to_all(x, 'dom', split_axis=0, concat_axis=0, tiled=True)]
    ppermute x0 -> x6, waiting for transfers between devices: none -> 20.2 us  [quad(): return lambda v: lax.ppermute(v, ('dom', 'rep'), pairs)]
    all_to_all x3, waiting for transfers between devices: 31.5 us -> 43.3 us  [exchange(): return lax.all_to_all(x, 'dom', split_axis=0, concat_axis=0, tiled=True)]
    unnamed x43 -> x56, local copies, waits for them, and re-layouts: 9.46 us -> 18.5 us
    ppermute x0 -> x6, starting transfers between devices: none -> 7.11 us  [quad(): return lambda v: lax.ppermute(v, ('dom', 'rep'), pairs)]
    all_to_all x3, starting transfers between devices: 11.3 us -> 16.8 us  [exchange(): return lax.all_to_all(x, 'dom', split_axis=0, concat_axis=0, tiled=True)]
    all_to_all x1 -> x0, starting transfers between devices: 4.23 us -> none  [local(): lax.all_to_all(jnp.broadcast_to(summed[None], (4, 2, stripe, columns)), '...]
    pallas_call x9 -> x13, Pallas kernels: 19.9 us -> 23.2 us  [call(): pl.pallas_call(kernel, out_shape=[jax.ShapeDtypeStruct(s, d) for s, d in...]
  transfers between devices with their start and end apart: 17 -> 26, of which waited for: 12 -> 18; matrix products, arithmetic and copies ran while one was open for 2% -> 0% of each run, Pallas kernels for 7% -> 6%
where the time goes in v2:
time: 170 us; the launch traced here: 169 us
  waiting for transfers between devices  88.3 us (52%)
  starting transfers between devices  37.4 us (22%)
  Pallas kernels  23.2 us (14%)
  local copies, waits for them, and re-layouts  18.5 us (11%)
    all_to_all x3, waiting for transfers between devices, exchange(): return lax.all_to_all(x, 'dom', split_axis=0, concat_axis=0, tiled=True)  43.3 us
    ppermute x17, waiting for transfers between devices, flip(): return lax.ppermute(x, axis, [(i, i ^ bit) for i in range(size)])  24.8 us
    pallas_call x13, Pallas kernels, call(): pl.pallas_call(kernel, out_shape=[jax.ShapeDtypeStruct(s, d) for s, d in...  23.2 us
    ppermute x6, waiting for transfers between devices, quad(): return lambda v: lax.ppermute(v, ('dom', 'rep'), pairs)  20.2 us
    unnamed x56, local copies, waits for them, and re-layouts  18.5 us
    all_to_all x3, starting transfers between devices, exchange(): return lax.all_to_all(x, 'dom', split_axis=0, concat_axis=0, tiled=True)  16.8 us
    ppermute x17, starting transfers between devices, flip(): return lax.ppermute(x, axis, [(i, i ^ bit) for i in range(size)])  13.5 us
    ppermute x6, starting transfers between devices, quad(): return lambda v: lax.ppermute(v, ('dom', 'rep'), pairs)  7.11 us
  transfers between devices with their start and end apart: 26, of which 18 were waited for; matrix products, arithmetic and copies ran while one was open for 0% of the time, Pallas kernels for 6%

profile of v2, /device:TPU:0, one launch (start us, length us, event | category | flops | bytes accessed | tf_op | source)
XLA Modules:
  0.0 168.8 jit_solution(8745318494639197778)
XLA Ops:
  0.7 1.2 copy-done
  2.0 0.7 copy-done.24
  2.6 0.7 copy-done.25
  3.3 0.7 copy-done.26
  4.0 2.5 %shard_map.94 = (s32[1,512]{1,0:T(1,128)S(1)}, s32[1,32]{1,0:T(1,128)S(1)}, bf16[8,8,640]{2,1,0:T(8,128)(2,1)}) custom-call(s32[3]{0:T(128)S(1)} %pad_add_fusion.refs_0_.refs_1_, s32[1,512]{1,0:T(1,128)S(1)} %bitcast.32, s32[1,512]{1,0:T(1,128)S(1)} %bitcast.33, s32[1,32]{1,0:T(1,128)S(1)} %bitcast.34, bf16[1024,512]{1,0:T(8,128)(2,1)S(1)} %copy-done), custom_call_target="tpu_custom_call" | custom-call | tf_op jit(solution)/shard_map/pallas_call | solution.py:45
  6.5 7.3 %all-to-all-start = ((bf16[8,8,640]{2,1,0:T(8,128)(2,1)}), bf16[8,8,640]{2,1,0:T(8,128)(2,1)S(1)}, u32[]{:S(2)}, u32[]{:S(2)}) async-start(bf16[8,8,640]{2,1,0:T(8,128)(2,1)} %get-tuple-element.30), calls=%async_computation | async-start | bytes 163840 | tf_op jit(solution)/shard_map/all_to_all | solution.py:315
  13.8 1.2 copy-done.1
  15.0 1.6 copy-done.3
  16.6 0.7 copy-done.20
  17.3 0.7 copy-done.22
  18.0 2.6 %shard_map.95 = (bf16[512,512]{1,0:T(8,128)(2,1)S(1)}, bf16[512,512]{1,0:T(8,128)(2,1)S(1)}) custom-call(s32[1,512]{1,0:T(1,128)S(1)} %get-tuple-element.31.refs_0_.refs_3_, s32[1,512]{1,0:T(1,128)S(1)} %bitcast.29, s32[1,512]{1,0:T(1,128)S(1)} %bitcast.26, bf16[1024,512]{1,0:T(8,128)(2,1)S(1)} %copy-done.1, bf16[4,512,512]{2,1,0:T(8,128)(2,1)S(1)} %copy-done.3), custom_call_target="tpu_custom_call" | custom-call | tf_op jit(solution)/shard_map/pallas_call | solution.py:45
  20.8 2.7 %shard_map.96 = (s32[1,1024]{1,0:T(1,128)S(1)}, bf16[1024,512]{1,0:T(8,128)(2,1)}, bf16[64,512]{1,0:T(8,128)(2,1)S(1)}) custom-call(bf16[8,8,640]{2,1,0:T(8,128)(2,1)S(1)} %all-to-all-done.refs_0_, bf16[1024,512]{1,0:T(8,128)(2,1)S(1)} %copy-done.2), custom_call_target="tpu_custom_call" | custom-call | tf_op jit(solution)/shard_map/pallas_call | solution.py:45
  23.5 5.8 %all-to-all-start.1 = ((bf16[8,128,512]{2,1,0:T(8,128)(2,1)}), bf16[8,128,512]{2,1,0:T(8,128)(2,1)S(1)}, u32[]{:S(2)}, u32[]{:S(2)}) async-start(bf16[8,128,512]{2,1,0:T(8,128)(2,1)} %bitcast.21), calls=%async_computation.1 | async-start | bytes 2097152 | tf_op jit(solution)/shard_map/all_to_all | solution.py:315
  29.4 1.5 collective-permute-start.1
  31.3 2.4 %collective-permute-done.2.refs_7_ = bf16[64,512]{1,0:T(8,128)(2,1)S(1)} collective-permute-done((bf16[64,512]{1,0:T(8,128)(2,1)S(1)}, bf16[64,512]{1,0:T(8,128)(2,1)S(1)}, u32[]{:S(2)}, u32[]{:S(2)}) %collective-permute-start.2) | collective-permute-done | bytes 65568 | tf_op jit(solution)/shard_map/ppermute | solution.py:311
  33.6 1.5 collective-permute-done.1.refs_6_
  35.1 19.6 %all-to-all-done.1 = bf16[8,128,512]{2,1,0:T(8,128)(2,1)S(1)} async-done(((bf16[8,128,512]{2,1,0:T(8,128)(2,1)}), bf16[8,128,512]{2,1,0:T(8,128)(2,1)S(1)}, u32[]{:S(2)}, u32[]{:S(2)}) %all-to-all-start.1) | async-done | bytes 1048608 | tf_op jit(solution)/shard_map/all_to_all | solution.py:315
  54.8 2.9 %shard_map.97 = (f32[1,512]{1,0:T(1,128)}, f32[512,1]{1,0:T(8,128)S(1)}, bf16[512,512]{1,0:T(8,128)(2,1)S(1)}, bf16[512,256]{1,0:T(8,128)(2,1)S(1)}, bf16[4,256,512]{2,1,0:T(8,128)(2,1)S(1)}) custom-call(s32[16]{0:T(128)S(1)} %stack.71.refs_0_, bf16[512,512]{1,0:T(8,128)(2,1)S(1)} %get-tuple-element.36.refs_1_.refs_0_, bf16[1024,512]{1,0:T(8,128)(2,1)S(1)} %bitcast.25, ...), custom_call_target="tpu_custom_call" | custom-call | tf_op jit(solution)/shard_map/pallas_call | solution.py:45
  57.7 0.8 copy-done.18
  58.5 1.0 copy-done.27
  59.5 1.0 copy-done.11
  60.5 0.9 shard_map.98
  61.5 1.0 copy-done.5
  62.6 3.8 %all-to-all-start.2 = ((bf16[8,160,512]{2,1,0:T(8,128)(2,1)}), bf16[8,160,512]{2,1,0:T(8,128)(2,1)S(1)}, u32[]{:S(2)}, u32[]{:S(2)}) async-start(bf16[8,160,512]{2,1,0:T(8,128)(2,1)} %copy-done.5), calls=%async_computation.2 | async-start | bytes 2621440 | tf_op jit(solution)/shard_map/all_to_all | solution.py:315
  66.4 1.0 copy-done.9
  67.4 1.0 copy-done.19
  68.4 2.8 %shard_map.99 = (f32[4,256,512]{2,1,0:T(8,128)S(1)}, bf16[512,512]{1,0:T(8,128)(2,1)S(1)}, bf16[512,512]{1,0:T(8,128)(2,1)S(1)}) custom-call(s32[16]{0:T(128)S(1)} %stack.71.refs_0_, bf16[512,512]{1,0:T(8,128)(2,1)S(1)} %copy-done.9, s32[1,512]{1,0:T(1,128)S(1)} %bitcast.28, bf16[512,512]{1,0:T(8,128)(2,1)S(1)} %copy-done.19, bf16[4,512,512]{2,1,0:T(8,128)(2,1)S(1)} %copy-done.4), custom_call_target="tpu_custom_call" | custom-call | tf_op jit(solution)/shard_map/pallas_call | solution.py:45
  71.3 1.3 copy-done.6
  72.6 0.8 copy-done.12
  73.4 0.8 copy-done.15
  74.2 23.4 %all-to-all-done.2.refs_2_ = bf16[8,160,512]{2,1,0:T(8,128)(2,1)S(1)} async-done(((bf16[8,160,512]{2,1,0:T(8,128)(2,1)}), bf16[8,160,512]{2,1,0:T(8,128)(2,1)S(1)}, u32[]{:S(2)}, u32[]{:S(2)}) %all-to-all-start.2) | async-done | bytes 1310752 | tf_op jit(solution)/shard_map/all_to_all | solution.py:315
  97.6 1.0 copy-done.13
  98.7 1.0 copy-done.16
  99.7 1.5 shard_map.101
  101.3 0.5 collective-permute-start.6
  101.8 1.5 shard_map.100
  103.5 1.6 collective-permute-start.4
  105.1 12.4 %collective-permute-done.4 = bf16[512,512]{1,0:T(8,128)(2,1)S(1)} collective-permute-done((bf16[512,512]{1,0:T(8,128)(2,1)S(1)}, bf16[512,512]{1,0:T(8,128)(2,1)S(1)}, u32[]{:S(2)}, u32[]{:S(2)}) %collective-permute-start.4) | collective-permute-done | bytes 524320 | tf_op jit(solution)/shard_map/ppermute | solution.py:311
  117.9 1.4 collective-permute-start.7
  119.3 1.5 collective-permute-start.8
  120.8 0.7 collective-permute-start.9
  121.5 5.6 %collective-permute-done.7.refs_2_ = bf16[256,512]{1,0:T(8,128)(2,1)S(1)} collective-permute-done((bf16[256,512]{1,0:T(8,128)(2,1)S(1)}, bf16[256,512]{1,0:T(8,128)(2,1)S(1)}, u32[]{:S(2)}, u32[]{:S(2)}) %collective-permute-start.7) | collective-permute-done | bytes 262176 | tf_op jit(solution)/shard_map/ppermute | solution.py:422
  127.1 5.3 %collective-permute-done.8.refs_3_ = bf16[256,512]{1,0:T(8,128)(2,1)S(1)} collective-permute-done((bf16[256,512]{1,0:T(8,128)(2,1)S(1)}, bf16[256,512]{1,0:T(8,128)(2,1)S(1)}, u32[]{:S(2)}, u32[]{:S(2)}) %collective-permute-start.8) | collective-permute-done | bytes 262176 | tf_op jit(solution)/shard_map/ppermute | solution.py:422
  132.4 1.0 collective-permute-done.9.refs_4_
  133.3 0.7 shard_map.104
  134.1 2.1 %collective-permute-start.11 = (bf16[64,512]{1,0:T(8,128)(2,1)S(1)}, bf16[64,512]{1,0:T(8,128)(2,1)S(1)}, u32[]{:S(2)}, u32[]{:S(2)}) collective-permute-start(bf16[64,512]{1,0:T(8,128)(2,1)S(1)} %get-tuple-element.54), channel_id=1, source_target_pairs={{0,16},{4,20},{8,24},{12,28},{16,0},{20,4},{24,8},{28,12},{1,17},{... | collective-permute-start | bytes 196616 | tf_op jit(solution)/shard_map/ppermute | solution.py:311
  136.1 2.3 %collective-permute-start.12 = (bf16[64,512]{1,0:T(8,128)(2,1)S(1)}, bf16[64,512]{1,0:T(8,128)(2,1)S(1)}, u32[]{:S(2)}, u32[]{:S(2)}) collective-permute-start(bf16[64,512]{1,0:T(8,128)(2,1)S(1)} %get-tuple-element.55), channel_id=1, source_target_pairs={{0,24},{4,28},{8,16},{12,20},{16,8},{20,12},{24,0},{28,4},{1,25},{... | collective-permute-start | bytes 196616 | tf_op jit(solution)/shard_map/ppermute | solution.py:311
  138.7 2.8 %collective-permute-done.11.refs_2_ = bf16[64,512]{1,0:T(8,128)(2,1)S(1)} collective-permute-done((bf16[64,512]{1,0:T(8,128)(2,1)S(1)}, bf16[64,512]{1,0:T(8,128)(2,1)S(1)}, u32[]{:S(2)}, u32[]{:S(2)}) %collective-permute-start.11) | collective-permute-done | bytes 65568 | tf_op jit(solution)/shard_map/ppermute | solution.py:311
  141.5 0.8 collective-permute-done.12.refs_3_
  142.3 2.4 %collective-permute-start.15 = (bf16[64,512]{1,0:T(8,128)(2,1)S(1)}, bf16[64,512]{1,0:T(8,128)(2,1)S(1)}, u32[]{:S(2)}, u32[]{:S(2)}) collective-permute-start(bf16[64,512]{1,0:T(8,128)(2,1)S(1)} %shard_map.105), channel_id=1, source_target_pairs={{0,24},{4,28},{8,16},{12,20},{16,8},{20,12},{24,0},{28,4},{1,25},{... | collective-permute-start | bytes 196616 | tf_op jit(solution)/shard_map/ppermute | solution.py:311
  144.7 0.3 collective-permute-start.14
  145.0 1.8 %collective-permute-start.13 = (bf16[64,512]{1,0:T(8,128)(2,1)S(1)}, bf16[64,512]{1,0:T(8,128)(2,1)S(1)}, u32[]{:S(2)}, u32[]{:S(2)}) collective-permute-start(bf16[64,512]{1,0:T(8,128)(2,1)S(1)} %shard_map.105), channel_id=1, source_target_pairs={{0,8},{4,12},{8,0},{12,4},{16,24},{20,28},{24,16},{28,20},{1,9},{5... | collective-permute-start | bytes 196616 | tf_op jit(solution)/shard_map/ppermute | solution.py:311
  146.8 1.9 %collective-permute-done.15 = bf16[64,512]{1,0:T(8,128)(2,1)S(1)} collective-permute-done((bf16[64,512]{1,0:T(8,128)(2,1)S(1)}, bf16[64,512]{1,0:T(8,128)(2,1)S(1)}, u32[]{:S(2)}, u32[]{:S(2)}) %collective-permute-start.15) | collective-permute-done | bytes 65568 | tf_op jit(solution)/shard_map/ppermute | solution.py:311
  148.7 1.4 collective-permute-done.14
  150.1 1.6 collective-permute-start.18
  151.8 1.1 collective-permute-start.17
  152.9 0.8 collective-permute-start.16
  153.7 5.7 %collective-permute-done.18.refs_5_ = bf16[256,512]{1,0:T(8,128)(2,1)S(1)} collective-permute-done((bf16[256,512]{1,0:T(8,128)(2,1)S(1)}, bf16[256,512]{1,0:T(8,128)(2,1)S(1)}, u32[]{:S(2)}, u32[]{:S(2)}) %collective-permute-start.18) | collective-permute-done | bytes 262176 | tf_op jit(solution)/shard_map/ppermute | solution.py:422
  159.4 2.7 %collective-permute-done.17.refs_4_ = bf16[256,512]{1,0:T(8,128)(2,1)S(1)} collective-permute-done((bf16[256,512]{1,0:T(8,128)(2,1)S(1)}, bf16[256,512]{1,0:T(8,128)(2,1)S(1)}, u32[]{:S(2)}, u32[]{:S(2)}) %collective-permute-start.17) | collective-permute-done | bytes 262176 | tf_op jit(solution)/shard_map/ppermute | solution.py:422
  162.0 0.5 collective-permute-start.20
  162.5 1.0 collective-permute-done.21.refs_8_
  163.6 0.4 collective-permute-done.20.refs_7_
  163.9 2.8 %shard_map.106 = f32[4,512,512]{2,1,0:T(8,128)} custom-call(s32[16]{0:T(128)S(1)} %stack.71.refs_0_, s32[3]{0:T(128)S(1)} %pad_add_fusion.refs_0_.refs_1_, bf16[256,512]{1,0:T(8,128)(2,1)S(1)} %pad_maximum_fusion.refs_2_, bf16[256,512]{1,0:T(8,128)(2,1)S(1)} %collective-permute-done.16.refs_3_, bf16[256,512]{1,0:T(8,128)(2,1)S(1)} %collective-permute-done.17.refs_4_, ...), custom_call_target="tpu_custom_call" | custom-call | tf_op jit(solution)/shard_map/pallas_call | solution.py:45
  166.8 2.0 %shard_map.102 = f32[1024,512]{1,0:T(8,128)} custom-call(s32[3]{0:T(128)S(1)} %pad_add_fusion.refs_0_.refs_1_, f32[512,512]{1,0:T(8,128)S(1)} %convert_add_fusion.refs_1_, f32[512,512]{1,0:T(8,128)S(1)} %collective-permute-done.5.refs_2_), custom_call_target="tpu_custom_call" | custom-call | tf_op jit(solution)/shard_map/pallas_call | solution.py:45
  (62 shorter events, 1.9 us)
Async XLA Ops:
  0.7 1.2 copy-start
  2.0 0.7 copy-start.24
  2.6 0.7 copy-start.25
  3.3 0.7 copy-start.26
  4.0 16.8 %copy-start.2 = (bf16[1024,512]{1,0:T(8,128)(2,1)S(1)}, bf16[1024,512]{1,0:T(8,128)(2,1)}, u32[]{:S(2)}) copy-start(bf16[1024,512]{1,0:T(8,128)(2,1)} %refs_1_.1) | copy-start | bytes 3145732
  6.5 14.3 %all-to-all-start = ((bf16[8,8,640]{2,1,0:T(8,128)(2,1)}), bf16[8,8,640]{2,1,0:T(8,128)(2,1)S(1)}, u32[]{:S(2)}, u32[]{:S(2)}) async-start(bf16[8,8,640]{2,1,0:T(8,128)(2,1)} %get-tuple-element.30), calls=%async_computation | async-start | bytes 163840 | tf_op jit(solution)/shard_map/all_to_all | solution.py:315
  13.8 1.2 copy-start.1
  15.0 1.6 copy-start.3
  16.6 0.7 copy-start.20
  17.3 0.7 copy-start.22
  20.5 37.1 %copy-start.8 = (bf16[512,512]{1,0:T(8,128)(2,1)}, bf16[512,512]{1,0:T(8,128)(2,1)S(1)}, u32[]{:S(2)}) copy-start(bf16[512,512]{1,0:T(8,128)(2,1)S(1)} %get-tuple-element.39.refs_8_.refs_1_) | copy-start | bytes 1572868
  20.5 37.1 %copy-start.10 = (bf16[512,512]{1,0:T(8,128)(2,1)}, bf16[512,512]{1,0:T(8,128)(2,1)S(1)}, u32[]{:S(2)}) copy-start(bf16[512,512]{1,0:T(8,128)(2,1)S(1)} %get-tuple-element.36.refs_1_.refs_0_) | copy-start | bytes 1572868
  20.6 34.2 %copy-start.21 = (s32[512]{0:T(512)S(1)}, s32[512]{0:T(512)}, u32[]{:S(2)}) copy-start(s32[512]{0:T(512)} %param.10) | copy-start | bytes 6148
  23.5 31.2 %all-to-all-start.1 = ((bf16[8,128,512]{2,1,0:T(8,128)(2,1)}), bf16[8,128,512]{2,1,0:T(8,128)(2,1)S(1)}, u32[]{:S(2)}, u32[]{:S(2)}) async-start(bf16[8,128,512]{2,1,0:T(8,128)(2,1)} %bitcast.21), calls=%async_computation.1 | async-start | bytes 2097152 | tf_op jit(solution)/shard_map/all_to_all | solution.py:315
  29.3 4.3 %collective-permute-start.2 = (bf16[64,512]{1,0:T(8,128)(2,1)S(1)}, bf16[64,512]{1,0:T(8,128)(2,1)S(1)}, u32[]{:S(2)}, u32[]{:S(2)}) collective-permute-start(bf16[64,512]{1,0:T(8,128)(2,1)S(1)} %get-tuple-element.38.refs_4_), channel_id=1, source_target_pairs={{0,3},{1,2},{2,1},{3,0},{4,7},{5,6},{6,5},{7,4},{8,11},{9,10},{10,... | collective-permute-start | bytes 196616 | tf_op jit(solution)/shard_map/ppermute | solution.py:311
  29.4 5.7 %collective-permute-start.1 = (bf16[64,512]{1,0:T(8,128)(2,1)S(1)}, bf16[64,512]{1,0:T(8,128)(2,1)S(1)}, u32[]{:S(2)}, u32[]{:S(2)}) collective-permute-start(bf16[64,512]{1,0:T(8,128)(2,1)S(1)} %get-tuple-element.38.refs_4_), channel_id=1, source_target_pairs={{0,2},{1,3},{2,0},{3,1},{4,6},{5,7},{6,4},{7,5},{8,10},{9,11},{10,... | collective-permute-start | bytes 196616 | tf_op jit(solution)/shard_map/ppermute | solution.py:311
  30.9 4.2 %collective-permute-start = (bf16[64,512]{1,0:T(8,128)(2,1)S(1)}, bf16[64,512]{1,0:T(8,128)(2,1)S(1)}, u32[]{:S(2)}, u32[]{:S(2)}) collective-permute-start(bf16[64,512]{1,0:T(8,128)(2,1)S(1)} %get-tuple-element.38.refs_4_), channel_id=1, source_target_pairs={{0,1},{1,0},{2,3},{3,2},{4,5},{5,4},{6,7},{7,6},{8,9},{9,8},{10,11... | collective-permute-start | bytes 196616 | tf_op jit(solution)/shard_map/ppermute | solution.py:311
  57.7 0.8 copy-start.18
  58.5 1.0 copy-start.27
  59.5 1.0 copy-start.11
  60.5 5.8 %copy-start.4 = (bf16[4,512,512]{2,1,0:T(8,128)(2,1)S(1)}, bf16[4,512,512]{2,1,0:T(8,128)(2,1)}, u32[]{:S(2)}) copy-start(bf16[4,512,512]{2,1,0:T(8,128)(2,1)} %refs_4_.5) | copy-start | bytes 6291460
  61.5 1.1 copy-start.5
  62.6 35.0 %all-to-all-start.2 = ((bf16[8,160,512]{2,1,0:T(8,128)(2,1)}), bf16[8,160,512]{2,1,0:T(8,128)(2,1)S(1)}, u32[]{:S(2)}, u32[]{:S(2)}) async-start(bf16[8,160,512]{2,1,0:T(8,128)(2,1)} %copy-done.5), calls=%async_computation.2 | async-start | bytes 2621440 | tf_op jit(solution)/shard_map/all_to_all | solution.py:315
  66.3 31.3 %copy-start.23 = (s32[512]{0:T(512)S(1)}, s32[512]{0:T(512)}, u32[]{:S(2)}) copy-start(s32[512]{0:T(512)} %param.9) | copy-start | bytes 6148
  66.3 1.0 copy-start.9
  67.4 1.0 copy-start.19
  71.2 1.3 copy-start.6
  72.6 0.8 copy-start.12
  73.4 0.8 copy-start.15
  97.6 1.0 copy-start.13
  98.7 1.0 copy-start.16
  99.7 2.1 %copy-start.14 = (bf16[512,512]{1,0:T(8,128)(2,1)S(1)}, bf16[512,512]{1,0:T(8,128)(2,1)}, u32[]{:S(2)}) copy-start(bf16[512,512]{1,0:T(8,128)(2,1)} %copy-done.12) | copy-start | bytes 1572868
  99.7 2.1 %copy-start.17 = (bf16[512,512]{1,0:T(8,128)(2,1)S(1)}, bf16[512,512]{1,0:T(8,128)(2,1)}, u32[]{:S(2)}) copy-start(bf16[512,512]{1,0:T(8,128)(2,1)} %copy-done.15) | copy-start | bytes 1572868
  101.2 2.1 %collective-permute-start.3 = (bf16[512,512]{1,0:T(8,128)(2,1)S(1)}, bf16[512,512]{1,0:T(8,128)(2,1)S(1)}, u32[]{:S(2)}, u32[]{:S(2)}) collective-permute-start(bf16[512,512]{1,0:T(8,128)(2,1)S(1)} %shard_map.101), channel_id=1, source_target_pairs={{0,1},{1,0},{2,3},{3,2},{4,5},{5,4},{6,7},{7,6},{8,9},{9,8},{10,11... | collective-permute-start | bytes 1572872 | tf_op jit(solution)/shard_map/ppermute | solution.py:311
  101.3 16.4 %collective-permute-start.6 = (bf16[4,256,512]{2,1,0:T(8,128)(2,1)}, bf16[4,256,512]{2,1,0:T(8,128)(2,1)S(1)}, u32[]{:S(2)}, u32[]{:S(2)}) collective-permute-start(bf16[4,256,512]{2,1,0:T(8,128)(2,1)} %copy-done.27), channel_id=1, source_target_pairs={{0,1},{1,0},{2,3},{3,2},{4,5},{5,4},{6,7},{7,6},{8,9},{9,8},{10,11... | collective-permute-start | bytes 3145736 | tf_op jit(solution)/shard_map/ppermute | solution.py:311
  103.3 14.4 %copy-start.7 = (f32[4,256,512]{2,1,0:T(8,128)S(1)}, f32[4,256,512]{2,1,0:T(8,128)}, u32[]{:S(2)}) copy-start(f32[4,256,512]{2,1,0:T(8,128)} %copy-done.6) | copy-start | bytes 6291460
  103.5 14.0 %collective-permute-start.4 = (bf16[512,512]{1,0:T(8,128)(2,1)S(1)}, bf16[512,512]{1,0:T(8,128)(2,1)S(1)}, u32[]{:S(2)}, u32[]{:S(2)}) collective-permute-start(bf16[512,512]{1,0:T(8,128)(2,1)S(1)} %add_convert_fusion), channel_id=1, source_target_pairs={{0,2},{1,3},{2,0},{3,1},{4,6},{5,7},{6,4},{7,5},{8,10},{9,11},{10,... | collective-permute-start | bytes 1572872 | tf_op jit(solution)/shard_map/ppermute | solution.py:311
  117.6 49.1 %collective-permute-start.5 = (f32[512,512]{1,0:T(8,128)S(1)}, f32[512,512]{1,0:T(8,128)S(1)}, u32[]{:S(2)}, u32[]{:S(2)}) collective-permute-start(f32[512,512]{1,0:T(8,128)S(1)} %convert_add_fusion.refs_1_), channel_id=1, source_target_pairs={{0,1},{1,0},{2,3},{3,2},{4,5},{5,4},{6,7},{7,6},{8,9},{9,8},{10,11... | collective-permute-start | bytes 3145736 | tf_op jit(solution)/shard_map/ppermute | solution.py:311
  117.9 9.2 %collective-permute-start.7 = (bf16[256,512]{1,0:T(8,128)(2,1)S(1)}, bf16[256,512]{1,0:T(8,128)(2,1)S(1)}, u32[]{:S(2)}, u32[]{:S(2)}) collective-permute-start(bf16[256,512]{1,0:T(8,128)(2,1)S(1)} %get-tuple-element.49), channel_id=1, source_target_pairs={{0,4},{1,5},{2,6},{3,7},{4,0},{5,1},{6,2},{7,3},{8,12},{9,13},{10,... | collective-permute-start | bytes 786440 | tf_op jit(solution)/shard_map/ppermute | solution.py:422
  119.3 13.1 %collective-permute-start.8 = (bf16[256,512]{1,0:T(8,128)(2,1)S(1)}, bf16[256,512]{1,0:T(8,128)(2,1)S(1)}, u32[]{:S(2)}, u32[]{:S(2)}) collective-permute-start(bf16[256,512]{1,0:T(8,128)(2,1)S(1)} %get-tuple-element.50), channel_id=1, source_target_pairs={{0,2},{1,3},{2,0},{3,1},{4,6},{5,7},{6,4},{7,5},{8,10},{9,11},{10,... | collective-permute-start | bytes 786440 | tf_op jit(solution)/shard_map/ppermute | solution.py:422
  120.8 12.5 %collective-permute-start.9 = (bf16[256,512]{1,0:T(8,128)(2,1)S(1)}, bf16[256,512]{1,0:T(8,128)(2,1)S(1)}, u32[]{:S(2)}, u32[]{:S(2)}) collective-permute-start(bf16[256,512]{1,0:T(8,128)(2,1)S(1)} %get-tuple-element.51), channel_id=1, source_target_pairs={{0,6},{1,7},{2,4},{3,5},{4,2},{5,3},{6,0},{7,1},{8,14},{9,15},{10,... | collective-permute-start | bytes 786440 | tf_op jit(solution)/shard_map/ppermute | solution.py:422
  134.0 4.7 %collective-permute-start.10 = (bf16[64,512]{1,0:T(8,128)(2,1)S(1)}, bf16[64,512]{1,0:T(8,128)(2,1)S(1)}, u32[]{:S(2)}, u32[]{:S(2)}) collective-permute-start(bf16[64,512]{1,0:T(8,128)(2,1)S(1)} %get-tuple-element.53), channel_id=1, source_target_pairs={{0,8},{4,12},{8,0},{12,4},{16,24},{20,28},{24,16},{28,20},{1,9},{5... | collective-permute-start | bytes 196616 | tf_op jit(solution)/shard_map/ppermute | solution.py:311
  134.1 7.4 %collective-permute-start.11 = (bf16[64,512]{1,0:T(8,128)(2,1)S(1)}, bf16[64,512]{1,0:T(8,128)(2,1)S(1)}, u32[]{:S(2)}, u32[]{:S(2)}) collective-permute-start(bf16[64,512]{1,0:T(8,128)(2,1)S(1)} %get-tuple-element.54), channel_id=1, source_target_pairs={{0,16},{4,20},{8,24},{12,28},{16,0},{20,4},{24,8},{28,12},{1,17},{... | collective-permute-start | bytes 196616 | tf_op jit(solution)/shard_map/ppermute | solution.py:311
  136.1 6.2 %collective-permute-start.12 = (bf16[64,512]{1,0:T(8,128)(2,1)S(1)}, bf16[64,512]{1,0:T(8,128)(2,1)S(1)}, u32[]{:S(2)}, u32[]{:S(2)}) collective-permute-start(bf16[64,512]{1,0:T(8,128)(2,1)S(1)} %get-tuple-element.55), channel_id=1, source_target_pairs={{0,24},{4,28},{8,16},{12,20},{16,8},{20,12},{24,0},{28,4},{1,25},{... | collective-permute-start | bytes 196616 | tf_op jit(solution)/shard_map/ppermute | solution.py:311
  142.3 6.4 %collective-permute-start.15 = (bf16[64,512]{1,0:T(8,128)(2,1)S(1)}, bf16[64,512]{1,0:T(8,128)(2,1)S(1)}, u32[]{:S(2)}, u32[]{:S(2)}) collective-permute-start(bf16[64,512]{1,0:T(8,128)(2,1)S(1)} %shard_map.105), channel_id=1, source_target_pairs={{0,24},{4,28},{8,16},{12,20},{16,8},{20,12},{24,0},{28,4},{1,25},{... | collective-permute-start | bytes 196616 | tf_op jit(solution)/shard_map/ppermute | solution.py:311
  144.7 5.4 %collective-permute-start.14 = (bf16[64,512]{1,0:T(8,128)(2,1)S(1)}, bf16[64,512]{1,0:T(8,128)(2,1)S(1)}, u32[]{:S(2)}, u32[]{:S(2)}) collective-permute-start(bf16[64,512]{1,0:T(8,128)(2,1)S(1)} %shard_map.105), channel_id=1, source_target_pairs={{0,16},{4,20},{8,24},{12,28},{16,0},{20,4},{24,8},{28,12},{1,17},{... | collective-permute-start | bytes 196616 | tf_op jit(solution)/shard_map/ppermute | solution.py:311
  145.0 5.1 %collective-permute-start.13 = (bf16[64,512]{1,0:T(8,128)(2,1)S(1)}, bf16[64,512]{1,0:T(8,128)(2,1)S(1)}, u32[]{:S(2)}, u32[]{:S(2)}) collective-permute-start(bf16[64,512]{1,0:T(8,128)(2,1)S(1)} %shard_map.105), channel_id=1, source_target_pairs={{0,8},{4,12},{8,0},{12,4},{16,24},{20,28},{24,16},{28,20},{1,9},{5... | collective-permute-start | bytes 196616 | tf_op jit(solution)/shard_map/ppermute | solution.py:311
  150.1 9.2 %collective-permute-start.18 = (bf16[256,512]{1,0:T(8,128)(2,1)S(1)}, bf16[256,512]{1,0:T(8,128)(2,1)S(1)}, u32[]{:S(2)}, u32[]{:S(2)}) collective-permute-start(bf16[256,512]{1,0:T(8,128)(2,1)S(1)} %pad_maximum_fusion.refs_2_), channel_id=1, source_target_pairs={{0,6},{1,7},{2,4},{3,5},{4,2},{5,3},{6,0},{7,1},{8,14},{9,15},{10,... | collective-permute-start | bytes 786440 | tf_op jit(solution)/shard_map/ppermute | solution.py:422
  151.8 10.2 %collective-permute-start.17 = (bf16[256,512]{1,0:T(8,128)(2,1)S(1)}, bf16[256,512]{1,0:T(8,128)(2,1)S(1)}, u32[]{:S(2)}, u32[]{:S(2)}) collective-permute-start(bf16[256,512]{1,0:T(8,128)(2,1)S(1)} %pad_maximum_fusion.refs_2_), channel_id=1, source_target_pairs={{0,2},{1,3},{2,0},{3,1},{4,6},{5,7},{6,4},{7,5},{8,10},{9,11},{10,... | collective-permute-start | bytes 786440 | tf_op jit(solution)/shard_map/ppermute | solution.py:422
  152.9 9.1 %collective-permute-start.16 = (bf16[256,512]{1,0:T(8,128)(2,1)S(1)}, bf16[256,512]{1,0:T(8,128)(2,1)S(1)}, u32[]{:S(2)}, u32[]{:S(2)}) collective-permute-start(bf16[256,512]{1,0:T(8,128)(2,1)S(1)} %pad_maximum_fusion.refs_2_), channel_id=1, source_target_pairs={{0,4},{1,5},{2,6},{3,7},{4,0},{5,1},{6,2},{7,3},{8,12},{9,13},{10,... | collective-permute-start | bytes 786440 | tf_op jit(solution)/shard_map/ppermute | solution.py:422
  153.7 8.8 %collective-permute-start.19 = (bf16[256,512]{1,0:T(8,128)(2,1)S(1)}, bf16[256,512]{1,0:T(8,128)(2,1)S(1)}, u32[]{:S(2)}, u32[]{:S(2)}) collective-permute-start(bf16[256,512]{1,0:T(8,128)(2,1)S(1)} %pad_maximum_fusion.refs_2_), channel_id=1, source_target_pairs={{0,1},{1,0},{2,3},{3,2},{4,5},{5,4},{6,7},{7,6},{8,9},{9,8},{10,11... | collective-permute-start | bytes 786440 | tf_op jit(solution)/shard_map/ppermute | solution.py:311
  159.4 3.2 %collective-permute-start.22 = (bf16[256,512]{1,0:T(8,128)(2,1)S(1)}, bf16[256,512]{1,0:T(8,128)(2,1)S(1)}, u32[]{:S(2)}, u32[]{:S(2)}) collective-permute-start(bf16[256,512]{1,0:T(8,128)(2,1)S(1)} %collective-permute-done.18.refs_5_), channel_id=1, source_target_pairs={{0,1},{1,0},{2,3},{3,2},{4,5},{5,4},{6,7},{7,6},{8,9},{9,8},{10,11... | collective-permute-start | bytes 786440 | tf_op jit(solution)/shard_map/ppermute | solution.py:311
  162.0 1.5 collective-permute-start.21
  162.0 1.9 %collective-permute-start.20 = (bf16[256,512]{1,0:T(8,128)(2,1)S(1)}, bf16[256,512]{1,0:T(8,128)(2,1)S(1)}, u32[]{:S(2)}, u32[]{:S(2)}) collective-permute-start(bf16[256,512]{1,0:T(8,128)(2,1)S(1)} %collective-permute-done.16.refs_3_), channel_id=1, source_target_pairs={{0,1},{1,0},{2,3},{3,2},{4,5},{5,4},{6,7},{7,6},{8,9},{9,8},{10,11... | collective-permute-start | bytes 786440 | tf_op jit(solution)/shard_map/ppermute | solution.py:311

commit v3 on v2

--- a/solution.py
+++ b/solution.py
@@ -13,21 +13,22 @@
 I32 = jnp.int32
 VMEM = pl.BlockSpec(memory_space=pltpu.VMEM)
 SMEM = pl.BlockSpec(memory_space=pltpu.SMEM)
-FAR = pl.BlockSpec(memory_space=pl.ANY)
-
-
-def call(body, outs, scalars, near, far=()):
-    counts = len(scalars), len(near), len(far), len(outs)
+FAR = pl.BlockSpec(memory_space=pltpu.HBM)
+
+
+def call(body, outs, scalars, near, far=(), after=()):
+    counts = len(scalars), len(near), len(far), len(after), len(outs), len(far)
+    away = [index for index, out in enumerate(outs) if len(out) == 3]
 
     def kernel(*refs):
         refs = list(refs)
         groups = []
-        for size in counts + (len(far),):
+        for size in counts:
             groups.append(refs[:size])
             refs = refs[size:]
-        scalar_refs, near_refs, far_refs, out_refs, held = groups
+        scalar_refs, near_refs, far_refs, _, out_refs, held = groups
         copies = [
-            pltpu.make_async_copy(source, target, refs[0].at[index])
+            pltpu.make_async_copy(source, target, refs[len(away)].at[index])
             for index, (source, target) in enumerate(zip(far_refs, held))
         ]
         for copy in copies:
@@ -37,19 +38,35 @@
             copies[index].wait()
             return held[index]
 
-        body(*scalar_refs, *near_refs, *([take] if far else []), *out_refs)
+        filled = list(out_refs)
+        for place, index in enumerate(away):
+            filled[index] = refs[place]
+        body(*scalar_refs, *near_refs, *([take] if far else []), *filled)
+        copies_out = [
+            pltpu.make_async_copy(refs[place], out_refs[index], refs[-1].at[place])
+            for place, index in enumerate(away)
+        ]
+        for copy in copies_out:
+            copy.start()
+        for copy in copies_out:
+            copy.wait()
 
     scratch = [pltpu.VMEM(x.shape, x.dtype) for x in far]
+    scratch += [pltpu.VMEM(outs[index][0], outs[index][1]) for index in away]
     if far:
         scratch.append(pltpu.SemaphoreType.DMA((len(far),)))
+    if away:
+        scratch.append(pltpu.SemaphoreType.DMA((len(away),)))
     return pl.pallas_call(
         kernel,
-        out_shape=[jax.ShapeDtypeStruct(s, d) for s, d in outs],
-        in_specs=[SMEM] * len(scalars) + [VMEM] * len(near) + [FAR] * len(far),
-        out_specs=[VMEM] * len(outs),
+        out_shape=[jax.ShapeDtypeStruct(out[0], out[1]) for out in outs],
+        in_specs=[SMEM] * len(scalars)
+        + [VMEM] * len(near)
+        + [FAR] * (len(far) + len(after)),
+        out_specs=[FAR if len(out) == 3 else VMEM for out in outs],
         scratch_shapes=scratch,
-        compiler_params=pltpu.CompilerParams(vmem_limit_bytes=40 * 1024 * 1024),
-    )(*scalars, *near, *far)
+        compiler_params=pltpu.CompilerParams(vmem_limit_bytes=60 * 1024 * 1024),
+    )(*scalars, *near, *far, *after)
 
 
 def iota(shape, axis):
@@ -136,7 +153,7 @@
         request_ref[index, :, columns:] = ids
 
 
-def query_kernel(slot_ref, take, rows_ref, query_ref):
+def query_kernel(take, rows_ref, query_ref):
     head, rel = take(0), take(1)
     entities = take(2)
     rows = dot(hot_rows(head[...], entities.shape[0]), entities[...]).astype(BF)
@@ -177,30 +194,26 @@
 def edge_kernel(
     factor,
     picks_ref,
-    query_ref,
-    got_ref,
     slot_ref,
     near_ref,
     core_ref,
     across_ref,
     both_ref,
-    rows_ref,
-    rel_ref,
+    take,
     loss_ref,
     weight_ref,
     grad_ref,
     prob_ref,
     away_ref,
 ):
-    queries = query_ref[...]
+    queries = take(0)[...]
     negatives = jnp.concatenate(
         [near_ref[...], core_ref[...], across_ref[...], both_ref[...]], axis=0
     )
-    slots = got_ref.shape[0]
-    edges = queries.shape[0]
     scores = dot_t1(queries, negatives) * factor
-    placed = as_column(slot_ref[...]) == iota((edges, slots), 1)
-    tails = dot(hot(placed), got_ref[...])
+    got = take(1)
+    placed = as_column(slot_ref[...]) == iota((queries.shape[0], got.shape[0]), 1)
+    tails = dot(hot(placed), got[...])
     positive = jnp.sum(queries.astype(F32) * tails, axis=1, keepdims=True) * factor
     row_max = jnp.maximum(positive, jnp.max(scores, axis=1, keepdims=True))
     exp_pos = jnp.exp(positive - row_max)
@@ -213,18 +226,20 @@
     grad = (factor * (pull * tails + dot(prob, negatives))).astype(BF)
     grad_ref[...] = grad
     weight_ref[...] = factor * pull
-    operator_terms(picks_ref, 0, rows_ref, as_column(rel_ref[...]), grad, away_ref)
-
-
-def back_kernel(factor, cap, query_ref, prob_ref, weight_ref, slot_ref, back_ref):
-    queries = query_ref[...]
+    rows = take(2)
+    operator_terms(picks_ref, 0, rows, as_column(take(3)[...]), grad, away_ref)
+
+
+def back_kernel(factor, cap, weight_ref, slot_ref, take, back_ref):
     parts = back_ref.shape[0]
-    share = prob_ref.shape[1] // parts // 4
+    queries = take(0)[...]
     slots, edges = parts * cap, queries.shape[0]
     placed = hot(iota((slots, edges), 0) == slot_ref[...])
     weighted = (weight_ref[...] * queries.astype(F32)).astype(BF)
     tails = dot(placed, weighted).astype(BF)
-    negs = factor * dot_t0(prob_ref[...], queries)
+    prob = take(1)
+    share = prob.shape[1] // parts // 4
+    negs = factor * dot_t0(prob[...], queries)
     for index in range(parts):
         back_ref[index, :cap] = tails[index * cap : (index + 1) * cap]
         pieces = [
@@ -234,21 +249,37 @@
         back_ref[index, cap:] = jnp.concatenate(pieces, axis=0).astype(BF)
 
 
-def keep_kernel(picks_ref, rows_ref, rel_ref, grad_ref, op_ref, keep_ref, high_ref, low_ref):
-    rel = as_column(rel_ref[...])
-    grad = grad_ref[...]
-    operator_terms(picks_ref, 4, rows_ref, rel, grad, keep_ref)
+def keep_kernel(picks_ref, take, keep_ref):
+    rel = as_column(take(2)[...])
+    rows = take(0)
+    operator_terms(picks_ref, 4, rows, rel, take(1)[...], keep_ref)
+
+
+def pair_kernel(picks_ref, take, own_ref, *out_refs):
+    rel = as_column(take(2)[...])
+    rows, grad = take(0), take(1)[...]
+    width = own_ref.shape[0]
+    got = take(3)
+    for place in (1, 2, 3, 0):
+        relation = picks_ref[2 * (4 + place)]
+        at = pl.multiple_of(picks_ref[2 * (4 + place) + 1] * width, width)
+        picked = jnp.where(rel == relation, grad, jnp.zeros_like(grad))
+        term = dot_t0(rows[:, pl.ds(at, width)], picked) + got[place].astype(F32)
+        if place:
+            out_refs[place - 1][...] = term.astype(BF)
+        else:
+            own_ref[...] = term
+
+
+def head_kernel(take, high_ref, low_ref):
+    rel = as_column(take(1)[...])
+    grad = take(0)[...]
+    operators = take(2)
     total = jnp.zeros(grad.shape, F32)
-    for relation in range(op_ref.shape[0]):
+    for relation in range(operators.shape[0]):
         picked = jnp.where(rel == relation, grad, jnp.zeros_like(grad))
-        total = total + dot_t1(picked, op_ref[relation])
+        total = total + dot_t1(picked, operators[relation])
     high_ref[...], low_ref[...] = split(total)
-
-
-def pair_kernel(keep_ref, got_ref, own_ref, *out_refs):
-    own_ref[...] = keep_ref[0] + got_ref[0].astype(F32)
-    for index, out_ref in enumerate(out_refs):
-        out_ref[...] = (keep_ref[index + 1] + got_ref[index + 1].astype(F32)).astype(BF)
 
 
 def quad_kernel(place_ref, own_ref, first_ref, second_ref, third_ref, *out_refs):
@@ -267,31 +298,39 @@
 
 
 def operator_kernel(picks_ref, place_ref, *refs):
-    out_ref = refs[-1]
-    size, width = refs[0].shape[0] // 4, refs[0].shape[0]
-    for index, source in enumerate(refs[:-1]):
+    sources, (out_ref, wide, sems) = refs[:-3], refs[-3:]
+    width = sources[0].shape[0]
+    size = width // 4
+    copies = []
+    for index, source in enumerate(sources):
+        wide[index] = source[...].astype(F32)
         pick = 2 * ((index + 4) % 8)
         for turn in range(4):
             at = picks_ref[pick + 1] * width + (place_ref[1] ^ turn) * size
-            out_ref[picks_ref[pick], pl.ds(pl.multiple_of(at, size), size), :] = source[
-                turn * size : (turn + 1) * size
-            ].astype(F32)
-
-
-def add_kernel(
-    cap, base_ref, ids_ref, back_ref, head_ref, high_ref, low_ref, neg_ref, out_ref
-):
+            copy = pltpu.make_async_copy(
+                wide.at[index, pl.ds(turn * size, size)],
+                out_ref.at[picks_ref[pick], pl.ds(pl.multiple_of(at, size), size)],
+                sems.at[index, turn],
+            )
+            copy.start()
+            copies.append(copy)
+    for copy in copies:
+        copy.wait()
+
+
+def add_kernel(cap, base_ref, ids_ref, neg_ref, take, out_ref):
     count = out_ref.shape[0]
     base = base_ref[0]
-    parts = back_ref.shape[0]
 
     def pick(row):
         return hot((iota((count, row.shape[1]), 0) + base) == row)
 
+    heads = pick(take(0)[...])
+    total = dot(heads, take(1)[...]) + dot(heads, take(2)[...])
+    back_ref = take(3)
+    parts = back_ref.shape[0]
     tails = jnp.concatenate([back_ref[index, :cap] for index in range(parts)], axis=0)
-    total = dot(pick(ids_ref[...]), tails)
-    heads = pick(head_ref[...])
-    total = total + dot(heads, high_ref[...]) + dot(heads, low_ref[...])
+    total = total + dot(pick(ids_ref[...]), tails)
     negs = back_ref[0, cap:].astype(F32)
     for index in range(1, parts):
         negs = negs + back_ref[index, cap:].astype(F32)
@@ -300,11 +339,38 @@
     out_ref[...] = (total + (dot(own, high) + dot(own, low))).astype(out_ref.dtype)
 
 
-def join_kernel(place_ref, mine_ref, other_ref, out_ref):
+def both_kernel(kept_ref, arrived_ref, out_ref):
+    out_ref[...] = (kept_ref[...] + arrived_ref[...].astype(F32)).astype(BF)
+
+
+def join_kernel(place_ref, mine_ref, over_ref, other_ref, far_ref, out_ref, wide, sems):
     half = mine_ref.shape[0]
     core = place_ref[2]
-    out_ref[pl.ds(pl.multiple_of(core * half, half), half), :] = mine_ref[...]
-    out_ref[pl.ds(pl.multiple_of((1 - core) * half, half), half), :] = other_ref[...]
+    copies = []
+    for index, (first, second, at) in enumerate(
+        ((mine_ref, over_ref, core), (other_ref, far_ref, 1 - core))
+    ):
+        wide[index] = first[...].astype(F32) + second[...].astype(F32)
+        copy = pltpu.make_async_copy(
+            wide.at[index],
+            out_ref.at[pl.ds(pl.multiple_of(at * half, half), half)],
+            sems.at[index],
+        )
+        copy.start()
+        copies.append(copy)
+    for copy in copies:
+        copy.wait()
+
+
+def write(body, out, scalars, near, scratch):
+    return pl.pallas_call(
+        body,
+        out_shape=jax.ShapeDtypeStruct(*out),
+        in_specs=[SMEM] * len(scalars) + [VMEM] * len(near),
+        out_specs=FAR,
+        scratch_shapes=scratch,
+        compiler_params=pltpu.CompilerParams(vmem_limit_bytes=60 * 1024 * 1024),
+    )(*scalars, *near)
 
 
 def flip(x, axis, size, bit):
@@ -357,60 +423,76 @@
     requests = exchange(request)
     rows, queries = call(
         query_kernel,
-        [((edges, columns), BF), ((edges, columns), BF)],
-        (),
+        [((edges, columns), BF, True), ((edges, columns), BF, True)],
+        (),
+        (),
+        (head, rel, entities, relations),
         (slot,),
-        (head, rel, entities, relations),
-    )
-    requests, rows, queries = lax.optimization_barrier((requests, rows, queries))
+    )
     asked, found, neg_near = call(
         functools.partial(lookup_kernel, cap),
-        [((1, slots), I32), ((slots, columns), BF), ((parts * share, columns), BF)],
+        [((1, slots), I32), ((slots, columns), BF, True), ((parts * share, columns), BF)],
         (),
         (requests,),
         (entities,),
+        (rows,),
     )
     got = exchange(found.reshape(parts, cap, columns)).reshape(slots, columns)
     neg_core, neg_across, neg_both = [flip(neg_near, "rep", reps, k) for k in (1, 2, 3)]
 
-    terms = F32 if not special else BF
     loss, weight, grad, prob, away = call(
         functools.partial(edge_kernel, factor),
         [
             ((1, edges), F32),
             ((edges, 1), F32),
-            ((edges, columns), BF),
-            ((edges, negs), BF),
-            ((4, columns // 2, columns), terms),
+            ((edges, columns), BF, True),
+            ((edges, negs), BF, True),
+            ((4, columns // 2, columns), BF if special else F32, True),
         ],
         (picks,),
-        (queries, got, slot, neg_near, neg_core, neg_across, neg_both, rows, rel),
+        (slot, neg_near, neg_core, neg_across, neg_both),
+        (queries, got, rows, rel),
     )
     (back,) = call(
         functools.partial(back_kernel, factor, cap),
-        [((parts, cap + neg_dev, columns), BF)],
-        (),
-        (queries, prob, weight, slot),
+        [((parts, cap + neg_dev, columns), BF, True)],
+        (),
+        (weight, slot),
+        (queries, prob),
     )
     returned = exchange(back)
-    keep, high, low = call(
-        keep_kernel,
-        [((4, columns // 2, columns), F32), ((edges, columns), BF), ((edges, columns), BF)],
-        (picks,),
-        (rows, rel, grad, relations),
-    )
-
-    def add(base, size, kind):
+
+    def add(base, size, kind, after):
         return call(
             functools.partial(add_kernel, cap),
             [((size, columns), kind)],
             (base.reshape(1),),
-            (asked, returned, head, high, low, neg_own),
+            (asked, neg_own),
+            (head, high, low, returned),
+            after,
         )[0]
 
+    def head_grads(after):
+        return call(
+            head_kernel,
+            [((edges, columns), BF, True), ((edges, columns), BF, True)],
+            (),
+            (),
+            (grad, rel, relations),
+            after,
+        )
+
     if not special:
+        (keep,) = call(
+            keep_kernel,
+            [((4, columns // 2, columns), F32, True)],
+            (picks,),
+            (),
+            (rows, grad, rel),
+        )
         whole = jnp.concatenate([away, keep], axis=0).reshape(count, columns, columns)
-        entity_grad = lax.psum(add(jnp.zeros((), I32), ent_dev, F32), "rep")
+        high, low = head_grads(())
+        entity_grad = lax.psum(add(jnp.zeros((), I32), ent_dev, F32, ()), "rep")
         return entity_grad, lax.psum(whole, ("dom", "rep")), loss.reshape(edges)
 
     half, quarter = columns // 2, columns // 8
@@ -423,35 +505,51 @@
 
     other = flip(away, "rep", 4, 1)
     own, *sent = call(
-        pair_kernel, [((half, columns), F32)] + [((half, columns), BF)] * 3, (), (keep, other)
+        pair_kernel,
+        [((half, columns), F32)] + [((half, columns), BF)] * 3,
+        (picks,),
+        (),
+        (rows, grad, rel, other),
+        (back,),
     )
     met = [quad(k + 1)(v) for k, v in enumerate(sent)]
+    high, low = head_grads((sent[0],))
     own, *sent = call(
         quad_kernel,
         [((quarter, columns), F32)] + [((quarter, columns), BF)] * 3,
         (place,),
         (own, *met),
+        (),
+        (high,),
     )
     met = [flip(v, "dom", 8, 2 * (k + 1)) for k, v in enumerate(sent)]
     (own,) = call(sum_kernel, [((quarter, columns), BF)], (), (own, *met))
     stripes = [own] + [flip(own, "dom", 8, 2 * (k + 1)) for k in range(3)]
     own = jnp.concatenate(stripes, axis=0)
-    mine = [own] + [quad(k)(own) for k in range(1, 4)]
+    over_y = quad(2)(own)
+    mine = [own, quad(1)(own), over_y, quad(1)(over_y)]
     others = [flip(v, "rep", 4, 1) for v in mine]
-    (relation_grad,) = call(
-        operator_kernel, [((count, columns, columns), F32)], (picks, place), (*mine, *others)
+    relation_grad = write(
+        operator_kernel,
+        ((count, columns, columns), F32),
+        (picks, place),
+        (*mine, *others),
+        [pltpu.VMEM((8, half, columns), F32), pltpu.SemaphoreType.DMA((8, 4))],
     )
 
     rows_half = ent_dev // 2
-    leaving = add((1 - core) * rows_half, rows_half, BF)
+    leaving = add((1 - core) * rows_half, rows_half, BF, (own,))
     arrived = flip(leaving, "rep", 4, 1)
-    kept = add(core * rows_half, rows_half, F32)
-    both = (kept + arrived.astype(F32)).astype(BF)
+    kept = add(core * rows_half, rows_half, F32, (leaving, over_y))
+    (both,) = call(both_kernel, [((rows_half, columns), BF)], (), (kept, arrived))
     across = flip(both, "rep", 4, 2)
-    done = both.astype(F32) + across.astype(F32)
-    partner = flip(done, "rep", 4, 1)
-    (entity_grad,) = call(
-        join_kernel, [((ent_dev, columns), F32)], (place,), (done, partner)
+    pieces = (both, across, flip(both, "rep", 4, 1), flip(across, "rep", 4, 1))
+    entity_grad = write(
+        join_kernel,
+        ((ent_dev, columns), F32),
+        (place,),
+        pieces,
+        [pltpu.VMEM((2, rows_half, columns), F32), pltpu.SemaphoreType.DMA((2,))],
     )
     return entity_grad, relation_grad, loss.reshape(edges)
 

time: 170 us -> 175 us (1.029)
  Pallas kernels: 23.2 us -> 53.9 us
  waiting for transfers between devices: 88.3 us -> 71.5 us
  local copies, waits for them, and re-layouts: 18.5 us -> 9.44 us
  other arithmetic: 0.4 us -> 2.18 us
    pallas_call x13 -> x14, Pallas kernels: 23.2 us -> 53.9 us  [the longest x12 47.2 us: call(): pl.pallas_call(kernel, out_shape=[jax.ShapeDtypeStruct(out[0], out[1]) fo...]
    all_to_all x3, waiting for transfers between devices: 43.3 us -> 22 us  [exchange(): return lax.all_to_all(x, 'dom', split_axis=0, concat_axis=0, tiled=True)]
    unnamed x56, local copies, waits for them, and re-layouts: 18.5 us -> 8.78 us
    ppermute x17 -> x18, waiting for transfers between devices: 24.8 us -> 27.3 us  [flip(): return lax.ppermute(x, axis, [(i, i ^ bit) for i in range(size)])]
    ppermute x6, waiting for transfers between devices: 20.2 us -> 22.3 us  [quad(): return lambda v: lax.ppermute(v, ('dom', 'rep'), pairs)]
    all_to_all x3, starting transfers between devices: 16.8 us -> 14.7 us  [exchange(): return lax.all_to_all(x, 'dom', split_axis=0, concat_axis=0, tiled=True)]
    ppermute x17 -> x18, starting transfers between devices: 13.5 us -> 13.8 us  [flip(): return lax.ppermute(x, axis, [(i, i ^ bit) for i in range(size)])]
  transfers between devices with their start and end apart: 26 -> 27, of which waited for: 18 -> 18; matrix products, arithmetic and copies ran while one was open for 0% -> 1% of each run, Pallas kernels for 6% -> 14%
where the time goes in v3:
time: 175 us; the launch traced here: 174 us
  waiting for transfers between devices  71.5 us (41%)
  Pallas kernels  53.9 us (31%)
  starting transfers between devices  35.7 us (20%)
  local copies, waits for them, and re-layouts  9.44 us (5%)
  other arithmetic  2.18 us (1%)
    pallas_call x12, Pallas kernels, call(): pl.pallas_call(kernel, out_shape=[jax.ShapeDtypeStruct(out[0], out[1]) fo...  47.2 us
    ppermute x18, waiting for transfers between devices, flip(): return lax.ppermute(x, axis, [(i, i ^ bit) for i in range(size)])  27.3 us
    ppermute x6, waiting for transfers between devices, quad(): return lambda v: lax.ppermute(v, ('dom', 'rep'), pairs)  22.3 us
    all_to_all x3, waiting for transfers between devices, exchange(): return lax.all_to_all(x, 'dom', split_axis=0, concat_axis=0, tiled=True)  22 us
    all_to_all x3, starting transfers between devices, exchange(): return lax.all_to_all(x, 'dom', split_axis=0, concat_axis=0, tiled=True)  14.7 us
    ppermute x18, starting transfers between devices, flip(): return lax.ppermute(x, axis, [(i, i ^ bit) for i in range(size)])  13.8 us
    unnamed x56, local copies, waits for them, and re-layouts  8.78 us
    ppermute x6, starting transfers between devices, quad(): return lambda v: lax.ppermute(v, ('dom', 'rep'), pairs)  7.17 us
  transfers between devices with their start and end apart: 27, of which 18 were waited for; matrix products, arithmetic and copies ran while one was open for 1% of the time, Pallas kernels for 14%

profile of v3, /device:TPU:0, one launch (start us, length us, event | category | flops | bytes accessed | tf_op | source)
XLA Modules:
  0.0 173.9 jit_solution(9927571484420329131)
XLA Ops:
  0.7 0.6 pad_add_fusion.refs_0_.place_ref
  1.3 3.3 %shard_map.94 = (s32[1,512]{1,0:T(1,128)}, s32[1,32]{1,0:T(1,128)}, bf16[8,8,640]{2,1,0:T(8,128)(2,1)}) custom-call(s32[3]{0:T(128)} %pad_add_fusion.refs_0_.place_ref, s32[1,512]{1,0:T(1,128)} %bitcast.34, s32[1,512]{1,0:T(1,128)} %bitcast.35, s32[1,32]{1,0:T(1,128)} %bitcast.36, bf16[1024,512]{1,0:T(8,128)(2,1)} %refs_1_.1), custom_call_target="tpu_custom_call" | custom-call | tf_op jit(solution)/shard_map/pallas_call | solution.py:60
  4.5 7.3 %all-to-all-start = ((bf16[8,8,640]{2,1,0:T(8,128)(2,1)}), bf16[8,8,640]{2,1,0:T(8,128)(2,1)S(1)}, u32[]{:S(2)}, u32[]{:S(2)}) async-start(bf16[8,8,640]{2,1,0:T(8,128)(2,1)} %get-tuple-element.26), calls=%async_computation | async-start | bytes 163840 | tf_op jit(solution)/shard_map/all_to_all | solution.py:381
  11.8 4.4 %shard_map.95 = (bf16[512,512]{1,0:T(8,128)(2,1)}, bf16[512,512]{1,0:T(8,128)(2,1)}) custom-call(s32[1,512]{1,0:T(1,128)} %bitcast.31, s32[1,512]{1,0:T(1,128)} %bitcast.27, bf16[1024,512]{1,0:T(8,128)(2,1)} %refs_1_.1, bf16[4,512,512]{2,1,0:T(8,128)(2,1)} %refs_2_.3, s32[1,512]{1,0:T(1,128)} %get-tuple-element.27.refs_4_.refs_1_), custom_call_target="tpu_custom_call" | custom-call | tf_op jit(solution)/shard_map/pallas_call | solution.py:60
  16.2 2.6 %all-to-all-done.refs_0_ = bf16[8,8,640]{2,1,0:T(8,128)(2,1)S(1)} async-done(((bf16[8,8,640]{2,1,0:T(8,128)(2,1)}), bf16[8,8,640]{2,1,0:T(8,128)(2,1)S(1)}, u32[]{:S(2)}, u32[]{:S(2)}) %all-to-all-start) | async-done | bytes 81952 | tf_op jit(solution)/shard_map/all_to_all | solution.py:381
  18.8 0.6 copy-done.10
  19.4 5.4 %shard_map.96 = (s32[1,1024]{1,0:T(1,128)}, bf16[1024,512]{1,0:T(8,128)(2,1)}, bf16[64,512]{1,0:T(8,128)(2,1)}) custom-call(bf16[8,8,640]{2,1,0:T(8,128)(2,1)} %copy-done.10, bf16[1024,512]{1,0:T(8,128)(2,1)} %refs_1_.1, bf16[512,512]{1,0:T(8,128)(2,1)} %get-tuple-element.28.refs_2_.refs_8_.refs_1_), custom_call_target="tpu_custom_call" | custom-call | tf_op jit(solution)/shard_map/pallas_call | solution.py:60
  24.8 3.7 %all-to-all-start.1 = ((bf16[8,128,512]{2,1,0:T(8,128)(2,1)}), bf16[8,128,512]{2,1,0:T(8,128)(2,1)S(1)}, u32[]{:S(2)}, u32[]{:S(2)}) async-start(bf16[8,128,512]{2,1,0:T(8,128)(2,1)} %bitcast.26), calls=%async_computation.1 | async-start | bytes 2097152 | tf_op jit(solution)/shard_map/all_to_all | solution.py:381
  28.6 1.6 collective-permute-start.1
  30.2 0.3 collective-permute-start
  30.5 0.7 stack.71.refs_0_.picks_ref
  31.2 1.8 %collective-permute-done.2.refs_5_ = bf16[64,512]{1,0:T(8,128)(2,1)S(1)} collective-permute-done((bf16[64,512]{1,0:T(8,128)(2,1)S(1)}, bf16[64,512]{1,0:T(8,128)(2,1)S(1)}, u32[]{:S(2)}, u32[]{:S(2)}) %collective-permute-start.2) | collective-permute-done | bytes 65568 | tf_op jit(solution)/shard_map/ppermute | solution.py:377
  32.9 1.5 collective-permute-done.1.refs_4_
  34.4 19.4 %all-to-all-done.1 = bf16[8,128,512]{2,1,0:T(8,128)(2,1)S(1)} async-done(((bf16[8,128,512]{2,1,0:T(8,128)(2,1)}), bf16[8,128,512]{2,1,0:T(8,128)(2,1)S(1)}, u32[]{:S(2)}, u32[]{:S(2)}) %all-to-all-start.1) | async-done | bytes 1048608 | tf_op jit(solution)/shard_map/all_to_all | solution.py:381
  53.9 1.0 copy-done.1
  54.8 6.9 %shard_map.97 = (f32[1,512]{1,0:T(1,128)}, f32[512,1]{1,0:T(8,128)}, bf16[512,512]{1,0:T(8,128)(2,1)}, bf16[512,256]{1,0:T(8,128)(2,1)}, bf16[4,256,512]{2,1,0:T(8,128)(2,1)}) custom-call(s32[16]{0:T(128)} %stack.71.refs_0_.picks_ref, s32[1,512]{1,0:T(1,128)} %get-tuple-element.27.refs_4_.refs_1_, bf16[64,512]{1,0:T(8,128)(2,1)} %get-tuple-element.31.refs_2_, ...), custom_call_target="tpu_custom_call" | custom-call | tf_op jit(solution)/shard_map/pallas_call | solution.py:60
  61.7 4.4 %shard_map.98.refs_5_ = bf16[8,160,512]{2,1,0:T(8,128)(2,1)} custom-call(f32[512,1]{1,0:T(8,128)} %get-tuple-element.36.refs_0_, s32[1,512]{1,0:T(1,128)} %get-tuple-element.27.refs_4_.refs_1_, bf16[512,512]{1,0:T(8,128)(2,1)} %get-tuple-element.32.refs_6_.refs_2_, bf16[512,256]{1,0:T(8,128)(2,1)} %get-tuple-element.37.refs_3_), custom_call_target="tpu_custom_call" | custom-call | tf_op jit(solution)/shard_map/pallas_call | solution.py:60
  66.1 3.8 %all-to-all-start.2 = ((bf16[8,160,512]{2,1,0:T(8,128)(2,1)}), bf16[8,160,512]{2,1,0:T(8,128)(2,1)S(1)}, u32[]{:S(2)}, u32[]{:S(2)}) async-start(bf16[8,160,512]{2,1,0:T(8,128)(2,1)} %shard_map.98.refs_5_), calls=%async_computation.2 | async-start | bytes 2621440 | tf_op jit(solution)/shard_map/all_to_all | solution.py:381
  69.9 2.6 %collective-permute-done.3.refs_4_ = bf16[4,256,512]{2,1,0:T(8,128)(2,1)S(1)} collective-permute-done((bf16[4,256,512]{2,1,0:T(8,128)(2,1)S(1)}, bf16[4,256,512]{2,1,0:T(8,128)(2,1)S(1)}, u32[]{:S(2)}, u32[]{:S(2)}) %collective-permute-start.3) | collective-permute-done | bytes 1048608 | tf_op jit(solution)/shard_map/ppermute | solution.py:377
  72.6 1.0 copy-done.3
  73.6 4.0 %shard_map.99 = (f32[256,512]{1,0:T(8,128)}, bf16[256,512]{1,0:T(8,128)(2,1)}, bf16[256,512]{1,0:T(8,128)(2,1)}, bf16[256,512]{1,0:T(8,128)(2,1)}) custom-call(s32[16]{0:T(128)} %stack.71.refs_0_.picks_ref, bf16[512,512]{1,0:T(8,128)(2,1)} %get-tuple-element.28.refs_2_.refs_8_.refs_1_, bf16[512,512]{1,0:T(8,128)(2,1)} %get-tuple-element.34.refs_2_.refs_0_, ...), custom_call_target="tpu_custom_call" | custom-call | tf_op jit(solution)/shard_map/pallas_call | solution.py:60
  77.6 1.6 collective-permute-start.5
  79.2 1.6 collective-permute-start.6
  80.8 0.4 collective-permute-start.4
  81.1 4.2 %shard_map.100 = (bf16[512,512]{1,0:T(8,128)(2,1)}, bf16[512,512]{1,0:T(8,128)(2,1)}) custom-call(bf16[512,512]{1,0:T(8,128)(2,1)} %get-tuple-element.34.refs_2_.refs_0_, s32[1,512]{1,0:T(1,128)} %bitcast.30, bf16[4,512,512]{2,1,0:T(8,128)(2,1)} %refs_2_.3, bf16[256,512]{1,0:T(8,128)(2,1)} %get-tuple-element.38.refs_3_), custom_call_target="tpu_custom_call" | custom-call | tf_op jit(solution)/shard_map/pallas_call | solution.py:60
  85.3 5.3 %collective-permute-done.5.refs_3_ = bf16[256,512]{1,0:T(8,128)(2,1)S(1)} collective-permute-done((bf16[256,512]{1,0:T(8,128)(2,1)}, bf16[256,512]{1,0:T(8,128)(2,1)S(1)}, u32[]{:S(2)}, u32[]{:S(2)}) %collective-permute-start.5) | collective-permute-done | bytes 262176 | tf_op jit(solution)/shard_map/ppermute | solution.py:504
  90.6 4.2 %collective-permute-done.6.refs_4_ = bf16[256,512]{1,0:T(8,128)(2,1)S(1)} collective-permute-done((bf16[256,512]{1,0:T(8,128)(2,1)}, bf16[256,512]{1,0:T(8,128)(2,1)S(1)}, u32[]{:S(2)}, u32[]{:S(2)}) %collective-permute-start.6) | collective-permute-done | bytes 262176 | tf_op jit(solution)/shard_map/ppermute | solution.py:504
  94.8 4.1 %collective-permute-done.4.refs_2_ = bf16[256,512]{1,0:T(8,128)(2,1)S(1)} collective-permute-done((bf16[256,512]{1,0:T(8,128)(2,1)}, bf16[256,512]{1,0:T(8,128)(2,1)S(1)}, u32[]{:S(2)}, u32[]{:S(2)}) %collective-permute-start.4) | collective-permute-done | bytes 262176 | tf_op jit(solution)/shard_map/ppermute | solution.py:504
  98.9 0.7 copy-done.13
  99.6 2.1 %shard_map.101 = (f32[64,512]{1,0:T(8,128)}, bf16[64,512]{1,0:T(8,128)(2,1)}, bf16[64,512]{1,0:T(8,128)(2,1)}, bf16[64,512]{1,0:T(8,128)(2,1)}) custom-call(s32[3]{0:T(128)} %pad_add_fusion.refs_0_.place_ref, f32[256,512]{1,0:T(8,128)} %get-tuple-element.41.refs_1_, bf16[256,512]{1,0:T(8,128)(2,1)} %copy-done.13, bf16[256,512]{1,0:T(8,128)(2,1)} %copy-done.11, ...), custom_call_target="tpu_custom_call" | custom-call | tf_op jit(solution)/shard_map/pallas_call | solution.py:60
  101.6 2.9 %collective-permute-start.7 = (bf16[64,512]{1,0:T(8,128)(2,1)}, bf16[64,512]{1,0:T(8,128)(2,1)S(1)}, u32[]{:S(2)}, u32[]{:S(2)}) collective-permute-start(bf16[64,512]{1,0:T(8,128)(2,1)} %get-tuple-element.45), channel_id=1, source_target_pairs={{0,8},{4,12},{8,0},{12,4},{16,24},{20,28},{24,16},{28,20},{1,9},{5... | collective-permute-start | bytes 196616 | tf_op jit(solution)/shard_map/ppermute | solution.py:377
  104.5 2.3 %collective-permute-start.8 = (bf16[64,512]{1,0:T(8,128)(2,1)}, bf16[64,512]{1,0:T(8,128)(2,1)S(1)}, u32[]{:S(2)}, u32[]{:S(2)}) collective-permute-start(bf16[64,512]{1,0:T(8,128)(2,1)} %get-tuple-element.46), channel_id=1, source_target_pairs={{0,16},{4,20},{8,24},{12,28},{16,0},{20,4},{24,8},{28,12},{1,17},{... | collective-permute-start | bytes 196616 | tf_op jit(solution)/shard_map/ppermute | solution.py:377
  106.8 0.1 collective-permute-start.9
  107.0 4.8 %collective-permute-done.8.refs_2_ = bf16[64,512]{1,0:T(8,128)(2,1)S(1)} collective-permute-done((bf16[64,512]{1,0:T(8,128)(2,1)}, bf16[64,512]{1,0:T(8,128)(2,1)S(1)}, u32[]{:S(2)}, u32[]{:S(2)}) %collective-permute-start.8) | collective-permute-done | bytes 65568 | tf_op jit(solution)/shard_map/ppermute | solution.py:377
  111.8 1.4 collective-permute-done.9.refs_3_
  113.2 0.6 copy-done.22
  113.8 1.6 shard_map.102
  115.4 1.8 %collective-permute-start.12 = (bf16[64,512]{1,0:T(8,128)(2,1)}, bf16[64,512]{1,0:T(8,128)(2,1)S(1)}, u32[]{:S(2)}, u32[]{:S(2)}) collective-permute-start(bf16[64,512]{1,0:T(8,128)(2,1)} %shard_map.102), channel_id=1, source_target_pairs={{0,24},{4,28},{8,16},{12,20},{16,8},{20,12},{24,0},{28,4},{1,25},{... | collective-permute-start | bytes 196616 | tf_op jit(solution)/shard_map/ppermute | solution.py:377
  117.1 0.3 collective-permute-start.11
  117.4 2.3 %collective-permute-start.10 = (bf16[64,512]{1,0:T(8,128)(2,1)}, bf16[64,512]{1,0:T(8,128)(2,1)S(1)}, u32[]{:S(2)}, u32[]{:S(2)}) collective-permute-start(bf16[64,512]{1,0:T(8,128)(2,1)} %shard_map.102), channel_id=1, source_target_pairs={{0,8},{4,12},{8,0},{12,4},{16,24},{20,28},{24,16},{28,20},{1,9},{5... | collective-permute-start | bytes 196616 | tf_op jit(solution)/shard_map/ppermute | solution.py:377
  119.8 2.0 %collective-permute-done.12 = bf16[64,512]{1,0:T(8,128)(2,1)S(1)} collective-permute-done((bf16[64,512]{1,0:T(8,128)(2,1)}, bf16[64,512]{1,0:T(8,128)(2,1)S(1)}, u32[]{:S(2)}, u32[]{:S(2)}) %collective-permute-start.12) | collective-permute-done | bytes 65568 | tf_op jit(solution)/shard_map/ppermute | solution.py:377
  121.8 1.4 collective-permute-done.11
  123.2 1.6 pad_maximum_fusion.refs_7_.refs_0_
  124.8 1.1 copy-done
  125.8 4.3 %shard_map.103.refs_7_ = bf16[512,512]{1,0:T(8,128)(2,1)} custom-call(s32[1]{0:T(128)} %bitcast.23.refs_0_, s32[1,1024]{1,0:T(1,128)} %get-tuple-element.29.refs_1_, s32[1,32]{1,0:T(1,128)} %get-tuple-element.30.refs_2_, s32[1,512]{1,0:T(1,128)} %bitcast.32, bf16[512,512]{1,0:T(8,128)(2,1)} %get-tuple-element.39.refs_5_.refs_4_, ...), custom_call_target="tpu_custom_call" | custom-call | tf_op jit(solution)/shard_map/pallas_call | solution.py:60
  130.2 1.6 collective-permute-start.13
  131.8 7.1 %collective-permute-done.13.refs_8_.refs_2_ = bf16[256,512]{1,0:T(8,128)(2,1)S(1)} collective-permute-done((bf16[256,512]{1,0:T(8,128)(2,1)S(1)}, bf16[256,512]{1,0:T(8,128)(2,1)S(1)}, u32[]{:S(2)}, u32[]{:S(2)}) %collective-permute-start.13) | collective-permute-done | bytes 262176 | tf_op jit(solution)/shard_map/ppermute | solution.py:504
  138.9 0.7 copy-done.4
  139.7 4.5 %shard_map.104.refs_0_ = f32[512,512]{1,0:T(8,128)} custom-call(s32[1]{0:T(128)} %bitcast.3.refs_0_, s32[1,1024]{1,0:T(1,128)} %get-tuple-element.29.refs_1_, s32[1,32]{1,0:T(1,128)} %get-tuple-element.30.refs_2_, s32[1,512]{1,0:T(1,128)} %bitcast.33, bf16[512,512]{1,0:T(8,128)(2,1)} %get-tuple-element.39.refs_5_.refs_4_, ...), custom_call_target="tpu_custom_call" | custom-call | tf_op jit(solution)/shard_map/pallas_call | solution.py:60
  144.2 0.8 copy-done.9
  144.9 2.3 %shard_map.105.mine_ref = bf16[512,512]{1,0:T(8,128)(2,1)} custom-call(f32[512,512]{1,0:T(8,128)} %shard_map.104.refs_0_, bf16[512,512]{1,0:T(8,128)(2,1)} %copy-done.9), custom_call_target="tpu_custom_call" | custom-call | tf_op jit(solution)/shard_map/pallas_call | solution.py:60
  147.2 1.5 collective-permute-start.15
  148.7 2.0 %collective-permute-start.19 = (bf16[256,512]{1,0:T(8,128)(2,1)S(1)}, bf16[256,512]{1,0:T(8,128)(2,1)S(1)}, u32[]{:S(2)}, u32[]{:S(2)}) collective-permute-start(bf16[256,512]{1,0:T(8,128)(2,1)S(1)} %copy-done.5), channel_id=1, source_target_pairs={{0,4},{1,5},{2,6},{3,7},{4,0},{5,1},{6,2},{7,3},{8,12},{9,13},{10,... | collective-permute-start | bytes 786440 | tf_op jit(solution)/shard_map/ppermute | solution.py:504
  150.8 10.1 %collective-permute-done.15.over_ref = bf16[512,512]{1,0:T(8,128)(2,1)S(1)} collective-permute-done((bf16[512,512]{1,0:T(8,128)(2,1)}, bf16[512,512]{1,0:T(8,128)(2,1)S(1)}, u32[]{:S(2)}, u32[]{:S(2)}) %collective-permute-start.15) | collective-permute-done | bytes 524320 | tf_op jit(solution)/shard_map/ppermute | solution.py:377
  160.9 0.5 collective-permute-start.22
  161.4 0.1 collective-permute-start.21
  161.5 1.6 collective-permute-done.19.refs_3_
  163.1 0.5 collective-permute-done.21.refs_5_
  163.6 1.1 collective-permute-done.23.refs_7_
  164.7 0.7 copy-done.19
  165.3 3.8 %shard_map.107 = f32[4,512,512]{2,1,0:T(8,128)} custom-call(s32[16]{0:T(128)} %stack.71.refs_0_.picks_ref, s32[3]{0:T(128)} %pad_add_fusion.refs_0_.place_ref, bf16[256,512]{1,0:T(8,128)(2,1)} %pad_maximum_fusion.refs_7_.refs_0_, bf16[256,512]{1,0:T(8,128)(2,1)} %copy-done.15, bf16[256,512]{1,0:T(8,128)(2,1)} %copy-done.4, bf16[256,512]{1,0:T(8,128)(2,1)} %copy-done.16, ...), custom_call_target="tpu_custom_call" | custom-call | tf_op jit(solution)/shard_map/pallas_call | solution.py:366
  169.2 0.8 copy-done.7
  170.0 0.8 copy-done.8
  170.8 3.0 %shard_map.106 = f32[1024,512]{1,0:T(8,128)} custom-call(s32[3]{0:T(128)} %pad_add_fusion.refs_0_.place_ref, bf16[512,512]{1,0:T(8,128)(2,1)} %shard_map.105.mine_ref, bf16[512,512]{1,0:T(8,128)(2,1)} %copy-done.6, bf16[512,512]{1,0:T(8,128)(2,1)} %copy-done.7, bf16[512,512]{1,0:T(8,128)(2,1)} %copy-done.8), custom_call_target="tpu_custom_call" | custom-call | tf_op jit(solution)/shard_map/pallas_call | solution.py:366
  (63 shorter events, 0.4 us)
Async XLA Ops:
  4.5 14.3 %all-to-all-start = ((bf16[8,8,640]{2,1,0:T(8,128)(2,1)}), bf16[8,8,640]{2,1,0:T(8,128)(2,1)S(1)}, u32[]{:S(2)}, u32[]{:S(2)}) async-start(bf16[8,8,640]{2,1,0:T(8,128)(2,1)} %get-tuple-element.26), calls=%async_computation | async-start | bytes 163840 | tf_op jit(solution)/shard_map/all_to_all | solution.py:381
  18.8 0.6 copy-start.10
  24.8 3.7 %copy-start.23 = (bf16[64,512]{1,0:T(8,128)(2,1)S(1)}, bf16[64,512]{1,0:T(8,128)(2,1)}, u32[]{:S(2)}) copy-start(bf16[64,512]{1,0:T(8,128)(2,1)} %get-tuple-element.31.refs_2_) | copy-start | bytes 196612
  24.8 29.0 %all-to-all-start.1 = ((bf16[8,128,512]{2,1,0:T(8,128)(2,1)}), bf16[8,128,512]{2,1,0:T(8,128)(2,1)S(1)}, u32[]{:S(2)}, u32[]{:S(2)}) async-start(bf16[8,128,512]{2,1,0:T(8,128)(2,1)} %bitcast.26), calls=%async_computation.1 | async-start | bytes 2097152 | tf_op jit(solution)/shard_map/all_to_all | solution.py:381
  28.6 4.4 %collective-permute-start.2 = (bf16[64,512]{1,0:T(8,128)(2,1)S(1)}, bf16[64,512]{1,0:T(8,128)(2,1)S(1)}, u32[]{:S(2)}, u32[]{:S(2)}) collective-permute-start(bf16[64,512]{1,0:T(8,128)(2,1)S(1)} %copy-done.23), channel_id=1, source_target_pairs={{0,3},{1,2},{2,1},{3,0},{4,7},{5,6},{6,5},{7,4},{8,11},{9,10},{10,... | collective-permute-start | bytes 196616 | tf_op jit(solution)/shard_map/ppermute | solution.py:377
  28.6 5.8 %collective-permute-start.1 = (bf16[64,512]{1,0:T(8,128)(2,1)S(1)}, bf16[64,512]{1,0:T(8,128)(2,1)S(1)}, u32[]{:S(2)}, u32[]{:S(2)}) collective-permute-start(bf16[64,512]{1,0:T(8,128)(2,1)S(1)} %copy-done.23), channel_id=1, source_target_pairs={{0,2},{1,3},{2,0},{3,1},{4,6},{5,7},{6,4},{7,5},{8,10},{9,11},{10,... | collective-permute-start | bytes 196616 | tf_op jit(solution)/shard_map/ppermute | solution.py:377
  30.2 4.2 %collective-permute-start = (bf16[64,512]{1,0:T(8,128)(2,1)S(1)}, bf16[64,512]{1,0:T(8,128)(2,1)S(1)}, u32[]{:S(2)}, u32[]{:S(2)}) collective-permute-start(bf16[64,512]{1,0:T(8,128)(2,1)S(1)} %copy-done.23), channel_id=1, source_target_pairs={{0,1},{1,0},{2,3},{3,2},{4,5},{5,4},{6,7},{7,6},{8,9},{9,8},{10,11... | collective-permute-start | bytes 196616 | tf_op jit(solution)/shard_map/ppermute | solution.py:377
  32.9 20.9 %copy-start.24 = (bf16[64,512]{1,0:T(8,128)(2,1)}, bf16[64,512]{1,0:T(8,128)(2,1)S(1)}, u32[]{:S(2)}) copy-start(bf16[64,512]{1,0:T(8,128)(2,1)S(1)} %collective-permute-done.2.refs_5_) | copy-start | bytes 196612
  34.4 19.4 %copy-start.25 = (bf16[64,512]{1,0:T(8,128)(2,1)}, bf16[64,512]{1,0:T(8,128)(2,1)S(1)}, u32[]{:S(2)}) copy-start(bf16[64,512]{1,0:T(8,128)(2,1)S(1)} %collective-permute-done.1.refs_4_) | copy-start | bytes 196612
  34.4 19.4 %copy-start.26 = (bf16[64,512]{1,0:T(8,128)(2,1)}, bf16[64,512]{1,0:T(8,128)(2,1)S(1)}, u32[]{:S(2)}) copy-start(bf16[64,512]{1,0:T(8,128)(2,1)S(1)} %collective-permute-done.refs_3_) | copy-start | bytes 196612
  53.8 1.0 copy-start.1
  61.7 8.1 %copy-start.27 = (bf16[4,256,512]{2,1,0:T(8,128)(2,1)S(1)}, bf16[4,256,512]{2,1,0:T(8,128)(2,1)}, u32[]{:S(2)}) copy-start(bf16[4,256,512]{2,1,0:T(8,128)(2,1)} %get-tuple-element.35) | copy-start | bytes 3145732
  66.1 58.7 %all-to-all-start.2 = ((bf16[8,160,512]{2,1,0:T(8,128)(2,1)}), bf16[8,160,512]{2,1,0:T(8,128)(2,1)S(1)}, u32[]{:S(2)}, u32[]{:S(2)}) async-start(bf16[8,160,512]{2,1,0:T(8,128)(2,1)} %shard_map.98.refs_5_), calls=%async_computation.2 | async-start | bytes 2621440 | tf_op jit(solution)/shard_map/all_to_all | solution.py:381
  69.9 2.7 %collective-permute-start.3 = (bf16[4,256,512]{2,1,0:T(8,128)(2,1)S(1)}, bf16[4,256,512]{2,1,0:T(8,128)(2,1)S(1)}, u32[]{:S(2)}, u32[]{:S(2)}) collective-permute-start(bf16[4,256,512]{2,1,0:T(8,128)(2,1)S(1)} %copy-done.27), channel_id=1, source_target_pairs={{0,1},{1,0},{2,3},{3,2},{4,5},{5,4},{6,7},{7,6},{8,9},{9,8},{10,11... | collective-permute-start | bytes 3145736 | tf_op jit(solution)/shard_map/ppermute | solution.py:377
  72.6 1.0 copy-start.3
  77.6 13.0 %collective-permute-start.5 = (bf16[256,512]{1,0:T(8,128)(2,1)}, bf16[256,512]{1,0:T(8,128)(2,1)S(1)}, u32[]{:S(2)}, u32[]{:S(2)}) collective-permute-start(bf16[256,512]{1,0:T(8,128)(2,1)} %get-tuple-element.42), channel_id=1, source_target_pairs={{0,2},{1,3},{2,0},{3,1},{4,6},{5,7},{6,4},{7,5},{8,10},{9,11},{10,... | collective-permute-start | bytes 786440 | tf_op jit(solution)/shard_map/ppermute | solution.py:504
  79.2 15.6 %collective-permute-start.6 = (bf16[256,512]{1,0:T(8,128)(2,1)}, bf16[256,512]{1,0:T(8,128)(2,1)S(1)}, u32[]{:S(2)}, u32[]{:S(2)}) collective-permute-start(bf16[256,512]{1,0:T(8,128)(2,1)} %get-tuple-element.43), channel_id=1, source_target_pairs={{0,6},{1,7},{2,4},{3,5},{4,2},{5,3},{6,0},{7,1},{8,14},{9,15},{10,... | collective-permute-start | bytes 786440 | tf_op jit(solution)/shard_map/ppermute | solution.py:504
  80.8 18.1 %collective-permute-start.4 = (bf16[256,512]{1,0:T(8,128)(2,1)}, bf16[256,512]{1,0:T(8,128)(2,1)S(1)}, u32[]{:S(2)}, u32[]{:S(2)}) collective-permute-start(bf16[256,512]{1,0:T(8,128)(2,1)} %get-tuple-element.38.refs_3_), channel_id=1, source_target_pairs={{0,4},{1,5},{2,6},{3,7},{4,0},{5,1},{6,2},{7,3},{8,12},{9,13},{10,... | collective-permute-start | bytes 786440 | tf_op jit(solution)/shard_map/ppermute | solution.py:504
  90.6 8.3 %copy-start.11 = (bf16[256,512]{1,0:T(8,128)(2,1)}, bf16[256,512]{1,0:T(8,128)(2,1)S(1)}, u32[]{:S(2)}) copy-start(bf16[256,512]{1,0:T(8,128)(2,1)S(1)} %collective-permute-done.5.refs_3_) | copy-start | bytes 786436
  94.8 4.1 %copy-start.12 = (bf16[256,512]{1,0:T(8,128)(2,1)}, bf16[256,512]{1,0:T(8,128)(2,1)S(1)}, u32[]{:S(2)}) copy-start(bf16[256,512]{1,0:T(8,128)(2,1)S(1)} %collective-permute-done.6.refs_4_) | copy-start | bytes 786436
  98.9 0.7 copy-start.13
  101.6 5.3 %collective-permute-start.7 = (bf16[64,512]{1,0:T(8,128)(2,1)}, bf16[64,512]{1,0:T(8,128)(2,1)S(1)}, u32[]{:S(2)}, u32[]{:S(2)}) collective-permute-start(bf16[64,512]{1,0:T(8,128)(2,1)} %get-tuple-element.45), channel_id=1, source_target_pairs={{0,8},{4,12},{8,0},{12,4},{16,24},{20,28},{24,16},{28,20},{1,9},{5... | collective-permute-start | bytes 196616 | tf_op jit(solution)/shard_map/ppermute | solution.py:377
  104.5 7.3 %collective-permute-start.8 = (bf16[64,512]{1,0:T(8,128)(2,1)}, bf16[64,512]{1,0:T(8,128)(2,1)S(1)}, u32[]{:S(2)}, u32[]{:S(2)}) collective-permute-start(bf16[64,512]{1,0:T(8,128)(2,1)} %get-tuple-element.46), channel_id=1, source_target_pairs={{0,16},{4,20},{8,24},{12,28},{16,0},{20,4},{24,8},{28,12},{1,17},{... | collective-permute-start | bytes 196616 | tf_op jit(solution)/shard_map/ppermute | solution.py:377
  106.8 6.4 %collective-permute-start.9 = (bf16[64,512]{1,0:T(8,128)(2,1)}, bf16[64,512]{1,0:T(8,128)(2,1)S(1)}, u32[]{:S(2)}, u32[]{:S(2)}) collective-permute-start(bf16[64,512]{1,0:T(8,128)(2,1)} %get-tuple-element.47), channel_id=1, source_target_pairs={{0,24},{4,28},{8,16},{12,20},{16,8},{20,12},{24,0},{28,4},{1,25},{... | collective-permute-start | bytes 196616 | tf_op jit(solution)/shard_map/ppermute | solution.py:377
  107.0 6.2 %copy-start.20 = (bf16[64,512]{1,0:T(8,128)(2,1)}, bf16[64,512]{1,0:T(8,128)(2,1)S(1)}, u32[]{:S(2)}) copy-start(bf16[64,512]{1,0:T(8,128)(2,1)S(1)} %collective-permute-done.7.refs_1_) | copy-start | bytes 196612
  111.8 1.4 copy-start.21
  113.2 0.6 copy-start.22
  115.4 6.4 %collective-permute-start.12 = (bf16[64,512]{1,0:T(8,128)(2,1)}, bf16[64,512]{1,0:T(8,128)(2,1)S(1)}, u32[]{:S(2)}, u32[]{:S(2)}) collective-permute-start(bf16[64,512]{1,0:T(8,128)(2,1)} %shard_map.102), channel_id=1, source_target_pairs={{0,24},{4,28},{8,16},{12,20},{16,8},{20,12},{24,0},{28,4},{1,25},{... | collective-permute-start | bytes 196616 | tf_op jit(solution)/shard_map/ppermute | solution.py:377
  117.1 6.0 %collective-permute-start.11 = (bf16[64,512]{1,0:T(8,128)(2,1)}, bf16[64,512]{1,0:T(8,128)(2,1)S(1)}, u32[]{:S(2)}, u32[]{:S(2)}) collective-permute-start(bf16[64,512]{1,0:T(8,128)(2,1)} %shard_map.102), channel_id=1, source_target_pairs={{0,16},{4,20},{8,24},{12,28},{16,0},{20,4},{24,8},{28,12},{1,17},{... | collective-permute-start | bytes 196616 | tf_op jit(solution)/shard_map/ppermute | solution.py:377
  117.4 5.7 %collective-permute-start.10 = (bf16[64,512]{1,0:T(8,128)(2,1)}, bf16[64,512]{1,0:T(8,128)(2,1)S(1)}, u32[]{:S(2)}, u32[]{:S(2)}) collective-permute-start(bf16[64,512]{1,0:T(8,128)(2,1)} %shard_map.102), channel_id=1, source_target_pairs={{0,8},{4,12},{8,0},{12,4},{16,24},{20,28},{24,16},{28,20},{1,9},{5... | collective-permute-start | bytes 196616 | tf_op jit(solution)/shard_map/ppermute | solution.py:377
  124.8 5.4 %copy-start.2 = (bf16[256,512]{1,0:T(8,128)(2,1)S(1)}, bf16[256,512]{1,0:T(8,128)(2,1)}, u32[]{:S(2)}) copy-start(bf16[256,512]{1,0:T(8,128)(2,1)} %pad_maximum_fusion.refs_7_.refs_0_) | copy-start | bytes 786436
  124.8 1.1 copy-start
  130.1 14.0 %collective-permute-start.14 = (bf16[512,512]{1,0:T(8,128)(2,1)}, bf16[512,512]{1,0:T(8,128)(2,1)S(1)}, u32[]{:S(2)}, u32[]{:S(2)}) collective-permute-start(bf16[512,512]{1,0:T(8,128)(2,1)} %shard_map.103.refs_7_), channel_id=1, source_target_pairs={{0,1},{1,0},{2,3},{3,2},{4,5},{5,4},{6,7},{7,6},{8,9},{9,8},{10,11... | collective-permute-start | bytes 1572872 | tf_op jit(solution)/shard_map/ppermute | solution.py:377
  130.2 8.7 %collective-permute-start.13 = (bf16[256,512]{1,0:T(8,128)(2,1)S(1)}, bf16[256,512]{1,0:T(8,128)(2,1)S(1)}, u32[]{:S(2)}, u32[]{:S(2)}) collective-permute-start(bf16[256,512]{1,0:T(8,128)(2,1)S(1)} %copy-done.2), channel_id=1, source_target_pairs={{0,2},{1,3},{2,0},{3,1},{4,6},{5,7},{6,4},{7,5},{8,10},{9,11},{10,... | collective-permute-start | bytes 786440 | tf_op jit(solution)/shard_map/ppermute | solution.py:504
  138.9 0.7 copy-start.4
  144.1 4.6 %copy-start.5 = (bf16[256,512]{1,0:T(8,128)(2,1)S(1)}, bf16[256,512]{1,0:T(8,128)(2,1)}, u32[]{:S(2)}) copy-start(bf16[256,512]{1,0:T(8,128)(2,1)} %copy-done.4) | copy-start | bytes 786436
  144.1 0.8 copy-start.9
  147.2 13.7 %collective-permute-start.15 = (bf16[512,512]{1,0:T(8,128)(2,1)}, bf16[512,512]{1,0:T(8,128)(2,1)S(1)}, u32[]{:S(2)}, u32[]{:S(2)}) collective-permute-start(bf16[512,512]{1,0:T(8,128)(2,1)} %shard_map.105.mine_ref), channel_id=1, source_target_pairs={{0,2},{1,3},{2,0},{3,1},{4,6},{5,7},{6,4},{7,5},{8,10},{9,11},{10,... | collective-permute-start | bytes 1572872 | tf_op jit(solution)/shard_map/ppermute | solution.py:377
  148.7 12.2 %collective-permute-start.20 = (bf16[256,512]{1,0:T(8,128)(2,1)S(1)}, bf16[256,512]{1,0:T(8,128)(2,1)S(1)}, u32[]{:S(2)}, u32[]{:S(2)}) collective-permute-start(bf16[256,512]{1,0:T(8,128)(2,1)S(1)} %copy-done.2), channel_id=1, source_target_pairs={{0,1},{1,0},{2,3},{3,2},{4,5},{5,4},{6,7},{7,6},{8,9},{9,8},{10,11... | collective-permute-start | bytes 786440 | tf_op jit(solution)/shard_map/ppermute | solution.py:377
  148.7 12.7 %collective-permute-start.18 = (bf16[256,512]{1,0:T(8,128)(2,1)S(1)}, bf16[256,512]{1,0:T(8,128)(2,1)S(1)}, u32[]{:S(2)}, u32[]{:S(2)}) collective-permute-start(bf16[256,512]{1,0:T(8,128)(2,1)S(1)} %copy-done.2), channel_id=1, source_target_pairs={{0,4},{1,5},{2,6},{3,7},{4,0},{5,1},{6,2},{7,3},{8,12},{9,13},{10,... | collective-permute-start | bytes 786440 | tf_op jit(solution)/shard_map/ppermute | solution.py:504
  148.7 14.3 %collective-permute-start.19 = (bf16[256,512]{1,0:T(8,128)(2,1)S(1)}, bf16[256,512]{1,0:T(8,128)(2,1)S(1)}, u32[]{:S(2)}, u32[]{:S(2)}) collective-permute-start(bf16[256,512]{1,0:T(8,128)(2,1)S(1)} %copy-done.5), channel_id=1, source_target_pairs={{0,4},{1,5},{2,6},{3,7},{4,0},{5,1},{6,2},{7,3},{8,12},{9,13},{10,... | collective-permute-start | bytes 786440 | tf_op jit(solution)/shard_map/ppermute | solution.py:504
  150.8 18.4 %collective-permute-start.16 = (bf16[512,512]{1,0:T(8,128)(2,1)}, bf16[512,512]{1,0:T(8,128)(2,1)S(1)}, u32[]{:S(2)}, u32[]{:S(2)}) collective-permute-start(bf16[512,512]{1,0:T(8,128)(2,1)} %shard_map.105.mine_ref), channel_id=1, source_target_pairs={{0,1},{1,0},{2,3},{3,2},{4,5},{5,4},{6,7},{7,6},{8,9},{9,8},{10,11... | collective-permute-start | bytes 1572872 | tf_op jit(solution)/shard_map/ppermute | solution.py:377
  160.9 8.3 %copy-start.6 = (bf16[512,512]{1,0:T(8,128)(2,1)}, bf16[512,512]{1,0:T(8,128)(2,1)S(1)}, u32[]{:S(2)}) copy-start(bf16[512,512]{1,0:T(8,128)(2,1)S(1)} %collective-permute-done.15.over_ref) | copy-start | bytes 1572868
  160.9 8.3 %collective-permute-start.17 = (bf16[512,512]{1,0:T(8,128)(2,1)S(1)}, bf16[512,512]{1,0:T(8,128)(2,1)S(1)}, u32[]{:S(2)}, u32[]{:S(2)}) collective-permute-start(bf16[512,512]{1,0:T(8,128)(2,1)S(1)} %collective-permute-done.15.over_ref), channel_id=1, source_target_pairs={{0,1},{1,0},{2,3},{3,2},{4,5},{5,4},{6,7},{7,6},{8,9},{9,8},{10,11... | collective-permute-start | bytes 1572872 | tf_op jit(solution)/shard_map/ppermute | solution.py:377
  160.9 3.7 %copy-start.14 = (bf16[256,512]{1,0:T(8,128)(2,1)}, bf16[256,512]{1,0:T(8,128)(2,1)S(1)}, u32[]{:S(2)}) copy-start(bf16[256,512]{1,0:T(8,128)(2,1)S(1)} %collective-permute-done.20.refs_4_) | copy-start | bytes 786436
  160.9 2.6 %collective-permute-start.22 = (bf16[256,512]{1,0:T(8,128)(2,1)S(1)}, bf16[256,512]{1,0:T(8,128)(2,1)S(1)}, u32[]{:S(2)}, u32[]{:S(2)}) collective-permute-start(bf16[256,512]{1,0:T(8,128)(2,1)S(1)} %copy-done.5), channel_id=1, source_target_pairs={{0,1},{1,0},{2,3},{3,2},{4,5},{5,4},{6,7},{7,6},{8,9},{9,8},{10,11... | collective-permute-start | bytes 786440 | tf_op jit(solution)/shard_map/ppermute | solution.py:377
  161.4 3.2 %copy-start.15 = (bf16[256,512]{1,0:T(8,128)(2,1)}, bf16[256,512]{1,0:T(8,128)(2,1)S(1)}, u32[]{:S(2)}) copy-start(bf16[256,512]{1,0:T(8,128)(2,1)S(1)} %collective-permute-done.18.refs_1_) | copy-start | bytes 786436
  161.4 2.1 %collective-permute-start.21 = (bf16[256,512]{1,0:T(8,128)(2,1)S(1)}, bf16[256,512]{1,0:T(8,128)(2,1)S(1)}, u32[]{:S(2)}, u32[]{:S(2)}) collective-permute-start(bf16[256,512]{1,0:T(8,128)(2,1)S(1)} %collective-permute-done.18.refs_1_), channel_id=1, source_target_pairs={{0,1},{1,0},{2,3},{3,2},{4,5},{5,4},{6,7},{7,6},{8,9},{9,8},{10,11... | collective-permute-start | bytes 786440 | tf_op jit(solution)/shard_map/ppermute | solution.py:377
  163.1 1.5 copy-start.16
  163.1 1.5 collective-permute-start.23
  163.6 1.1 copy-start.18
  163.6 1.1 copy-start.17
  164.7 0.7 copy-start.19
  169.2 0.8 copy-start.7
  170.0 0.8 copy-start.8

commit v4 on v3

--- a/solution.py
+++ b/solution.py
@@ -16,7 +16,7 @@
 FAR = pl.BlockSpec(memory_space=pltpu.HBM)
 
 
-def call(body, outs, scalars, near, far=(), after=()):
+def call(body, outs, scalars, near, far=(), after=(), room=40):
     counts = len(scalars), len(near), len(far), len(after), len(outs), len(far)
     away = [index for index, out in enumerate(outs) if len(out) == 3]
 
@@ -65,7 +65,7 @@
         + [FAR] * (len(far) + len(after)),
         out_specs=[FAR if len(out) == 3 else VMEM for out in outs],
         scratch_shapes=scratch,
-        compiler_params=pltpu.CompilerParams(vmem_limit_bytes=60 * 1024 * 1024),
+        compiler_params=pltpu.CompilerParams(vmem_limit_bytes=room * 1024 * 1024),
     )(*scalars, *near, *far, *after)
 
 
@@ -167,9 +167,8 @@
     query_ref[...] = total.astype(BF)
 
 
-def lookup_kernel(cap, request_ref, take, ids_ref, rows_ref, negs_ref):
+def lookup_kernel(cap, request_ref, entities, ids_ref, rows_ref, negs_ref):
     parts, share, width = request_ref.shape
-    entities = take(0)
     columns = entities.shape[1]
     pieces = []
     for index in range(parts):
@@ -199,21 +198,24 @@
     core_ref,
     across_ref,
     both_ref,
-    take,
+    query_ref,
+    got_ref,
+    rows_ref,
+    rel_ref,
     loss_ref,
-    weight_ref,
     grad_ref,
-    prob_ref,
     away_ref,
+    back_ref,
+    keep_ref,
 ):
-    queries = take(0)[...]
+    queries = query_ref[...]
     negatives = jnp.concatenate(
         [near_ref[...], core_ref[...], across_ref[...], both_ref[...]], axis=0
     )
+    edges, slots = queries.shape[0], got_ref.shape[0]
+    slot = slot_ref[...]
     scores = dot_t1(queries, negatives) * factor
-    got = take(1)
-    placed = as_column(slot_ref[...]) == iota((queries.shape[0], got.shape[0]), 1)
-    tails = dot(hot(placed), got[...])
+    tails = dot(hot(as_column(slot) == iota((edges, slots), 1)), got_ref[...])
     positive = jnp.sum(queries.astype(F32) * tails, axis=1, keepdims=True) * factor
     row_max = jnp.maximum(positive, jnp.max(scores, axis=1, keepdims=True))
     exp_pos = jnp.exp(positive - row_max)
@@ -222,26 +224,19 @@
     loss_ref[...] = as_row(jnp.log(total) + row_max - positive)
     pull = exp_pos / total - 1.0
     prob = (exp_neg / total).astype(BF)
-    prob_ref[...] = prob
     grad = (factor * (pull * tails + dot(prob, negatives))).astype(BF)
     grad_ref[...] = grad
-    weight_ref[...] = factor * pull
-    rows = take(2)
-    operator_terms(picks_ref, 0, rows, as_column(take(3)[...]), grad, away_ref)
-
-
-def back_kernel(factor, cap, weight_ref, slot_ref, take, back_ref):
+    rel = as_column(rel_ref[...])
+    operator_terms(picks_ref, 0, rows_ref, rel, grad, away_ref)
+    operator_terms(picks_ref, 4, rows_ref, rel, grad, keep_ref)
     parts = back_ref.shape[0]
-    queries = take(0)[...]
-    slots, edges = parts * cap, queries.shape[0]
-    placed = hot(iota((slots, edges), 0) == slot_ref[...])
-    weighted = (weight_ref[...] * queries.astype(F32)).astype(BF)
-    tails = dot(placed, weighted).astype(BF)
-    prob = take(1)
-    share = prob.shape[1] // parts // 4
-    negs = factor * dot_t0(prob[...], queries)
+    cap = slots // parts
+    weighted = (factor * pull * queries.astype(F32)).astype(BF)
+    rows = dot(hot(iota((slots, edges), 0) == slot), weighted).astype(BF)
+    negs = factor * dot_t0(prob, queries)
+    share = negs.shape[0] // parts // 4
     for index in range(parts):
-        back_ref[index, :cap] = tails[index * cap : (index + 1) * cap]
+        back_ref[index, :cap] = rows[index * cap : (index + 1) * cap]
         pieces = [
             negs[(turn * parts + index) * share : (turn * parts + index + 1) * share]
             for turn in range(4)
@@ -249,37 +244,22 @@
         back_ref[index, cap:] = jnp.concatenate(pieces, axis=0).astype(BF)
 
 
-def keep_kernel(picks_ref, take, keep_ref):
-    rel = as_column(take(2)[...])
-    rows = take(0)
-    operator_terms(picks_ref, 4, rows, rel, take(1)[...], keep_ref)
-
-
-def pair_kernel(picks_ref, take, own_ref, *out_refs):
-    rel = as_column(take(2)[...])
-    rows, grad = take(0), take(1)[...]
-    width = own_ref.shape[0]
-    got = take(3)
-    for place in (1, 2, 3, 0):
-        relation = picks_ref[2 * (4 + place)]
-        at = pl.multiple_of(picks_ref[2 * (4 + place) + 1] * width, width)
-        picked = jnp.where(rel == relation, grad, jnp.zeros_like(grad))
-        term = dot_t0(rows[:, pl.ds(at, width)], picked) + got[place].astype(F32)
-        if place:
-            out_refs[place - 1][...] = term.astype(BF)
-        else:
-            own_ref[...] = term
-
-
-def head_kernel(take, high_ref, low_ref):
-    rel = as_column(take(1)[...])
-    grad = take(0)[...]
-    operators = take(2)
+def pair_kernel(keep_ref, got_ref, own_ref, *out_refs):
+    for index, out_ref in enumerate(out_refs):
+        term = keep_ref[index + 1].astype(F32) + got_ref[index + 1].astype(F32)
+        out_ref[...] = term.astype(BF)
+    own_ref[...] = keep_ref[0].astype(F32) + got_ref[0].astype(F32)
+
+
+def head_kernel(grad_ref, rel_ref, operators, out_ref):
+    rel = as_column(rel_ref[...])
+    grad = grad_ref[...]
+    edges = grad.shape[0]
     total = jnp.zeros(grad.shape, F32)
     for relation in range(operators.shape[0]):
         picked = jnp.where(rel == relation, grad, jnp.zeros_like(grad))
         total = total + dot_t1(picked, operators[relation])
-    high_ref[...], low_ref[...] = split(total)
+    out_ref[:edges], out_ref[edges:] = split(total)
 
 
 def quad_kernel(place_ref, own_ref, first_ref, second_ref, third_ref, *out_refs):
@@ -318,17 +298,17 @@
         copy.wait()
 
 
-def add_kernel(cap, base_ref, ids_ref, neg_ref, take, out_ref):
+def add_kernel(base_ref, ids_ref, neg_ref, head_ref, grads_ref, back_ref, out_ref):
     count = out_ref.shape[0]
     base = base_ref[0]
 
     def pick(row):
         return hot((iota((count, row.shape[1]), 0) + base) == row)
 
-    heads = pick(take(0)[...])
-    total = dot(heads, take(1)[...]) + dot(heads, take(2)[...])
-    back_ref = take(3)
+    heads = pick(head_ref[...])
+    total = dot(jnp.concatenate([heads, heads], axis=1), grads_ref[...])
     parts = back_ref.shape[0]
+    cap = ids_ref.shape[1] // parts
     tails = jnp.concatenate([back_ref[index, :cap] for index in range(parts)], axis=0)
     total = total + dot(pick(ids_ref[...]), tails)
     negs = back_ref[0, cap:].astype(F32)
@@ -369,7 +349,7 @@
         in_specs=[SMEM] * len(scalars) + [VMEM] * len(near),
         out_specs=FAR,
         scratch_shapes=scratch,
-        compiler_params=pltpu.CompilerParams(vmem_limit_bytes=60 * 1024 * 1024),
+        compiler_params=pltpu.CompilerParams(vmem_limit_bytes=40 * 1024 * 1024),
     )(*scalars, *near)
 
 
@@ -419,6 +399,7 @@
             neg_local.reshape(1, neg_dev),
             entities,
         ),
+        room=60,
     )
     requests = exchange(request)
     rows, queries = call(
@@ -428,70 +409,48 @@
         (),
         (head, rel, entities, relations),
         (slot,),
+        room=60,
     )
     asked, found, neg_near = call(
         functools.partial(lookup_kernel, cap),
-        [((1, slots), I32), ((slots, columns), BF, True), ((parts * share, columns), BF)],
-        (),
-        (requests,),
-        (entities,),
+        [((1, slots), I32), ((slots, columns), BF), ((parts * share, columns), BF)],
+        (),
+        (requests, entities),
+        (),
         (rows,),
     )
     got = exchange(found.reshape(parts, cap, columns)).reshape(slots, columns)
     neg_core, neg_across, neg_both = [flip(neg_near, "rep", reps, k) for k in (1, 2, 3)]
 
-    loss, weight, grad, prob, away = call(
+    loss, grad, away, back, keep = call(
         functools.partial(edge_kernel, factor),
         [
             ((1, edges), F32),
-            ((edges, 1), F32),
-            ((edges, columns), BF, True),
-            ((edges, negs), BF, True),
-            ((4, columns // 2, columns), BF if special else F32, True),
+            ((edges, columns), BF),
+            ((4, columns // 2, columns), BF if special else F32),
+            ((parts, cap + neg_dev, columns), BF),
+            ((4, columns // 2, columns), F32),
         ],
         (picks,),
-        (slot, neg_near, neg_core, neg_across, neg_both),
-        (queries, got, rows, rel),
-    )
-    (back,) = call(
-        functools.partial(back_kernel, factor, cap),
-        [((parts, cap + neg_dev, columns), BF, True)],
-        (),
-        (weight, slot),
-        (queries, prob),
+        (slot, neg_near, neg_core, neg_across, neg_both, queries, got, rows, rel),
     )
     returned = exchange(back)
 
     def add(base, size, kind, after):
         return call(
-            functools.partial(add_kernel, cap),
+            add_kernel,
             [((size, columns), kind)],
             (base.reshape(1),),
-            (asked, neg_own),
-            (head, high, low, returned),
+            (asked, neg_own, head, head_grads, returned),
+            (),
             after,
         )[0]
 
-    def head_grads(after):
-        return call(
-            head_kernel,
-            [((edges, columns), BF, True), ((edges, columns), BF, True)],
-            (),
-            (),
-            (grad, rel, relations),
-            after,
+    if not special:
+        whole = jnp.concatenate([away, keep], axis=0).reshape(count, columns, columns)
+        (head_grads,) = call(
+            head_kernel, [((2 * edges, columns), BF)], (), (grad, rel, relations)
         )
-
-    if not special:
-        (keep,) = call(
-            keep_kernel,
-            [((4, columns // 2, columns), F32, True)],
-            (picks,),
-            (),
-            (rows, grad, rel),
-        )
-        whole = jnp.concatenate([away, keep], axis=0).reshape(count, columns, columns)
-        high, low = head_grads(())
         entity_grad = lax.psum(add(jnp.zeros((), I32), ent_dev, F32, ()), "rep")
         return entity_grad, lax.psum(whole, ("dom", "rep")), loss.reshape(edges)
 
@@ -507,20 +466,25 @@
     own, *sent = call(
         pair_kernel,
         [((half, columns), F32)] + [((half, columns), BF)] * 3,
-        (picks,),
-        (),
-        (rows, grad, rel, other),
-        (back,),
+        (),
+        (keep, other),
     )
     met = [quad(k + 1)(v) for k, v in enumerate(sent)]
-    high, low = head_grads((sent[0],))
+    (head_grads,) = call(
+        head_kernel,
+        [((2 * edges, columns), BF)],
+        (),
+        (grad, rel, relations),
+        (),
+        (sent[0],),
+    )
     own, *sent = call(
         quad_kernel,
         [((quarter, columns), F32)] + [((quarter, columns), BF)] * 3,
         (place,),
         (own, *met),
         (),
-        (high,),
+        (head_grads,),
     )
     met = [flip(v, "dom", 8, 2 * (k + 1)) for k, v in enumerate(sent)]
     (own,) = call(sum_kernel, [((quarter, columns), BF)], (), (own, *met))

time: 175 us -> 147 us (0.84)
  Pallas kernels: 53.9 us -> 27.1 us
  waiting for transfers between devices: 71.5 us -> 76.3 us
  local copies, waits for them, and re-layouts: 9.44 us -> 5.08 us
    pallas_call x12 -> x11, Pallas kernels: 47.2 us -> 22.3 us  [call(): pl.pallas_call(kernel, out_shape=[jax.ShapeDtypeStruct(out[0], out[1]) fo...]
    ppermute x6, waiting for transfers between devices: 22.3 us -> 27.2 us  [quad(): return lambda v: lax.ppermute(v, ('dom', 'rep'), pairs)]
    unnamed x56 -> x28, local copies, waits for them, and re-layouts: 8.78 us -> 4.99 us
    pallas_call x2, Pallas kernels: 6.77 us -> 4.82 us  [write(): pl.pallas_call(body, out_shape=jax.ShapeDtypeStruct(*out), in_specs=[SMEM...]
  transfers between devices with their start and end apart: 27 -> 27, of which waited for: 18 -> 17; matrix products, arithmetic and copies ran while one was open for 1% -> 0% of each run, Pallas kernels for 14% -> 8%
where the time goes in v4:
time: 147 us; the launch traced here: 146 us
  waiting for transfers between devices  76.3 us (52%)
  starting transfers between devices  35.9 us (24%)
  Pallas kernels  27.1 us (18%)
  local copies, waits for them, and re-layouts  5.08 us (3%)
    ppermute x6, waiting for transfers between devices, quad(): return lambda v: lax.ppermute(v, ('dom', 'rep'), pairs)  27.2 us
    ppermute x18, waiting for transfers between devices, flip(): return lax.ppermute(x, axis, [(i, i ^ bit) for i in range(size)])  27.1 us
    pallas_call x11, Pallas kernels, call(): pl.pallas_call(kernel, out_shape=[jax.ShapeDtypeStruct(out[0], out[1]) fo...  22.3 us
    all_to_all x3, waiting for transfers between devices, exchange(): return lax.all_to_all(x, 'dom', split_axis=0, concat_axis=0, tiled=True)  22 us
    all_to_all x3, starting transfers between devices, exchange(): return lax.all_to_all(x, 'dom', split_axis=0, concat_axis=0, tiled=True)  14.7 us
    ppermute x18, starting transfers between devices, flip(): return lax.ppermute(x, axis, [(i, i ^ bit) for i in range(size)])  14 us
    ppermute x6, starting transfers between devices, quad(): return lambda v: lax.ppermute(v, ('dom', 'rep'), pairs)  7.17 us
    unnamed x28, local copies, waits for them, and re-layouts  4.99 us
  transfers between devices with their start and end apart: 27, of which 17 were waited for; matrix products, arithmetic and copies ran while one was open for 0% of the time, Pallas kernels for 8%

profile of v4, /device:TPU:0, one launch (start us, length us, event | category | flops | bytes accessed | tf_op | source)
XLA Modules:
  0.0 146.2 jit_solution(2535309852153708907)
XLA Ops:
  0.7 0.6 pad_add_fusion.refs_0_.place_ref
  1.3 3.4 %shard_map.94 = (s32[1,512]{1,0:T(1,128)}, s32[1,32]{1,0:T(1,128)}, bf16[8,8,640]{2,1,0:T(8,128)(2,1)}) custom-call(s32[3]{0:T(128)} %pad_add_fusion.refs_0_.place_ref, s32[1,512]{1,0:T(1,128)} %bitcast.32, s32[1,512]{1,0:T(1,128)} %bitcast.33, s32[1,32]{1,0:T(1,128)} %bitcast.34, bf16[1024,512]{1,0:T(8,128)(2,1)} %refs_1_.1), custom_call_target="tpu_custom_call" | custom-call | tf_op jit(solution)/shard_map/pallas_call | solution.py:60
  4.7 7.3 %all-to-all-start = ((bf16[8,8,640]{2,1,0:T(8,128)(2,1)}), bf16[8,8,640]{2,1,0:T(8,128)(2,1)S(1)}, u32[]{:S(2)}, u32[]{:S(2)}) async-start(bf16[8,8,640]{2,1,0:T(8,128)(2,1)} %get-tuple-element.24), calls=%async_computation | async-start | bytes 163840 | tf_op jit(solution)/shard_map/all_to_all | solution.py:361
  12.0 0.0 copy-start.10
  12.0 4.4 %shard_map.95 = (bf16[512,512]{1,0:T(8,128)(2,1)}, bf16[512,512]{1,0:T(8,128)(2,1)}) custom-call(s32[1,512]{1,0:T(1,128)} %bitcast.26, s32[1,512]{1,0:T(1,128)} %bitcast.29, bf16[1024,512]{1,0:T(8,128)(2,1)} %refs_1_.1, bf16[4,512,512]{2,1,0:T(8,128)(2,1)} %refs_2_.3, s32[1,512]{1,0:T(1,128)} %get-tuple-element.25.refs_4_.refs_1_), custom_call_target="tpu_custom_call" | custom-call | tf_op jit(solution)/shard_map/pallas_call | solution.py:60
  16.4 2.5 %all-to-all-done.refs_0_ = bf16[8,8,640]{2,1,0:T(8,128)(2,1)S(1)} async-done(((bf16[8,8,640]{2,1,0:T(8,128)(2,1)}), bf16[8,8,640]{2,1,0:T(8,128)(2,1)S(1)}, u32[]{:S(2)}, u32[]{:S(2)}) %all-to-all-start) | async-done | bytes 81952 | tf_op jit(solution)/shard_map/all_to_all | solution.py:361
  19.0 1.0 copy-done.4
  20.0 2.6 %shard_map.96 = (s32[1,1024]{1,0:T(1,128)S(1)}, bf16[1024,512]{1,0:T(8,128)(2,1)}, bf16[64,512]{1,0:T(8,128)(2,1)S(1)}) custom-call(bf16[8,8,640]{2,1,0:T(8,128)(2,1)S(1)} %all-to-all-done.refs_0_, bf16[1024,512]{1,0:T(8,128)(2,1)S(1)} %copy-done, bf16[512,512]{1,0:T(8,128)(2,1)S(1)} %copy-done.4), custom_call_target="tpu_custom_call" | custom-call | tf_op jit(solution)/shard_map/pallas_call | solution.py:60
  22.7 3.6 %all-to-all-start.1 = ((bf16[8,128,512]{2,1,0:T(8,128)(2,1)}), bf16[8,128,512]{2,1,0:T(8,128)(2,1)S(1)}, u32[]{:S(2)}, u32[]{:S(2)}) async-start(bf16[8,128,512]{2,1,0:T(8,128)(2,1)} %bitcast.21), calls=%async_computation.1 | async-start | bytes 2097152 | tf_op jit(solution)/shard_map/all_to_all | solution.py:361
  26.2 0.1 collective-permute-start.2
  26.3 1.6 %collective-permute-start.1 = (bf16[64,512]{1,0:T(8,128)(2,1)S(1)}, bf16[64,512]{1,0:T(8,128)(2,1)S(1)}, u32[]{:S(2)}, u32[]{:S(2)}) collective-permute-start(bf16[64,512]{1,0:T(8,128)(2,1)S(1)} %get-tuple-element.29.refs_2_), channel_id=1, source_target_pairs={{0,2},{1,3},{2,0},{3,1},{4,6},{5,7},{6,4},{7,5},{8,10},{9,11},{10,... | collective-permute-start | bytes 196616 | tf_op jit(solution)/shard_map/ppermute | solution.py:357
  27.9 0.3 collective-permute-start
  28.2 0.1 stack.71.refs_0_.picks_ref
  28.3 2.4 %collective-permute-done.2.refs_5_ = bf16[64,512]{1,0:T(8,128)(2,1)S(1)} collective-permute-done((bf16[64,512]{1,0:T(8,128)(2,1)S(1)}, bf16[64,512]{1,0:T(8,128)(2,1)S(1)}, u32[]{:S(2)}, u32[]{:S(2)}) %collective-permute-start.2) | collective-permute-done | bytes 65568 | tf_op jit(solution)/shard_map/ppermute | solution.py:357
  30.6 1.5 %collective-permute-done.1.refs_4_ = bf16[64,512]{1,0:T(8,128)(2,1)S(1)} collective-permute-done((bf16[64,512]{1,0:T(8,128)(2,1)S(1)}, bf16[64,512]{1,0:T(8,128)(2,1)S(1)}, u32[]{:S(2)}, u32[]{:S(2)}) %collective-permute-start.1) | collective-permute-done | bytes 65568 | tf_op jit(solution)/shard_map/ppermute | solution.py:357
  32.1 0.0 collective-permute-done.refs_3_
  32.1 19.5 %all-to-all-done.1 = bf16[8,128,512]{2,1,0:T(8,128)(2,1)S(1)} async-done(((bf16[8,128,512]{2,1,0:T(8,128)(2,1)}), bf16[8,128,512]{2,1,0:T(8,128)(2,1)S(1)}, u32[]{:S(2)}, u32[]{:S(2)}) %all-to-all-start.1) | async-done | bytes 1048608 | tf_op jit(solution)/shard_map/all_to_all | solution.py:361
  51.6 5.2 %shard_map.97 = (f32[1,512]{1,0:T(1,128)}, bf16[512,512]{1,0:T(8,128)(2,1)S(1)}, bf16[4,256,512]{2,1,0:T(8,128)(2,1)S(1)}, bf16[8,160,512]{2,1,0:T(8,128)(2,1)}, f32[4,256,512]{2,1,0:T(8,128)S(1)}) custom-call(s32[16]{0:T(128)S(1)} %stack.71.refs_0_.picks_ref, s32[1,512]{1,0:T(1,128)S(1)} %copy-done.10, bf16[64,512]{1,0:T(8,128)(2,1)S(1)} %get-tuple-element.29.refs_2_, ...), custom_call_target="tpu_custom_call" | custom-call | tf_op jit(solution)/shard_map/pallas_call | solution.py:60
  56.8 1.3 copy-done.2
  58.1 1.0 copy-done.12
  59.1 3.9 %all-to-all-start.2 = ((bf16[8,160,512]{2,1,0:T(8,128)(2,1)}), bf16[8,160,512]{2,1,0:T(8,128)(2,1)S(1)}, u32[]{:S(2)}, u32[]{:S(2)}) async-start(bf16[8,160,512]{2,1,0:T(8,128)(2,1)} %get-tuple-element.36), calls=%async_computation.2 | async-start | bytes 2621440 | tf_op jit(solution)/shard_map/all_to_all | solution.py:361
  63.0 0.0 copy-start.1
  63.0 0.1 collective-permute-start.3
  63.1 2.6 %collective-permute-done.3.refs_1_ = bf16[4,256,512]{2,1,0:T(8,128)(2,1)S(1)} collective-permute-done((bf16[4,256,512]{2,1,0:T(8,128)(2,1)S(1)}, bf16[4,256,512]{2,1,0:T(8,128)(2,1)S(1)}, u32[]{:S(2)}, u32[]{:S(2)}) %collective-permute-start.3) | collective-permute-done | bytes 1048608 | tf_op jit(solution)/shard_map/ppermute | solution.py:357
  65.8 1.6 %copy-done.3 = f32[4,256,512]{2,1,0:T(8,128)S(1)} copy-done((f32[4,256,512]{2,1,0:T(8,128)S(1)}, f32[4,256,512]{2,1,0:T(8,128)}, u32[]{:S(2)}) %copy-start.3) | copy-done | bytes 2097176
  67.3 0.2 shard_map.98
  67.5 1.6 %collective-permute-start.5 = (bf16[256,512]{1,0:T(8,128)(2,1)S(1)}, bf16[256,512]{1,0:T(8,128)(2,1)S(1)}, u32[]{:S(2)}, u32[]{:S(2)}) collective-permute-start(bf16[256,512]{1,0:T(8,128)(2,1)S(1)} %get-tuple-element.38), channel_id=1, source_target_pairs={{0,2},{1,3},{2,0},{3,1},{4,6},{5,7},{6,4},{7,5},{8,10},{9,11},{10,... | collective-permute-start | bytes 786440 | tf_op jit(solution)/shard_map/ppermute | solution.py:463
  69.1 1.7 %collective-permute-start.6 = (bf16[256,512]{1,0:T(8,128)(2,1)S(1)}, bf16[256,512]{1,0:T(8,128)(2,1)S(1)}, u32[]{:S(2)}, u32[]{:S(2)}) collective-permute-start(bf16[256,512]{1,0:T(8,128)(2,1)S(1)} %get-tuple-element.39), channel_id=1, source_target_pairs={{0,6},{1,7},{2,4},{3,5},{4,2},{5,3},{6,0},{7,1},{8,14},{9,15},{10,... | collective-permute-start | bytes 786440 | tf_op jit(solution)/shard_map/ppermute | solution.py:463
  70.8 0.3 collective-permute-start.4
  71.1 1.6 %shard_map.99.refs_5_.refs_4_ = bf16[1024,512]{1,0:T(8,128)(2,1)S(1)} custom-call(bf16[512,512]{1,0:T(8,128)(2,1)S(1)} %get-tuple-element.32.refs_0_, s32[1,512]{1,0:T(1,128)S(1)} %bitcast.31, bf16[4,512,512]{2,1,0:T(8,128)(2,1)S(1)} %copy-done.1, bf16[256,512]{1,0:T(8,128)(2,1)S(1)} %get-tuple-element.35.refs_3_), custom_call_target="tpu_custom_call" | custom-call | tf_op jit(solution)/shard_map/pallas_call | solution.py:60
  72.7 0.0 copy-start.7
  72.7 6.2 %collective-permute-done.5.refs_3_ = bf16[256,512]{1,0:T(8,128)(2,1)S(1)} collective-permute-done((bf16[256,512]{1,0:T(8,128)(2,1)S(1)}, bf16[256,512]{1,0:T(8,128)(2,1)S(1)}, u32[]{:S(2)}, u32[]{:S(2)}) %collective-permute-start.5) | collective-permute-done | bytes 262176 | tf_op jit(solution)/shard_map/ppermute | solution.py:463
  78.9 6.3 %collective-permute-done.6.refs_4_ = bf16[256,512]{1,0:T(8,128)(2,1)S(1)} collective-permute-done((bf16[256,512]{1,0:T(8,128)(2,1)S(1)}, bf16[256,512]{1,0:T(8,128)(2,1)S(1)}, u32[]{:S(2)}, u32[]{:S(2)}) %collective-permute-start.6) | collective-permute-done | bytes 262176 | tf_op jit(solution)/shard_map/ppermute | solution.py:463
  85.2 5.7 %collective-permute-done.4.refs_2_ = bf16[256,512]{1,0:T(8,128)(2,1)S(1)} collective-permute-done((bf16[256,512]{1,0:T(8,128)(2,1)S(1)}, bf16[256,512]{1,0:T(8,128)(2,1)S(1)}, u32[]{:S(2)}, u32[]{:S(2)}) %collective-permute-start.4) | collective-permute-done | bytes 262176 | tf_op jit(solution)/shard_map/ppermute | solution.py:463
  90.9 0.7 shard_map.100
  91.6 0.1 collective-permute-start.7
  91.7 5.3 %collective-permute-start.8 = (bf16[64,512]{1,0:T(8,128)(2,1)S(1)}, bf16[64,512]{1,0:T(8,128)(2,1)S(1)}, u32[]{:S(2)}, u32[]{:S(2)}) collective-permute-start(bf16[64,512]{1,0:T(8,128)(2,1)S(1)} %get-tuple-element.42), channel_id=1, source_target_pairs={{0,16},{4,20},{8,24},{12,28},{16,0},{20,4},{24,8},{28,12},{1,17},{... | collective-permute-start | bytes 196616 | tf_op jit(solution)/shard_map/ppermute | solution.py:357
  97.0 4.3 %collective-permute-done.8.refs_2_ = bf16[64,512]{1,0:T(8,128)(2,1)S(1)} collective-permute-done((bf16[64,512]{1,0:T(8,128)(2,1)S(1)}, bf16[64,512]{1,0:T(8,128)(2,1)S(1)}, u32[]{:S(2)}, u32[]{:S(2)}) %collective-permute-start.8) | collective-permute-done | bytes 65568 | tf_op jit(solution)/shard_map/ppermute | solution.py:357
  101.3 1.7 %collective-permute-done.9.refs_3_ = bf16[64,512]{1,0:T(8,128)(2,1)S(1)} collective-permute-done((bf16[64,512]{1,0:T(8,128)(2,1)S(1)}, bf16[64,512]{1,0:T(8,128)(2,1)S(1)}, u32[]{:S(2)}, u32[]{:S(2)}) %collective-permute-start.9) | collective-permute-done | bytes 65568 | tf_op jit(solution)/shard_map/ppermute | solution.py:357
  103.1 1.5 %collective-permute-start.12 = (bf16[64,512]{1,0:T(8,128)(2,1)S(1)}, bf16[64,512]{1,0:T(8,128)(2,1)S(1)}, u32[]{:S(2)}, u32[]{:S(2)}) collective-permute-start(bf16[64,512]{1,0:T(8,128)(2,1)S(1)} %shard_map.101), channel_id=1, source_target_pairs={{0,24},{4,28},{8,16},{12,20},{16,8},{20,12},{24,0},{28,4},{1,25},{... | collective-permute-start | bytes 196616 | tf_op jit(solution)/shard_map/ppermute | solution.py:357
  104.5 0.0 collective-permute-start.11
  104.5 3.0 %collective-permute-start.10 = (bf16[64,512]{1,0:T(8,128)(2,1)S(1)}, bf16[64,512]{1,0:T(8,128)(2,1)S(1)}, u32[]{:S(2)}, u32[]{:S(2)}) collective-permute-start(bf16[64,512]{1,0:T(8,128)(2,1)S(1)} %shard_map.101), channel_id=1, source_target_pairs={{0,8},{4,12},{8,0},{12,4},{16,24},{20,28},{24,16},{28,20},{1,9},{5... | collective-permute-start | bytes 196616 | tf_op jit(solution)/shard_map/ppermute | solution.py:357
  107.5 1.7 %collective-permute-done.12 = bf16[64,512]{1,0:T(8,128)(2,1)S(1)} collective-permute-done((bf16[64,512]{1,0:T(8,128)(2,1)S(1)}, bf16[64,512]{1,0:T(8,128)(2,1)S(1)}, u32[]{:S(2)}, u32[]{:S(2)}) %collective-permute-start.12) | collective-permute-done | bytes 65568 | tf_op jit(solution)/shard_map/ppermute | solution.py:357
  109.2 1.4 collective-permute-done.11
  110.6 0.0 collective-permute-done.10
  110.6 0.0 all-to-all-done.2.refs_5_
  110.7 1.5 %shard_map.102.refs_6_ = bf16[512,512]{1,0:T(8,128)(2,1)S(1)} custom-call(s32[1]{0:T(128)} %bitcast.23.refs_0_, s32[1,1024]{1,0:T(1,128)S(1)} %get-tuple-element.27.refs_1_, s32[1,32]{1,0:T(1,128)S(1)} %copy-done.11, s32[1,512]{1,0:T(1,128)S(1)} %bitcast.27, bf16[1024,512]{1,0:T(8,128)(2,1)S(1)} %shard_map.99.refs_5_.refs_4_, ...), custom_call_target="tpu_custom_call" | custom-call | tf_op jit(solution)/shard_map/pallas_call | solution.py:60
  112.2 0.1 collective-permute-start.14
  112.3 1.6 %collective-permute-start.13 = (bf16[256,512]{1,0:T(8,128)(2,1)S(1)}, bf16[256,512]{1,0:T(8,128)(2,1)S(1)}, u32[]{:S(2)}, u32[]{:S(2)}) collective-permute-start(bf16[256,512]{1,0:T(8,128)(2,1)S(1)} %pad_maximum_fusion.refs_6_.refs_0_), channel_id=1, source_target_pairs={{0,2},{1,3},{2,0},{3,1},{4,6},{5,7},{6,4},{7,5},{8,10},{9,11},{10,... | collective-permute-start | bytes 786440 | tf_op jit(solution)/shard_map/ppermute | solution.py:463
  113.8 7.1 %collective-permute-done.13.refs_7_.refs_2_ = bf16[256,512]{1,0:T(8,128)(2,1)S(1)} collective-permute-done((bf16[256,512]{1,0:T(8,128)(2,1)S(1)}, bf16[256,512]{1,0:T(8,128)(2,1)S(1)}, u32[]{:S(2)}, u32[]{:S(2)}) %collective-permute-start.13) | collective-permute-done | bytes 262176 | tf_op jit(solution)/shard_map/ppermute | solution.py:463
  121.0 1.5 %shard_map.103.refs_0_ = f32[512,512]{1,0:T(8,128)S(1)} custom-call(s32[1]{0:T(128)} %bitcast.3.refs_0_, s32[1,1024]{1,0:T(1,128)S(1)} %get-tuple-element.27.refs_1_, s32[1,32]{1,0:T(1,128)S(1)} %copy-done.11, s32[1,512]{1,0:T(1,128)S(1)} %bitcast.28, bf16[1024,512]{1,0:T(8,128)(2,1)S(1)} %shard_map.99.refs_5_.refs_4_, ...), custom_call_target="tpu_custom_call" | custom-call | tf_op jit(solution)/shard_map/pallas_call | solution.py:60
  122.5 0.0 collective-permute-done.14.refs_1_
  122.5 1.2 shard_map.104.mine_ref
  123.7 1.6 %collective-permute-start.15 = (bf16[512,512]{1,0:T(8,128)(2,1)S(1)}, bf16[512,512]{1,0:T(8,128)(2,1)S(1)}, u32[]{:S(2)}, u32[]{:S(2)}) collective-permute-start(bf16[512,512]{1,0:T(8,128)(2,1)S(1)} %shard_map.104.mine_ref), channel_id=1, source_target_pairs={{0,2},{1,3},{2,0},{3,1},{4,6},{5,7},{6,4},{7,5},{8,10},{9,11},{10,... | collective-permute-start | bytes 1572872 | tf_op jit(solution)/shard_map/ppermute | solution.py:357
  125.3 0.0 collective-permute-start.20
  125.3 2.0 %collective-permute-start.19 = (bf16[256,512]{1,0:T(8,128)(2,1)S(1)}, bf16[256,512]{1,0:T(8,128)(2,1)S(1)}, u32[]{:S(2)}, u32[]{:S(2)}) collective-permute-start(bf16[256,512]{1,0:T(8,128)(2,1)S(1)} %collective-permute-done.13.refs_7_.refs_2_), channel_id=1, source_target_pairs={{0,4},{1,5},{2,6},{3,7},{4,0},{5,1},{6,2},{7,3},{8,12},{9,13},{10,... | collective-permute-start | bytes 786440 | tf_op jit(solution)/shard_map/ppermute | solution.py:463
  127.3 9.9 %collective-permute-done.15.over_ref = bf16[512,512]{1,0:T(8,128)(2,1)S(1)} collective-permute-done((bf16[512,512]{1,0:T(8,128)(2,1)S(1)}, bf16[512,512]{1,0:T(8,128)(2,1)S(1)}, u32[]{:S(2)}, u32[]{:S(2)}) %collective-permute-start.15) | collective-permute-done | bytes 524320 | tf_op jit(solution)/shard_map/ppermute | solution.py:357
  137.2 0.5 collective-permute-start.22
  137.8 0.1 collective-permute-start.21
  137.8 1.8 %collective-permute-done.19.refs_3_ = bf16[256,512]{1,0:T(8,128)(2,1)S(1)} collective-permute-done((bf16[256,512]{1,0:T(8,128)(2,1)S(1)}, bf16[256,512]{1,0:T(8,128)(2,1)S(1)}, u32[]{:S(2)}, u32[]{:S(2)}) %collective-permute-start.19) | collective-permute-done | bytes 262176 | tf_op jit(solution)/shard_map/ppermute | solution.py:463
  139.6 0.3 collective-permute-done.21.refs_5_
  139.9 1.2 collective-permute-done.23.refs_7_
  141.1 2.8 %shard_map.106 = f32[4,512,512]{2,1,0:T(8,128)} custom-call(s32[16]{0:T(128)S(1)} %stack.71.refs_0_.picks_ref, s32[3]{0:T(128)S(1)} %copy-done.9, bf16[256,512]{1,0:T(8,128)(2,1)S(1)} %pad_maximum_fusion.refs_6_.refs_0_, bf16[256,512]{1,0:T(8,128)(2,1)S(1)} %collective-permute-done.18.refs_1_, bf16[256,512]{1,0:T(8,128)(2,1)S(1)} %collective-permute-done.13.refs_7_.refs_2_, ...), custom_call_target="tpu_custom_call" | custom-call | tf_op jit(solution)/shard_map/pallas_call | solution.py:346
  144.0 2.0 %shard_map.105 = f32[1024,512]{1,0:T(8,128)} custom-call(s32[3]{0:T(128)S(1)} %copy-done.9, bf16[512,512]{1,0:T(8,128)(2,1)S(1)} %shard_map.104.mine_ref, bf16[512,512]{1,0:T(8,128)(2,1)S(1)} %collective-permute-done.15.over_ref, bf16[512,512]{1,0:T(8,128)(2,1)S(1)} %collective-permute-done.16.other_ref, bf16[512,512]{1,0:T(8,128)(2,1)S(1)} %collective-permute-done.17.far_ref), custom_call_target="tpu_custom_call" | custom-call | tf_op jit(solution)/shard_map/pallas_call | solution.py:346
  (34 shorter events, 0.1 us)
Async XLA Ops:
  1.3 17.7 %copy-start = (bf16[1024,512]{1,0:T(8,128)(2,1)S(1)}, bf16[1024,512]{1,0:T(8,128)(2,1)}, u32[]{:S(2)}) copy-start(bf16[1024,512]{1,0:T(8,128)(2,1)} %refs_1_.1) | copy-start | bytes 3145732
  4.7 14.3 %all-to-all-start = ((bf16[8,8,640]{2,1,0:T(8,128)(2,1)}), bf16[8,8,640]{2,1,0:T(8,128)(2,1)S(1)}, u32[]{:S(2)}, u32[]{:S(2)}) async-start(bf16[8,8,640]{2,1,0:T(8,128)(2,1)} %get-tuple-element.24), calls=%async_computation | async-start | bytes 163840 | tf_op jit(solution)/shard_map/all_to_all | solution.py:361
  12.0 39.6 %copy-start.8 = (s32[512]{0:T(512)S(1)}, s32[512]{0:T(512)}, u32[]{:S(2)}) copy-start(s32[512]{0:T(512)} %param.10) | copy-start | bytes 6148
  12.0 39.6 %copy-start.10 = (s32[1,512]{1,0:T(1,128)S(1)}, s32[1,512]{1,0:T(1,128)}, u32[]{:S(2)}) copy-start(s32[1,512]{1,0:T(1,128)} %get-tuple-element.25.refs_4_.refs_1_) | copy-start | bytes 6148
  19.0 1.0 copy-start.4
  20.0 31.5 %copy-start.5 = (bf16[512,512]{1,0:T(8,128)(2,1)S(1)}, bf16[512,512]{1,0:T(8,128)(2,1)}, u32[]{:S(2)}) copy-start(bf16[512,512]{1,0:T(8,128)(2,1)} %get-tuple-element.26.refs_2_.refs_8_) | copy-start | bytes 1572868
  20.0 31.6 %copy-start.6 = (bf16[512,512]{1,0:T(8,128)(2,1)S(1)}, bf16[512,512]{1,0:T(8,128)(2,1)}, u32[]{:S(2)}) copy-start(bf16[512,512]{1,0:T(8,128)(2,1)} %get-tuple-element.30.refs_6_) | copy-start | bytes 1572868
  22.7 28.9 %all-to-all-start.1 = ((bf16[8,128,512]{2,1,0:T(8,128)(2,1)}), bf16[8,128,512]{2,1,0:T(8,128)(2,1)S(1)}, u32[]{:S(2)}, u32[]{:S(2)}) async-start(bf16[8,128,512]{2,1,0:T(8,128)(2,1)} %bitcast.21), calls=%async_computation.1 | async-start | bytes 2097152 | tf_op jit(solution)/shard_map/all_to_all | solution.py:361
  26.2 4.4 %collective-permute-start.2 = (bf16[64,512]{1,0:T(8,128)(2,1)S(1)}, bf16[64,512]{1,0:T(8,128)(2,1)S(1)}, u32[]{:S(2)}, u32[]{:S(2)}) collective-permute-start(bf16[64,512]{1,0:T(8,128)(2,1)S(1)} %get-tuple-element.29.refs_2_), channel_id=1, source_target_pairs={{0,3},{1,2},{2,1},{3,0},{4,7},{5,6},{6,5},{7,4},{8,11},{9,10},{10,... | collective-permute-start | bytes 196616 | tf_op jit(solution)/shard_map/ppermute | solution.py:357
  26.3 5.8 %collective-permute-start.1 = (bf16[64,512]{1,0:T(8,128)(2,1)S(1)}, bf16[64,512]{1,0:T(8,128)(2,1)S(1)}, u32[]{:S(2)}, u32[]{:S(2)}) collective-permute-start(bf16[64,512]{1,0:T(8,128)(2,1)S(1)} %get-tuple-element.29.refs_2_), channel_id=1, source_target_pairs={{0,2},{1,3},{2,0},{3,1},{4,6},{5,7},{6,4},{7,5},{8,10},{9,11},{10,... | collective-permute-start | bytes 196616 | tf_op jit(solution)/shard_map/ppermute | solution.py:357
  27.9 4.2 %collective-permute-start = (bf16[64,512]{1,0:T(8,128)(2,1)S(1)}, bf16[64,512]{1,0:T(8,128)(2,1)S(1)}, u32[]{:S(2)}, u32[]{:S(2)}) collective-permute-start(bf16[64,512]{1,0:T(8,128)(2,1)S(1)} %get-tuple-element.29.refs_2_), channel_id=1, source_target_pairs={{0,1},{1,0},{2,3},{3,2},{4,5},{5,4},{6,7},{7,6},{8,9},{9,8},{10,11... | collective-permute-start | bytes 196616 | tf_op jit(solution)/shard_map/ppermute | solution.py:357
  56.8 1.3 copy-start.2
  58.1 1.0 copy-start.12
  59.1 3.9 %copy-start.13 = (bf16[4,256,512]{2,1,0:T(8,128)(2,1)S(1)}, bf16[4,256,512]{2,1,0:T(8,128)(2,1)}, u32[]{:S(2)}) copy-start(bf16[4,256,512]{2,1,0:T(8,128)(2,1)} %copy-done.12) | copy-start | bytes 3145732
  59.1 51.5 %all-to-all-start.2 = ((bf16[8,160,512]{2,1,0:T(8,128)(2,1)}), bf16[8,160,512]{2,1,0:T(8,128)(2,1)S(1)}, u32[]{:S(2)}, u32[]{:S(2)}) async-start(bf16[8,160,512]{2,1,0:T(8,128)(2,1)} %get-tuple-element.36), calls=%async_computation.2 | async-start | bytes 2621440 | tf_op jit(solution)/shard_map/all_to_all | solution.py:361
  63.0 8.1 %copy-start.1 = (bf16[4,512,512]{2,1,0:T(8,128)(2,1)S(1)}, bf16[4,512,512]{2,1,0:T(8,128)(2,1)}, u32[]{:S(2)}) copy-start(bf16[4,512,512]{2,1,0:T(8,128)(2,1)} %refs_2_.3) | copy-start | bytes 6291460
  63.0 2.7 %collective-permute-start.3 = (bf16[4,256,512]{2,1,0:T(8,128)(2,1)S(1)}, bf16[4,256,512]{2,1,0:T(8,128)(2,1)S(1)}, u32[]{:S(2)}, u32[]{:S(2)}) collective-permute-start(bf16[4,256,512]{2,1,0:T(8,128)(2,1)S(1)} %copy-done.13), channel_id=1, source_target_pairs={{0,1},{1,0},{2,3},{3,2},{4,5},{5,4},{6,7},{7,6},{8,9},{9,8},{10,11... | collective-permute-start | bytes 3145736 | tf_op jit(solution)/shard_map/ppermute | solution.py:357
  65.7 1.6 %copy-start.3 = (f32[4,256,512]{2,1,0:T(8,128)S(1)}, f32[4,256,512]{2,1,0:T(8,128)}, u32[]{:S(2)}) copy-start(f32[4,256,512]{2,1,0:T(8,128)} %copy-done.2) | copy-start | bytes 6291460
  67.5 23.4 %copy-start.9 = (s32[3]{0:T(128)S(1)}, s32[3]{0:T(128)}, u32[]{:S(2)}) copy-start(s32[3]{0:T(128)} %pad_add_fusion.refs_0_.place_ref) | copy-start | bytes 40
  67.5 11.4 %collective-permute-start.5 = (bf16[256,512]{1,0:T(8,128)(2,1)S(1)}, bf16[256,512]{1,0:T(8,128)(2,1)S(1)}, u32[]{:S(2)}, u32[]{:S(2)}) collective-permute-start(bf16[256,512]{1,0:T(8,128)(2,1)S(1)} %get-tuple-element.38), channel_id=1, source_target_pairs={{0,2},{1,3},{2,0},{3,1},{4,6},{5,7},{6,4},{7,5},{8,10},{9,11},{10,... | collective-permute-start | bytes 786440 | tf_op jit(solution)/shard_map/ppermute | solution.py:463
  69.1 16.1 %collective-permute-start.6 = (bf16[256,512]{1,0:T(8,128)(2,1)S(1)}, bf16[256,512]{1,0:T(8,128)(2,1)S(1)}, u32[]{:S(2)}, u32[]{:S(2)}) collective-permute-start(bf16[256,512]{1,0:T(8,128)(2,1)S(1)} %get-tuple-element.39), channel_id=1, source_target_pairs={{0,6},{1,7},{2,4},{3,5},{4,2},{5,3},{6,0},{7,1},{8,14},{9,15},{10,... | collective-permute-start | bytes 786440 | tf_op jit(solution)/shard_map/ppermute | solution.py:463
  70.8 20.2 %collective-permute-start.4 = (bf16[256,512]{1,0:T(8,128)(2,1)S(1)}, bf16[256,512]{1,0:T(8,128)(2,1)S(1)}, u32[]{:S(2)}, u32[]{:S(2)}) collective-permute-start(bf16[256,512]{1,0:T(8,128)(2,1)S(1)} %get-tuple-element.35.refs_3_), channel_id=1, source_target_pairs={{0,4},{1,5},{2,6},{3,7},{4,0},{5,1},{6,2},{7,3},{8,12},{9,13},{10,... | collective-permute-start | bytes 786440 | tf_op jit(solution)/shard_map/ppermute | solution.py:463
  72.7 38.0 %copy-start.7 = (s32[512]{0:T(512)S(1)}, s32[512]{0:T(512)}, u32[]{:S(2)}) copy-start(s32[512]{0:T(512)} %param.9) | copy-start | bytes 6148
  72.7 38.0 %copy-start.11 = (s32[1,32]{1,0:T(1,128)S(1)}, s32[1,32]{1,0:T(1,128)}, u32[]{:S(2)}) copy-start(s32[1,32]{1,0:T(1,128)} %get-tuple-element.28.refs_2_) | copy-start | bytes 388
  91.6 5.4 %collective-permute-start.7 = (bf16[64,512]{1,0:T(8,128)(2,1)S(1)}, bf16[64,512]{1,0:T(8,128)(2,1)S(1)}, u32[]{:S(2)}, u32[]{:S(2)}) collective-permute-start(bf16[64,512]{1,0:T(8,128)(2,1)S(1)} %get-tuple-element.41), channel_id=1, source_target_pairs={{0,8},{4,12},{8,0},{12,4},{16,24},{20,28},{24,16},{28,20},{1,9},{5... | collective-permute-start | bytes 196616 | tf_op jit(solution)/shard_map/ppermute | solution.py:357
  91.7 9.6 %collective-permute-start.8 = (bf16[64,512]{1,0:T(8,128)(2,1)S(1)}, bf16[64,512]{1,0:T(8,128)(2,1)S(1)}, u32[]{:S(2)}, u32[]{:S(2)}) collective-permute-start(bf16[64,512]{1,0:T(8,128)(2,1)S(1)} %get-tuple-element.42), channel_id=1, source_target_pairs={{0,16},{4,20},{8,24},{12,28},{16,0},{20,4},{24,8},{28,12},{1,17},{... | collective-permute-start | bytes 196616 | tf_op jit(solution)/shard_map/ppermute | solution.py:357
  97.0 6.1 %collective-permute-start.9 = (bf16[64,512]{1,0:T(8,128)(2,1)S(1)}, bf16[64,512]{1,0:T(8,128)(2,1)S(1)}, u32[]{:S(2)}, u32[]{:S(2)}) collective-permute-start(bf16[64,512]{1,0:T(8,128)(2,1)S(1)} %get-tuple-element.43), channel_id=1, source_target_pairs={{0,24},{4,28},{8,16},{12,20},{16,8},{20,12},{24,0},{28,4},{1,25},{... | collective-permute-start | bytes 196616 | tf_op jit(solution)/shard_map/ppermute | solution.py:357
  103.1 6.2 %collective-permute-start.12 = (bf16[64,512]{1,0:T(8,128)(2,1)S(1)}, bf16[64,512]{1,0:T(8,128)(2,1)S(1)}, u32[]{:S(2)}, u32[]{:S(2)}) collective-permute-start(bf16[64,512]{1,0:T(8,128)(2,1)S(1)} %shard_map.101), channel_id=1, source_target_pairs={{0,24},{4,28},{8,16},{12,20},{16,8},{20,12},{24,0},{28,4},{1,25},{... | collective-permute-start | bytes 196616 | tf_op jit(solution)/shard_map/ppermute | solution.py:357
  104.5 6.1 %collective-permute-start.11 = (bf16[64,512]{1,0:T(8,128)(2,1)S(1)}, bf16[64,512]{1,0:T(8,128)(2,1)S(1)}, u32[]{:S(2)}, u32[]{:S(2)}) collective-permute-start(bf16[64,512]{1,0:T(8,128)(2,1)S(1)} %shard_map.101), channel_id=1, source_target_pairs={{0,16},{4,20},{8,24},{12,28},{16,0},{20,4},{24,8},{28,12},{1,17},{... | collective-permute-start | bytes 196616 | tf_op jit(solution)/shard_map/ppermute | solution.py:357
  104.5 6.1 %collective-permute-start.10 = (bf16[64,512]{1,0:T(8,128)(2,1)S(1)}, bf16[64,512]{1,0:T(8,128)(2,1)S(1)}, u32[]{:S(2)}, u32[]{:S(2)}) collective-permute-start(bf16[64,512]{1,0:T(8,128)(2,1)S(1)} %shard_map.101), channel_id=1, source_target_pairs={{0,8},{4,12},{8,0},{12,4},{16,24},{20,28},{24,16},{28,20},{1,9},{5... | collective-permute-start | bytes 196616 | tf_op jit(solution)/shard_map/ppermute | solution.py:357
  112.2 10.3 %collective-permute-start.14 = (bf16[512,512]{1,0:T(8,128)(2,1)S(1)}, bf16[512,512]{1,0:T(8,128)(2,1)}, u32[]{:S(2)}, u32[]{:S(2)}) collective-permute-start(bf16[512,512]{1,0:T(8,128)(2,1)S(1)} %shard_map.102.refs_6_), channel_id=1, source_target_pairs={{0,1},{1,0},{2,3},{3,2},{4,5},{5,4},{6,7},{7,6},{8,9},{9,8},{10,11... | collective-permute-start | bytes 1572872 | tf_op jit(solution)/shard_map/ppermute | solution.py:357
  112.3 8.7 %collective-permute-start.13 = (bf16[256,512]{1,0:T(8,128)(2,1)S(1)}, bf16[256,512]{1,0:T(8,128)(2,1)S(1)}, u32[]{:S(2)}, u32[]{:S(2)}) collective-permute-start(bf16[256,512]{1,0:T(8,128)(2,1)S(1)} %pad_maximum_fusion.refs_6_.refs_0_), channel_id=1, source_target_pairs={{0,2},{1,3},{2,0},{3,1},{4,6},{5,7},{6,4},{7,5},{8,10},{9,11},{10,... | collective-permute-start | bytes 786440 | tf_op jit(solution)/shard_map/ppermute | solution.py:463
  123.7 13.6 %collective-permute-start.15 = (bf16[512,512]{1,0:T(8,128)(2,1)S(1)}, bf16[512,512]{1,0:T(8,128)(2,1)S(1)}, u32[]{:S(2)}, u32[]{:S(2)}) collective-permute-start(bf16[512,512]{1,0:T(8,128)(2,1)S(1)} %shard_map.104.mine_ref), channel_id=1, source_target_pairs={{0,2},{1,3},{2,0},{3,1},{4,6},{5,7},{6,4},{7,5},{8,10},{9,11},{10,... | collective-permute-start | bytes 1572872 | tf_op jit(solution)/shard_map/ppermute | solution.py:357
  125.3 12.0 %collective-permute-start.20 = (bf16[256,512]{1,0:T(8,128)(2,1)S(1)}, bf16[256,512]{1,0:T(8,128)(2,1)S(1)}, u32[]{:S(2)}, u32[]{:S(2)}) collective-permute-start(bf16[256,512]{1,0:T(8,128)(2,1)S(1)} %pad_maximum_fusion.refs_6_.refs_0_), channel_id=1, source_target_pairs={{0,1},{1,0},{2,3},{3,2},{4,5},{5,4},{6,7},{7,6},{8,9},{9,8},{10,11... | collective-permute-start | bytes 786440 | tf_op jit(solution)/shard_map/ppermute | solution.py:357
  125.3 12.5 %collective-permute-start.18 = (bf16[256,512]{1,0:T(8,128)(2,1)S(1)}, bf16[256,512]{1,0:T(8,128)(2,1)S(1)}, u32[]{:S(2)}, u32[]{:S(2)}) collective-permute-start(bf16[256,512]{1,0:T(8,128)(2,1)S(1)} %pad_maximum_fusion.refs_6_.refs_0_), channel_id=1, source_target_pairs={{0,4},{1,5},{2,6},{3,7},{4,0},{5,1},{6,2},{7,3},{8,12},{9,13},{10,... | collective-permute-start | bytes 786440 | tf_op jit(solution)/shard_map/ppermute | solution.py:463
  125.3 14.3 %collective-permute-start.19 = (bf16[256,512]{1,0:T(8,128)(2,1)S(1)}, bf16[256,512]{1,0:T(8,128)(2,1)S(1)}, u32[]{:S(2)}, u32[]{:S(2)}) collective-permute-start(bf16[256,512]{1,0:T(8,128)(2,1)S(1)} %collective-permute-done.13.refs_7_.refs_2_), channel_id=1, source_target_pairs={{0,4},{1,5},{2,6},{3,7},{4,0},{5,1},{6,2},{7,3},{8,12},{9,13},{10,... | collective-permute-start | bytes 786440 | tf_op jit(solution)/shard_map/ppermute | solution.py:463
  127.3 16.7 %collective-permute-start.16 = (bf16[512,512]{1,0:T(8,128)(2,1)S(1)}, bf16[512,512]{1,0:T(8,128)(2,1)S(1)}, u32[]{:S(2)}, u32[]{:S(2)}) collective-permute-start(bf16[512,512]{1,0:T(8,128)(2,1)S(1)} %shard_map.104.mine_ref), channel_id=1, source_target_pairs={{0,1},{1,0},{2,3},{3,2},{4,5},{5,4},{6,7},{7,6},{8,9},{9,8},{10,11... | collective-permute-start | bytes 1572872 | tf_op jit(solution)/shard_map/ppermute | solution.py:357
  137.2 6.8 %collective-permute-start.17 = (bf16[512,512]{1,0:T(8,128)(2,1)S(1)}, bf16[512,512]{1,0:T(8,128)(2,1)S(1)}, u32[]{:S(2)}, u32[]{:S(2)}) collective-permute-start(bf16[512,512]{1,0:T(8,128)(2,1)S(1)} %collective-permute-done.15.over_ref), channel_id=1, source_target_pairs={{0,1},{1,0},{2,3},{3,2},{4,5},{5,4},{6,7},{7,6},{8,9},{9,8},{10,11... | collective-permute-start | bytes 1572872 | tf_op jit(solution)/shard_map/ppermute | solution.py:357
  137.2 2.7 %collective-permute-start.22 = (bf16[256,512]{1,0:T(8,128)(2,1)S(1)}, bf16[256,512]{1,0:T(8,128)(2,1)S(1)}, u32[]{:S(2)}, u32[]{:S(2)}) collective-permute-start(bf16[256,512]{1,0:T(8,128)(2,1)S(1)} %collective-permute-done.13.refs_7_.refs_2_), channel_id=1, source_target_pairs={{0,1},{1,0},{2,3},{3,2},{4,5},{5,4},{6,7},{7,6},{8,9},{9,8},{10,11... | collective-permute-start | bytes 786440 | tf_op jit(solution)/shard_map/ppermute | solution.py:357
  137.8 2.1 %collective-permute-start.21 = (bf16[256,512]{1,0:T(8,128)(2,1)S(1)}, bf16[256,512]{1,0:T(8,128)(2,1)S(1)}, u32[]{:S(2)}, u32[]{:S(2)}) collective-permute-start(bf16[256,512]{1,0:T(8,128)(2,1)S(1)} %collective-permute-done.18.refs_1_), channel_id=1, source_target_pairs={{0,1},{1,0},{2,3},{3,2},{4,5},{5,4},{6,7},{7,6},{8,9},{9,8},{10,11... | collective-permute-start | bytes 786440 | tf_op jit(solution)/shard_map/ppermute | solution.py:357
  139.6 1.5 %collective-permute-start.23 = (bf16[256,512]{1,0:T(8,128)(2,1)S(1)}, bf16[256,512]{1,0:T(8,128)(2,1)S(1)}, u32[]{:S(2)}, u32[]{:S(2)}) collective-permute-start(bf16[256,512]{1,0:T(8,128)(2,1)S(1)} %collective-permute-done.19.refs_3_), channel_id=1, source_target_pairs={{0,1},{1,0},{2,3},{3,2},{4,5},{5,4},{6,7},{7,6},{8,9},{9,8},{10,11... | collective-permute-start | bytes 786440 | tf_op jit(solution)/shard_map/ppermute | solution.py:357

commit v5 on v4

--- a/solution.py
+++ b/solution.py
@@ -167,15 +167,16 @@
     query_ref[...] = total.astype(BF)
 
 
-def lookup_kernel(cap, request_ref, entities, ids_ref, rows_ref, negs_ref):
+def lookup_kernel(cap, request_ref, take, ids_ref, rows_ref, negs_ref):
     parts, share, width = request_ref.shape
-    columns = entities.shape[1]
+    columns = rows_ref.shape[1]
     pieces = []
     for index in range(parts):
         digits = request_ref[index, :, columns : columns + cap].astype(F32)
         pieces.append(digits[0:1] * 128.0 + digits[1:2])
     ids = jnp.concatenate(pieces, axis=1).astype(I32)
     ids_ref[...] = ids
+    entities = take(0)
     rows_ref[...] = dot(hot_rows(ids, entities.shape[0]), entities[...]).astype(BF)
     negs_ref[...] = jnp.concatenate(
         [request_ref[index, :, :columns].astype(F32) for index in range(parts)], axis=0
@@ -203,9 +204,10 @@
     rows_ref,
     rel_ref,
     loss_ref,
+    weight_ref,
+    prob_ref,
     grad_ref,
     away_ref,
-    back_ref,
     keep_ref,
 ):
     queries = query_ref[...]
@@ -213,9 +215,8 @@
         [near_ref[...], core_ref[...], across_ref[...], both_ref[...]], axis=0
     )
     edges, slots = queries.shape[0], got_ref.shape[0]
-    slot = slot_ref[...]
     scores = dot_t1(queries, negatives) * factor
-    tails = dot(hot(as_column(slot) == iota((edges, slots), 1)), got_ref[...])
+    tails = dot(hot(as_column(slot_ref[...]) == iota((edges, slots), 1)), got_ref[...])
     positive = jnp.sum(queries.astype(F32) * tails, axis=1, keepdims=True) * factor
     row_max = jnp.maximum(positive, jnp.max(scores, axis=1, keepdims=True))
     exp_pos = jnp.exp(positive - row_max)
@@ -223,17 +224,25 @@
     total = exp_pos + jnp.sum(exp_neg, axis=1, keepdims=True)
     loss_ref[...] = as_row(jnp.log(total) + row_max - positive)
     pull = exp_pos / total - 1.0
+    weight_ref[...] = factor * pull
     prob = (exp_neg / total).astype(BF)
+    prob_ref[...] = prob
     grad = (factor * (pull * tails + dot(prob, negatives))).astype(BF)
     grad_ref[...] = grad
     rel = as_column(rel_ref[...])
     operator_terms(picks_ref, 0, rows_ref, rel, grad, away_ref)
     operator_terms(picks_ref, 4, rows_ref, rel, grad, keep_ref)
+
+
+def back_kernel(factor, weight_ref, prob_ref, query_ref, slot_ref, back_ref):
+    queries = query_ref[...]
+    edges = queries.shape[0]
     parts = back_ref.shape[0]
+    slots = 2 * edges
     cap = slots // parts
-    weighted = (factor * pull * queries.astype(F32)).astype(BF)
-    rows = dot(hot(iota((slots, edges), 0) == slot), weighted).astype(BF)
-    negs = factor * dot_t0(prob, queries)
+    weighted = (weight_ref[...] * queries.astype(F32)).astype(BF)
+    rows = dot(hot(iota((slots, edges), 0) == slot_ref[...]), weighted).astype(BF)
+    negs = factor * dot_t0(prob_ref[...], queries)
     share = negs.shape[0] // parts // 4
     for index in range(parts):
         back_ref[index, :cap] = rows[index * cap : (index + 1) * cap]
@@ -415,28 +424,44 @@
         functools.partial(lookup_kernel, cap),
         [((1, slots), I32), ((slots, columns), BF), ((parts * share, columns), BF)],
         (),
-        (requests, entities),
-        (),
+        (requests,),
+        (entities,),
         (rows,),
+        room=60,
     )
     got = exchange(found.reshape(parts, cap, columns)).reshape(slots, columns)
     neg_core, neg_across, neg_both = [flip(neg_near, "rep", reps, k) for k in (1, 2, 3)]
 
-    loss, grad, away, back, keep = call(
+    terms = ((4, columns // 2, columns), BF if special else F32)
+    loss, weight, prob, grad, away, keep = call(
         functools.partial(edge_kernel, factor),
         [
             ((1, edges), F32),
+            ((edges, 1), F32),
+            ((edges, negs), BF),
             ((edges, columns), BF),
-            ((4, columns // 2, columns), BF if special else F32),
-            ((parts, cap + neg_dev, columns), BF),
-            ((4, columns // 2, columns), F32),
+            terms,
+            terms,
         ],
         (picks,),
         (slot, neg_near, neg_core, neg_across, neg_both, queries, got, rows, rel),
     )
-    returned = exchange(back)
-
-    def add(base, size, kind, after):
+    (head_grads,) = call(
+        head_kernel, [((2 * edges, columns), BF)], (), (grad, rel, relations)
+    )
+
+    def give_back(after):
+        (back,) = call(
+            functools.partial(back_kernel, factor),
+            [((parts, cap + neg_dev, columns), BF)],
+            (),
+            (weight, prob, queries, slot),
+            (),
+            after,
+        )
+        return back, exchange(back)
+
+    def add(base, size, kind, returned, after):
         return call(
             add_kernel,
             [((size, columns), kind)],
@@ -448,10 +473,8 @@
 
     if not special:
         whole = jnp.concatenate([away, keep], axis=0).reshape(count, columns, columns)
-        (head_grads,) = call(
-            head_kernel, [((2 * edges, columns), BF)], (), (grad, rel, relations)
-        )
-        entity_grad = lax.psum(add(jnp.zeros((), I32), ent_dev, F32, ()), "rep")
+        back, returned = give_back(())
+        entity_grad = lax.psum(add(jnp.zeros((), I32), ent_dev, F32, returned, ()), "rep")
         return entity_grad, lax.psum(whole, ("dom", "rep")), loss.reshape(edges)
 
     half, quarter = columns // 2, columns // 8
@@ -468,30 +491,26 @@
         [((half, columns), F32)] + [((half, columns), BF)] * 3,
         (),
         (keep, other),
+        (),
+        (head_grads,),
     )
     met = [quad(k + 1)(v) for k, v in enumerate(sent)]
-    (head_grads,) = call(
-        head_kernel,
-        [((2 * edges, columns), BF)],
-        (),
-        (grad, rel, relations),
-        (),
-        (sent[0],),
-    )
+    back, returned = give_back((sent[0],))
     own, *sent = call(
         quad_kernel,
         [((quarter, columns), F32)] + [((quarter, columns), BF)] * 3,
         (place,),
         (own, *met),
         (),
-        (head_grads,),
+        (back,),
     )
     met = [flip(v, "dom", 8, 2 * (k + 1)) for k, v in enumerate(sent)]
     (own,) = call(sum_kernel, [((quarter, columns), BF)], (), (own, *met))
     stripes = [own] + [flip(own, "dom", 8, 2 * (k + 1)) for k in range(3)]
     own = jnp.concatenate(stripes, axis=0)
     over_y = quad(2)(own)
-    mine = [own, quad(1)(own), over_y, quad(1)(over_y)]
+    over_x = quad(1)(own)
+    mine = [own, over_x, over_y, quad(1)(over_y)]
     others = [flip(v, "rep", 4, 1) for v in mine]
     relation_grad = write(
         operator_kernel,
@@ -502,9 +521,9 @@
     )
 
     rows_half = ent_dev // 2
-    leaving = add((1 - core) * rows_half, rows_half, BF, (own,))
+    leaving = add((1 - core) * rows_half, rows_half, BF, returned, (own,))
     arrived = flip(leaving, "rep", 4, 1)
-    kept = add(core * rows_half, rows_half, F32, (leaving, over_y))
+    kept = add(core * rows_half, rows_half, F32, returned, (leaving, over_x))
     (both,) = call(both_kernel, [((rows_half, columns), BF)], (), (kept, arrived))
     across = flip(both, "rep", 4, 2)
     pieces = (both, across, flip(both, "rep", 4, 1), flip(across, "rep", 4, 1))

time: 147 us -> 163 us (1.11)
  waiting for transfers between devices: 76.3 us -> 93.1 us
  starting transfers between devices: 35.9 us -> 33 us
    ppermute x6, waiting for transfers between devices: 27.2 us -> 55.6 us  [quad(): return lambda v: lax.ppermute(v, ('dom', 'rep'), pairs)]
    ppermute x18, waiting for transfers between devices: 27.1 us -> 15.6 us  [flip(): return lax.ppermute(x, axis, [(i, i ^ bit) for i in range(size)])]
    ppermute x6, starting transfers between devices: 7.17 us -> 4.6 us  [quad(): return lambda v: lax.ppermute(v, ('dom', 'rep'), pairs)]
    pallas_call x11 -> x12, Pallas kernels: 22.3 us -> 23.4 us  [call(): pl.pallas_call(kernel, out_shape=[jax.ShapeDtypeStruct(out[0], out[1]) fo...]
  transfers between devices with their start and end apart: 27 -> 27, of which waited for: 17 -> 17; matrix products, arithmetic and copies ran while one was open for 0% -> 0% of each run, Pallas kernels for 8% -> 7%
where the time goes in v5:
time: 163 us; the launch traced here: 162 us
  waiting for transfers between devices  93.1 us (57%)
  starting transfers between devices  33 us (20%)
  Pallas kernels  28.2 us (17%)
  local copies, waits for them, and re-layouts  5.91 us (4%)
    ppermute x6, waiting for transfers between devices, quad(): return lambda v: lax.ppermute(v, ('dom', 'rep'), pairs)  55.6 us
    pallas_call x12, Pallas kernels, call(): pl.pallas_call(kernel, out_shape=[jax.ShapeDtypeStruct(out[0], out[1]) fo...  23.4 us
    all_to_all x3, waiting for transfers between devices, exchange(): return lax.all_to_all(x, 'dom', split_axis=0, concat_axis=0, tiled=True)  22 us
    ppermute x18, waiting for transfers between devices, flip(): return lax.ppermute(x, axis, [(i, i ^ bit) for i in range(size)])  15.6 us
    all_to_all x3, starting transfers between devices, exchange(): return lax.all_to_all(x, 'dom', split_axis=0, concat_axis=0, tiled=True)  14.9 us
    ppermute x18, starting transfers between devices, flip(): return lax.ppermute(x, axis, [(i, i ^ bit) for i in range(size)])  13.6 us
    unnamed x28, local copies, waits for them, and re-layouts  5.82 us
    pallas_call x2, Pallas kernels, write(): pl.pallas_call(body, out_shape=jax.ShapeDtypeStruct(*out), in_specs=[SMEM...  4.82 us
  transfers between devices with their start and end apart: 27, of which 17 were waited for; matrix products, arithmetic and copies ran while one was open for 0% of the time, Pallas kernels for 7%

profile of v5, /device:TPU:0, one launch (start us, length us, event | category | flops | bytes accessed | tf_op | source)
XLA Modules:
  0.0 162.0 jit_solution(10810786796338719819)
XLA Ops:
  0.7 0.6 pad_add_fusion.refs_0_.place_ref
  1.2 3.3 %shard_map.94 = (s32[1,512]{1,0:T(1,128)}, s32[1,32]{1,0:T(1,128)}, bf16[8,8,640]{2,1,0:T(8,128)(2,1)}) custom-call(s32[3]{0:T(128)} %pad_add_fusion.refs_0_.place_ref, s32[1,512]{1,0:T(1,128)} %bitcast.33, s32[1,512]{1,0:T(1,128)} %bitcast.34, s32[1,32]{1,0:T(1,128)} %bitcast.35, bf16[1024,512]{1,0:T(8,128)(2,1)} %refs_1_.1), custom_call_target="tpu_custom_call" | custom-call | tf_op jit(solution)/shard_map/pallas_call | solution.py:60
  4.5 7.3 %all-to-all-start = ((bf16[8,8,640]{2,1,0:T(8,128)(2,1)}), bf16[8,8,640]{2,1,0:T(8,128)(2,1)S(1)}, u32[]{:S(2)}, u32[]{:S(2)}) async-start(bf16[8,8,640]{2,1,0:T(8,128)(2,1)} %get-tuple-element.25), calls=%async_computation | async-start | bytes 163840 | tf_op jit(solution)/shard_map/all_to_all | solution.py:370
  11.8 4.4 %shard_map.95 = (bf16[512,512]{1,0:T(8,128)(2,1)}, bf16[512,512]{1,0:T(8,128)(2,1)}) custom-call(s32[1,512]{1,0:T(1,128)} %bitcast.26, s32[1,512]{1,0:T(1,128)} %bitcast.29, bf16[1024,512]{1,0:T(8,128)(2,1)} %refs_1_.1, bf16[4,512,512]{2,1,0:T(8,128)(2,1)} %refs_2_.3, s32[1,512]{1,0:T(1,128)} %get-tuple-element.26.refs_4_.refs_1_.refs_3_), custom_call_target="tpu_custom_call" | custom-call | tf_op jit(solution)/shard_map/pallas_call | solution.py:60
  16.2 0.0 copy-start.7
  16.2 2.6 %all-to-all-done.refs_0_ = bf16[8,8,640]{2,1,0:T(8,128)(2,1)S(1)} async-done(((bf16[8,8,640]{2,1,0:T(8,128)(2,1)}), bf16[8,8,640]{2,1,0:T(8,128)(2,1)S(1)}, u32[]{:S(2)}, u32[]{:S(2)}) %all-to-all-start) | async-done | bytes 81952 | tf_op jit(solution)/shard_map/all_to_all | solution.py:370
  18.8 0.6 copy-done.13
  19.4 4.7 %shard_map.96 = (s32[1,1024]{1,0:T(1,128)}, bf16[1024,512]{1,0:T(8,128)(2,1)}, bf16[64,512]{1,0:T(8,128)(2,1)}) custom-call(bf16[8,8,640]{2,1,0:T(8,128)(2,1)} %copy-done.13, bf16[1024,512]{1,0:T(8,128)(2,1)} %refs_1_.1, bf16[512,512]{1,0:T(8,128)(2,1)} %get-tuple-element.27.refs_2_.refs_8_), custom_call_target="tpu_custom_call" | custom-call | tf_op jit(solution)/shard_map/pallas_call | solution.py:60
  24.2 3.7 %all-to-all-start.1 = ((bf16[8,128,512]{2,1,0:T(8,128)(2,1)}), bf16[8,128,512]{2,1,0:T(8,128)(2,1)S(1)}, u32[]{:S(2)}, u32[]{:S(2)}) async-start(bf16[8,128,512]{2,1,0:T(8,128)(2,1)} %bitcast.32), calls=%async_computation.1 | async-start | bytes 2097152 | tf_op jit(solution)/shard_map/all_to_all | solution.py:370
  27.9 0.1 collective-permute-start.2
  28.0 1.6 collective-permute-start.1
  29.6 0.3 collective-permute-start
  29.8 0.1 stack.71.refs_0_.picks_ref
  29.9 2.4 %collective-permute-done.2.refs_5_ = bf16[64,512]{1,0:T(8,128)(2,1)S(1)} collective-permute-done((bf16[64,512]{1,0:T(8,128)(2,1)S(1)}, bf16[64,512]{1,0:T(8,128)(2,1)S(1)}, u32[]{:S(2)}, u32[]{:S(2)}) %collective-permute-start.2) | collective-permute-done | bytes 65568 | tf_op jit(solution)/shard_map/ppermute | solution.py:366
  32.3 1.5 collective-permute-done.1.refs_4_
  33.8 19.4 %all-to-all-done.1 = bf16[8,128,512]{2,1,0:T(8,128)(2,1)S(1)} async-done(((bf16[8,128,512]{2,1,0:T(8,128)(2,1)}), bf16[8,128,512]{2,1,0:T(8,128)(2,1)S(1)}, u32[]{:S(2)}, u32[]{:S(2)}) %all-to-all-start.1) | async-done | bytes 1048608 | tf_op jit(solution)/shard_map/all_to_all | solution.py:370
  53.2 1.0 copy-done.3
  54.3 1.0 copy-done.4
  55.3 3.3 %shard_map.97 = (f32[1,512]{1,0:T(1,128)}, f32[512,1]{1,0:T(8,128)S(1)}, bf16[512,256]{1,0:T(8,128)(2,1)S(1)}, bf16[512,512]{1,0:T(8,128)(2,1)S(1)}, bf16[4,256,...) custom-call(s32[16]{0:T(128)S(1)} %stack.71.refs_0_.picks_ref, s32[1,512]{1,0:T(1,128)S(1)} %copy-done.8, ...), custom_call_target="tpu_custom_call" | custom-call | tf_op jit(solution)/shard_map/pallas_call | solution.py:60
  58.7 0.1 collective-permute-start.3
  58.7 1.6 shard_map.98.refs_2_.refs_4_
  60.3 1.1 collective-permute-done.3.refs_1_
  61.4 0.2 shard_map.99
  61.6 0.0 copy-start.12
  61.6 0.7 copy-done.12
  62.3 0.9 shard_map.100.refs_5_
  63.3 0.0 copy-start
  63.3 1.0 copy-done
  64.3 3.9 %all-to-all-start.2 = ((bf16[8,160,512]{2,1,0:T(8,128)(2,1)}), bf16[8,160,512]{2,1,0:T(8,128)(2,1)S(1)}, u32[]{:S(2)}, u32[]{:S(2)}) async-start(bf16[8,160,512]{2,1,0:T(8,128)(2,1)} %copy-done), calls=%async_computation.2 | async-start | bytes 2621440 | tf_op jit(solution)/shard_map/all_to_all | solution.py:370
  68.2 1.6 collective-permute-start.5
  69.8 1.7 %collective-permute-start.6 = (bf16[256,512]{1,0:T(8,128)(2,1)S(1)}, bf16[256,512]{1,0:T(8,128)(2,1)S(1)}, u32[]{:S(2)}, u32[]{:S(2)}) collective-permute-start(bf16[256,512]{1,0:T(8,128)(2,1)S(1)} %get-tuple-element.41), channel_id=1, source_target_pairs={{0,6},{1,7},{2,4},{3,5},{4,2},{5,3},{6,0},{7,1},{8,14},{9,15},{10,... | collective-permute-start | bytes 786440 | tf_op jit(solution)/shard_map/ppermute | solution.py:486
  71.5 0.3 collective-permute-start.4
  71.8 5.8 %collective-permute-done.5.refs_3_ = bf16[256,512]{1,0:T(8,128)(2,1)S(1)} collective-permute-done((bf16[256,512]{1,0:T(8,128)(2,1)}, bf16[256,512]{1,0:T(8,128)(2,1)S(1)}, u32[]{:S(2)}, u32[]{:S(2)}) %collective-permute-start.5) | collective-permute-done | bytes 262176 | tf_op jit(solution)/shard_map/ppermute | solution.py:486
  77.6 12.0 %collective-permute-done.6.refs_4_ = bf16[256,512]{1,0:T(8,128)(2,1)S(1)} collective-permute-done((bf16[256,512]{1,0:T(8,128)(2,1)S(1)}, bf16[256,512]{1,0:T(8,128)(2,1)S(1)}, u32[]{:S(2)}, u32[]{:S(2)}) %collective-permute-start.6) | collective-permute-done | bytes 262176 | tf_op jit(solution)/shard_map/ppermute | solution.py:486
  89.6 6.6 %collective-permute-done.4.refs_2_ = bf16[256,512]{1,0:T(8,128)(2,1)S(1)} collective-permute-done((bf16[256,512]{1,0:T(8,128)(2,1)S(1)}, bf16[256,512]{1,0:T(8,128)(2,1)S(1)}, u32[]{:S(2)}, u32[]{:S(2)}) %collective-permute-start.4) | collective-permute-done | bytes 262176 | tf_op jit(solution)/shard_map/ppermute | solution.py:486
  96.2 1.3 copy-done.1
  97.5 0.7 shard_map.101
  98.1 0.1 collective-permute-start.7
  98.2 3.9 %collective-permute-start.8 = (bf16[64,512]{1,0:T(8,128)(2,1)S(1)}, bf16[64,512]{1,0:T(8,128)(2,1)S(1)}, u32[]{:S(2)}, u32[]{:S(2)}) collective-permute-start(bf16[64,512]{1,0:T(8,128)(2,1)S(1)} %get-tuple-element.44), channel_id=1, source_target_pairs={{0,16},{4,20},{8,24},{12,28},{16,0},{20,4},{24,8},{28,12},{1,17},{... | collective-permute-start | bytes 196616 | tf_op jit(solution)/shard_map/ppermute | solution.py:366
  102.1 0.5 collective-permute-start.9
  102.6 0.6 collective-permute-done.7.refs_1_
  103.2 3.5 %collective-permute-done.8.refs_2_ = bf16[64,512]{1,0:T(8,128)(2,1)S(1)} collective-permute-done((bf16[64,512]{1,0:T(8,128)(2,1)S(1)}, bf16[64,512]{1,0:T(8,128)(2,1)S(1)}, u32[]{:S(2)}, u32[]{:S(2)}) %collective-permute-start.8) | collective-permute-done | bytes 65568 | tf_op jit(solution)/shard_map/ppermute | solution.py:366
  106.7 1.6 collective-permute-done.9.refs_3_
  108.3 1.7 %collective-permute-start.12 = (bf16[64,512]{1,0:T(8,128)(2,1)S(1)}, bf16[64,512]{1,0:T(8,128)(2,1)S(1)}, u32[]{:S(2)}, u32[]{:S(2)}) collective-permute-start(bf16[64,512]{1,0:T(8,128)(2,1)S(1)} %shard_map.102), channel_id=1, source_target_pairs={{0,24},{4,28},{8,16},{12,20},{16,8},{20,12},{24,0},{28,4},{1,25},{... | collective-permute-start | bytes 196616 | tf_op jit(solution)/shard_map/ppermute | solution.py:366
  110.1 0.4 collective-permute-start.11
  110.4 2.4 %collective-permute-start.10 = (bf16[64,512]{1,0:T(8,128)(2,1)S(1)}, bf16[64,512]{1,0:T(8,128)(2,1)S(1)}, u32[]{:S(2)}, u32[]{:S(2)}) collective-permute-start(bf16[64,512]{1,0:T(8,128)(2,1)S(1)} %shard_map.102), channel_id=1, source_target_pairs={{0,8},{4,12},{8,0},{12,4},{16,24},{20,28},{24,16},{28,20},{1,9},{5... | collective-permute-start | bytes 196616 | tf_op jit(solution)/shard_map/ppermute | solution.py:366
  112.8 2.3 %collective-permute-done.12 = bf16[64,512]{1,0:T(8,128)(2,1)S(1)} collective-permute-done((bf16[64,512]{1,0:T(8,128)(2,1)S(1)}, bf16[64,512]{1,0:T(8,128)(2,1)S(1)}, u32[]{:S(2)}, u32[]{:S(2)}) %collective-permute-start.12) | collective-permute-done | bytes 65568 | tf_op jit(solution)/shard_map/ppermute | solution.py:366
  115.1 1.1 collective-permute-done.11
  116.3 1.5 shard_map.103.refs_6_
  117.8 0.1 collective-permute-start.14
  117.9 0.1 collective-permute-start.13
  118.0 8.6 %collective-permute-done.13.refs_7_.refs_1_ = bf16[256,512]{1,0:T(8,128)(2,1)S(1)} collective-permute-done((bf16[256,512]{1,0:T(8,128)(2,1)S(1)}, bf16[256,512]{1,0:T(8,128)(2,1)S(1)}, u32[]{:S(2)}, u32[]{:S(2)}) %collective-permute-start.13) | collective-permute-done | bytes 262176 | tf_op jit(solution)/shard_map/ppermute | solution.py:486
  126.6 1.5 shard_map.104.refs_0_
  128.2 1.1 shard_map.105.mine_ref
  129.3 1.6 collective-permute-start.15
  130.9 0.5 collective-permute-start.18
  131.4 17.1 %collective-permute-done.18.refs_2_ = bf16[256,512]{1,0:T(8,128)(2,1)S(1)} collective-permute-done((bf16[256,512]{1,0:T(8,128)(2,1)S(1)}, bf16[256,512]{1,0:T(8,128)(2,1)S(1)}, u32[]{:S(2)}, u32[]{:S(2)}) %collective-permute-start.18) | collective-permute-done | bytes 262176 | tf_op jit(solution)/shard_map/ppermute | solution.py:486
  148.5 0.5 collective-permute-start.19
  148.9 0.5 collective-permute-start.17
  149.4 0.5 collective-permute-start.21
  149.9 5.5 %collective-permute-done.19.refs_3_ = bf16[256,512]{1,0:T(8,128)(2,1)S(1)} collective-permute-done((bf16[256,512]{1,0:T(8,128)(2,1)S(1)}, bf16[256,512]{1,0:T(8,128)(2,1)S(1)}, u32[]{:S(2)}, u32[]{:S(2)}) %collective-permute-start.19) | collective-permute-done | bytes 262176 | tf_op jit(solution)/shard_map/ppermute | solution.py:486
  155.4 1.5 collective-permute-done.23.refs_7_
  157.0 2.8 %shard_map.107 = f32[4,512,512]{2,1,0:T(8,128)} custom-call(s32[16]{0:T(128)S(1)} %stack.71.refs_0_.picks_ref, s32[3]{0:T(128)S(1)} %copy-done.10, bf16[256,512]{1,0:T(8,128)(2,1)S(1)} %pad_maximum_fusion.refs_6_.refs_0_, bf16[256,512]{1,0:T(8,128)(2,1)S(1)} %collective-permute-done.13.refs_7_.refs_1_, bf16[256,512]{1,0:T(8,128)(2,1)S(1)} %collective-permute-done.18.refs_2_, ...), custom_call_target="tpu_custom_call" | custom-call | tf_op jit(solution)/shard_map/pallas_call | solution.py:355
  159.8 2.0 %shard_map.106 = f32[1024,512]{1,0:T(8,128)} custom-call(s32[3]{0:T(128)S(1)} %copy-done.10, bf16[512,512]{1,0:T(8,128)(2,1)S(1)} %shard_map.105.mine_ref, bf16[512,512]{1,0:T(8,128)(2,1)S(1)} %collective-permute-done.15.over_ref, bf16[512,512]{1,0:T(8,128)(2,1)S(1)} %collective-permute-done.16.other_ref, bf16[512,512]{1,0:T(8,128)(2,1)S(1)} %collective-permute-done.17.far_ref), custom_call_target="tpu_custom_call" | custom-call | tf_op jit(solution)/shard_map/pallas_call | solution.py:355
  (35 shorter events, 0.1 us)
Async XLA Ops:
  4.5 14.3 %all-to-all-start = ((bf16[8,8,640]{2,1,0:T(8,128)(2,1)}), bf16[8,8,640]{2,1,0:T(8,128)(2,1)S(1)}, u32[]{:S(2)}, u32[]{:S(2)}) async-start(bf16[8,8,640]{2,1,0:T(8,128)(2,1)} %get-tuple-element.25), calls=%async_computation | async-start | bytes 163840 | tf_op jit(solution)/shard_map/all_to_all | solution.py:370
  16.2 37.0 %copy-start.7 = (s32[512]{0:T(512)S(1)}, s32[512]{0:T(512)}, u32[]{:S(2)}) copy-start(s32[512]{0:T(512)} %param.10) | copy-start | bytes 6148
  16.2 37.0 %copy-start.8 = (s32[1,512]{1,0:T(1,128)S(1)}, s32[1,512]{1,0:T(1,128)}, u32[]{:S(2)}) copy-start(s32[1,512]{1,0:T(1,128)} %get-tuple-element.26.refs_4_.refs_1_.refs_3_) | copy-start | bytes 6148
  18.8 0.6 copy-start.13
  24.2 3.7 %copy-start.5 = (bf16[64,512]{1,0:T(8,128)(2,1)S(1)}, bf16[64,512]{1,0:T(8,128)(2,1)}, u32[]{:S(2)}) copy-start(bf16[64,512]{1,0:T(8,128)(2,1)} %get-tuple-element.30.refs_2_) | copy-start | bytes 196612
  24.2 34.6 %copy-start.2 = (bf16[4,512,512]{2,1,0:T(8,128)(2,1)S(1)}, bf16[4,512,512]{2,1,0:T(8,128)(2,1)}, u32[]{:S(2)}) copy-start(bf16[4,512,512]{2,1,0:T(8,128)(2,1)} %refs_2_.3) | copy-start | bytes 6291460
  24.2 29.0 %all-to-all-start.1 = ((bf16[8,128,512]{2,1,0:T(8,128)(2,1)}), bf16[8,128,512]{2,1,0:T(8,128)(2,1)S(1)}, u32[]{:S(2)}, u32[]{:S(2)}) async-start(bf16[8,128,512]{2,1,0:T(8,128)(2,1)} %bitcast.32), calls=%async_computation.1 | async-start | bytes 2097152 | tf_op jit(solution)/shard_map/all_to_all | solution.py:370
  27.9 4.4 %collective-permute-start.2 = (bf16[64,512]{1,0:T(8,128)(2,1)S(1)}, bf16[64,512]{1,0:T(8,128)(2,1)S(1)}, u32[]{:S(2)}, u32[]{:S(2)}) collective-permute-start(bf16[64,512]{1,0:T(8,128)(2,1)S(1)} %copy-done.5), channel_id=1, source_target_pairs={{0,3},{1,2},{2,1},{3,0},{4,7},{5,6},{6,5},{7,4},{8,11},{9,10},{10,... | collective-permute-start | bytes 196616 | tf_op jit(solution)/shard_map/ppermute | solution.py:366
  28.0 5.8 %collective-permute-start.1 = (bf16[64,512]{1,0:T(8,128)(2,1)S(1)}, bf16[64,512]{1,0:T(8,128)(2,1)S(1)}, u32[]{:S(2)}, u32[]{:S(2)}) collective-permute-start(bf16[64,512]{1,0:T(8,128)(2,1)S(1)} %copy-done.5), channel_id=1, source_target_pairs={{0,2},{1,3},{2,0},{3,1},{4,6},{5,7},{6,4},{7,5},{8,10},{9,11},{10,... | collective-permute-start | bytes 196616 | tf_op jit(solution)/shard_map/ppermute | solution.py:366
  29.6 4.2 %collective-permute-start = (bf16[64,512]{1,0:T(8,128)(2,1)S(1)}, bf16[64,512]{1,0:T(8,128)(2,1)S(1)}, u32[]{:S(2)}, u32[]{:S(2)}) collective-permute-start(bf16[64,512]{1,0:T(8,128)(2,1)S(1)} %copy-done.5), channel_id=1, source_target_pairs={{0,1},{1,0},{2,3},{3,2},{4,5},{5,4},{6,7},{7,6},{8,9},{9,8},{10,11... | collective-permute-start | bytes 196616 | tf_op jit(solution)/shard_map/ppermute | solution.py:366
  53.2 1.0 copy-start.3
  54.3 1.0 copy-start.4
  58.7 2.7 %collective-permute-start.3 = (bf16[4,256,512]{2,1,0:T(8,128)(2,1)S(1)}, bf16[4,256,512]{2,1,0:T(8,128)(2,1)S(1)}, u32[]{:S(2)}, u32[]{:S(2)}) collective-permute-start(bf16[4,256,512]{2,1,0:T(8,128)(2,1)S(1)} %get-tuple-element.37), channel_id=1, source_target_pairs={{0,1},{1,0},{2,3},{3,2},{4,5},{5,4},{6,7},{7,6},{8,9},{9,8},{10,11... | collective-permute-start | bytes 3145736 | tf_op jit(solution)/shard_map/ppermute | solution.py:366
  61.6 0.7 copy-start.12
  62.3 33.8 %copy-start.10 = (s32[3]{0:T(128)S(1)}, s32[3]{0:T(128)}, u32[]{:S(2)}) copy-start(s32[3]{0:T(128)} %pad_add_fusion.refs_0_.place_ref) | copy-start | bytes 40
  63.3 1.1 copy-start
  64.3 51.9 %copy-start.9 = (s32[1,1024]{1,0:T(1,128)S(1)}, s32[1,1024]{1,0:T(1,128)}, u32[]{:S(2)}) copy-start(s32[1,1024]{1,0:T(1,128)} %get-tuple-element.28.refs_1_) | copy-start | bytes 12292
  64.3 51.9 %all-to-all-start.2 = ((bf16[8,160,512]{2,1,0:T(8,128)(2,1)}), bf16[8,160,512]{2,1,0:T(8,128)(2,1)S(1)}, u32[]{:S(2)}, u32[]{:S(2)}) async-start(bf16[8,160,512]{2,1,0:T(8,128)(2,1)} %copy-done), calls=%async_computation.2 | async-start | bytes 2621440 | tf_op jit(solution)/shard_map/all_to_all | solution.py:370
  68.2 48.1 %copy-start.6 = (s32[512]{0:T(512)S(1)}, s32[512]{0:T(512)}, u32[]{:S(2)}) copy-start(s32[512]{0:T(512)} %param.9) | copy-start | bytes 6148
  68.2 48.1 %copy-start.11 = (s32[1,32]{1,0:T(1,128)S(1)}, s32[1,32]{1,0:T(1,128)}, u32[]{:S(2)}) copy-start(s32[1,32]{1,0:T(1,128)} %get-tuple-element.29.refs_2_) | copy-start | bytes 388
  68.2 9.4 %collective-permute-start.5 = (bf16[256,512]{1,0:T(8,128)(2,1)}, bf16[256,512]{1,0:T(8,128)(2,1)S(1)}, u32[]{:S(2)}, u32[]{:S(2)}) collective-permute-start(bf16[256,512]{1,0:T(8,128)(2,1)} %copy-done.12), channel_id=1, source_target_pairs={{0,2},{1,3},{2,0},{3,1},{4,6},{5,7},{6,4},{7,5},{8,10},{9,11},{10,... | collective-permute-start | bytes 786440 | tf_op jit(solution)/shard_map/ppermute | solution.py:486
  69.8 19.8 %collective-permute-start.6 = (bf16[256,512]{1,0:T(8,128)(2,1)S(1)}, bf16[256,512]{1,0:T(8,128)(2,1)S(1)}, u32[]{:S(2)}, u32[]{:S(2)}) collective-permute-start(bf16[256,512]{1,0:T(8,128)(2,1)S(1)} %get-tuple-element.41), channel_id=1, source_target_pairs={{0,6},{1,7},{2,4},{3,5},{4,2},{5,3},{6,0},{7,1},{8,14},{9,15},{10,... | collective-permute-start | bytes 786440 | tf_op jit(solution)/shard_map/ppermute | solution.py:486
  71.5 24.7 %collective-permute-start.4 = (bf16[256,512]{1,0:T(8,128)(2,1)S(1)}, bf16[256,512]{1,0:T(8,128)(2,1)S(1)}, u32[]{:S(2)}, u32[]{:S(2)}) collective-permute-start(bf16[256,512]{1,0:T(8,128)(2,1)S(1)} %get-tuple-element.38.refs_4_), channel_id=1, source_target_pairs={{0,4},{1,5},{2,6},{3,7},{4,0},{5,1},{6,2},{7,3},{8,12},{9,13},{10,... | collective-permute-start | bytes 786440 | tf_op jit(solution)/shard_map/ppermute | solution.py:486
  96.2 1.3 copy-start.1
  98.1 5.0 %collective-permute-start.7 = (bf16[64,512]{1,0:T(8,128)(2,1)S(1)}, bf16[64,512]{1,0:T(8,128)(2,1)S(1)}, u32[]{:S(2)}, u32[]{:S(2)}) collective-permute-start(bf16[64,512]{1,0:T(8,128)(2,1)S(1)} %get-tuple-element.43), channel_id=1, source_target_pairs={{0,8},{4,12},{8,0},{12,4},{16,24},{20,28},{24,16},{28,20},{1,9},{5... | collective-permute-start | bytes 196616 | tf_op jit(solution)/shard_map/ppermute | solution.py:366
  98.2 8.5 %collective-permute-start.8 = (bf16[64,512]{1,0:T(8,128)(2,1)S(1)}, bf16[64,512]{1,0:T(8,128)(2,1)S(1)}, u32[]{:S(2)}, u32[]{:S(2)}) collective-permute-start(bf16[64,512]{1,0:T(8,128)(2,1)S(1)} %get-tuple-element.44), channel_id=1, source_target_pairs={{0,16},{4,20},{8,24},{12,28},{16,0},{20,4},{24,8},{28,12},{1,17},{... | collective-permute-start | bytes 196616 | tf_op jit(solution)/shard_map/ppermute | solution.py:366
  102.1 6.2 %collective-permute-start.9 = (bf16[64,512]{1,0:T(8,128)(2,1)S(1)}, bf16[64,512]{1,0:T(8,128)(2,1)S(1)}, u32[]{:S(2)}, u32[]{:S(2)}) collective-permute-start(bf16[64,512]{1,0:T(8,128)(2,1)S(1)} %get-tuple-element.45), channel_id=1, source_target_pairs={{0,24},{4,28},{8,16},{12,20},{16,8},{20,12},{24,0},{28,4},{1,25},{... | collective-permute-start | bytes 196616 | tf_op jit(solution)/shard_map/ppermute | solution.py:366
  108.3 6.8 %collective-permute-start.12 = (bf16[64,512]{1,0:T(8,128)(2,1)S(1)}, bf16[64,512]{1,0:T(8,128)(2,1)S(1)}, u32[]{:S(2)}, u32[]{:S(2)}) collective-permute-start(bf16[64,512]{1,0:T(8,128)(2,1)S(1)} %shard_map.102), channel_id=1, source_target_pairs={{0,24},{4,28},{8,16},{12,20},{16,8},{20,12},{24,0},{28,4},{1,25},{... | collective-permute-start | bytes 196616 | tf_op jit(solution)/shard_map/ppermute | solution.py:366
  110.1 6.2 %collective-permute-start.11 = (bf16[64,512]{1,0:T(8,128)(2,1)S(1)}, bf16[64,512]{1,0:T(8,128)(2,1)S(1)}, u32[]{:S(2)}, u32[]{:S(2)}) collective-permute-start(bf16[64,512]{1,0:T(8,128)(2,1)S(1)} %shard_map.102), channel_id=1, source_target_pairs={{0,16},{4,20},{8,24},{12,28},{16,0},{20,4},{24,8},{28,12},{1,17},{... | collective-permute-start | bytes 196616 | tf_op jit(solution)/shard_map/ppermute | solution.py:366
  110.4 5.8 %collective-permute-start.10 = (bf16[64,512]{1,0:T(8,128)(2,1)S(1)}, bf16[64,512]{1,0:T(8,128)(2,1)S(1)}, u32[]{:S(2)}, u32[]{:S(2)}) collective-permute-start(bf16[64,512]{1,0:T(8,128)(2,1)S(1)} %shard_map.102), channel_id=1, source_target_pairs={{0,8},{4,12},{8,0},{12,4},{16,24},{20,28},{24,16},{28,20},{1,9},{5... | collective-permute-start | bytes 196616 | tf_op jit(solution)/shard_map/ppermute | solution.py:366
  117.8 10.3 %collective-permute-start.14 = (bf16[512,512]{1,0:T(8,128)(2,1)S(1)}, bf16[512,512]{1,0:T(8,128)(2,1)}, u32[]{:S(2)}, u32[]{:S(2)}) collective-permute-start(bf16[512,512]{1,0:T(8,128)(2,1)S(1)} %shard_map.103.refs_6_), channel_id=1, source_target_pairs={{0,1},{1,0},{2,3},{3,2},{4,5},{5,4},{6,7},{7,6},{8,9},{9,8},{10,11... | collective-permute-start | bytes 1572872 | tf_op jit(solution)/shard_map/ppermute | solution.py:366
  117.9 8.7 %collective-permute-start.13 = (bf16[256,512]{1,0:T(8,128)(2,1)S(1)}, bf16[256,512]{1,0:T(8,128)(2,1)S(1)}, u32[]{:S(2)}, u32[]{:S(2)}) collective-permute-start(bf16[256,512]{1,0:T(8,128)(2,1)S(1)} %pad_maximum_fusion.refs_6_.refs_0_), channel_id=1, source_target_pairs={{0,4},{1,5},{2,6},{3,7},{4,0},{5,1},{6,2},{7,3},{8,12},{9,13},{10,... | collective-permute-start | bytes 786440 | tf_op jit(solution)/shard_map/ppermute | solution.py:486
  129.3 19.6 %collective-permute-start.15 = (bf16[512,512]{1,0:T(8,128)(2,1)S(1)}, bf16[512,512]{1,0:T(8,128)(2,1)S(1)}, u32[]{:S(2)}, u32[]{:S(2)}) collective-permute-start(bf16[512,512]{1,0:T(8,128)(2,1)S(1)} %shard_map.105.mine_ref), channel_id=1, source_target_pairs={{0,2},{1,3},{2,0},{3,1},{4,6},{5,7},{6,4},{7,5},{8,10},{9,11},{10,... | collective-permute-start | bytes 1572872 | tf_op jit(solution)/shard_map/ppermute | solution.py:366
  130.9 17.6 %collective-permute-start.18 = (bf16[256,512]{1,0:T(8,128)(2,1)S(1)}, bf16[256,512]{1,0:T(8,128)(2,1)S(1)}, u32[]{:S(2)}, u32[]{:S(2)}) collective-permute-start(bf16[256,512]{1,0:T(8,128)(2,1)S(1)} %pad_maximum_fusion.refs_6_.refs_0_), channel_id=1, source_target_pairs={{0,2},{1,3},{2,0},{3,1},{4,6},{5,7},{6,4},{7,5},{8,10},{9,11},{10,... | collective-permute-start | bytes 786440 | tf_op jit(solution)/shard_map/ppermute | solution.py:486
  131.4 18.1 %collective-permute-start.20 = (bf16[256,512]{1,0:T(8,128)(2,1)S(1)}, bf16[256,512]{1,0:T(8,128)(2,1)S(1)}, u32[]{:S(2)}, u32[]{:S(2)}) collective-permute-start(bf16[256,512]{1,0:T(8,128)(2,1)S(1)} %pad_maximum_fusion.refs_6_.refs_0_), channel_id=1, source_target_pairs={{0,1},{1,0},{2,3},{3,2},{4,5},{5,4},{6,7},{7,6},{8,9},{9,8},{10,11... | collective-permute-start | bytes 786440 | tf_op jit(solution)/shard_map/ppermute | solution.py:366
  148.5 7.0 %collective-permute-start.19 = (bf16[256,512]{1,0:T(8,128)(2,1)S(1)}, bf16[256,512]{1,0:T(8,128)(2,1)S(1)}, u32[]{:S(2)}, u32[]{:S(2)}) collective-permute-start(bf16[256,512]{1,0:T(8,128)(2,1)S(1)} %collective-permute-done.18.refs_2_), channel_id=1, source_target_pairs={{0,4},{1,5},{2,6},{3,7},{4,0},{5,1},{6,2},{7,3},{8,12},{9,13},{10,... | collective-permute-start | bytes 786440 | tf_op jit(solution)/shard_map/ppermute | solution.py:486
  148.9 10.9 %collective-permute-start.16 = (bf16[512,512]{1,0:T(8,128)(2,1)S(1)}, bf16[512,512]{1,0:T(8,128)(2,1)S(1)}, u32[]{:S(2)}, u32[]{:S(2)}) collective-permute-start(bf16[512,512]{1,0:T(8,128)(2,1)S(1)} %shard_map.105.mine_ref), channel_id=1, source_target_pairs={{0,1},{1,0},{2,3},{3,2},{4,5},{5,4},{6,7},{7,6},{8,9},{9,8},{10,11... | collective-permute-start | bytes 1572872 | tf_op jit(solution)/shard_map/ppermute | solution.py:366
  148.9 10.9 %collective-permute-start.17 = (bf16[512,512]{1,0:T(8,128)(2,1)S(1)}, bf16[512,512]{1,0:T(8,128)(2,1)S(1)}, u32[]{:S(2)}, u32[]{:S(2)}) collective-permute-start(bf16[512,512]{1,0:T(8,128)(2,1)S(1)} %collective-permute-done.15.over_ref), channel_id=1, source_target_pairs={{0,1},{1,0},{2,3},{3,2},{4,5},{5,4},{6,7},{7,6},{8,9},{9,8},{10,11... | collective-permute-start | bytes 1572872 | tf_op jit(solution)/shard_map/ppermute | solution.py:366
  149.4 6.0 %collective-permute-start.22 = (bf16[256,512]{1,0:T(8,128)(2,1)S(1)}, bf16[256,512]{1,0:T(8,128)(2,1)S(1)}, u32[]{:S(2)}, u32[]{:S(2)}) collective-permute-start(bf16[256,512]{1,0:T(8,128)(2,1)S(1)} %collective-permute-done.18.refs_2_), channel_id=1, source_target_pairs={{0,1},{1,0},{2,3},{3,2},{4,5},{5,4},{6,7},{7,6},{8,9},{9,8},{10,11... | collective-permute-start | bytes 786440 | tf_op jit(solution)/shard_map/ppermute | solution.py:366
  149.4 6.0 %collective-permute-start.21 = (bf16[256,512]{1,0:T(8,128)(2,1)S(1)}, bf16[256,512]{1,0:T(8,128)(2,1)S(1)}, u32[]{:S(2)}, u32[]{:S(2)}) collective-permute-start(bf16[256,512]{1,0:T(8,128)(2,1)S(1)} %collective-permute-done.13.refs_7_.refs_1_), channel_id=1, source_target_pairs={{0,1},{1,0},{2,3},{3,2},{4,5},{5,4},{6,7},{7,6},{8,9},{9,8},{10,11... | collective-permute-start | bytes 786440 | tf_op jit(solution)/shard_map/ppermute | solution.py:366
  155.4 1.5 collective-permute-start.23

commit v6 on v5

--- a/solution.py
+++ b/solution.py
@@ -16,7 +16,7 @@
 FAR = pl.BlockSpec(memory_space=pltpu.HBM)
 
 
-def call(body, outs, scalars, near, far=(), after=(), room=40):
+def call(body, outs, scalars, near, far=(), after=(), room=40, cost=0):
     counts = len(scalars), len(near), len(far), len(after), len(outs), len(far)
     away = [index for index, out in enumerate(outs) if len(out) == 3]
 
@@ -66,7 +66,14 @@
         out_specs=[FAR if len(out) == 3 else VMEM for out in outs],
         scratch_shapes=scratch,
         compiler_params=pltpu.CompilerParams(vmem_limit_bytes=room * 1024 * 1024),
+        cost_estimate=estimate(cost),
     )(*scalars, *near, *far, *after)
+
+
+def estimate(cost):
+    if not cost:
+        return None
+    return pl.CostEstimate(flops=0, bytes_accessed=int(cost * 3.6e6), transcendentals=0)
 
 
 def iota(shape, axis):
@@ -120,7 +127,7 @@
     return high, (x - high.astype(F32)).astype(BF)
 
 
-def slots_kernel(parts, cap, place_ref, take, slot_ref, neg_ref, request_ref):
+def slots_kernel(parts, cap, take, slot_ref, neg_ref, request_ref):
     part = take(0)[...]
     edges = part.shape[1]
     slots = parts * cap
@@ -138,7 +145,7 @@
     neg = as_column(take(2)[...])
     negs = neg.shape[0]
     share = request_ref.shape[1]
-    turned = iota((negs, negs), 0) == (iota((negs, negs), 1) ^ (place_ref[0] * share))
+    turned = iota((negs, negs), 0) == (iota((negs, negs), 1) ^ (lax.axis_index("rep") * share))
     ordered = jnp.sum(jnp.where(turned, neg, 0), axis=0, keepdims=True)
     neg_ref[...] = ordered
     entities = take(3)
@@ -167,7 +174,7 @@
     query_ref[...] = total.astype(BF)
 
 
-def lookup_kernel(cap, request_ref, take, ids_ref, rows_ref, negs_ref):
+def lookup_kernel(cap, request_ref, entities, ids_ref, rows_ref, negs_ref):
     parts, share, width = request_ref.shape
     columns = rows_ref.shape[1]
     pieces = []
@@ -176,7 +183,6 @@
         pieces.append(digits[0:1] * 128.0 + digits[1:2])
     ids = jnp.concatenate(pieces, axis=1).astype(I32)
     ids_ref[...] = ids
-    entities = take(0)
     rows_ref[...] = dot(hot_rows(ids, entities.shape[0]), entities[...]).astype(BF)
     negs_ref[...] = jnp.concatenate(
         [request_ref[index, :, :columns].astype(F32) for index in range(parts)], axis=0
@@ -253,11 +259,20 @@
         back_ref[index, cap:] = jnp.concatenate(pieces, axis=0).astype(BF)
 
 
-def pair_kernel(keep_ref, got_ref, own_ref, *out_refs):
-    for index, out_ref in enumerate(out_refs):
-        term = keep_ref[index + 1].astype(F32) + got_ref[index + 1].astype(F32)
-        out_ref[...] = term.astype(BF)
-    own_ref[...] = keep_ref[0].astype(F32) + got_ref[0].astype(F32)
+def pair_kernel(keep_ref, got_ref, own_ref, sent_ref):
+    half = own_ref.shape[0] // 2
+    for place in range(4):
+        term = keep_ref[place].astype(F32) + got_ref[place].astype(F32)
+        if place < 2:
+            own_ref[place * half : (place + 1) * half] = term
+        else:
+            sent_ref[(place - 2) * half : (place - 1) * half] = term.astype(BF)
+
+
+def middle_kernel(own_ref, got_ref, keep_ref, sent_ref):
+    half = keep_ref.shape[0]
+    keep_ref[...] = own_ref[:half] + got_ref[:half].astype(F32)
+    sent_ref[...] = (own_ref[half:] + got_ref[half:].astype(F32)).astype(BF)
 
 
 def head_kernel(grad_ref, rel_ref, operators, out_ref):
@@ -271,12 +286,11 @@
     out_ref[:edges], out_ref[edges:] = split(total)
 
 
-def quad_kernel(place_ref, own_ref, first_ref, second_ref, third_ref, *out_refs):
+def spread_kernel(place_ref, own_ref, got_ref, *out_refs):
     size = out_refs[0].shape[0]
     for turn, out_ref in enumerate(out_refs):
         rows = pl.ds(pl.multiple_of((place_ref[1] ^ turn) * size, size), size)
-        total = own_ref[rows, :] + first_ref[rows, :].astype(F32)
-        total = total + (second_ref[rows, :].astype(F32) + third_ref[rows, :].astype(F32))
+        total = own_ref[rows, :] + got_ref[rows, :].astype(F32)
         out_ref[...] = total.astype(out_ref.dtype)
 
 
@@ -286,24 +300,28 @@
     out_ref[...] = total.astype(BF)
 
 
-def operator_kernel(picks_ref, place_ref, *refs):
-    sources, (out_ref, wide, sems) = refs[:-3], refs[-3:]
+def place_operators(picks_ref, place_ref, indices, sources, out_ref, wide, sems):
     width = sources[0].shape[0]
     size = width // 4
     copies = []
-    for index, source in enumerate(sources):
-        wide[index] = source[...].astype(F32)
+    for slot, (index, source) in enumerate(zip(indices, sources)):
+        wide[slot] = source[...].astype(F32)
         pick = 2 * ((index + 4) % 8)
         for turn in range(4):
             at = picks_ref[pick + 1] * width + (place_ref[1] ^ turn) * size
             copy = pltpu.make_async_copy(
-                wide.at[index, pl.ds(turn * size, size)],
+                wide.at[slot, pl.ds(turn * size, size)],
                 out_ref.at[picks_ref[pick], pl.ds(pl.multiple_of(at, size), size)],
-                sems.at[index, turn],
+                sems.at[slot, turn],
             )
             copy.start()
             copies.append(copy)
-    for copy in copies:
+    return copies
+
+
+def operator_kernel(indices, picks_ref, place_ref, *refs):
+    sources, (out_ref, wide, sems) = refs[:-3], refs[-3:]
+    for copy in place_operators(picks_ref, place_ref, indices, sources, out_ref, wide, sems):
         copy.wait()
 
 
@@ -332,7 +350,11 @@
     out_ref[...] = (kept_ref[...] + arrived_ref[...].astype(F32)).astype(BF)
 
 
-def join_kernel(place_ref, mine_ref, over_ref, other_ref, far_ref, out_ref, wide, sems):
+def join_kernel(
+    indices, picks_ref, place_ref, mine_ref, other_ref, over_ref, far_ref, *refs
+):
+    sources, rest = refs[: len(indices)], refs[len(indices) :]
+    _, out_ref, operators_ref, wide, sems, operators_wide, operators_sems = rest
     half = mine_ref.shape[0]
     core = place_ref[2]
     copies = []
@@ -347,19 +369,11 @@
         )
         copy.start()
         copies.append(copy)
+    copies += place_operators(
+        picks_ref, place_ref, indices, sources, operators_ref, operators_wide, operators_sems
+    )
     for copy in copies:
         copy.wait()
-
-
-def write(body, out, scalars, near, scratch):
-    return pl.pallas_call(
-        body,
-        out_shape=jax.ShapeDtypeStruct(*out),
-        in_specs=[SMEM] * len(scalars) + [VMEM] * len(near),
-        out_specs=FAR,
-        scratch_shapes=scratch,
-        compiler_params=pltpu.CompilerParams(vmem_limit_bytes=40 * 1024 * 1024),
-    )(*scalars, *near)
 
 
 def flip(x, axis, size, bit):
@@ -400,7 +414,7 @@
     slot, neg_own, request = call(
         functools.partial(slots_kernel, parts, cap),
         [((1, edges), I32), ((1, neg_dev), I32), ((parts, share, columns + 128), BF)],
-        (place,),
+        (),
         (),
         (
             tail_part.reshape(1, edges),
@@ -424,10 +438,9 @@
         functools.partial(lookup_kernel, cap),
         [((1, slots), I32), ((slots, columns), BF), ((parts * share, columns), BF)],
         (),
-        (requests,),
-        (entities,),
+        (requests, entities),
+        (),
         (rows,),
-        room=60,
     )
     got = exchange(found.reshape(parts, cap, columns)).reshape(slots, columns)
     neg_core, neg_across, neg_both = [flip(neg_near, "rep", reps, k) for k in (1, 2, 3)]
@@ -447,7 +460,7 @@
         (slot, neg_near, neg_core, neg_across, neg_both, queries, got, rows, rel),
     )
     (head_grads,) = call(
-        head_kernel, [((2 * edges, columns), BF)], (), (grad, rel, relations)
+        head_kernel, [((2 * edges, columns), BF)], (), (grad, rel, relations), cost=4
     )
 
     def give_back(after):
@@ -469,6 +482,7 @@
             (asked, neg_own, head, head_grads, returned),
             (),
             after,
+            cost=5,
         )[0]
 
     if not special:
@@ -479,60 +493,93 @@
 
     half, quarter = columns // 2, columns // 8
 
-    def quad(k):
-        pairs = [
-            (d * 4 + r, (d ^ (k & 1)) * 4 + (r ^ (k & 2))) for d in range(8) for r in range(4)
-        ]
-        return lambda v: lax.ppermute(v, ("dom", "rep"), pairs)
-
-    other = flip(away, "rep", 4, 1)
+    def over_y(v):
+        return flip(v, "rep", 4, 2)
+
+    def over_x(v):
+        return flip(v, "dom", 8, 1)
+
+    def over_core(v):
+        return flip(v, "rep", 4, 1)
+
+    own, sent = call(
+        pair_kernel,
+        [((columns, columns), F32), ((columns, columns), BF)],
+        (),
+        (keep, over_core(away)),
+        (),
+        (head_grads,),
+    )
+    met = over_y(sent)
+    back, returned = give_back((sent,))
+    own, sent = call(
+        middle_kernel,
+        [((half, columns), F32), ((half, columns), BF)],
+        (),
+        (own, met),
+        (),
+        (back,),
+        cost=15,
+    )
     own, *sent = call(
-        pair_kernel,
-        [((half, columns), F32)] + [((half, columns), BF)] * 3,
-        (),
-        (keep, other),
-        (),
-        (head_grads,),
-    )
-    met = [quad(k + 1)(v) for k, v in enumerate(sent)]
-    back, returned = give_back((sent[0],))
-    own, *sent = call(
-        quad_kernel,
+        spread_kernel,
         [((quarter, columns), F32)] + [((quarter, columns), BF)] * 3,
         (place,),
-        (own, *met),
-        (),
-        (back,),
+        (own, over_x(sent)),
+        cost=15,
     )
     met = [flip(v, "dom", 8, 2 * (k + 1)) for k, v in enumerate(sent)]
-    (own,) = call(sum_kernel, [((quarter, columns), BF)], (), (own, *met))
+    (own,) = call(sum_kernel, [((quarter, columns), BF)], (), (own, *met), cost=15)
     stripes = [own] + [flip(own, "dom", 8, 2 * (k + 1)) for k in range(3)]
-    own = jnp.concatenate(stripes, axis=0)
-    over_y = quad(2)(own)
-    over_x = quad(1)(own)
-    mine = [own, over_x, over_y, quad(1)(over_y)]
-    others = [flip(v, "rep", 4, 1) for v in mine]
-    relation_grad = write(
-        operator_kernel,
-        ((count, columns, columns), F32),
-        (picks, place),
-        (*mine, *others),
-        [pltpu.VMEM((8, half, columns), F32), pltpu.SemaphoreType.DMA((8, 4))],
-    )
+    whole = jnp.concatenate(stripes, axis=0)
 
     rows_half = ent_dev // 2
     leaving = add((1 - core) * rows_half, rows_half, BF, returned, (own,))
-    arrived = flip(leaving, "rep", 4, 1)
-    kept = add(core * rows_half, rows_half, F32, returned, (leaving, over_x))
+    arrived = over_core(leaving)
+    kept = add(core * rows_half, rows_half, F32, returned, (leaving,))
     (both,) = call(both_kernel, [((rows_half, columns), BF)], (), (kept, arrived))
-    across = flip(both, "rep", 4, 2)
-    pieces = (both, across, flip(both, "rep", 4, 1), flip(across, "rep", 4, 1))
-    entity_grad = write(
-        join_kernel,
-        ((ent_dev, columns), F32),
-        (place,),
-        pieces,
-        [pltpu.VMEM((2, rows_half, columns), F32), pltpu.SemaphoreType.DMA((2,))],
+    across = over_y(both)
+
+    y_whole = over_y(whole)
+    mine = [whole, over_x(whole), y_whole, over_x(y_whole)]
+    others = [over_core(v) for v in mine]
+    early, late = (0, 1, 2, 4, 5, 6), (3, 7)
+    quarters = mine + others
+    limit = pltpu.CompilerParams(vmem_limit_bytes=40 * 1024 * 1024)
+    shape = jax.ShapeDtypeStruct((count, columns, columns), F32)
+    relation_grad = pl.pallas_call(
+        functools.partial(operator_kernel, early),
+        out_shape=shape,
+        in_specs=[SMEM] * 2 + [VMEM] * len(early),
+        out_specs=FAR,
+        scratch_shapes=[
+            pltpu.VMEM((len(early), half, columns), F32),
+            pltpu.SemaphoreType.DMA((len(early), 4)),
+        ],
+        compiler_params=limit,
+    )(picks, place, *[quarters[k] for k in early])
+    entity_grad, relation_grad = pl.pallas_call(
+        functools.partial(join_kernel, late),
+        out_shape=[jax.ShapeDtypeStruct((ent_dev, columns), F32), shape],
+        in_specs=[SMEM] * 2 + [VMEM] * (4 + len(late)) + [FAR],
+        out_specs=[FAR, FAR],
+        scratch_shapes=[
+            pltpu.VMEM((2, rows_half, columns), F32),
+            pltpu.SemaphoreType.DMA((2,)),
+            pltpu.VMEM((len(late), half, columns), F32),
+            pltpu.SemaphoreType.DMA((len(late), 4)),
+        ],
+        input_output_aliases={6 + len(late): 1},
+        compiler_params=limit,
+    )(
+        picks,
+        place,
+        both,
+        over_core(both),
+        across,
+        over_core(across),
+        *[quarters[k] for k in late],
+        relation_grad,
     )
     return entity_grad, relation_grad, loss.reshape(edges)
 

time: 163 us -> 144 us (0.88)
  waiting for transfers between devices: 93.1 us -> 73 us
  local copies, waits for them, and re-layouts: 5.91 us -> 10.6 us
  Pallas kernels: 28.2 us -> 25.2 us
    ppermute x6 -> x0, waiting for transfers between devices: 55.6 us -> none  [quad(): return lambda v: lax.ppermute(v, ('dom', 'rep'), pairs)]
    ppermute x18 -> x23, waiting for transfers between devices: 15.6 us -> 50.9 us  [flip(): return lax.ppermute(x, axis, [(i, i ^ bit) for i in range(size)])]
    ppermute x18 -> x23, starting transfers between devices: 13.6 us -> 18.4 us  [flip(): return lax.ppermute(x, axis, [(i, i ^ bit) for i in range(size)])]
    unnamed x28 -> x32, local copies, waits for them, and re-layouts: 5.82 us -> 10.5 us
    ppermute x6 -> x0, starting transfers between devices: 4.6 us -> none  [quad(): return lambda v: lax.ppermute(v, ('dom', 'rep'), pairs)]
    pallas_call x12 -> x13, Pallas kernels: 23.4 us -> 20.5 us  [call(): pl.pallas_call(kernel, out_shape=[jax.ShapeDtypeStruct(out[0], out[1]) fo...]
  transfers between devices with their start and end apart: 27 -> 26, of which waited for: 17 -> 14; matrix products, arithmetic and copies ran while one was open for 0% -> 0% of each run, Pallas kernels for 7% -> 8%
where the time goes in v6:
time: 144 us; the launch traced here: 143 us
  waiting for transfers between devices  73 us (51%)
  starting transfers between devices  33.2 us (23%)
  Pallas kernels  25.2 us (18%)
  local copies, waits for them, and re-layouts  10.6 us (7%)
    ppermute x23, waiting for transfers between devices, flip(): return lax.ppermute(x, axis, [(i, i ^ bit) for i in range(size)])  50.9 us
    all_to_all x3, waiting for transfers between devices, exchange(): return lax.all_to_all(x, 'dom', split_axis=0, concat_axis=0, tiled=True)  22 us
    pallas_call x13, Pallas kernels, call(): pl.pallas_call(kernel, out_shape=[jax.ShapeDtypeStruct(out[0], out[1]) fo...  20.5 us
    ppermute x23, starting transfers between devices, flip(): return lax.ppermute(x, axis, [(i, i ^ bit) for i in range(size)])  18.4 us
    all_to_all x3, starting transfers between devices, exchange(): return lax.all_to_all(x, 'dom', split_axis=0, concat_axis=0, tiled=True)  14.8 us
    unnamed x32, local copies, waits for them, and re-layouts  10.5 us
  transfers between devices with their start and end apart: 26, of which 14 were waited for; matrix products, arithmetic and copies ran while one was open for 0% of the time, Pallas kernels for 8%

profile of v6, /device:TPU:0, one launch (start us, length us, event | category | flops | bytes accessed | tf_op | source)
XLA Modules:
  0.0 143.2 jit_solution(782598979430446596)
XLA Ops:
  0.6 2.7 %shard_map.94 = (s32[1,512]{1,0:T(1,128)}, s32[1,32]{1,0:T(1,128)}, bf16[8,8,640]{2,1,0:T(8,128)(2,1)}) custom-call(s32[1,512]{1,0:T(1,128)} %bitcast.33, s32[1,512]{1,0:T(1,128)} %bitcast.34, s32[1,32]{1,0:T(1,128)} %bitcast.35, bf16[1024,512]{1,0:T(8,128)(2,1)} %refs_1_.1), custom_call_target="tpu_custom_call" | custom-call | tf_op jit(solution)/shard_map/pallas_call | solution.py:60
  3.3 7.3 %all-to-all-start = ((bf16[8,8,640]{2,1,0:T(8,128)(2,1)}), bf16[8,8,640]{2,1,0:T(8,128)(2,1)S(1)}, u32[]{:S(2)}, u32[]{:S(2)}) async-start(bf16[8,8,640]{2,1,0:T(8,128)(2,1)} %get-tuple-element.27), calls=%async_computation | async-start | bytes 163840 | tf_op jit(solution)/shard_map/all_to_all | solution.py:384
  10.6 4.4 %shard_map.95 = (bf16[512,512]{1,0:T(8,128)(2,1)}, bf16[512,512]{1,0:T(8,128)(2,1)}) custom-call(s32[1,512]{1,0:T(1,128)} %bitcast.27, s32[1,512]{1,0:T(1,128)} %bitcast.30, bf16[1024,512]{1,0:T(8,128)(2,1)} %refs_1_.1, bf16[4,512,512]{2,1,0:T(8,128)(2,1)} %refs_2_.3, s32[1,512]{1,0:T(1,128)} %get-tuple-element.28.refs_4_.refs_1_.refs_3_), custom_call_target="tpu_custom_call" | custom-call | tf_op jit(solution)/shard_map/pallas_call | solution.py:60
  15.0 2.6 %all-to-all-done.refs_0_ = bf16[8,8,640]{2,1,0:T(8,128)(2,1)S(1)} async-done(((bf16[8,8,640]{2,1,0:T(8,128)(2,1)}), bf16[8,8,640]{2,1,0:T(8,128)(2,1)S(1)}, u32[]{:S(2)}, u32[]{:S(2)}) %all-to-all-start) | async-done | bytes 81952 | tf_op jit(solution)/shard_map/all_to_all | solution.py:384
  17.6 1.0 copy-done.5
  18.7 1.7 %shard_map.96 = (s32[1,1024]{1,0:T(1,128)S(1)}, bf16[1024,512]{1,0:T(8,128)(2,1)S(1)}, bf16[64,512]{1,0:T(8,128)(2,1)S(1)}) custom-call(bf16[8,8,640]{2,1,0:T(8,128)(2,1)S(1)} %all-to-all-done.refs_0_, bf16[1024,512]{1,0:T(8,128)(2,1)S(1)} %copy-done.2, bf16[512,512]{1,0:T(8,128)(2,1)S(1)} %copy-done.5), custom_call_target="tpu_custom_call" | custom-call | tf_op jit(solution)/shard_map/pallas_call | solution.py:60
  20.3 0.0 copy-start.7
  20.3 1.0 copy-done.7
  21.3 3.7 %all-to-all-start.1 = ((bf16[8,128,512]{2,1,0:T(8,128)(2,1)}), bf16[8,128,512]{2,1,0:T(8,128)(2,1)S(1)}, u32[]{:S(2)}, u32[]{:S(2)}) async-start(bf16[8,128,512]{2,1,0:T(8,128)(2,1)} %bitcast.26), calls=%async_computation.1 | async-start | bytes 2097152 | tf_op jit(solution)/shard_map/all_to_all | solution.py:384
  25.0 0.1 collective-permute-start.2
  25.1 1.6 %collective-permute-start.1 = (bf16[64,512]{1,0:T(8,128)(2,1)S(1)}, bf16[64,512]{1,0:T(8,128)(2,1)S(1)}, u32[]{:S(2)}, u32[]{:S(2)}) collective-permute-start(bf16[64,512]{1,0:T(8,128)(2,1)S(1)} %get-tuple-element.32.refs_2_), channel_id=1, source_target_pairs={{0,2},{1,3},{2,0},{3,1},{4,6},{5,7},{6,4},{7,5},{8,10},{9,11},{10,... | collective-permute-start | bytes 196616 | tf_op jit(solution)/shard_map/ppermute | solution.py:380
  26.7 0.2 collective-permute-start
  26.9 0.1 stack.67.refs_0_.picks_ref
  27.0 2.3 %collective-permute-done.2.refs_5_ = bf16[64,512]{1,0:T(8,128)(2,1)S(1)} collective-permute-done((bf16[64,512]{1,0:T(8,128)(2,1)S(1)}, bf16[64,512]{1,0:T(8,128)(2,1)S(1)}, u32[]{:S(2)}, u32[]{:S(2)}) %collective-permute-start.2) | collective-permute-done | bytes 65568 | tf_op jit(solution)/shard_map/ppermute | solution.py:380
  29.4 1.5 %collective-permute-done.1.refs_4_ = bf16[64,512]{1,0:T(8,128)(2,1)S(1)} collective-permute-done((bf16[64,512]{1,0:T(8,128)(2,1)S(1)}, bf16[64,512]{1,0:T(8,128)(2,1)S(1)}, u32[]{:S(2)}, u32[]{:S(2)}) %collective-permute-start.1) | collective-permute-done | bytes 65568 | tf_op jit(solution)/shard_map/ppermute | solution.py:380
  30.9 19.5 %all-to-all-done.1 = bf16[8,128,512]{2,1,0:T(8,128)(2,1)S(1)} async-done(((bf16[8,128,512]{2,1,0:T(8,128)(2,1)}), bf16[8,128,512]{2,1,0:T(8,128)(2,1)S(1)}, u32[]{:S(2)}, u32[]{:S(2)}) %all-to-all-start.1) | async-done | bytes 1048608 | tf_op jit(solution)/shard_map/all_to_all | solution.py:384
  50.3 1.0 copy-done.4
  51.4 1.0 copy-done.6
  52.4 3.4 %shard_map.97 = (f32[1,512]{1,0:T(1,128)}, f32[512,1]{1,0:T(8,128)S(1)}, bf16[512,256]{1,0:T(8,128)(2,1)S(1)}, bf16[512,512]{1,0:T(8,128)(2,1)S(1)}, bf16[4,256,...) custom-call(s32[16]{0:T(128)S(1)} %stack.67.refs_0_.picks_ref, s32[1,512]{1,0:T(1,128)S(1)} %copy-done.14, ...), custom_call_target="tpu_custom_call" | custom-call | tf_op jit(solution)/shard_map/pallas_call | solution.py:60
  55.8 0.1 collective-permute-start.3
  55.9 1.6 %shard_map.98.refs_2_.refs_4_ = bf16[1024,512]{1,0:T(8,128)(2,1)S(1)} custom-call(bf16[512,512]{1,0:T(8,128)(2,1)S(1)} %get-tuple-element.35.refs_0_, s32[1,512]{1,0:T(1,128)S(1)} %bitcast.32, bf16[4,512,512]{2,1,0:T(8,128)(2,1)S(1)} %copy-done.3), custom_call_target="tpu_custom_call" | custom-call | bytes 14400000 | tf_op jit(solution)/shard_map/pallas_call | solution.py:60
  57.5 1.0 collective-permute-done.3.refs_1_
  58.5 0.2 shard_map.99
  58.8 1.0 copy-done.8
  59.7 0.9 shard_map.100.refs_2_
  60.7 0.0 copy-start
  60.7 1.0 copy-done
  61.7 3.9 %all-to-all-start.2 = ((bf16[8,160,512]{2,1,0:T(8,128)(2,1)}), bf16[8,160,512]{2,1,0:T(8,128)(2,1)S(1)}, u32[]{:S(2)}, u32[]{:S(2)}) async-start(bf16[8,160,512]{2,1,0:T(8,128)(2,1)} %copy-done), calls=%async_computation.2 | async-start | bytes 2621440 | tf_op jit(solution)/shard_map/all_to_all | solution.py:384
  65.6 1.6 %collective-permute-start.4 = (bf16[512,512]{1,0:T(8,128)(2,1)S(1)}, bf16[512,512]{1,0:T(8,128)(2,1)S(1)}, u32[]{:S(2)}, u32[]{:S(2)}) collective-permute-start(bf16[512,512]{1,0:T(8,128)(2,1)S(1)} %get-tuple-element.40.refs_4_), channel_id=1, source_target_pairs={{0,2},{1,3},{2,0},{3,1},{4,6},{5,7},{6,4},{7,5},{8,10},{9,11},{10,... | collective-permute-start | bytes 1572872 | tf_op jit(solution)/shard_map/ppermute | solution.py:380
  67.2 12.4 %collective-permute-done.4.refs_1_ = bf16[512,512]{1,0:T(8,128)(2,1)S(1)} collective-permute-done((bf16[512,512]{1,0:T(8,128)(2,1)S(1)}, bf16[512,512]{1,0:T(8,128)(2,1)S(1)}, u32[]{:S(2)}, u32[]{:S(2)}) %collective-permute-start.4) | collective-permute-done | bytes 524320 | tf_op jit(solution)/shard_map/ppermute | solution.py:380
  79.7 1.3 copy-done.1
  81.0 1.2 copy-done.9
  82.2 0.1 shard_map.101
  82.3 0.8 copy-done.10
  83.1 1.4 collective-permute-start.5
  84.5 0.1 pad_add_fusion.refs_0_.place_ref
  84.6 9.2 %collective-permute-done.5.refs_2_ = bf16[256,512]{1,0:T(8,128)(2,1)S(1)} collective-permute-done((bf16[256,512]{1,0:T(8,128)(2,1)S(1)}, bf16[256,512]{1,0:T(8,128)(2,1)S(1)}, u32[]{:S(2)}, u32[]{:S(2)}) %collective-permute-start.5) | collective-permute-done | bytes 262176 | tf_op jit(solution)/shard_map/ppermute | solution.py:380
  93.8 1.0 copy-done.11
  94.9 1.2 shard_map.102
  96.1 2.4 %collective-permute-start.6 = (bf16[64,512]{1,0:T(8,128)(2,1)}, bf16[64,512]{1,0:T(8,128)(2,1)S(1)}, u32[]{:S(2)}, u32[]{:S(2)}) collective-permute-start(bf16[64,512]{1,0:T(8,128)(2,1)} %get-tuple-element.45), channel_id=1, source_target_pairs={{0,8},{4,12},{8,0},{12,4},{16,24},{20,28},{24,16},{28,20},{1,9},{5... | collective-permute-start | bytes 196616 | tf_op jit(solution)/shard_map/ppermute | solution.py:380
  98.4 0.2 collective-permute-start.7
  98.7 2.1 %collective-permute-start.8 = (bf16[64,512]{1,0:T(8,128)(2,1)S(1)}, bf16[64,512]{1,0:T(8,128)(2,1)S(1)}, u32[]{:S(2)}, u32[]{:S(2)}) collective-permute-start(bf16[64,512]{1,0:T(8,128)(2,1)S(1)} %get-tuple-element.47), channel_id=1, source_target_pairs={{0,24},{4,28},{8,16},{12,20},{16,8},{20,12},{24,0},{28,4},{1,25},{... | collective-permute-start | bytes 196616 | tf_op jit(solution)/shard_map/ppermute | solution.py:380
  100.8 0.3 collective-permute-done.6.refs_1_
  101.1 5.0 %collective-permute-done.7.refs_2_ = bf16[64,512]{1,0:T(8,128)(2,1)S(1)} collective-permute-done((bf16[64,512]{1,0:T(8,128)(2,1)S(1)}, bf16[64,512]{1,0:T(8,128)(2,1)S(1)}, u32[]{:S(2)}, u32[]{:S(2)}) %collective-permute-start.7) | collective-permute-done | bytes 65568 | tf_op jit(solution)/shard_map/ppermute | solution.py:380
  106.2 1.5 %shard_map.104.refs_6_ = bf16[512,512]{1,0:T(8,128)(2,1)S(1)} custom-call(s32[1]{0:T(128)} %bitcast.23.refs_0_, s32[1,1024]{1,0:T(1,128)S(1)} %get-tuple-element.30.refs_1_, s32[1,32]{1,0:T(1,128)S(1)} %copy-done.15, s32[1,512]{1,0:T(1,128)S(1)} %bitcast.28, bf16[1024,512]{1,0:T(8,128)(2,1)S(1)} %shard_map.98.refs_2_.refs_4_, ...), custom_call_target="tpu_custom_call" | custom-call | bytes 18000000 | tf_op jit(solution)/shard_map/pallas_call | solution.py:60
  107.7 0.1 collective-permute-start.9
  107.8 1.5 %shard_map.105.refs_0_ = f32[512,512]{1,0:T(8,128)S(1)} custom-call(s32[1]{0:T(128)} %bitcast.15.refs_0_, s32[1,1024]{1,0:T(1,128)S(1)} %get-tuple-element.30.refs_1_, s32[1,32]{1,0:T(1,128)S(1)} %copy-done.15, s32[1,512]{1,0:T(1,128)S(1)} %bitcast.29, bf16[1024,512]{1,0:T(8,128)(2,1)S(1)} %shard_map.98.refs_2_.refs_4_, ...), custom_call_target="tpu_custom_call" | custom-call | bytes 18000000 | tf_op jit(solution)/shard_map/pallas_call | solution.py:60
  109.3 0.5 collective-permute-done.9.refs_1_
  109.8 1.2 shard_map.106.mine_ref
  111.0 1.6 %collective-permute-start.11 = (bf16[512,512]{1,0:T(8,128)(2,1)S(1)}, bf16[512,512]{1,0:T(8,128)(2,1)S(1)}, u32[]{:S(2)}, u32[]{:S(2)}) collective-permute-start(bf16[512,512]{1,0:T(8,128)(2,1)S(1)} %shard_map.106.mine_ref), channel_id=1, source_target_pairs={{0,2},{1,3},{2,0},{3,1},{4,6},{5,7},{6,4},{7,5},{8,10},{9,11},{10,... | collective-permute-start | bytes 1572872 | tf_op jit(solution)/shard_map/ppermute | solution.py:380
  112.6 1.7 %collective-permute-start.15 = (bf16[64,512]{1,0:T(8,128)(2,1)S(1)}, bf16[64,512]{1,0:T(8,128)(2,1)S(1)}, u32[]{:S(2)}, u32[]{:S(2)}) collective-permute-start(bf16[64,512]{1,0:T(8,128)(2,1)S(1)} %shard_map.103.refs_6_), channel_id=1, source_target_pairs={{0,24},{4,28},{8,16},{12,20},{16,8},{20,12},{24,0},{28,4},{1,25},{... | collective-permute-start | bytes 196616 | tf_op jit(solution)/shard_map/ppermute | solution.py:380
  114.3 1.0 collective-permute-start.14
  115.3 1.7 %collective-permute-start.13 = (bf16[64,512]{1,0:T(8,128)(2,1)S(1)}, bf16[64,512]{1,0:T(8,128)(2,1)S(1)}, u32[]{:S(2)}, u32[]{:S(2)}) collective-permute-start(bf16[64,512]{1,0:T(8,128)(2,1)S(1)} %shard_map.103.refs_6_), channel_id=1, source_target_pairs={{0,8},{4,12},{8,0},{12,4},{16,24},{20,28},{24,16},{28,20},{1,9},{5... | collective-permute-start | bytes 196616 | tf_op jit(solution)/shard_map/ppermute | solution.py:380
  117.0 2.4 %collective-permute-done.15 = bf16[64,512]{1,0:T(8,128)(2,1)S(1)} collective-permute-done((bf16[64,512]{1,0:T(8,128)(2,1)S(1)}, bf16[64,512]{1,0:T(8,128)(2,1)S(1)}, u32[]{:S(2)}, u32[]{:S(2)}) %collective-permute-start.15) | collective-permute-done | bytes 65568 | tf_op jit(solution)/shard_map/ppermute | solution.py:380
  119.4 2.4 %collective-permute-done.14 = bf16[64,512]{1,0:T(8,128)(2,1)S(1)} collective-permute-done((bf16[64,512]{1,0:T(8,128)(2,1)S(1)}, bf16[64,512]{1,0:T(8,128)(2,1)S(1)}, u32[]{:S(2)}, u32[]{:S(2)}) %collective-permute-start.14) | collective-permute-done | bytes 65568 | tf_op jit(solution)/shard_map/ppermute | solution.py:380
  121.8 0.6 collective-permute-start.16
  122.4 8.3 %collective-permute-done.16.refs_2_ = bf16[256,512]{1,0:T(8,128)(2,1)S(1)} collective-permute-done((bf16[256,512]{1,0:T(8,128)(2,1)S(1)}, bf16[256,512]{1,0:T(8,128)(2,1)S(1)}, u32[]{:S(2)}, u32[]{:S(2)}) %collective-permute-start.16) | collective-permute-done | bytes 262176 | tf_op jit(solution)/shard_map/ppermute | solution.py:380
  130.6 1.1 collective-permute-start.17
  131.7 0.5 collective-permute-start.12
  132.2 0.1 collective-permute-start.21
  132.3 0.4 collective-permute-start.22
  132.7 5.4 %collective-permute-done.17.refs_0_ = bf16[256,512]{1,0:T(8,128)(2,1)S(1)} collective-permute-done((bf16[256,512]{1,0:T(8,128)(2,1)S(1)}, bf16[256,512]{1,0:T(8,128)(2,1)S(1)}, u32[]{:S(2)}, u32[]{:S(2)}) %collective-permute-start.17) | collective-permute-done | bytes 262176 | tf_op jit(solution)/shard_map/ppermute | solution.py:380
  138.2 2.4 %shard_map.107.refs_2_ = f32[4,512,512]{2,1,0:T(8,128)} custom-call(s32[16]{0:T(128)S(1)} %stack.67.refs_0_.picks_ref, s32[3]{0:T(128)S(1)} %pad_add_fusion.refs_0_.place_ref, bf16[256,512]{1,0:T(8,128)(2,1)S(1)} %pad_maximum_fusion.refs_0_, bf16[256,512]{1,0:T(8,128)(2,1)S(1)} %collective-permute-done.19.refs_1_, ...), custom_call_target="tpu_custom_call" | custom-call | tf_op jit(solution)/shard_map/pallas_call | solution.py:550
  140.7 2.3 %shard_map.108 = (f32[1024,512]{1,0:T(8,128)}, f32[4,512,512]{2,1,0:T(8,128)}) custom-call(s32[16]{0:T(128)S(1)} %stack.67.refs_0_.picks_ref, s32[3]{0:T(128)S(1)} %pad_add_fusion.refs_0_.place_ref, bf16[512,512]{1,0:T(8,128)(2,1)S(1)} %shard_map.106.mine_ref, ...), custom_call_target="tpu_custom_call", output_to_operand_aliasing={{1}: (8, {})} | custom-call | tf_op jit(solution)/shard_map/pallas_call | solution.py:561
  (38 shorter events, 0.1 us)
Async XLA Ops:
  0.6 17.0 %copy-start.2 = (bf16[1024,512]{1,0:T(8,128)(2,1)S(1)}, bf16[1024,512]{1,0:T(8,128)(2,1)}, u32[]{:S(2)}) copy-start(bf16[1024,512]{1,0:T(8,128)(2,1)} %refs_1_.1) | copy-start | bytes 3145732
  3.3 14.3 %all-to-all-start = ((bf16[8,8,640]{2,1,0:T(8,128)(2,1)}), bf16[8,8,640]{2,1,0:T(8,128)(2,1)S(1)}, u32[]{:S(2)}, u32[]{:S(2)}) async-start(bf16[8,8,640]{2,1,0:T(8,128)(2,1)} %get-tuple-element.27), calls=%async_computation | async-start | bytes 163840 | tf_op jit(solution)/shard_map/all_to_all | solution.py:384
  10.6 39.7 %copy-start.13 = (s32[512]{0:T(512)S(1)}, s32[512]{0:T(512)}, u32[]{:S(2)}) copy-start(s32[512]{0:T(512)} %param.10) | copy-start | bytes 6148
  10.6 39.7 %copy-start.14 = (s32[1,512]{1,0:T(1,128)S(1)}, s32[1,512]{1,0:T(1,128)}, u32[]{:S(2)}) copy-start(s32[1,512]{1,0:T(1,128)} %get-tuple-element.28.refs_4_.refs_1_.refs_3_) | copy-start | bytes 6148
  17.6 1.0 copy-start.5
  20.3 1.0 copy-start.7
  21.3 34.6 %copy-start.3 = (bf16[4,512,512]{2,1,0:T(8,128)(2,1)S(1)}, bf16[4,512,512]{2,1,0:T(8,128)(2,1)}, u32[]{:S(2)}) copy-start(bf16[4,512,512]{2,1,0:T(8,128)(2,1)} %refs_2_.3) | copy-start | bytes 6291460
  21.3 29.0 %all-to-all-start.1 = ((bf16[8,128,512]{2,1,0:T(8,128)(2,1)}), bf16[8,128,512]{2,1,0:T(8,128)(2,1)S(1)}, u32[]{:S(2)}, u32[]{:S(2)}) async-start(bf16[8,128,512]{2,1,0:T(8,128)(2,1)} %bitcast.26), calls=%async_computation.1 | async-start | bytes 2097152 | tf_op jit(solution)/shard_map/all_to_all | solution.py:384
  25.0 4.4 %collective-permute-start.2 = (bf16[64,512]{1,0:T(8,128)(2,1)S(1)}, bf16[64,512]{1,0:T(8,128)(2,1)S(1)}, u32[]{:S(2)}, u32[]{:S(2)}) collective-permute-start(bf16[64,512]{1,0:T(8,128)(2,1)S(1)} %get-tuple-element.32.refs_2_), channel_id=1, source_target_pairs={{0,3},{1,2},{2,1},{3,0},{4,7},{5,6},{6,5},{7,4},{8,11},{9,10},{10,... | collective-permute-start | bytes 196616 | tf_op jit(solution)/shard_map/ppermute | solution.py:380
  25.1 5.8 %collective-permute-start.1 = (bf16[64,512]{1,0:T(8,128)(2,1)S(1)}, bf16[64,512]{1,0:T(8,128)(2,1)S(1)}, u32[]{:S(2)}, u32[]{:S(2)}) collective-permute-start(bf16[64,512]{1,0:T(8,128)(2,1)S(1)} %get-tuple-element.32.refs_2_), channel_id=1, source_target_pairs={{0,2},{1,3},{2,0},{3,1},{4,6},{5,7},{6,4},{7,5},{8,10},{9,11},{10,... | collective-permute-start | bytes 196616 | tf_op jit(solution)/shard_map/ppermute | solution.py:380
  26.7 4.2 %collective-permute-start = (bf16[64,512]{1,0:T(8,128)(2,1)S(1)}, bf16[64,512]{1,0:T(8,128)(2,1)S(1)}, u32[]{:S(2)}, u32[]{:S(2)}) collective-permute-start(bf16[64,512]{1,0:T(8,128)(2,1)S(1)} %get-tuple-element.32.refs_2_), channel_id=1, source_target_pairs={{0,1},{1,0},{2,3},{3,2},{4,5},{5,4},{6,7},{7,6},{8,9},{9,8},{10,11... | collective-permute-start | bytes 196616 | tf_op jit(solution)/shard_map/ppermute | solution.py:380
  50.3 1.0 copy-start.4
  51.4 1.0 copy-start.6
  55.8 2.7 %collective-permute-start.3 = (bf16[4,256,512]{2,1,0:T(8,128)(2,1)S(1)}, bf16[4,256,512]{2,1,0:T(8,128)(2,1)S(1)}, u32[]{:S(2)}, u32[]{:S(2)}) collective-permute-start(bf16[4,256,512]{2,1,0:T(8,128)(2,1)S(1)} %get-tuple-element.39), channel_id=1, source_target_pairs={{0,1},{1,0},{2,3},{3,2},{4,5},{5,4},{6,7},{7,6},{8,9},{9,8},{10,11... | collective-permute-start | bytes 3145736 | tf_op jit(solution)/shard_map/ppermute | solution.py:380
  58.8 1.0 copy-start.8
  60.7 1.1 copy-start
  61.7 44.4 %copy-start.12 = (s32[512]{0:T(512)S(1)}, s32[512]{0:T(512)}, u32[]{:S(2)}) copy-start(s32[512]{0:T(512)} %param.9) | copy-start | bytes 6148
  61.7 44.4 %all-to-all-start.2 = ((bf16[8,160,512]{2,1,0:T(8,128)(2,1)}), bf16[8,160,512]{2,1,0:T(8,128)(2,1)S(1)}, u32[]{:S(2)}, u32[]{:S(2)}) async-start(bf16[8,160,512]{2,1,0:T(8,128)(2,1)} %copy-done), calls=%async_computation.2 | async-start | bytes 2621440 | tf_op jit(solution)/shard_map/all_to_all | solution.py:384
  65.6 40.6 %copy-start.15 = (s32[1,32]{1,0:T(1,128)S(1)}, s32[1,32]{1,0:T(1,128)}, u32[]{:S(2)}) copy-start(s32[1,32]{1,0:T(1,128)} %get-tuple-element.31.refs_2_) | copy-start | bytes 388
  65.6 14.0 %collective-permute-start.4 = (bf16[512,512]{1,0:T(8,128)(2,1)S(1)}, bf16[512,512]{1,0:T(8,128)(2,1)S(1)}, u32[]{:S(2)}, u32[]{:S(2)}) collective-permute-start(bf16[512,512]{1,0:T(8,128)(2,1)S(1)} %get-tuple-element.40.refs_4_), channel_id=1, source_target_pairs={{0,2},{1,3},{2,0},{3,1},{4,6},{5,7},{6,4},{7,5},{8,10},{9,11},{10,... | collective-permute-start | bytes 1572872 | tf_op jit(solution)/shard_map/ppermute | solution.py:380
  79.7 1.3 copy-start.1
  81.0 1.2 copy-start.9
  82.3 0.8 copy-start.10
  83.1 10.7 %collective-permute-start.5 = (bf16[256,512]{1,0:T(8,128)(2,1)S(1)}, bf16[256,512]{1,0:T(8,128)(2,1)S(1)}, u32[]{:S(2)}, u32[]{:S(2)}) collective-permute-start(bf16[256,512]{1,0:T(8,128)(2,1)S(1)} %get-tuple-element.43), channel_id=1, source_target_pairs={{0,4},{4,0},{8,12},{12,8},{16,20},{20,16},{24,28},{28,24},{1,5},{5... | collective-permute-start | bytes 786440 | tf_op jit(solution)/shard_map/ppermute | solution.py:380
  93.8 1.0 copy-start.11
  96.1 5.0 %collective-permute-start.6 = (bf16[64,512]{1,0:T(8,128)(2,1)}, bf16[64,512]{1,0:T(8,128)(2,1)S(1)}, u32[]{:S(2)}, u32[]{:S(2)}) collective-permute-start(bf16[64,512]{1,0:T(8,128)(2,1)} %get-tuple-element.45), channel_id=1, source_target_pairs={{0,8},{4,12},{8,0},{12,4},{16,24},{20,28},{24,16},{28,20},{1,9},{5... | collective-permute-start | bytes 196616 | tf_op jit(solution)/shard_map/ppermute | solution.py:380
  98.4 7.7 %collective-permute-start.7 = (bf16[64,512]{1,0:T(8,128)(2,1)S(1)}, bf16[64,512]{1,0:T(8,128)(2,1)S(1)}, u32[]{:S(2)}, u32[]{:S(2)}) collective-permute-start(bf16[64,512]{1,0:T(8,128)(2,1)S(1)} %get-tuple-element.46), channel_id=1, source_target_pairs={{0,16},{4,20},{8,24},{12,28},{16,0},{20,4},{24,8},{28,12},{1,17},{... | collective-permute-start | bytes 196616 | tf_op jit(solution)/shard_map/ppermute | solution.py:380
  98.7 7.5 %collective-permute-start.8 = (bf16[64,512]{1,0:T(8,128)(2,1)S(1)}, bf16[64,512]{1,0:T(8,128)(2,1)S(1)}, u32[]{:S(2)}, u32[]{:S(2)}) collective-permute-start(bf16[64,512]{1,0:T(8,128)(2,1)S(1)} %get-tuple-element.47), channel_id=1, source_target_pairs={{0,24},{4,28},{8,16},{12,20},{16,8},{20,12},{24,0},{28,4},{1,25},{... | collective-permute-start | bytes 196616 | tf_op jit(solution)/shard_map/ppermute | solution.py:380
  107.7 2.1 %collective-permute-start.9 = (bf16[512,512]{1,0:T(8,128)(2,1)S(1)}, bf16[512,512]{1,0:T(8,128)(2,1)}, u32[]{:S(2)}, u32[]{:S(2)}) collective-permute-start(bf16[512,512]{1,0:T(8,128)(2,1)S(1)} %shard_map.104.refs_6_), channel_id=1, source_target_pairs={{0,1},{1,0},{2,3},{3,2},{4,5},{5,4},{6,7},{7,6},{8,9},{9,8},{10,11... | collective-permute-start | bytes 1572872 | tf_op jit(solution)/shard_map/ppermute | solution.py:380
  111.0 20.7 %collective-permute-start.11 = (bf16[512,512]{1,0:T(8,128)(2,1)S(1)}, bf16[512,512]{1,0:T(8,128)(2,1)S(1)}, u32[]{:S(2)}, u32[]{:S(2)}) collective-permute-start(bf16[512,512]{1,0:T(8,128)(2,1)S(1)} %shard_map.106.mine_ref), channel_id=1, source_target_pairs={{0,2},{1,3},{2,0},{3,1},{4,6},{5,7},{6,4},{7,5},{8,10},{9,11},{10,... | collective-permute-start | bytes 1572872 | tf_op jit(solution)/shard_map/ppermute | solution.py:380
  112.6 6.8 %collective-permute-start.15 = (bf16[64,512]{1,0:T(8,128)(2,1)S(1)}, bf16[64,512]{1,0:T(8,128)(2,1)S(1)}, u32[]{:S(2)}, u32[]{:S(2)}) collective-permute-start(bf16[64,512]{1,0:T(8,128)(2,1)S(1)} %shard_map.103.refs_6_), channel_id=1, source_target_pairs={{0,24},{4,28},{8,16},{12,20},{16,8},{20,12},{24,0},{28,4},{1,25},{... | collective-permute-start | bytes 196616 | tf_op jit(solution)/shard_map/ppermute | solution.py:380
  114.3 7.4 %collective-permute-start.14 = (bf16[64,512]{1,0:T(8,128)(2,1)S(1)}, bf16[64,512]{1,0:T(8,128)(2,1)S(1)}, u32[]{:S(2)}, u32[]{:S(2)}) collective-permute-start(bf16[64,512]{1,0:T(8,128)(2,1)S(1)} %shard_map.103.refs_6_), channel_id=1, source_target_pairs={{0,16},{4,20},{8,24},{12,28},{16,0},{20,4},{24,8},{28,12},{1,17},{... | collective-permute-start | bytes 196616 | tf_op jit(solution)/shard_map/ppermute | solution.py:380
  115.3 6.4 %collective-permute-start.13 = (bf16[64,512]{1,0:T(8,128)(2,1)S(1)}, bf16[64,512]{1,0:T(8,128)(2,1)S(1)}, u32[]{:S(2)}, u32[]{:S(2)}) collective-permute-start(bf16[64,512]{1,0:T(8,128)(2,1)S(1)} %shard_map.103.refs_6_), channel_id=1, source_target_pairs={{0,8},{4,12},{8,0},{12,4},{16,24},{20,28},{24,16},{28,20},{1,9},{5... | collective-permute-start | bytes 196616 | tf_op jit(solution)/shard_map/ppermute | solution.py:380
  121.8 8.9 %collective-permute-start.16 = (bf16[256,512]{1,0:T(8,128)(2,1)S(1)}, bf16[256,512]{1,0:T(8,128)(2,1)S(1)}, u32[]{:S(2)}, u32[]{:S(2)}) collective-permute-start(bf16[256,512]{1,0:T(8,128)(2,1)S(1)} %pad_maximum_fusion.refs_0_), channel_id=1, source_target_pairs={{0,2},{1,3},{2,0},{3,1},{4,6},{5,7},{6,4},{7,5},{8,10},{9,11},{10,... | collective-permute-start | bytes 786440 | tf_op jit(solution)/shard_map/ppermute | solution.py:380
  122.3 9.9 %collective-permute-start.19 = (bf16[256,512]{1,0:T(8,128)(2,1)S(1)}, bf16[256,512]{1,0:T(8,128)(2,1)S(1)}, u32[]{:S(2)}, u32[]{:S(2)}) collective-permute-start(bf16[256,512]{1,0:T(8,128)(2,1)S(1)} %pad_maximum_fusion.refs_0_), channel_id=1, source_target_pairs={{0,4},{4,0},{8,12},{12,8},{16,20},{20,16},{24,28},{28,24},{1,5},{5... | collective-permute-start | bytes 786440 | tf_op jit(solution)/shard_map/ppermute | solution.py:380
  122.3 9.9 %collective-permute-start.20 = (bf16[256,512]{1,0:T(8,128)(2,1)S(1)}, bf16[256,512]{1,0:T(8,128)(2,1)S(1)}, u32[]{:S(2)}, u32[]{:S(2)}) collective-permute-start(bf16[256,512]{1,0:T(8,128)(2,1)S(1)} %pad_maximum_fusion.refs_0_), channel_id=1, source_target_pairs={{0,1},{1,0},{2,3},{3,2},{4,5},{5,4},{6,7},{7,6},{8,9},{9,8},{10,11... | collective-permute-start | bytes 786440 | tf_op jit(solution)/shard_map/ppermute | solution.py:380
  130.6 7.5 %collective-permute-start.17 = (bf16[256,512]{1,0:T(8,128)(2,1)S(1)}, bf16[256,512]{1,0:T(8,128)(2,1)S(1)}, u32[]{:S(2)}, u32[]{:S(2)}) collective-permute-start(bf16[256,512]{1,0:T(8,128)(2,1)S(1)} %collective-permute-done.16.refs_2_), channel_id=1, source_target_pairs={{0,4},{4,0},{8,12},{12,8},{16,20},{20,16},{24,28},{28,24},{1,5},{5... | collective-permute-start | bytes 786440 | tf_op jit(solution)/shard_map/ppermute | solution.py:380
  131.7 8.9 %collective-permute-start.10 = (bf16[512,512]{1,0:T(8,128)(2,1)S(1)}, bf16[512,512]{1,0:T(8,128)(2,1)S(1)}, u32[]{:S(2)}, u32[]{:S(2)}) collective-permute-start(bf16[512,512]{1,0:T(8,128)(2,1)S(1)} %shard_map.106.mine_ref), channel_id=1, source_target_pairs={{0,1},{1,0},{2,3},{3,2},{4,5},{5,4},{6,7},{7,6},{8,9},{9,8},{10,11... | collective-permute-start | bytes 1572872 | tf_op jit(solution)/shard_map/ppermute | solution.py:380
  131.7 8.9 %collective-permute-start.12 = (bf16[512,512]{1,0:T(8,128)(2,1)S(1)}, bf16[512,512]{1,0:T(8,128)(2,1)S(1)}, u32[]{:S(2)}, u32[]{:S(2)}) collective-permute-start(bf16[512,512]{1,0:T(8,128)(2,1)S(1)} %collective-permute-done.11.over_ref), channel_id=1, source_target_pairs={{0,1},{1,0},{2,3},{3,2},{4,5},{5,4},{6,7},{7,6},{8,9},{9,8},{10,11... | collective-permute-start | bytes 1572872 | tf_op jit(solution)/shard_map/ppermute | solution.py:380
  132.2 6.0 %collective-permute-start.21 = (bf16[256,512]{1,0:T(8,128)(2,1)S(1)}, bf16[256,512]{1,0:T(8,128)(2,1)S(1)}, u32[]{:S(2)}, u32[]{:S(2)}) collective-permute-start(bf16[256,512]{1,0:T(8,128)(2,1)S(1)} %collective-permute-done.19.refs_1_), channel_id=1, source_target_pairs={{0,1},{1,0},{2,3},{3,2},{4,5},{5,4},{6,7},{7,6},{8,9},{9,8},{10,11... | collective-permute-start | bytes 786440 | tf_op jit(solution)/shard_map/ppermute | solution.py:380
  132.3 5.9 %collective-permute-start.22 = (bf16[256,512]{1,0:T(8,128)(2,1)S(1)}, bf16[256,512]{1,0:T(8,128)(2,1)S(1)}, u32[]{:S(2)}, u32[]{:S(2)}) collective-permute-start(bf16[256,512]{1,0:T(8,128)(2,1)S(1)} %collective-permute-done.16.refs_2_), channel_id=1, source_target_pairs={{0,1},{1,0},{2,3},{3,2},{4,5},{5,4},{6,7},{7,6},{8,9},{9,8},{10,11... | collective-permute-start | bytes 786440 | tf_op jit(solution)/shard_map/ppermute | solution.py:380
  138.2 2.5 %collective-permute-start.18 = (bf16[256,512]{1,0:T(8,128)(2,1)S(1)}, bf16[256,512]{1,0:T(8,128)(2,1)S(1)}, u32[]{:S(2)}, u32[]{:S(2)}) collective-permute-start(bf16[256,512]{1,0:T(8,128)(2,1)S(1)} %collective-permute-done.17.refs_0_), channel_id=1, source_target_pairs={{0,1},{1,0},{2,3},{3,2},{4,5},{5,4},{6,7},{7,6},{8,9},{9,8},{10,11... | collective-permute-start | bytes 786440 | tf_op jit(solution)/shard_map/ppermute | solution.py:380

commit v7 on v6

--- a/solution.py
+++ b/solution.py
@@ -71,9 +71,7 @@
 
 
 def estimate(cost):
-    if not cost:
-        return None
-    return pl.CostEstimate(flops=0, bytes_accessed=int(cost * 3.6e6), transcendentals=0)
+    return pl.CostEstimate(flops=1 + int(cost * 1e9), bytes_accessed=1, transcendentals=0)
 
 
 def iota(shape, axis):
@@ -189,40 +187,46 @@
     ).astype(BF)
 
 
-def operator_terms(picks_ref, first, rows_ref, rel, grad, out_ref):
-    width = out_ref.shape[1]
-    for place in range(out_ref.shape[0]):
-        at = pl.multiple_of(picks_ref[2 * (first + place) + 1] * width, width)
-        picked = jnp.where(rel == picks_ref[2 * (first + place)], grad, jnp.zeros_like(grad))
-        out_ref[place] = dot_t0(rows_ref[:, pl.ds(at, width)], picked).astype(out_ref.dtype)
+def quarter_of(special, index):
+    if not special:
+        return index // 2, index % 2
+    rep, x = lax.axis_index("rep"), lax.axis_index("dom") & 1
+    quarter = ((rep & 2) + x) ^ (index % 4)
+    core = (rep & 1) ^ (1 if index < 4 else 0)
+    return 2 * core + (quarter >> 1), quarter & 1
+
+
+def operator_terms(special, first, rows_ref, rel, grad, out_ref):
+    width = grad.shape[1] // 2
+    for place in range(4):
+        relation, part = quarter_of(special, first + place)
+        at = part * width if isinstance(part, int) else pl.multiple_of(part * width, width)
+        picked = jnp.where(rel == relation, grad, jnp.zeros_like(grad))
+        term = dot_t0(rows_ref[:, pl.ds(at, width)], picked)
+        out_ref[place * width : (place + 1) * width] = term.astype(out_ref.dtype)
 
 
 def edge_kernel(
     factor,
-    picks_ref,
     slot_ref,
     near_ref,
     core_ref,
     across_ref,
     both_ref,
-    query_ref,
     got_ref,
-    rows_ref,
-    rel_ref,
+    take,
     loss_ref,
-    weight_ref,
-    prob_ref,
     grad_ref,
-    away_ref,
-    keep_ref,
+    back_ref,
 ):
-    queries = query_ref[...]
+    edges = slot_ref.shape[1]
     negatives = jnp.concatenate(
         [near_ref[...], core_ref[...], across_ref[...], both_ref[...]], axis=0
     )
-    edges, slots = queries.shape[0], got_ref.shape[0]
+    slots = got_ref.shape[0]
+    tails = dot(hot(as_column(slot_ref[...]) == iota((edges, slots), 1)), got_ref[...])
+    queries = take(0)[...]
     scores = dot_t1(queries, negatives) * factor
-    tails = dot(hot(as_column(slot_ref[...]) == iota((edges, slots), 1)), got_ref[...])
     positive = jnp.sum(queries.astype(F32) * tails, axis=1, keepdims=True) * factor
     row_max = jnp.maximum(positive, jnp.max(scores, axis=1, keepdims=True))
     exp_pos = jnp.exp(positive - row_max)
@@ -230,25 +234,14 @@
     total = exp_pos + jnp.sum(exp_neg, axis=1, keepdims=True)
     loss_ref[...] = as_row(jnp.log(total) + row_max - positive)
     pull = exp_pos / total - 1.0
-    weight_ref[...] = factor * pull
     prob = (exp_neg / total).astype(BF)
-    prob_ref[...] = prob
     grad = (factor * (pull * tails + dot(prob, negatives))).astype(BF)
     grad_ref[...] = grad
-    rel = as_column(rel_ref[...])
-    operator_terms(picks_ref, 0, rows_ref, rel, grad, away_ref)
-    operator_terms(picks_ref, 4, rows_ref, rel, grad, keep_ref)
-
-
-def back_kernel(factor, weight_ref, prob_ref, query_ref, slot_ref, back_ref):
-    queries = query_ref[...]
-    edges = queries.shape[0]
     parts = back_ref.shape[0]
-    slots = 2 * edges
     cap = slots // parts
-    weighted = (weight_ref[...] * queries.astype(F32)).astype(BF)
+    weighted = (factor * pull * queries.astype(F32)).astype(BF)
     rows = dot(hot(iota((slots, edges), 0) == slot_ref[...]), weighted).astype(BF)
-    negs = factor * dot_t0(prob_ref[...], queries)
+    negs = factor * dot_t0(prob, queries)
     share = negs.shape[0] // parts // 4
     for index in range(parts):
         back_ref[index, :cap] = rows[index * cap : (index + 1) * cap]
@@ -259,10 +252,19 @@
         back_ref[index, cap:] = jnp.concatenate(pieces, axis=0).astype(BF)
 
 
+def terms_kernel(special, grad_ref, take, away_ref, keep_ref):
+    grad = grad_ref[...]
+    rel = as_column(take(1)[...])
+    rows_ref = take(0)
+    operator_terms(special, 0, rows_ref, rel, grad, away_ref)
+    operator_terms(special, 4, rows_ref, rel, grad, keep_ref)
+
+
 def pair_kernel(keep_ref, got_ref, own_ref, sent_ref):
     half = own_ref.shape[0] // 2
     for place in range(4):
-        term = keep_ref[place].astype(F32) + got_ref[place].astype(F32)
+        at = slice(place * half, (place + 1) * half)
+        term = keep_ref[at].astype(F32) + got_ref[at].astype(F32)
         if place < 2:
             own_ref[place * half : (place + 1) * half] = term
         else:
@@ -286,10 +288,10 @@
     out_ref[:edges], out_ref[edges:] = split(total)
 
 
-def spread_kernel(place_ref, own_ref, got_ref, *out_refs):
+def spread_kernel(own_ref, got_ref, *out_refs):
     size = out_refs[0].shape[0]
     for turn, out_ref in enumerate(out_refs):
-        rows = pl.ds(pl.multiple_of((place_ref[1] ^ turn) * size, size), size)
+        rows = pl.ds(pl.multiple_of(((lax.axis_index("dom") >> 1) ^ turn) * size, size), size)
         total = own_ref[rows, :] + got_ref[rows, :].astype(F32)
         out_ref[...] = total.astype(out_ref.dtype)
 
@@ -300,18 +302,24 @@
     out_ref[...] = total.astype(BF)
 
 
-def place_operators(picks_ref, place_ref, indices, sources, out_ref, wide, sems):
+def stack_kernel(*refs):
+    size = refs[0].shape[0]
+    for index, ref in enumerate(refs[:-1]):
+        refs[-1][index * size : (index + 1) * size] = ref[...]
+
+
+def place_operators(indices, sources, out_ref, wide, sems):
     width = sources[0].shape[0]
     size = width // 4
     copies = []
     for slot, (index, source) in enumerate(zip(indices, sources)):
         wide[slot] = source[...].astype(F32)
-        pick = 2 * ((index + 4) % 8)
+        relation, part = quarter_of(True, (index + 4) % 8)
         for turn in range(4):
-            at = picks_ref[pick + 1] * width + (place_ref[1] ^ turn) * size
+            at = part * width + ((lax.axis_index("dom") >> 1) ^ turn) * size
             copy = pltpu.make_async_copy(
                 wide.at[slot, pl.ds(turn * size, size)],
-                out_ref.at[picks_ref[pick], pl.ds(pl.multiple_of(at, size), size)],
+                out_ref.at[relation, pl.ds(pl.multiple_of(at, size), size)],
                 sems.at[slot, turn],
             )
             copy.start()
@@ -319,31 +327,36 @@
     return copies
 
 
-def operator_kernel(indices, picks_ref, place_ref, *refs):
+def operator_kernel(indices, *refs):
     sources, (out_ref, wide, sems) = refs[:-3], refs[-3:]
-    for copy in place_operators(picks_ref, place_ref, indices, sources, out_ref, wide, sems):
+    for copy in place_operators(indices, sources, out_ref, wide, sems):
         copy.wait()
 
 
-def add_kernel(base_ref, ids_ref, neg_ref, head_ref, grads_ref, back_ref, out_ref):
-    count = out_ref.shape[0]
-    base = base_ref[0]
-
-    def pick(row):
-        return hot((iota((count, row.shape[1]), 0) + base) == row)
-
-    heads = pick(head_ref[...])
-    total = dot(jnp.concatenate([heads, heads], axis=1), grads_ref[...])
+def add_kernel(halves, ids_ref, neg_ref, back_ref, take, *out_refs):
     parts = back_ref.shape[0]
     cap = ids_ref.shape[1] // parts
     tails = jnp.concatenate([back_ref[index, :cap] for index in range(parts)], axis=0)
-    total = total + dot(pick(ids_ref[...]), tails)
     negs = back_ref[0, cap:].astype(F32)
     for index in range(1, parts):
         negs = negs + back_ref[index, cap:].astype(F32)
-    own = pick(neg_ref[...])
     high, low = split(negs)
-    out_ref[...] = (total + (dot(own, high) + dot(own, low))).astype(out_ref.dtype)
+    negs = jnp.concatenate([high, low], axis=0)
+    head = take(0)[...]
+    grads = take(1)
+    for turn, out_ref in enumerate(out_refs):
+        count = out_ref.shape[0]
+        base = (lax.axis_index("rep") % 2 ^ (1 - turn)) * count if halves else 0
+
+        def pick(row):
+            return hot((iota((count, row.shape[1]), 0) + base) == row)
+
+        total = dot(pick(ids_ref[...]), tails)
+        heads = pick(head)
+        total = total + dot(jnp.concatenate([heads, heads], axis=1), grads[...])
+        own = pick(neg_ref[...])
+        total = total + dot(jnp.concatenate([own, own], axis=1), negs)
+        out_ref[...] = total.astype(out_ref.dtype)
 
 
 def both_kernel(kept_ref, arrived_ref, out_ref):
@@ -351,12 +364,12 @@
 
 
 def join_kernel(
-    indices, picks_ref, place_ref, mine_ref, other_ref, over_ref, far_ref, *refs
+    indices, mine_ref, other_ref, over_ref, far_ref, *refs
 ):
     sources, rest = refs[: len(indices)], refs[len(indices) :]
     _, out_ref, operators_ref, wide, sems, operators_wide, operators_sems = rest
     half = mine_ref.shape[0]
-    core = place_ref[2]
+    core = lax.axis_index("rep") & 1
     copies = []
     for index, (first, second, at) in enumerate(
         ((mine_ref, over_ref, core), (other_ref, far_ref, 1 - core))
@@ -370,7 +383,7 @@
         copy.start()
         copies.append(copy)
     copies += place_operators(
-        picks_ref, place_ref, indices, sources, operators_ref, operators_wide, operators_sems
+        indices, sources, operators_ref, operators_wide, operators_sems
     )
     for copy in copies:
         copy.wait()
@@ -399,18 +412,6 @@
     count = relations.shape[0]
     head = head_local.reshape(1, edges)
     rel = rel_ids.reshape(1, edges)
-    dom = lax.axis_index("dom")
-    rep = lax.axis_index("rep")
-    z, x, y, core = dom // 2, dom % 2, rep // 2, rep % 2
-    place = jnp.stack([rep, z, core])
-    if special:
-        quarters = [(2 * y + x) ^ k for k in range(4)]
-        order = [(2 * (1 - core) + q // 2, q % 2) for q in quarters]
-        order = order + [(2 * core + q // 2, q % 2) for q in quarters]
-    else:
-        order = [(k // 2, k % 2) for k in range(2 * count)]
-    picks = jnp.stack([jnp.asarray(v, I32) for pair in order for v in pair])
-
     slot, neg_own, request = call(
         functools.partial(slots_kernel, parts, cap),
         [((1, edges), I32), ((1, neg_dev), I32), ((parts, share, columns + 128), BF)],
@@ -445,50 +446,55 @@
     got = exchange(found.reshape(parts, cap, columns)).reshape(slots, columns)
     neg_core, neg_across, neg_both = [flip(neg_near, "rep", reps, k) for k in (1, 2, 3)]
 
-    terms = ((4, columns // 2, columns), BF if special else F32)
-    loss, weight, prob, grad, away, keep = call(
+    loss, grad, back = call(
         functools.partial(edge_kernel, factor),
         [
             ((1, edges), F32),
-            ((edges, 1), F32),
-            ((edges, negs), BF),
             ((edges, columns), BF),
-            terms,
-            terms,
+            ((parts, cap + neg_dev, columns), BF),
         ],
-        (picks,),
-        (slot, neg_near, neg_core, neg_across, neg_both, queries, got, rows, rel),
-    )
-    (head_grads,) = call(
-        head_kernel, [((2 * edges, columns), BF)], (), (grad, rel, relations), cost=4
-    )
-
-    def give_back(after):
-        (back,) = call(
-            functools.partial(back_kernel, factor),
-            [((parts, cap + neg_dev, columns), BF)],
+        (),
+        (slot, neg_near, neg_core, neg_across, neg_both, got),
+        (queries,),
+    )
+    returned = exchange(back)
+    kind = BF if special else F32
+    away, keep = call(
+        functools.partial(terms_kernel, special),
+        [((2 * columns, columns), kind), ((2 * columns, columns), kind)],
+        (),
+        (grad,),
+        (rows, rel),
+        (back,),
+    )
+
+    def head_terms(after):
+        return call(
+            head_kernel,
+            [((2 * edges, columns), BF)],
             (),
-            (weight, prob, queries, slot),
+            (grad, rel, relations),
             (),
             after,
+            cost=0,
+        )[0]
+
+    def add(outs, after):
+        return call(
+            functools.partial(add_kernel, special),
+            outs,
+            (),
+            (asked, neg_own, returned),
+            (head, head_grads),
+            after,
         )
-        return back, exchange(back)
-
-    def add(base, size, kind, returned, after):
-        return call(
-            add_kernel,
-            [((size, columns), kind)],
-            (base.reshape(1),),
-            (asked, neg_own, head, head_grads, returned),
-            (),
-            after,
-            cost=5,
-        )[0]
 
     if not special:
-        whole = jnp.concatenate([away, keep], axis=0).reshape(count, columns, columns)
-        back, returned = give_back(())
-        entity_grad = lax.psum(add(jnp.zeros((), I32), ent_dev, F32, returned, ()), "rep")
+        whole = jnp.concatenate([away, keep], axis=0)
+        whole = whole.reshape(count, columns, columns)
+        head_grads = head_terms(())
+        (added,) = add([((ent_dev, columns), F32)], ())
+        entity_grad = lax.psum(added, "rep")
         return entity_grad, lax.psum(whole, ("dom", "rep")), loss.reshape(edges)
 
     half, quarter = columns // 2, columns // 8
@@ -507,36 +513,37 @@
         [((columns, columns), F32), ((columns, columns), BF)],
         (),
         (keep, over_core(away)),
-        (),
-        (head_grads,),
-    )
-    met = over_y(sent)
-    back, returned = give_back((sent,))
+    )
     own, sent = call(
         middle_kernel,
         [((half, columns), F32), ((half, columns), BF)],
         (),
-        (own, met),
-        (),
-        (back,),
-        cost=15,
-    )
+        (own, over_y(sent)),
+        cost=0,
+    )
+    head_grads = head_terms((sent,))
     own, *sent = call(
         spread_kernel,
         [((quarter, columns), F32)] + [((quarter, columns), BF)] * 3,
-        (place,),
+        (),
         (own, over_x(sent)),
-        cost=15,
+        (),
+        (head_grads,),
+        cost=0,
     )
     met = [flip(v, "dom", 8, 2 * (k + 1)) for k, v in enumerate(sent)]
-    (own,) = call(sum_kernel, [((quarter, columns), BF)], (), (own, *met), cost=15)
+    rows_half = ent_dev // 2
+    leaving, kept = add(
+        [((rows_half, columns), BF), ((rows_half, columns), F32)], tuple(met)
+    )
+    arrived = over_core(leaving)
+    (own,) = call(
+        sum_kernel, [((quarter, columns), BF)], (), (own, *met), cost=0
+    )
     stripes = [own] + [flip(own, "dom", 8, 2 * (k + 1)) for k in range(3)]
-    whole = jnp.concatenate(stripes, axis=0)
-
-    rows_half = ent_dev // 2
-    leaving = add((1 - core) * rows_half, rows_half, BF, returned, (own,))
-    arrived = over_core(leaving)
-    kept = add(core * rows_half, rows_half, F32, returned, (leaving,))
+    (whole,) = call(
+        stack_kernel, [((half, columns), BF)], (), stripes, cost=0
+    )
     (both,) = call(both_kernel, [((rows_half, columns), BF)], (), (kept, arrived))
     across = over_y(both)
 
@@ -550,18 +557,18 @@
     relation_grad = pl.pallas_call(
         functools.partial(operator_kernel, early),
         out_shape=shape,
-        in_specs=[SMEM] * 2 + [VMEM] * len(early),
+        in_specs=[VMEM] * len(early),
         out_specs=FAR,
         scratch_shapes=[
             pltpu.VMEM((len(early), half, columns), F32),
             pltpu.SemaphoreType.DMA((len(early), 4)),
         ],
         compiler_params=limit,
-    )(picks, place, *[quarters[k] for k in early])
+    )(*[quarters[k] for k in early])
     entity_grad, relation_grad = pl.pallas_call(
         functools.partial(join_kernel, late),
         out_shape=[jax.ShapeDtypeStruct((ent_dev, columns), F32), shape],
-        in_specs=[SMEM] * 2 + [VMEM] * (4 + len(late)) + [FAR],
+        in_specs=[VMEM] * (4 + len(late)) + [FAR],
         out_specs=[FAR, FAR],
         scratch_shapes=[
             pltpu.VMEM((2, rows_half, columns), F32),
@@ -569,11 +576,9 @@
             pltpu.VMEM((len(late), half, columns), F32),
             pltpu.SemaphoreType.DMA((len(late), 4)),
         ],
-        input_output_aliases={6 + len(late): 1},
+        input_output_aliases={4 + len(late): 1},
         compiler_params=limit,
     )(
-        picks,
-        place,
         both,
         over_core(both),
         across,

time: 144 us -> 134 us (0.931)
  local copies, waits for them, and re-layouts: 10.6 us -> 1.08 us
  starting transfers between devices: 33.2 us -> 38.3 us
  waiting for transfers between devices: 73 us -> 69.4 us
    unnamed x32 -> x18, local copies, waits for them, and re-layouts: 10.5 us -> 1.08 us
    ppermute x23, starting transfers between devices: 18.4 us -> 23.7 us  [flip(): return lax.ppermute(x, axis, [(i, i ^ bit) for i in range(size)])]
    ppermute x23, waiting for transfers between devices: 50.9 us -> 47.4 us  [flip(): return lax.ppermute(x, axis, [(i, i ^ bit) for i in range(size)])]
where the time goes in v7:
time: 134 us
  waiting for transfers between devices  69.4 us (52%)
  starting transfers between devices  38.3 us (29%)
  Pallas kernels  24.1 us (18%)
    ppermute x23, waiting for transfers between devices, flip(): return lax.ppermute(x, axis, [(i, i ^ bit) for i in range(size)])  47.4 us
    ppermute x23, starting transfers between devices, flip(): return lax.ppermute(x, axis, [(i, i ^ bit) for i in range(size)])  23.7 us
    all_to_all x3, waiting for transfers between devices, exchange(): return lax.all_to_all(x, 'dom', split_axis=0, concat_axis=0, tiled=True)  22 us
    pallas_call x13, Pallas kernels, call(): pl.pallas_call(kernel, out_shape=[jax.ShapeDtypeStruct(out[0], out[1]) fo...  20.4 us
    all_to_all x3, starting transfers between devices, exchange(): return lax.all_to_all(x, 'dom', split_axis=0, concat_axis=0, tiled=True)  14.6 us
  transfers between devices with their start and end apart: 26, of which 14 were waited for; matrix products, arithmetic and copies ran while one was open for 0% of the time, Pallas kernels for 8%

profile of v7, /device:TPU:0, one launch (start us, length us, event | category | flops | bytes accessed | tf_op | source)
XLA Modules:
  0.0 133.9 jit_solution(7145094044826583145)
XLA Ops:
  0.6 0.0 copy-start
  0.6 2.7 %shard_map.94 = (s32[1,512]{1,0:T(1,128)}, s32[1,32]{1,0:T(1,128)}, bf16[8,8,640]{2,1,0:T(8,128)(2,1)}) custom-call(s32[1,512]{1,0:T(1,128)} %bitcast.14, s32[1,512]{1,0:T(1,128)} %bitcast.15, s32[1,32]{1,0:T(1,128)} %bitcast.16, bf16[1024,512]{1,0:T(8,128)(2,1)} %refs_1_.1), custom_call_target="tpu_custom_call" | custom-call | flops 1 | bytes 1 | tf_op jit(solution)/shard_map/pallas_call | solution.py:60
  3.3 7.3 %all-to-all-start = ((bf16[8,8,640]{2,1,0:T(8,128)(2,1)}), bf16[8,8,640]{2,1,0:T(8,128)(2,1)S(1)}, u32[]{:S(2)}, u32[]{:S(2)}) async-start(bf16[8,8,640]{2,1,0:T(8,128)(2,1)} %get-tuple-element.28), calls=%async_computation | async-start | bytes 163840 | tf_op jit(solution)/shard_map/all_to_all | solution.py:397
  10.6 4.4 %shard_map.95 = (bf16[512,512]{1,0:T(8,128)(2,1)}, bf16[512,512]{1,0:T(8,128)(2,1)}) custom-call(s32[1,512]{1,0:T(1,128)} %bitcast.12, s32[1,512]{1,0:T(1,128)} %bitcast.9, bf16[1024,512]{1,0:T(8,128)(2,1)} %refs_1_.1, bf16[4,512,512]{2,1,0:T(8,128)(2,1)} %refs_2_.3, s32[1,512]{1,0:T(1,128)} %get-tuple-element.29.refs_4_.refs_0_), custom_call_target="tpu_custom_call" | custom-call | flops 1 | bytes 1 | tf_op jit(solution)/shard_map/pallas_call | solution.py:60
  15.0 2.6 %all-to-all-done.refs_0_ = bf16[8,8,640]{2,1,0:T(8,128)(2,1)S(1)} async-done(((bf16[8,8,640]{2,1,0:T(8,128)(2,1)}), bf16[8,8,640]{2,1,0:T(8,128)(2,1)S(1)}, u32[]{:S(2)}, u32[]{:S(2)}) %all-to-all-start) | async-done | bytes 81952 | tf_op jit(solution)/shard_map/all_to_all | solution.py:397
  17.6 1.0 copy-done.2
  18.7 2.6 %shard_map.96 = (s32[1,1024]{1,0:T(1,128)S(1)}, bf16[1024,512]{1,0:T(8,128)(2,1)}, bf16[64,512]{1,0:T(8,128)(2,1)S(1)}) custom-call(bf16[8,8,640]{2,1,0:T(8,128)(2,1)S(1)} %all-to-all-done.refs_0_, bf16[1024,512]{1,0:T(8,128)(2,1)S(1)} %copy-done, bf16[512,512]{1,0:T(8,128)(2,1)S(1)} %copy-done.2), custom_call_target="tpu_custom_call" | custom-call | flops 1 | bytes 1 | tf_op jit(solution)/shard_map/pallas_call | solution.py:60
  21.3 3.6 %all-to-all-start.1 = ((bf16[8,128,512]{2,1,0:T(8,128)(2,1)}), bf16[8,128,512]{2,1,0:T(8,128)(2,1)S(1)}, u32[]{:S(2)}, u32[]{:S(2)}) async-start(bf16[8,128,512]{2,1,0:T(8,128)(2,1)} %bitcast.5), calls=%async_computation.1 | async-start | bytes 2097152 | tf_op jit(solution)/shard_map/all_to_all | solution.py:397
  24.9 0.1 collective-permute-start.2
  24.9 1.6 %collective-permute-start.1 = (bf16[64,512]{1,0:T(8,128)(2,1)S(1)}, bf16[64,512]{1,0:T(8,128)(2,1)S(1)}, u32[]{:S(2)}, u32[]{:S(2)}) collective-permute-start(bf16[64,512]{1,0:T(8,128)(2,1)S(1)} %get-tuple-element.33.refs_1_), channel_id=1, source_target_pairs={{0,2},{1,3},{2,0},{3,1},{4,6},{5,7},{6,4},{7,5},{8,10},{9,11},{10,... | collective-permute-start | bytes 196616 | tf_op jit(solution)/shard_map/ppermute | solution.py:393
  26.5 0.3 collective-permute-start
  26.8 2.4 %collective-permute-done.2.refs_4_ = bf16[64,512]{1,0:T(8,128)(2,1)S(1)} collective-permute-done((bf16[64,512]{1,0:T(8,128)(2,1)S(1)}, bf16[64,512]{1,0:T(8,128)(2,1)S(1)}, u32[]{:S(2)}, u32[]{:S(2)}) %collective-permute-start.2) | collective-permute-done | bytes 65568 | tf_op jit(solution)/shard_map/ppermute | solution.py:393
  29.2 1.5 %collective-permute-done.1.refs_3_ = bf16[64,512]{1,0:T(8,128)(2,1)S(1)} collective-permute-done((bf16[64,512]{1,0:T(8,128)(2,1)S(1)}, bf16[64,512]{1,0:T(8,128)(2,1)S(1)}, u32[]{:S(2)}, u32[]{:S(2)}) %collective-permute-start.1) | collective-permute-done | bytes 65568 | tf_op jit(solution)/shard_map/ppermute | solution.py:393
  30.7 0.0 collective-permute-done.refs_2_
  30.7 19.5 %all-to-all-done.1 = bf16[8,128,512]{2,1,0:T(8,128)(2,1)S(1)} async-done(((bf16[8,128,512]{2,1,0:T(8,128)(2,1)}), bf16[8,128,512]{2,1,0:T(8,128)(2,1)S(1)}, u32[]{:S(2)}, u32[]{:S(2)}) %all-to-all-start.1) | async-done | bytes 1048608 | tf_op jit(solution)/shard_map/all_to_all | solution.py:397
  50.2 4.0 %shard_map.97 = (f32[1,512]{1,0:T(1,128)}, bf16[512,512]{1,0:T(8,128)(2,1)S(1)}, bf16[8,160,512]{2,1,0:T(8,128)(2,1)}) custom-call(s32[1,512]{1,0:T(1,128)S(1)} %copy-done.7, bf16[64,512]{1,0:T(8,128)(2,1)S(1)} %get-tuple-element.33.refs_1_, bf16[64,512]{1,0:T(8,128)(2,1)S(1)} %collective-permute-done.refs_2_, ...), custom_call_target="tpu_custom_call" | custom-call | flops 1 | bytes 1 | tf_op jit(solution)/shard_map/pallas_call | solution.py:60
  54.2 3.8 %all-to-all-start.2 = ((bf16[8,160,512]{2,1,0:T(8,128)(2,1)}), bf16[8,160,512]{2,1,0:T(8,128)(2,1)S(1)}, u32[]{:S(2)}, u32[]{:S(2)}) async-start(bf16[8,160,512]{2,1,0:T(8,128)(2,1)} %get-tuple-element.36.refs_3_), calls=%async_computation.2 | async-start | bytes 2621440 | tf_op jit(solution)/shard_map/all_to_all | solution.py:397
  57.9 1.9 %shard_map.98 = (bf16[1024,512]{1,0:T(8,128)(2,1)S(1)}, bf16[1024,512]{1,0:T(8,128)(2,1)S(1)}) custom-call(bf16[512,512]{1,0:T(8,128)(2,1)S(1)} %get-tuple-element.37.refs_0_, bf16[512,512]{1,0:T(8,128)(2,1)S(1)} %copy-done.3, s32[1,512]{1,0:T(1,128)S(1)} %bitcast.10, bf16[8,160,512]{2,1,0:T(8,128)(2,1)} %get-tuple-element.36.refs_3_), custom_call_target="tpu_custom_call" | custom-call | flops 1 | bytes 1 | tf_op jit(solution)/shard_map/pallas_call | solution.py:60
  59.8 0.0 copy-start.1
  59.8 0.1 collective-permute-start.3
  59.9 2.6 %collective-permute-done.3.refs_1_ = bf16[1024,512]{1,0:T(8,128)(2,1)S(1)} collective-permute-done((bf16[1024,512]{1,0:T(8,128)(2,1)S(1)}, bf16[1024,512]{1,0:T(8,128)(2,1)S(1)}, u32[]{:S(2)}, u32[]{:S(2)}) %collective-permute-start.3) | collective-permute-done | bytes 1048608 | tf_op jit(solution)/shard_map/ppermute | solution.py:393
  62.5 0.2 shard_map.99
  62.8 1.6 %collective-permute-start.4 = (bf16[512,512]{1,0:T(8,128)(2,1)S(1)}, bf16[512,512]{1,0:T(8,128)(2,1)S(1)}, u32[]{:S(2)}, u32[]{:S(2)}) collective-permute-start(bf16[512,512]{1,0:T(8,128)(2,1)S(1)} %get-tuple-element.41), channel_id=1, source_target_pairs={{0,2},{1,3},{2,0},{3,1},{4,6},{5,7},{6,4},{7,5},{8,10},{9,11},{10,... | collective-permute-start | bytes 1572872 | tf_op jit(solution)/shard_map/ppermute | solution.py:393
  64.3 12.5 %collective-permute-done.4.refs_1_ = bf16[512,512]{1,0:T(8,128)(2,1)S(1)} collective-permute-done((bf16[512,512]{1,0:T(8,128)(2,1)S(1)}, bf16[512,512]{1,0:T(8,128)(2,1)S(1)}, u32[]{:S(2)}, u32[]{:S(2)}) %collective-permute-start.4) | collective-permute-done | bytes 524320 | tf_op jit(solution)/shard_map/ppermute | solution.py:393
  76.8 0.1 shard_map.100
  76.9 0.0 copy-start.6
  76.9 1.8 %collective-permute-start.5 = (bf16[256,512]{1,0:T(8,128)(2,1)S(1)}, bf16[256,512]{1,0:T(8,128)(2,1)S(1)}, u32[]{:S(2)}, u32[]{:S(2)}) collective-permute-start(bf16[256,512]{1,0:T(8,128)(2,1)S(1)} %get-tuple-element.42.refs_3_), channel_id=1, source_target_pairs={{0,4},{4,0},{8,12},{12,8},{16,20},{20,16},{24,28},{28,24},{1,5},{5... | collective-permute-start | bytes 786440 | tf_op jit(solution)/shard_map/ppermute | solution.py:393
  78.7 1.6 %shard_map.101.refs_2_.refs_4_ = bf16[1024,512]{1,0:T(8,128)(2,1)S(1)} custom-call(bf16[512,512]{1,0:T(8,128)(2,1)S(1)} %get-tuple-element.37.refs_0_, s32[1,512]{1,0:T(1,128)S(1)} %bitcast.11, bf16[4,512,512]{2,1,0:T(8,128)(2,1)S(1)} %copy-done.1, bf16[256,512]{1,0:T(8,128)(2,1)S(1)} %get-tuple-element.42.refs_3_), custom_call_target="tpu_custom_call" | custom-call | flops 1 | bytes 1 | tf_op jit(solution)/shard_map/pallas_call | solution.py:60
  80.3 5.8 %collective-permute-done.5.refs_1_ = bf16[256,512]{1,0:T(8,128)(2,1)S(1)} collective-permute-done((bf16[256,512]{1,0:T(8,128)(2,1)S(1)}, bf16[256,512]{1,0:T(8,128)(2,1)S(1)}, u32[]{:S(2)}, u32[]{:S(2)}) %collective-permute-start.5) | collective-permute-done | bytes 262176 | tf_op jit(solution)/shard_map/ppermute | solution.py:393
  86.1 2.7 %collective-permute-start.6 = (bf16[64,512]{1,0:T(8,128)(2,1)S(1)}, bf16[64,512]{1,0:T(8,128)(2,1)S(1)}, u32[]{:S(2)}, u32[]{:S(2)}) collective-permute-start(bf16[64,512]{1,0:T(8,128)(2,1)S(1)} %get-tuple-element.44), channel_id=1, source_target_pairs={{0,8},{4,12},{8,0},{12,4},{16,24},{20,28},{24,16},{28,20},{1,9},{5... | collective-permute-start | bytes 196616 | tf_op jit(solution)/shard_map/ppermute | solution.py:393
  88.8 2.3 %collective-permute-start.7 = (bf16[64,512]{1,0:T(8,128)(2,1)S(1)}, bf16[64,512]{1,0:T(8,128)(2,1)S(1)}, u32[]{:S(2)}, u32[]{:S(2)}) collective-permute-start(bf16[64,512]{1,0:T(8,128)(2,1)S(1)} %get-tuple-element.45), channel_id=1, source_target_pairs={{0,16},{4,20},{8,24},{12,28},{16,0},{20,4},{24,8},{28,12},{1,17},{... | collective-permute-start | bytes 196616 | tf_op jit(solution)/shard_map/ppermute | solution.py:393
  91.1 1.0 collective-permute-start.8
  92.1 0.0 collective-permute-done.6.refs_5_.refs_1_
  92.1 2.1 %collective-permute-done.7.refs_6_.refs_2_ = bf16[64,512]{1,0:T(8,128)(2,1)S(1)} collective-permute-done((bf16[64,512]{1,0:T(8,128)(2,1)S(1)}, bf16[64,512]{1,0:T(8,128)(2,1)S(1)}, u32[]{:S(2)}, u32[]{:S(2)}) %collective-permute-start.7) | collective-permute-done | bytes 65568 | tf_op jit(solution)/shard_map/ppermute | solution.py:393
  94.3 2.9 %collective-permute-done.8.refs_7_.refs_3_ = bf16[64,512]{1,0:T(8,128)(2,1)S(1)} collective-permute-done((bf16[64,512]{1,0:T(8,128)(2,1)S(1)}, bf16[64,512]{1,0:T(8,128)(2,1)S(1)}, u32[]{:S(2)}, u32[]{:S(2)}) %collective-permute-start.8) | collective-permute-done | bytes 65568 | tf_op jit(solution)/shard_map/ppermute | solution.py:393
  97.2 0.0 all-to-all-done.2.refs_2_
  97.2 2.8 %shard_map.103 = (bf16[512,512]{1,0:T(8,128)(2,1)S(1)}, f32[512,512]{1,0:T(8,128)S(1)}) custom-call(s32[1,1024]{1,0:T(1,128)S(1)} %get-tuple-element.31.refs_0_, s32[1,32]{1,0:T(1,128)S(1)} %copy-done.8, bf16[8,160,512]{2,1,0:T(8,128)(2,1)S(1)} %all-to-all-done.2.refs_2_, s32[1,512]{1,0:T(1,128)S(1)} %bitcast.13, ...), custom_call_target="tpu_custom_call" | custom-call | flops 1 | bytes 1 | tf_op jit(solution)/shard_map/pallas_call | solution.py:60
  100.0 0.1 collective-permute-start.9
  100.1 1.9 %collective-permute-done.9.refs_1_ = bf16[512,512]{1,0:T(8,128)(2,1)S(1)} collective-permute-done((bf16[512,512]{1,0:T(8,128)(2,1)S(1)}, bf16[512,512]{1,0:T(8,128)(2,1)S(1)}, u32[]{:S(2)}, u32[]{:S(2)}) %collective-permute-start.9) | collective-permute-done | bytes 524320 | tf_op jit(solution)/shard_map/ppermute | solution.py:393
  102.0 0.1 shard_map.104.mine_ref
  102.1 1.6 %collective-permute-start.11 = (bf16[512,512]{1,0:T(8,128)(2,1)S(1)}, bf16[512,512]{1,0:T(8,128)(2,1)S(1)}, u32[]{:S(2)}, u32[]{:S(2)}) collective-permute-start(bf16[512,512]{1,0:T(8,128)(2,1)S(1)} %shard_map.104.mine_ref), channel_id=1, source_target_pairs={{0,2},{1,3},{2,0},{3,1},{4,6},{5,7},{6,4},{7,5},{8,10},{9,11},{10,... | collective-permute-start | bytes 1572872 | tf_op jit(solution)/shard_map/ppermute | solution.py:393
  103.7 1.5 %collective-permute-start.15 = (bf16[64,512]{1,0:T(8,128)(2,1)S(1)}, bf16[64,512]{1,0:T(8,128)(2,1)S(1)}, u32[]{:S(2)}, u32[]{:S(2)}) collective-permute-start(bf16[64,512]{1,0:T(8,128)(2,1)S(1)} %shard_map.105.refs_0_), channel_id=1, source_target_pairs={{0,24},{4,28},{8,16},{12,20},{16,8},{20,12},{24,0},{28,4},{1,25},{... | collective-permute-start | bytes 196616 | tf_op jit(solution)/shard_map/ppermute | solution.py:393
  105.2 0.0 collective-permute-start.14
  105.2 2.9 %collective-permute-start.13 = (bf16[64,512]{1,0:T(8,128)(2,1)S(1)}, bf16[64,512]{1,0:T(8,128)(2,1)S(1)}, u32[]{:S(2)}, u32[]{:S(2)}) collective-permute-start(bf16[64,512]{1,0:T(8,128)(2,1)S(1)} %shard_map.105.refs_0_), channel_id=1, source_target_pairs={{0,8},{4,12},{8,0},{12,4},{16,24},{20,28},{24,16},{28,20},{1,9},{5... | collective-permute-start | bytes 196616 | tf_op jit(solution)/shard_map/ppermute | solution.py:393
  108.2 2.4 %collective-permute-done.15.refs_3_ = bf16[64,512]{1,0:T(8,128)(2,1)S(1)} collective-permute-done((bf16[64,512]{1,0:T(8,128)(2,1)S(1)}, bf16[64,512]{1,0:T(8,128)(2,1)S(1)}, u32[]{:S(2)}, u32[]{:S(2)}) %collective-permute-start.15) | collective-permute-done | bytes 65568 | tf_op jit(solution)/shard_map/ppermute | solution.py:393
  110.6 1.6 %collective-permute-done.14.refs_2_ = bf16[64,512]{1,0:T(8,128)(2,1)S(1)} collective-permute-done((bf16[64,512]{1,0:T(8,128)(2,1)S(1)}, bf16[64,512]{1,0:T(8,128)(2,1)S(1)}, u32[]{:S(2)}, u32[]{:S(2)}) %collective-permute-start.14) | collective-permute-done | bytes 65568 | tf_op jit(solution)/shard_map/ppermute | solution.py:393
  112.2 0.0 collective-permute-done.13.refs_1_
  112.3 0.6 collective-permute-start.16
  112.8 2.1 %collective-permute-start.19 = (bf16[256,512]{1,0:T(8,128)(2,1)S(1)}, bf16[256,512]{1,0:T(8,128)(2,1)S(1)}, u32[]{:S(2)}, u32[]{:S(2)}) collective-permute-start(bf16[256,512]{1,0:T(8,128)(2,1)S(1)} %shard_map.106.refs_0_), channel_id=1, source_target_pairs={{0,4},{4,0},{8,12},{12,8},{16,20},{20,16},{24,28},{28,24},{1,5},{5... | collective-permute-start | bytes 786440 | tf_op jit(solution)/shard_map/ppermute | solution.py:393
  115.0 0.0 collective-permute-start.20
  115.0 6.8 %collective-permute-done.16.refs_2_ = bf16[256,512]{1,0:T(8,128)(2,1)S(1)} collective-permute-done((bf16[256,512]{1,0:T(8,128)(2,1)S(1)}, bf16[256,512]{1,0:T(8,128)(2,1)S(1)}, u32[]{:S(2)}, u32[]{:S(2)}) %collective-permute-start.16) | collective-permute-done | bytes 262176 | tf_op jit(solution)/shard_map/ppermute | solution.py:393
  121.7 2.5 %collective-permute-start.17 = (bf16[256,512]{1,0:T(8,128)(2,1)S(1)}, bf16[256,512]{1,0:T(8,128)(2,1)S(1)}, u32[]{:S(2)}, u32[]{:S(2)}) collective-permute-start(bf16[256,512]{1,0:T(8,128)(2,1)S(1)} %collective-permute-done.16.refs_2_), channel_id=1, source_target_pairs={{0,4},{4,0},{8,12},{12,8},{16,20},{20,16},{24,28},{28,24},{1,5},{5... | collective-permute-start | bytes 786440 | tf_op jit(solution)/shard_map/ppermute | solution.py:393
  124.2 0.0 collective-permute-start.10
  124.2 0.0 collective-permute-done.11.over_ref
  124.2 0.5 collective-permute-start.12
  124.7 0.0 collective-permute-done.19.refs_1_
  124.7 0.1 collective-permute-start.21
  124.8 0.0 collective-permute-done.20.refs_3_
  124.8 0.4 collective-permute-start.22
  125.3 4.7 %collective-permute-done.17.refs_0_ = bf16[256,512]{1,0:T(8,128)(2,1)S(1)} collective-permute-done((bf16[256,512]{1,0:T(8,128)(2,1)S(1)}, bf16[256,512]{1,0:T(8,128)(2,1)S(1)}, u32[]{:S(2)}, u32[]{:S(2)}) %collective-permute-start.17) | collective-permute-done | bytes 262176 | tf_op jit(solution)/shard_map/ppermute | solution.py:393
  130.0 1.9 %shard_map.107.refs_2_ = f32[4,512,512]{2,1,0:T(8,128)} custom-call(bf16[256,512]{1,0:T(8,128)(2,1)S(1)} %shard_map.106.refs_0_, bf16[256,512]{1,0:T(8,128)(2,1)S(1)} %collective-permute-done.19.refs_1_, bf16[256,512]{1,0:T(8,128)(2,1)S(1)} %collective-permute-done.16.refs_2_, bf16[256,512]{1,0:T(8,128)(2,1)S(1)} %collective-permute-done.20.refs_3_, ...), custom_call_target="tpu_custom_call" | custom-call | tf_op jit(solution)/shard_map/pallas_call | solution.py:557
  131.9 0.0 collective-permute-done.18.refs_1_
  131.9 0.0 collective-permute-done.10.other_ref
  131.9 1.8 %shard_map.108 = (f32[1024,512]{1,0:T(8,128)}, f32[4,512,512]{2,1,0:T(8,128)}) custom-call(bf16[512,512]{1,0:T(8,128)(2,1)S(1)} %shard_map.104.mine_ref, bf16[512,512]{1,0:T(8,128)(2,1)S(1)} %collective-permute-done.10.other_ref, bf16[512,512]{1,0:T(8,128)(2,1)S(1)} %collective-permute-done.11.over_ref, ...), custom_call_target="tpu_custom_call", output_to_operand_aliasing={{1}: (6, {})} | custom-call | tf_op jit(solution)/shard_map/pallas_call | solution.py:568
  (21 shorter events, 0.1 us)
Async XLA Ops:
  0.6 17.0 %copy-start = (bf16[1024,512]{1,0:T(8,128)(2,1)S(1)}, bf16[1024,512]{1,0:T(8,128)(2,1)}, u32[]{:S(2)}) copy-start(bf16[1024,512]{1,0:T(8,128)(2,1)} %refs_1_.1) | copy-start | bytes 3145732
  3.3 14.3 %all-to-all-start = ((bf16[8,8,640]{2,1,0:T(8,128)(2,1)}), bf16[8,8,640]{2,1,0:T(8,128)(2,1)S(1)}, u32[]{:S(2)}, u32[]{:S(2)}) async-start(bf16[8,8,640]{2,1,0:T(8,128)(2,1)} %get-tuple-element.28), calls=%async_computation | async-start | bytes 163840 | tf_op jit(solution)/shard_map/all_to_all | solution.py:397
  10.6 39.6 %copy-start.7 = (s32[1,512]{1,0:T(1,128)S(1)}, s32[1,512]{1,0:T(1,128)}, u32[]{:S(2)}) copy-start(s32[1,512]{1,0:T(1,128)} %get-tuple-element.29.refs_4_.refs_0_) | copy-start | bytes 6148
  17.6 1.0 copy-start.2
  18.7 31.5 %copy-start.4 = (bf16[512,512]{1,0:T(8,128)(2,1)S(1)}, bf16[512,512]{1,0:T(8,128)(2,1)}, u32[]{:S(2)}) copy-start(bf16[512,512]{1,0:T(8,128)(2,1)} %get-tuple-element.35.refs_6_) | copy-start | bytes 1572868
  21.3 28.9 %all-to-all-start.1 = ((bf16[8,128,512]{2,1,0:T(8,128)(2,1)}), bf16[8,128,512]{2,1,0:T(8,128)(2,1)S(1)}, u32[]{:S(2)}, u32[]{:S(2)}) async-start(bf16[8,128,512]{2,1,0:T(8,128)(2,1)} %bitcast.5), calls=%async_computation.1 | async-start | bytes 2097152 | tf_op jit(solution)/shard_map/all_to_all | solution.py:397
  24.9 4.4 %collective-permute-start.2 = (bf16[64,512]{1,0:T(8,128)(2,1)S(1)}, bf16[64,512]{1,0:T(8,128)(2,1)S(1)}, u32[]{:S(2)}, u32[]{:S(2)}) collective-permute-start(bf16[64,512]{1,0:T(8,128)(2,1)S(1)} %get-tuple-element.33.refs_1_), channel_id=1, source_target_pairs={{0,3},{1,2},{2,1},{3,0},{4,7},{5,6},{6,5},{7,4},{8,11},{9,10},{10,... | collective-permute-start | bytes 196616 | tf_op jit(solution)/shard_map/ppermute | solution.py:393
  24.9 5.8 %collective-permute-start.1 = (bf16[64,512]{1,0:T(8,128)(2,1)S(1)}, bf16[64,512]{1,0:T(8,128)(2,1)S(1)}, u32[]{:S(2)}, u32[]{:S(2)}) collective-permute-start(bf16[64,512]{1,0:T(8,128)(2,1)S(1)} %get-tuple-element.33.refs_1_), channel_id=1, source_target_pairs={{0,2},{1,3},{2,0},{3,1},{4,6},{5,7},{6,4},{7,5},{8,10},{9,11},{10,... | collective-permute-start | bytes 196616 | tf_op jit(solution)/shard_map/ppermute | solution.py:393
  26.5 4.2 %collective-permute-start = (bf16[64,512]{1,0:T(8,128)(2,1)S(1)}, bf16[64,512]{1,0:T(8,128)(2,1)S(1)}, u32[]{:S(2)}, u32[]{:S(2)}) collective-permute-start(bf16[64,512]{1,0:T(8,128)(2,1)S(1)} %get-tuple-element.33.refs_1_), channel_id=1, source_target_pairs={{0,1},{1,0},{2,3},{3,2},{4,5},{5,4},{6,7},{7,6},{8,9},{9,8},{10,11... | collective-permute-start | bytes 196616 | tf_op jit(solution)/shard_map/ppermute | solution.py:393
  50.2 7.7 %copy-start.3 = (bf16[512,512]{1,0:T(8,128)(2,1)S(1)}, bf16[512,512]{1,0:T(8,128)(2,1)}, u32[]{:S(2)}) copy-start(bf16[512,512]{1,0:T(8,128)(2,1)} %get-tuple-element.30.refs_2_.refs_1_) | copy-start | bytes 1572868
  50.2 7.8 %copy-start.5 = (s32[512]{0:T(512)S(1)}, s32[512]{0:T(512)}, u32[]{:S(2)}) copy-start(s32[512]{0:T(512)} %param.10) | copy-start | bytes 6148
  54.2 43.1 %all-to-all-start.2 = ((bf16[8,160,512]{2,1,0:T(8,128)(2,1)}), bf16[8,160,512]{2,1,0:T(8,128)(2,1)S(1)}, u32[]{:S(2)}, u32[]{:S(2)}) async-start(bf16[8,160,512]{2,1,0:T(8,128)(2,1)} %get-tuple-element.36.refs_3_), calls=%async_computation.2 | async-start | bytes 2621440 | tf_op jit(solution)/shard_map/all_to_all | solution.py:397
  59.8 18.9 %copy-start.1 = (bf16[4,512,512]{2,1,0:T(8,128)(2,1)S(1)}, bf16[4,512,512]{2,1,0:T(8,128)(2,1)}, u32[]{:S(2)}) copy-start(bf16[4,512,512]{2,1,0:T(8,128)(2,1)} %refs_2_.3) | copy-start | bytes 6291460
  59.8 2.7 %collective-permute-start.3 = (bf16[1024,512]{1,0:T(8,128)(2,1)S(1)}, bf16[1024,512]{1,0:T(8,128)(2,1)S(1)}, u32[]{:S(2)}, u32[]{:S(2)}) collective-permute-start(bf16[1024,512]{1,0:T(8,128)(2,1)S(1)} %get-tuple-element.39), channel_id=1, source_target_pairs={{0,1},{1,0},{2,3},{3,2},{4,5},{5,4},{6,7},{7,6},{8,9},{9,8},{10,11... | collective-permute-start | bytes 3145736 | tf_op jit(solution)/shard_map/ppermute | solution.py:393
  62.8 14.0 %collective-permute-start.4 = (bf16[512,512]{1,0:T(8,128)(2,1)S(1)}, bf16[512,512]{1,0:T(8,128)(2,1)S(1)}, u32[]{:S(2)}, u32[]{:S(2)}) collective-permute-start(bf16[512,512]{1,0:T(8,128)(2,1)S(1)} %get-tuple-element.41), channel_id=1, source_target_pairs={{0,2},{1,3},{2,0},{3,1},{4,6},{5,7},{6,4},{7,5},{8,10},{9,11},{10,... | collective-permute-start | bytes 1572872 | tf_op jit(solution)/shard_map/ppermute | solution.py:393
  76.9 20.3 %copy-start.6 = (s32[512]{0:T(512)S(1)}, s32[512]{0:T(512)}, u32[]{:S(2)}) copy-start(s32[512]{0:T(512)} %param.9) | copy-start | bytes 6148
  76.9 20.3 %copy-start.8 = (s32[1,32]{1,0:T(1,128)S(1)}, s32[1,32]{1,0:T(1,128)}, u32[]{:S(2)}) copy-start(s32[1,32]{1,0:T(1,128)} %get-tuple-element.32.refs_1_) | copy-start | bytes 388
  76.9 9.2 %collective-permute-start.5 = (bf16[256,512]{1,0:T(8,128)(2,1)S(1)}, bf16[256,512]{1,0:T(8,128)(2,1)S(1)}, u32[]{:S(2)}, u32[]{:S(2)}) collective-permute-start(bf16[256,512]{1,0:T(8,128)(2,1)S(1)} %get-tuple-element.42.refs_3_), channel_id=1, source_target_pairs={{0,4},{4,0},{8,12},{12,8},{16,20},{20,16},{24,28},{28,24},{1,5},{5... | collective-permute-start | bytes 786440 | tf_op jit(solution)/shard_map/ppermute | solution.py:393
  86.1 6.0 %collective-permute-start.6 = (bf16[64,512]{1,0:T(8,128)(2,1)S(1)}, bf16[64,512]{1,0:T(8,128)(2,1)S(1)}, u32[]{:S(2)}, u32[]{:S(2)}) collective-permute-start(bf16[64,512]{1,0:T(8,128)(2,1)S(1)} %get-tuple-element.44), channel_id=1, source_target_pairs={{0,8},{4,12},{8,0},{12,4},{16,24},{20,28},{24,16},{28,20},{1,9},{5... | collective-permute-start | bytes 196616 | tf_op jit(solution)/shard_map/ppermute | solution.py:393
  88.8 5.5 %collective-permute-start.7 = (bf16[64,512]{1,0:T(8,128)(2,1)S(1)}, bf16[64,512]{1,0:T(8,128)(2,1)S(1)}, u32[]{:S(2)}, u32[]{:S(2)}) collective-permute-start(bf16[64,512]{1,0:T(8,128)(2,1)S(1)} %get-tuple-element.45), channel_id=1, source_target_pairs={{0,16},{4,20},{8,24},{12,28},{16,0},{20,4},{24,8},{28,12},{1,17},{... | collective-permute-start | bytes 196616 | tf_op jit(solution)/shard_map/ppermute | solution.py:393
  91.1 6.1 %collective-permute-start.8 = (bf16[64,512]{1,0:T(8,128)(2,1)S(1)}, bf16[64,512]{1,0:T(8,128)(2,1)S(1)}, u32[]{:S(2)}, u32[]{:S(2)}) collective-permute-start(bf16[64,512]{1,0:T(8,128)(2,1)S(1)} %get-tuple-element.46), channel_id=1, source_target_pairs={{0,24},{4,28},{8,16},{12,20},{16,8},{20,12},{24,0},{28,4},{1,25},{... | collective-permute-start | bytes 196616 | tf_op jit(solution)/shard_map/ppermute | solution.py:393
  100.0 2.0 %collective-permute-start.9 = (bf16[512,512]{1,0:T(8,128)(2,1)S(1)}, bf16[512,512]{1,0:T(8,128)(2,1)S(1)}, u32[]{:S(2)}, u32[]{:S(2)}) collective-permute-start(bf16[512,512]{1,0:T(8,128)(2,1)S(1)} %get-tuple-element.48), channel_id=1, source_target_pairs={{0,1},{1,0},{2,3},{3,2},{4,5},{5,4},{6,7},{7,6},{8,9},{9,8},{10,11... | collective-permute-start | bytes 1572872 | tf_op jit(solution)/shard_map/ppermute | solution.py:393
  102.1 22.1 %collective-permute-start.11 = (bf16[512,512]{1,0:T(8,128)(2,1)S(1)}, bf16[512,512]{1,0:T(8,128)(2,1)S(1)}, u32[]{:S(2)}, u32[]{:S(2)}) collective-permute-start(bf16[512,512]{1,0:T(8,128)(2,1)S(1)} %shard_map.104.mine_ref), channel_id=1, source_target_pairs={{0,2},{1,3},{2,0},{3,1},{4,6},{5,7},{6,4},{7,5},{8,10},{9,11},{10,... | collective-permute-start | bytes 1572872 | tf_op jit(solution)/shard_map/ppermute | solution.py:393
  103.7 6.9 %collective-permute-start.15 = (bf16[64,512]{1,0:T(8,128)(2,1)S(1)}, bf16[64,512]{1,0:T(8,128)(2,1)S(1)}, u32[]{:S(2)}, u32[]{:S(2)}) collective-permute-start(bf16[64,512]{1,0:T(8,128)(2,1)S(1)} %shard_map.105.refs_0_), channel_id=1, source_target_pairs={{0,24},{4,28},{8,16},{12,20},{16,8},{20,12},{24,0},{28,4},{1,25},{... | collective-permute-start | bytes 196616 | tf_op jit(solution)/shard_map/ppermute | solution.py:393
  105.2 7.0 %collective-permute-start.14 = (bf16[64,512]{1,0:T(8,128)(2,1)S(1)}, bf16[64,512]{1,0:T(8,128)(2,1)S(1)}, u32[]{:S(2)}, u32[]{:S(2)}) collective-permute-start(bf16[64,512]{1,0:T(8,128)(2,1)S(1)} %shard_map.105.refs_0_), channel_id=1, source_target_pairs={{0,16},{4,20},{8,24},{12,28},{16,0},{20,4},{24,8},{28,12},{1,17},{... | collective-permute-start | bytes 196616 | tf_op jit(solution)/shard_map/ppermute | solution.py:393
  105.2 7.0 %collective-permute-start.13 = (bf16[64,512]{1,0:T(8,128)(2,1)S(1)}, bf16[64,512]{1,0:T(8,128)(2,1)S(1)}, u32[]{:S(2)}, u32[]{:S(2)}) collective-permute-start(bf16[64,512]{1,0:T(8,128)(2,1)S(1)} %shard_map.105.refs_0_), channel_id=1, source_target_pairs={{0,8},{4,12},{8,0},{12,4},{16,24},{20,28},{24,16},{28,20},{1,9},{5... | collective-permute-start | bytes 196616 | tf_op jit(solution)/shard_map/ppermute | solution.py:393
  112.3 9.5 %collective-permute-start.16 = (bf16[256,512]{1,0:T(8,128)(2,1)S(1)}, bf16[256,512]{1,0:T(8,128)(2,1)S(1)}, u32[]{:S(2)}, u32[]{:S(2)}) collective-permute-start(bf16[256,512]{1,0:T(8,128)(2,1)S(1)} %shard_map.106.refs_0_), channel_id=1, source_target_pairs={{0,2},{1,3},{2,0},{3,1},{4,6},{5,7},{6,4},{7,5},{8,10},{9,11},{10,... | collective-permute-start | bytes 786440 | tf_op jit(solution)/shard_map/ppermute | solution.py:393
  112.8 11.9 %collective-permute-start.19 = (bf16[256,512]{1,0:T(8,128)(2,1)S(1)}, bf16[256,512]{1,0:T(8,128)(2,1)S(1)}, u32[]{:S(2)}, u32[]{:S(2)}) collective-permute-start(bf16[256,512]{1,0:T(8,128)(2,1)S(1)} %shard_map.106.refs_0_), channel_id=1, source_target_pairs={{0,4},{4,0},{8,12},{12,8},{16,20},{20,16},{24,28},{28,24},{1,5},{5... | collective-permute-start | bytes 786440 | tf_op jit(solution)/shard_map/ppermute | solution.py:393
  115.0 9.9 %collective-permute-start.20 = (bf16[256,512]{1,0:T(8,128)(2,1)S(1)}, bf16[256,512]{1,0:T(8,128)(2,1)S(1)}, u32[]{:S(2)}, u32[]{:S(2)}) collective-permute-start(bf16[256,512]{1,0:T(8,128)(2,1)S(1)} %shard_map.106.refs_0_), channel_id=1, source_target_pairs={{0,1},{1,0},{2,3},{3,2},{4,5},{5,4},{6,7},{7,6},{8,9},{9,8},{10,11... | collective-permute-start | bytes 786440 | tf_op jit(solution)/shard_map/ppermute | solution.py:393
  121.7 8.3 %collective-permute-start.17 = (bf16[256,512]{1,0:T(8,128)(2,1)S(1)}, bf16[256,512]{1,0:T(8,128)(2,1)S(1)}, u32[]{:S(2)}, u32[]{:S(2)}) collective-permute-start(bf16[256,512]{1,0:T(8,128)(2,1)S(1)} %collective-permute-done.16.refs_2_), channel_id=1, source_target_pairs={{0,4},{4,0},{8,12},{12,8},{16,20},{20,16},{24,28},{28,24},{1,5},{5... | collective-permute-start | bytes 786440 | tf_op jit(solution)/shard_map/ppermute | solution.py:393
  124.2 7.7 %collective-permute-start.10 = (bf16[512,512]{1,0:T(8,128)(2,1)S(1)}, bf16[512,512]{1,0:T(8,128)(2,1)S(1)}, u32[]{:S(2)}, u32[]{:S(2)}) collective-permute-start(bf16[512,512]{1,0:T(8,128)(2,1)S(1)} %shard_map.104.mine_ref), channel_id=1, source_target_pairs={{0,1},{1,0},{2,3},{3,2},{4,5},{5,4},{6,7},{7,6},{8,9},{9,8},{10,11... | collective-permute-start | bytes 1572872 | tf_op jit(solution)/shard_map/ppermute | solution.py:393
  124.2 7.7 %collective-permute-start.12 = (bf16[512,512]{1,0:T(8,128)(2,1)S(1)}, bf16[512,512]{1,0:T(8,128)(2,1)S(1)}, u32[]{:S(2)}, u32[]{:S(2)}) collective-permute-start(bf16[512,512]{1,0:T(8,128)(2,1)S(1)} %collective-permute-done.11.over_ref), channel_id=1, source_target_pairs={{0,1},{1,0},{2,3},{3,2},{4,5},{5,4},{6,7},{7,6},{8,9},{9,8},{10,11... | collective-permute-start | bytes 1572872 | tf_op jit(solution)/shard_map/ppermute | solution.py:393
  124.7 5.3 %collective-permute-start.21 = (bf16[256,512]{1,0:T(8,128)(2,1)S(1)}, bf16[256,512]{1,0:T(8,128)(2,1)S(1)}, u32[]{:S(2)}, u32[]{:S(2)}) collective-permute-start(bf16[256,512]{1,0:T(8,128)(2,1)S(1)} %collective-permute-done.19.refs_1_), channel_id=1, source_target_pairs={{0,1},{1,0},{2,3},{3,2},{4,5},{5,4},{6,7},{7,6},{8,9},{9,8},{10,11... | collective-permute-start | bytes 786440 | tf_op jit(solution)/shard_map/ppermute | solution.py:393
  124.8 5.2 %collective-permute-start.22 = (bf16[256,512]{1,0:T(8,128)(2,1)S(1)}, bf16[256,512]{1,0:T(8,128)(2,1)S(1)}, u32[]{:S(2)}, u32[]{:S(2)}) collective-permute-start(bf16[256,512]{1,0:T(8,128)(2,1)S(1)} %collective-permute-done.16.refs_2_), channel_id=1, source_target_pairs={{0,1},{1,0},{2,3},{3,2},{4,5},{5,4},{6,7},{7,6},{8,9},{9,8},{10,11... | collective-permute-start | bytes 786440 | tf_op jit(solution)/shard_map/ppermute | solution.py:393
  130.0 1.9 %collective-permute-start.18 = (bf16[256,512]{1,0:T(8,128)(2,1)S(1)}, bf16[256,512]{1,0:T(8,128)(2,1)S(1)}, u32[]{:S(2)}, u32[]{:S(2)}) collective-permute-start(bf16[256,512]{1,0:T(8,128)(2,1)S(1)} %collective-permute-done.17.refs_0_), channel_id=1, source_target_pairs={{0,1},{1,0},{2,3},{3,2},{4,5},{5,4},{6,7},{7,6},{8,9},{9,8},{10,11... | collective-permute-start | bytes 786440 | tf_op jit(solution)/shard_map/ppermute | solution.py:393

commit v8 on v7

--- a/solution.py
+++ b/solution.py
@@ -252,12 +252,8 @@
         back_ref[index, cap:] = jnp.concatenate(pieces, axis=0).astype(BF)
 
 
-def terms_kernel(special, grad_ref, take, away_ref, keep_ref):
-    grad = grad_ref[...]
-    rel = as_column(take(1)[...])
-    rows_ref = take(0)
-    operator_terms(special, 0, rows_ref, rel, grad, away_ref)
-    operator_terms(special, 4, rows_ref, rel, grad, keep_ref)
+def terms_kernel(special, first, grad_ref, rows_ref, rel_ref, out_ref):
+    operator_terms(special, first, rows_ref, as_column(rel_ref[...]), grad_ref[...], out_ref)
 
 
 def pair_kernel(keep_ref, got_ref, own_ref, sent_ref):
@@ -308,15 +304,20 @@
         refs[-1][index * size : (index + 1) * size] = ref[...]
 
 
-def place_operators(indices, sources, out_ref, wide, sems):
-    width = sources[0].shape[0]
+def half_kernel(which, in_ref, out_ref):
+    size = out_ref.shape[0]
+    out_ref[...] = in_ref[which * size : (which + 1) * size]
+
+
+def place_operators(places, sources, out_ref, wide, sems):
+    width = out_ref.shape[1] // 2
     size = width // 4
     copies = []
-    for slot, (index, source) in enumerate(zip(indices, sources)):
-        wide[slot] = source[...].astype(F32)
+    for slot, ((index, first), source) in enumerate(zip(places, sources)):
+        wide[slot, : source.shape[0]] = source[...].astype(F32)
         relation, part = quarter_of(True, (index + 4) % 8)
-        for turn in range(4):
-            at = part * width + ((lax.axis_index("dom") >> 1) ^ turn) * size
+        for turn in range(source.shape[0] // size):
+            at = part * width + ((lax.axis_index("dom") >> 1) ^ (first + turn)) * size
             copy = pltpu.make_async_copy(
                 wide.at[slot, pl.ds(turn * size, size)],
                 out_ref.at[relation, pl.ds(pl.multiple_of(at, size), size)],
@@ -333,7 +334,7 @@
         copy.wait()
 
 
-def add_kernel(halves, ids_ref, neg_ref, back_ref, take, *out_refs):
+def add_kernel(halves, away, ids_ref, neg_ref, back_ref, take, *out_refs):
     parts = back_ref.shape[0]
     cap = ids_ref.shape[1] // parts
     tails = jnp.concatenate([back_ref[index, :cap] for index in range(parts)], axis=0)
@@ -344,9 +345,9 @@
     negs = jnp.concatenate([high, low], axis=0)
     head = take(0)[...]
     grads = take(1)
-    for turn, out_ref in enumerate(out_refs):
+    for out_ref in out_refs:
         count = out_ref.shape[0]
-        base = (lax.axis_index("rep") % 2 ^ (1 - turn)) * count if halves else 0
+        base = ((lax.axis_index("rep") & 1) ^ away) * count if halves else 0
 
         def pick(row):
             return hot((iota((count, row.shape[1]), 0) + base) == row)
@@ -459,14 +460,19 @@
     )
     returned = exchange(back)
     kind = BF if special else F32
-    away, keep = call(
-        functools.partial(terms_kernel, special),
-        [((2 * columns, columns), kind), ((2 * columns, columns), kind)],
-        (),
-        (grad,),
-        (rows, rel),
-        (back,),
-    )
+
+    def terms(first, after):
+        return call(
+            functools.partial(terms_kernel, special, first),
+            [((2 * columns, columns), kind)],
+            (),
+            (grad, rows, rel),
+            (),
+            after,
+        )[0]
+
+    away = terms(0, (back,))
+    keep = terms(4, (away,))
 
     def head_terms(after):
         return call(
@@ -479,21 +485,22 @@
             cost=0,
         )[0]
 
-    def add(outs, after):
+    def add(away, outs, after, cost=0):
         return call(
-            functools.partial(add_kernel, special),
+            functools.partial(add_kernel, special, away),
             outs,
             (),
             (asked, neg_own, returned),
             (head, head_grads),
             after,
+            cost=cost,
         )
 
     if not special:
         whole = jnp.concatenate([away, keep], axis=0)
         whole = whole.reshape(count, columns, columns)
         head_grads = head_terms(())
-        (added,) = add([((ent_dev, columns), F32)], ())
+        (added,) = add(0, [((ent_dev, columns), F32)], ())
         entity_grad = lax.psum(added, "rep")
         return entity_grad, lax.psum(whole, ("dom", "rep")), loss.reshape(edges)
 
@@ -533,12 +540,11 @@
     )
     met = [flip(v, "dom", 8, 2 * (k + 1)) for k, v in enumerate(sent)]
     rows_half = ent_dev // 2
-    leaving, kept = add(
-        [((rows_half, columns), BF), ((rows_half, columns), F32)], tuple(met)
-    )
+    (leaving,) = add(1, [((rows_half, columns), BF)], (sent[0],))
+    (kept,) = add(0, [((rows_half, columns), F32)], (leaving,), 20)
     arrived = over_core(leaving)
     (own,) = call(
-        sum_kernel, [((quarter, columns), BF)], (), (own, *met), cost=0
+        sum_kernel, [((quarter, columns), BF)], (), (own, *met), (), (kept,), cost=100
     )
     stripes = [own] + [flip(own, "dom", 8, 2 * (k + 1)) for k in range(3)]
     (whole,) = call(
@@ -548,14 +554,23 @@
     across = over_y(both)
 
     y_whole = over_y(whole)
-    mine = [whole, over_x(whole), y_whole, over_x(y_whole)]
-    others = [over_core(v) for v in mine]
-    early, late = (0, 1, 2, 4, 5, 6), (3, 7)
-    quarters = mine + others
+    x_whole = over_x(whole)
+
+    def half_of(which, v):
+        return call(
+            functools.partial(half_kernel, which), [((half // 2, columns), BF)], (), (v,)
+        )[0]
+
+    mine = [whole, x_whole, y_whole]
+    mine += [over_y(half_of(0, x_whole)), over_x(half_of(1, y_whole))]
+    places = [(0, 0), (1, 0), (2, 0), (3, 0), (3, 2)]
+    places += [(4 + index, first) for index, first in places]
+    quarters = mine + [over_core(v) for v in mine]
+    early, late = (0, 1, 2, 5, 6, 7), (3, 4, 8, 9)
     limit = pltpu.CompilerParams(vmem_limit_bytes=40 * 1024 * 1024)
     shape = jax.ShapeDtypeStruct((count, columns, columns), F32)
     relation_grad = pl.pallas_call(
-        functools.partial(operator_kernel, early),
+        functools.partial(operator_kernel, [places[k] for k in early]),
         out_shape=shape,
         in_specs=[VMEM] * len(early),
         out_specs=FAR,
@@ -566,7 +581,7 @@
         compiler_params=limit,
     )(*[quarters[k] for k in early])
     entity_grad, relation_grad = pl.pallas_call(
-        functools.partial(join_kernel, late),
+        functools.partial(join_kernel, [places[k] for k in late]),
         out_shape=[jax.ShapeDtypeStruct((ent_dev, columns), F32), shape],
         in_specs=[VMEM] * (4 + len(late)) + [FAR],
         out_specs=[FAR, FAR],

time: 134 us -> 127 us (0.948)
  waiting for transfers between devices: 69.4 us -> 62.3 us
    ppermute x23 -> x25, waiting for transfers between devices: 47.4 us -> 40.3 us  [flip(): return lax.ppermute(x, axis, [(i, i ^ bit) for i in range(size)])]
    ppermute x23 -> x25, starting transfers between devices: 23.7 us -> 22.8 us  [flip(): return lax.ppermute(x, axis, [(i, i ^ bit) for i in range(size)])]
    pallas_call x13 -> x17, Pallas kernels: 20.4 us -> 21.2 us  [call(): pl.pallas_call(kernel, out_shape=[jax.ShapeDtypeStruct(out[0], out[1]) fo...]
  transfers between devices with their start and end apart: 26 -> 28, of which waited for: 14 -> 14; matrix products, arithmetic and copies ran while one was open for 0% -> 0% of each run, Pallas kernels for 8% -> 11%
where the time goes in v8:
time: 127 us
  waiting for transfers between devices  62.3 us (49%)
  starting transfers between devices  37.4 us (29%)
  Pallas kernels  25 us (20%)
    ppermute x25, waiting for transfers between devices, flip(): return lax.ppermute(x, axis, [(i, i ^ bit) for i in range(size)])  40.3 us
    ppermute x25, starting transfers between devices, flip(): return lax.ppermute(x, axis, [(i, i ^ bit) for i in range(size)])  22.8 us
    all_to_all x3, waiting for transfers between devices, exchange(): return lax.all_to_all(x, 'dom', split_axis=0, concat_axis=0, tiled=True)  22 us
    pallas_call x17, Pallas kernels, call(): pl.pallas_call(kernel, out_shape=[jax.ShapeDtypeStruct(out[0], out[1]) fo...  21.2 us
    all_to_all x3, starting transfers between devices, exchange(): return lax.all_to_all(x, 'dom', split_axis=0, concat_axis=0, tiled=True)  14.6 us
  transfers between devices with their start and end apart: 28, of which 14 were waited for; matrix products, arithmetic and copies ran while one was open for 0% of the time, Pallas kernels for 11%

profile of v8, /device:TPU:0, one launch (start us, length us, event | category | flops | bytes accessed | tf_op | source)
XLA Modules:
  0.0 126.8 jit_solution(17849149594175146541)
XLA Ops:
  0.6 0.0 copy-start
  0.6 2.7 %shard_map.94 = (s32[1,512]{1,0:T(1,128)}, s32[1,32]{1,0:T(1,128)}, bf16[8,8,640]{2,1,0:T(8,128)(2,1)}) custom-call(s32[1,512]{1,0:T(1,128)} %bitcast.16, s32[1,512]{1,0:T(1,128)} %bitcast.17, s32[1,32]{1,0:T(1,128)} %bitcast.18, bf16[1024,512]{1,0:T(8,128)(2,1)} %refs_1_.1), custom_call_target="tpu_custom_call" | custom-call | flops 1 | bytes 1 | tf_op jit(solution)/shard_map/pallas_call | solution.py:60
  3.3 7.3 %all-to-all-start = ((bf16[8,8,640]{2,1,0:T(8,128)(2,1)}), bf16[8,8,640]{2,1,0:T(8,128)(2,1)S(1)}, u32[]{:S(2)}, u32[]{:S(2)}) async-start(bf16[8,8,640]{2,1,0:T(8,128)(2,1)} %get-tuple-element.24), calls=%async_computation | async-start | bytes 163840 | tf_op jit(solution)/shard_map/all_to_all | solution.py:398
  10.6 4.4 %shard_map.95 = (bf16[512,512]{1,0:T(8,128)(2,1)}, bf16[512,512]{1,0:T(8,128)(2,1)}) custom-call(s32[1,512]{1,0:T(1,128)} %bitcast.13, s32[1,512]{1,0:T(1,128)} %bitcast.9, bf16[1024,512]{1,0:T(8,128)(2,1)} %refs_1_.1, bf16[4,512,512]{2,1,0:T(8,128)(2,1)} %refs_2_.3, s32[1,512]{1,0:T(1,128)} %get-tuple-element.25.refs_4_.refs_0_), custom_call_target="tpu_custom_call" | custom-call | flops 1 | bytes 1 | tf_op jit(solution)/shard_map/pallas_call | solution.py:60
  15.0 2.6 %all-to-all-done.refs_0_ = bf16[8,8,640]{2,1,0:T(8,128)(2,1)S(1)} async-done(((bf16[8,8,640]{2,1,0:T(8,128)(2,1)}), bf16[8,8,640]{2,1,0:T(8,128)(2,1)S(1)}, u32[]{:S(2)}, u32[]{:S(2)}) %all-to-all-start) | async-done | bytes 81952 | tf_op jit(solution)/shard_map/all_to_all | solution.py:398
  17.6 1.0 copy-done.2
  18.7 2.6 %shard_map.96 = (s32[1,1024]{1,0:T(1,128)S(1)}, bf16[1024,512]{1,0:T(8,128)(2,1)}, bf16[64,512]{1,0:T(8,128)(2,1)S(1)}) custom-call(bf16[8,8,640]{2,1,0:T(8,128)(2,1)S(1)} %all-to-all-done.refs_0_, bf16[1024,512]{1,0:T(8,128)(2,1)S(1)} %copy-done, bf16[512,512]{1,0:T(8,128)(2,1)S(1)} %copy-done.2), custom_call_target="tpu_custom_call" | custom-call | flops 1 | bytes 1 | tf_op jit(solution)/shard_map/pallas_call | solution.py:60
  21.3 3.6 %all-to-all-start.1 = ((bf16[8,128,512]{2,1,0:T(8,128)(2,1)}), bf16[8,128,512]{2,1,0:T(8,128)(2,1)S(1)}, u32[]{:S(2)}, u32[]{:S(2)}) async-start(bf16[8,128,512]{2,1,0:T(8,128)(2,1)} %bitcast.5), calls=%async_computation.1 | async-start | bytes 2097152 | tf_op jit(solution)/shard_map/all_to_all | solution.py:398
  24.9 0.1 collective-permute-start.2
  24.9 1.6 %collective-permute-start.1 = (bf16[64,512]{1,0:T(8,128)(2,1)S(1)}, bf16[64,512]{1,0:T(8,128)(2,1)S(1)}, u32[]{:S(2)}, u32[]{:S(2)}) collective-permute-start(bf16[64,512]{1,0:T(8,128)(2,1)S(1)} %get-tuple-element.29.refs_1_), channel_id=1, source_target_pairs={{0,2},{1,3},{2,0},{3,1},{4,6},{5,7},{6,4},{7,5},{8,10},{9,11},{10,... | collective-permute-start | bytes 196616 | tf_op jit(solution)/shard_map/ppermute | solution.py:394
  26.5 0.3 collective-permute-start
  26.8 2.4 %collective-permute-done.2.refs_4_ = bf16[64,512]{1,0:T(8,128)(2,1)S(1)} collective-permute-done((bf16[64,512]{1,0:T(8,128)(2,1)S(1)}, bf16[64,512]{1,0:T(8,128)(2,1)S(1)}, u32[]{:S(2)}, u32[]{:S(2)}) %collective-permute-start.2) | collective-permute-done | bytes 65568 | tf_op jit(solution)/shard_map/ppermute | solution.py:394
  29.2 1.5 %collective-permute-done.1.refs_3_ = bf16[64,512]{1,0:T(8,128)(2,1)S(1)} collective-permute-done((bf16[64,512]{1,0:T(8,128)(2,1)S(1)}, bf16[64,512]{1,0:T(8,128)(2,1)S(1)}, u32[]{:S(2)}, u32[]{:S(2)}) %collective-permute-start.1) | collective-permute-done | bytes 65568 | tf_op jit(solution)/shard_map/ppermute | solution.py:394
  30.7 0.0 collective-permute-done.refs_2_
  30.7 19.5 %all-to-all-done.1 = bf16[8,128,512]{2,1,0:T(8,128)(2,1)S(1)} async-done(((bf16[8,128,512]{2,1,0:T(8,128)(2,1)}), bf16[8,128,512]{2,1,0:T(8,128)(2,1)S(1)}, u32[]{:S(2)}, u32[]{:S(2)}) %all-to-all-start.1) | async-done | bytes 1048608 | tf_op jit(solution)/shard_map/all_to_all | solution.py:398
  50.2 4.0 %shard_map.97 = (f32[1,512]{1,0:T(1,128)}, bf16[512,512]{1,0:T(8,128)(2,1)S(1)}, bf16[8,160,512]{2,1,0:T(8,128)(2,1)}) custom-call(s32[1,512]{1,0:T(1,128)S(1)} %copy-done.7, bf16[64,512]{1,0:T(8,128)(2,1)S(1)} %get-tuple-element.29.refs_1_, bf16[64,512]{1,0:T(8,128)(2,1)S(1)} %collective-permute-done.refs_2_, ...), custom_call_target="tpu_custom_call" | custom-call | flops 1 | bytes 1 | tf_op jit(solution)/shard_map/pallas_call | solution.py:60
  54.2 3.8 %all-to-all-start.2 = ((bf16[8,160,512]{2,1,0:T(8,128)(2,1)}), bf16[8,160,512]{2,1,0:T(8,128)(2,1)S(1)}, u32[]{:S(2)}, u32[]{:S(2)}) async-start(bf16[8,160,512]{2,1,0:T(8,128)(2,1)} %get-tuple-element.32.refs_3_), calls=%async_computation.2 | async-start | bytes 2621440 | tf_op jit(solution)/shard_map/all_to_all | solution.py:398
  57.9 1.1 shard_map.98.refs_3_
  59.1 0.1 collective-permute-start.3
  59.2 1.1 shard_map.99.refs_0_
  60.3 0.0 copy-start.1
  60.3 1.5 %collective-permute-done.3.refs_1_ = bf16[1024,512]{1,0:T(8,128)(2,1)S(1)} collective-permute-done((bf16[1024,512]{1,0:T(8,128)(2,1)S(1)}, bf16[1024,512]{1,0:T(8,128)(2,1)S(1)}, u32[]{:S(2)}, u32[]{:S(2)}) %collective-permute-start.3) | collective-permute-done | bytes 1048608 | tf_op jit(solution)/shard_map/ppermute | solution.py:394
  61.8 0.2 shard_map.100
  62.0 1.6 %collective-permute-start.4 = (bf16[512,512]{1,0:T(8,128)(2,1)S(1)}, bf16[512,512]{1,0:T(8,128)(2,1)S(1)}, u32[]{:S(2)}, u32[]{:S(2)}) collective-permute-start(bf16[512,512]{1,0:T(8,128)(2,1)S(1)} %get-tuple-element.35), channel_id=1, source_target_pairs={{0,2},{1,3},{2,0},{3,1},{4,6},{5,7},{6,4},{7,5},{8,10},{9,11},{10,... | collective-permute-start | bytes 1572872 | tf_op jit(solution)/shard_map/ppermute | solution.py:394
  63.6 12.5 %collective-permute-done.4.refs_1_ = bf16[512,512]{1,0:T(8,128)(2,1)S(1)} collective-permute-done((bf16[512,512]{1,0:T(8,128)(2,1)S(1)}, bf16[512,512]{1,0:T(8,128)(2,1)S(1)}, u32[]{:S(2)}, u32[]{:S(2)}) %collective-permute-start.4) | collective-permute-done | bytes 524320 | tf_op jit(solution)/shard_map/ppermute | solution.py:394
  76.1 0.1 shard_map.101
  76.2 0.0 copy-start.6
  76.2 1.8 %collective-permute-start.5 = (bf16[256,512]{1,0:T(8,128)(2,1)S(1)}, bf16[256,512]{1,0:T(8,128)(2,1)S(1)}, u32[]{:S(2)}, u32[]{:S(2)}) collective-permute-start(bf16[256,512]{1,0:T(8,128)(2,1)S(1)} %get-tuple-element.36.refs_3_), channel_id=1, source_target_pairs={{0,4},{4,0},{8,12},{12,8},{16,20},{20,16},{24,28},{28,24},{1,5},{5... | collective-permute-start | bytes 786440 | tf_op jit(solution)/shard_map/ppermute | solution.py:394
  78.0 1.6 %shard_map.102.refs_2_.refs_4_ = bf16[1024,512]{1,0:T(8,128)(2,1)S(1)} custom-call(bf16[512,512]{1,0:T(8,128)(2,1)S(1)} %get-tuple-element.33.refs_0_, s32[1,512]{1,0:T(1,128)S(1)} %bitcast.12, bf16[4,512,512]{2,1,0:T(8,128)(2,1)S(1)} %copy-done.1, bf16[256,512]{1,0:T(8,128)(2,1)S(1)} %get-tuple-element.36.refs_3_), custom_call_target="tpu_custom_call" | custom-call | flops 1 | bytes 1 | tf_op jit(solution)/shard_map/pallas_call | solution.py:60
  79.6 6.4 %collective-permute-done.5.refs_1_ = bf16[256,512]{1,0:T(8,128)(2,1)S(1)} collective-permute-done((bf16[256,512]{1,0:T(8,128)(2,1)S(1)}, bf16[256,512]{1,0:T(8,128)(2,1)S(1)}, u32[]{:S(2)}, u32[]{:S(2)}) %collective-permute-start.5) | collective-permute-done | bytes 262176 | tf_op jit(solution)/shard_map/ppermute | solution.py:394
  86.0 4.0 %collective-permute-start.11 = (bf16[64,512]{1,0:T(8,128)(2,1)S(1)}, bf16[64,512]{1,0:T(8,128)(2,1)S(1)}, u32[]{:S(2)}, u32[]{:S(2)}) collective-permute-start(bf16[64,512]{1,0:T(8,128)(2,1)S(1)} %get-tuple-element.40), channel_id=1, source_target_pairs={{0,16},{4,20},{8,24},{12,28},{16,0},{20,4},{24,8},{28,12},{1,17},{... | collective-permute-start | bytes 196616 | tf_op jit(solution)/shard_map/ppermute | solution.py:394
  90.0 0.7 collective-permute-start.12
  90.7 0.0 collective-permute-start.10
  90.8 0.0 all-to-all-done.2.refs_2_
  90.8 1.6 %shard_map.104.refs_5_ = bf16[512,512]{1,0:T(8,128)(2,1)S(1)} custom-call(s32[1,1024]{1,0:T(1,128)S(1)} %get-tuple-element.27.refs_0_, s32[1,32]{1,0:T(1,128)S(1)} %copy-done.8, bf16[8,160,512]{2,1,0:T(8,128)(2,1)S(1)} %all-to-all-done.2.refs_2_, s32[1,512]{1,0:T(1,128)S(1)} %bitcast.14, bf16[1024,512]{1,0:T(8,128)(2,1)S(1)} %shard_map.102.refs_2_.refs_4_, ...), custom_call_target="tpu_custom_call" | custom-call | flops 1 | bytes 1 | tf_op jit(solution)/shard_map/pallas_call | solution.py:60
  92.4 0.1 collective-permute-start.6
  92.4 1.6 %shard_map.105.refs_0_.refs_4_ = f32[512,512]{1,0:T(8,128)S(1)} custom-call(s32[1,1024]{1,0:T(1,128)S(1)} %get-tuple-element.27.refs_0_, s32[1,32]{1,0:T(1,128)S(1)} %copy-done.8, bf16[8,160,512]{2,1,0:T(8,128)(2,1)S(1)} %all-to-all-done.2.refs_2_, s32[1,512]{1,0:T(1,128)S(1)} %bitcast.15, bf16[1024,512]{1,0:T(8,128)(2,1)S(1)} %shard_map.102.refs_2_.refs_4_, ...), custom_call_target="tpu_custom_call" | custom-call | flops 20000000000 | bytes 1 | tf_op jit(solution)/shard_map/pallas_call | solution.py:60
  94.0 0.3 collective-permute-done.6.refs_1_
  94.3 0.1 shard_map.106.mine_ref
  94.4 1.6 %collective-permute-start.8 = (bf16[512,512]{1,0:T(8,128)(2,1)S(1)}, bf16[512,512]{1,0:T(8,128)(2,1)S(1)}, u32[]{:S(2)}, u32[]{:S(2)}) collective-permute-start(bf16[512,512]{1,0:T(8,128)(2,1)S(1)} %shard_map.106.mine_ref), channel_id=1, source_target_pairs={{0,2},{1,3},{2,0},{3,1},{4,6},{5,7},{6,4},{7,5},{8,10},{9,11},{10,... | collective-permute-start | bytes 1572872 | tf_op jit(solution)/shard_map/ppermute | solution.py:394
  96.0 0.0 collective-permute-done.11.refs_2_
  96.0 0.1 collective-permute-done.12.refs_3_
  96.1 3.1 %collective-permute-start.15 = (bf16[64,512]{1,0:T(8,128)(2,1)S(1)}, bf16[64,512]{1,0:T(8,128)(2,1)S(1)}, u32[]{:S(2)}, u32[]{:S(2)}) collective-permute-start(bf16[64,512]{1,0:T(8,128)(2,1)S(1)} %shard_map.107.refs_0_), channel_id=1, source_target_pairs={{0,24},{4,28},{8,16},{12,20},{16,8},{20,12},{24,0},{28,4},{1,25},{... | collective-permute-start | bytes 196616 | tf_op jit(solution)/shard_map/ppermute | solution.py:394
  99.2 0.6 collective-permute-start.14
  99.9 0.7 collective-permute-start.13
  100.6 1.7 %collective-permute-done.15.refs_3_ = bf16[64,512]{1,0:T(8,128)(2,1)S(1)} collective-permute-done((bf16[64,512]{1,0:T(8,128)(2,1)S(1)}, bf16[64,512]{1,0:T(8,128)(2,1)S(1)}, u32[]{:S(2)}, u32[]{:S(2)}) %collective-permute-start.15) | collective-permute-done | bytes 65568 | tf_op jit(solution)/shard_map/ppermute | solution.py:394
  102.3 3.7 %collective-permute-done.14.refs_2_ = bf16[64,512]{1,0:T(8,128)(2,1)S(1)} collective-permute-done((bf16[64,512]{1,0:T(8,128)(2,1)S(1)}, bf16[64,512]{1,0:T(8,128)(2,1)S(1)}, u32[]{:S(2)}, u32[]{:S(2)}) %collective-permute-start.14) | collective-permute-done | bytes 65568 | tf_op jit(solution)/shard_map/ppermute | solution.py:394
  106.1 0.0 collective-permute-done.13.refs_1_
  106.1 0.6 collective-permute-start.18
  106.7 1.4 %collective-permute-start.16 = (bf16[256,512]{1,0:T(8,128)(2,1)S(1)}, bf16[256,512]{1,0:T(8,128)(2,1)S(1)}, u32[]{:S(2)}, u32[]{:S(2)}) collective-permute-start(bf16[256,512]{1,0:T(8,128)(2,1)S(1)} %shard_map.108.refs_0_), channel_id=1, source_target_pairs={{0,4},{4,0},{8,12},{12,8},{16,20},{20,16},{24,28},{28,24},{1,5},{5... | collective-permute-start | bytes 786440 | tf_op jit(solution)/shard_map/ppermute | solution.py:394
  108.1 0.0 collective-permute-start.22
  108.1 0.5 collective-permute-start.7
  108.6 0.0 collective-permute-done.8.over_ref
  108.6 0.0 collective-permute-start.9
  108.6 5.7 %collective-permute-done.18.refs_0_.refs_2_ = bf16[256,512]{1,0:T(8,128)(2,1)S(1)} collective-permute-done((bf16[256,512]{1,0:T(8,128)(2,1)S(1)}, bf16[256,512]{1,0:T(8,128)(2,1)S(1)}, u32[]{:S(2)}, u32[]{:S(2)}) %collective-permute-start.18) | collective-permute-done | bytes 262176 | tf_op jit(solution)/shard_map/ppermute | solution.py:394
  114.3 2.0 %collective-permute-start.19 = (bf16[128,512]{1,0:T(8,128)(2,1)S(1)}, bf16[128,512]{1,0:T(8,128)(2,1)S(1)}, u32[]{:S(2)}, u32[]{:S(2)}) collective-permute-start(bf16[128,512]{1,0:T(8,128)(2,1)S(1)} %shard_map.110), channel_id=1, source_target_pairs={{0,4},{4,0},{8,12},{12,8},{16,20},{20,16},{24,28},{28,24},{1,5},{5... | collective-permute-start | bytes 393224 | tf_op jit(solution)/shard_map/ppermute | solution.py:394
  116.3 0.0 collective-permute-done.16.refs_0_.refs_1_
  116.3 0.0 collective-permute-done.22.refs_3_
  116.4 1.6 %collective-permute-start.17 = (bf16[128,512]{1,0:T(8,128)(2,1)S(1)}, bf16[128,512]{1,0:T(8,128)(2,1)S(1)}, u32[]{:S(2)}, u32[]{:S(2)}) collective-permute-start(bf16[128,512]{1,0:T(8,128)(2,1)S(1)} %shard_map.109), channel_id=1, source_target_pairs={{0,2},{1,3},{2,0},{3,1},{4,6},{5,7},{6,4},{7,5},{8,10},{9,11},{10,... | collective-permute-start | bytes 393224 | tf_op jit(solution)/shard_map/ppermute | solution.py:394
  117.9 1.4 %collective-permute-done.19.refs_1_ = bf16[128,512]{1,0:T(8,128)(2,1)S(1)} collective-permute-done((bf16[128,512]{1,0:T(8,128)(2,1)S(1)}, bf16[128,512]{1,0:T(8,128)(2,1)S(1)}, u32[]{:S(2)}, u32[]{:S(2)}) %collective-permute-start.19) | collective-permute-done | bytes 131104 | tf_op jit(solution)/shard_map/ppermute | solution.py:394
  119.4 3.0 %collective-permute-done.17.refs_0_ = bf16[128,512]{1,0:T(8,128)(2,1)S(1)} collective-permute-done((bf16[128,512]{1,0:T(8,128)(2,1)S(1)}, bf16[128,512]{1,0:T(8,128)(2,1)S(1)}, u32[]{:S(2)}, u32[]{:S(2)}) %collective-permute-start.17) | collective-permute-done | bytes 131104 | tf_op jit(solution)/shard_map/ppermute | solution.py:394
  122.3 0.5 collective-permute-start.20
  122.8 1.9 %shard_map.111.refs_4_ = f32[4,512,512]{2,1,0:T(8,128)} custom-call(bf16[256,512]{1,0:T(8,128)(2,1)S(1)} %shard_map.108.refs_0_, bf16[256,512]{1,0:T(8,128)(2,1)S(1)} %collective-permute-done.16.refs_0_.refs_1_, bf16[256,512]{1,0:T(8,128)(2,1)S(1)} %collective-permute-done.18.refs_0_.refs_2_, bf16[256,512]{1,0:T(8,128)(2,1)S(1)} %collective-permute-done.22.refs_3_, ...), custom_call_target="tpu_custom_call" | custom-call | tf_op jit(solution)/shard_map/pallas_call | solution.py:572
  124.8 1.9 %shard_map.112 = (f32[1024,512]{1,0:T(8,128)}, f32[4,512,512]{2,1,0:T(8,128)}) custom-call(bf16[512,512]{1,0:T(8,128)(2,1)S(1)} %shard_map.106.mine_ref, bf16[512,512]{1,0:T(8,128)(2,1)S(1)} %collective-permute-done.7.other_ref, bf16[512,512]{1,0:T(8,128)(2,1)S(1)} %collective-permute-done.8.over_ref, ...), custom_call_target="tpu_custom_call", output_to_operand_aliasing={{1}: (8, {})} | custom-call | tf_op jit(solution)/shard_map/pallas_call | solution.py:583
  (29 shorter events, 0.2 us)
Async XLA Ops:
  0.6 17.0 %copy-start = (bf16[1024,512]{1,0:T(8,128)(2,1)S(1)}, bf16[1024,512]{1,0:T(8,128)(2,1)}, u32[]{:S(2)}) copy-start(bf16[1024,512]{1,0:T(8,128)(2,1)} %refs_1_.1) | copy-start | bytes 3145732
  3.3 14.3 %all-to-all-start = ((bf16[8,8,640]{2,1,0:T(8,128)(2,1)}), bf16[8,8,640]{2,1,0:T(8,128)(2,1)S(1)}, u32[]{:S(2)}, u32[]{:S(2)}) async-start(bf16[8,8,640]{2,1,0:T(8,128)(2,1)} %get-tuple-element.24), calls=%async_computation | async-start | bytes 163840 | tf_op jit(solution)/shard_map/all_to_all | solution.py:398
  10.6 39.6 %copy-start.7 = (s32[1,512]{1,0:T(1,128)S(1)}, s32[1,512]{1,0:T(1,128)}, u32[]{:S(2)}) copy-start(s32[1,512]{1,0:T(1,128)} %get-tuple-element.25.refs_4_.refs_0_) | copy-start | bytes 6148
  17.6 1.0 copy-start.2
  18.7 31.5 %copy-start.4 = (bf16[512,512]{1,0:T(8,128)(2,1)S(1)}, bf16[512,512]{1,0:T(8,128)(2,1)}, u32[]{:S(2)}) copy-start(bf16[512,512]{1,0:T(8,128)(2,1)} %get-tuple-element.31.refs_6_) | copy-start | bytes 1572868
  21.3 28.9 %all-to-all-start.1 = ((bf16[8,128,512]{2,1,0:T(8,128)(2,1)}), bf16[8,128,512]{2,1,0:T(8,128)(2,1)S(1)}, u32[]{:S(2)}, u32[]{:S(2)}) async-start(bf16[8,128,512]{2,1,0:T(8,128)(2,1)} %bitcast.5), calls=%async_computation.1 | async-start | bytes 2097152 | tf_op jit(solution)/shard_map/all_to_all | solution.py:398
  24.9 4.4 %collective-permute-start.2 = (bf16[64,512]{1,0:T(8,128)(2,1)S(1)}, bf16[64,512]{1,0:T(8,128)(2,1)S(1)}, u32[]{:S(2)}, u32[]{:S(2)}) collective-permute-start(bf16[64,512]{1,0:T(8,128)(2,1)S(1)} %get-tuple-element.29.refs_1_), channel_id=1, source_target_pairs={{0,3},{1,2},{2,1},{3,0},{4,7},{5,6},{6,5},{7,4},{8,11},{9,10},{10,... | collective-permute-start | bytes 196616 | tf_op jit(solution)/shard_map/ppermute | solution.py:394
  24.9 5.8 %collective-permute-start.1 = (bf16[64,512]{1,0:T(8,128)(2,1)S(1)}, bf16[64,512]{1,0:T(8,128)(2,1)S(1)}, u32[]{:S(2)}, u32[]{:S(2)}) collective-permute-start(bf16[64,512]{1,0:T(8,128)(2,1)S(1)} %get-tuple-element.29.refs_1_), channel_id=1, source_target_pairs={{0,2},{1,3},{2,0},{3,1},{4,6},{5,7},{6,4},{7,5},{8,10},{9,11},{10,... | collective-permute-start | bytes 196616 | tf_op jit(solution)/shard_map/ppermute | solution.py:394
  26.5 4.2 %collective-permute-start = (bf16[64,512]{1,0:T(8,128)(2,1)S(1)}, bf16[64,512]{1,0:T(8,128)(2,1)S(1)}, u32[]{:S(2)}, u32[]{:S(2)}) collective-permute-start(bf16[64,512]{1,0:T(8,128)(2,1)S(1)} %get-tuple-element.29.refs_1_), channel_id=1, source_target_pairs={{0,1},{1,0},{2,3},{3,2},{4,5},{5,4},{6,7},{7,6},{8,9},{9,8},{10,11... | collective-permute-start | bytes 196616 | tf_op jit(solution)/shard_map/ppermute | solution.py:394
  50.2 7.7 %copy-start.3 = (bf16[512,512]{1,0:T(8,128)(2,1)S(1)}, bf16[512,512]{1,0:T(8,128)(2,1)}, u32[]{:S(2)}) copy-start(bf16[512,512]{1,0:T(8,128)(2,1)} %get-tuple-element.26.refs_2_.refs_1_) | copy-start | bytes 1572868
  50.2 7.8 %copy-start.5 = (s32[512]{0:T(512)S(1)}, s32[512]{0:T(512)}, u32[]{:S(2)}) copy-start(s32[512]{0:T(512)} %param.10) | copy-start | bytes 6148
  54.2 36.6 %all-to-all-start.2 = ((bf16[8,160,512]{2,1,0:T(8,128)(2,1)}), bf16[8,160,512]{2,1,0:T(8,128)(2,1)S(1)}, u32[]{:S(2)}, u32[]{:S(2)}) async-start(bf16[8,160,512]{2,1,0:T(8,128)(2,1)} %get-tuple-element.32.refs_3_), calls=%async_computation.2 | async-start | bytes 2621440 | tf_op jit(solution)/shard_map/all_to_all | solution.py:398
  59.1 2.7 %collective-permute-start.3 = (bf16[1024,512]{1,0:T(8,128)(2,1)S(1)}, bf16[1024,512]{1,0:T(8,128)(2,1)S(1)}, u32[]{:S(2)}, u32[]{:S(2)}) collective-permute-start(bf16[1024,512]{1,0:T(8,128)(2,1)S(1)} %shard_map.98.refs_3_), channel_id=1, source_target_pairs={{0,1},{1,0},{2,3},{3,2},{4,5},{5,4},{6,7},{7,6},{8,9},{9,8},{10,11... | collective-permute-start | bytes 3145736 | tf_op jit(solution)/shard_map/ppermute | solution.py:394
  60.3 17.7 %copy-start.1 = (bf16[4,512,512]{2,1,0:T(8,128)(2,1)S(1)}, bf16[4,512,512]{2,1,0:T(8,128)(2,1)}, u32[]{:S(2)}) copy-start(bf16[4,512,512]{2,1,0:T(8,128)(2,1)} %refs_2_.3) | copy-start | bytes 6291460
  62.0 14.0 %collective-permute-start.4 = (bf16[512,512]{1,0:T(8,128)(2,1)S(1)}, bf16[512,512]{1,0:T(8,128)(2,1)S(1)}, u32[]{:S(2)}, u32[]{:S(2)}) collective-permute-start(bf16[512,512]{1,0:T(8,128)(2,1)S(1)} %get-tuple-element.35), channel_id=1, source_target_pairs={{0,2},{1,3},{2,0},{3,1},{4,6},{5,7},{6,4},{7,5},{8,10},{9,11},{10,... | collective-permute-start | bytes 1572872 | tf_op jit(solution)/shard_map/ppermute | solution.py:394
  76.2 14.6 %copy-start.6 = (s32[512]{0:T(512)S(1)}, s32[512]{0:T(512)}, u32[]{:S(2)}) copy-start(s32[512]{0:T(512)} %param.9) | copy-start | bytes 6148
  76.2 14.6 %copy-start.8 = (s32[1,32]{1,0:T(1,128)S(1)}, s32[1,32]{1,0:T(1,128)}, u32[]{:S(2)}) copy-start(s32[1,32]{1,0:T(1,128)} %get-tuple-element.28.refs_1_) | copy-start | bytes 388
  76.2 9.8 %collective-permute-start.5 = (bf16[256,512]{1,0:T(8,128)(2,1)S(1)}, bf16[256,512]{1,0:T(8,128)(2,1)S(1)}, u32[]{:S(2)}, u32[]{:S(2)}) collective-permute-start(bf16[256,512]{1,0:T(8,128)(2,1)S(1)} %get-tuple-element.36.refs_3_), channel_id=1, source_target_pairs={{0,4},{4,0},{8,12},{12,8},{16,20},{20,16},{24,28},{28,24},{1,5},{5... | collective-permute-start | bytes 786440 | tf_op jit(solution)/shard_map/ppermute | solution.py:394
  86.0 10.0 %collective-permute-start.11 = (bf16[64,512]{1,0:T(8,128)(2,1)S(1)}, bf16[64,512]{1,0:T(8,128)(2,1)S(1)}, u32[]{:S(2)}, u32[]{:S(2)}) collective-permute-start(bf16[64,512]{1,0:T(8,128)(2,1)S(1)} %get-tuple-element.40), channel_id=1, source_target_pairs={{0,16},{4,20},{8,24},{12,28},{16,0},{20,4},{24,8},{28,12},{1,17},{... | collective-permute-start | bytes 196616 | tf_op jit(solution)/shard_map/ppermute | solution.py:394
  90.0 6.1 %collective-permute-start.12 = (bf16[64,512]{1,0:T(8,128)(2,1)S(1)}, bf16[64,512]{1,0:T(8,128)(2,1)S(1)}, u32[]{:S(2)}, u32[]{:S(2)}) collective-permute-start(bf16[64,512]{1,0:T(8,128)(2,1)S(1)} %get-tuple-element.41), channel_id=1, source_target_pairs={{0,24},{4,28},{8,16},{12,20},{16,8},{20,12},{24,0},{28,4},{1,25},{... | collective-permute-start | bytes 196616 | tf_op jit(solution)/shard_map/ppermute | solution.py:394
  90.7 5.3 %collective-permute-start.10 = (bf16[64,512]{1,0:T(8,128)(2,1)S(1)}, bf16[64,512]{1,0:T(8,128)(2,1)S(1)}, u32[]{:S(2)}, u32[]{:S(2)}) collective-permute-start(bf16[64,512]{1,0:T(8,128)(2,1)S(1)} %get-tuple-element.38.refs_5_), channel_id=1, source_target_pairs={{0,8},{4,12},{8,0},{12,4},{16,24},{20,28},{24,16},{28,20},{1,9},{5... | collective-permute-start | bytes 196616 | tf_op jit(solution)/shard_map/ppermute | solution.py:394
  92.4 2.0 %collective-permute-start.6 = (bf16[512,512]{1,0:T(8,128)(2,1)S(1)}, bf16[512,512]{1,0:T(8,128)(2,1)S(1)}, u32[]{:S(2)}, u32[]{:S(2)}) collective-permute-start(bf16[512,512]{1,0:T(8,128)(2,1)S(1)} %shard_map.104.refs_5_), channel_id=1, source_target_pairs={{0,1},{1,0},{2,3},{3,2},{4,5},{5,4},{6,7},{7,6},{8,9},{9,8},{10,11... | collective-permute-start | bytes 1572872 | tf_op jit(solution)/shard_map/ppermute | solution.py:394
  94.4 14.1 %collective-permute-start.8 = (bf16[512,512]{1,0:T(8,128)(2,1)S(1)}, bf16[512,512]{1,0:T(8,128)(2,1)S(1)}, u32[]{:S(2)}, u32[]{:S(2)}) collective-permute-start(bf16[512,512]{1,0:T(8,128)(2,1)S(1)} %shard_map.106.mine_ref), channel_id=1, source_target_pairs={{0,2},{1,3},{2,0},{3,1},{4,6},{5,7},{6,4},{7,5},{8,10},{9,11},{10,... | collective-permute-start | bytes 1572872 | tf_op jit(solution)/shard_map/ppermute | solution.py:394
  96.1 6.2 %collective-permute-start.15 = (bf16[64,512]{1,0:T(8,128)(2,1)S(1)}, bf16[64,512]{1,0:T(8,128)(2,1)S(1)}, u32[]{:S(2)}, u32[]{:S(2)}) collective-permute-start(bf16[64,512]{1,0:T(8,128)(2,1)S(1)} %shard_map.107.refs_0_), channel_id=1, source_target_pairs={{0,24},{4,28},{8,16},{12,20},{16,8},{20,12},{24,0},{28,4},{1,25},{... | collective-permute-start | bytes 196616 | tf_op jit(solution)/shard_map/ppermute | solution.py:394
  99.2 6.8 %collective-permute-start.14 = (bf16[64,512]{1,0:T(8,128)(2,1)S(1)}, bf16[64,512]{1,0:T(8,128)(2,1)S(1)}, u32[]{:S(2)}, u32[]{:S(2)}) collective-permute-start(bf16[64,512]{1,0:T(8,128)(2,1)S(1)} %shard_map.107.refs_0_), channel_id=1, source_target_pairs={{0,16},{4,20},{8,24},{12,28},{16,0},{20,4},{24,8},{28,12},{1,17},{... | collective-permute-start | bytes 196616 | tf_op jit(solution)/shard_map/ppermute | solution.py:394
  99.9 6.2 %collective-permute-start.13 = (bf16[64,512]{1,0:T(8,128)(2,1)S(1)}, bf16[64,512]{1,0:T(8,128)(2,1)S(1)}, u32[]{:S(2)}, u32[]{:S(2)}) collective-permute-start(bf16[64,512]{1,0:T(8,128)(2,1)S(1)} %shard_map.107.refs_0_), channel_id=1, source_target_pairs={{0,8},{4,12},{8,0},{12,4},{16,24},{20,28},{24,16},{28,20},{1,9},{5... | collective-permute-start | bytes 196616 | tf_op jit(solution)/shard_map/ppermute | solution.py:394
  106.1 8.2 %collective-permute-start.18 = (bf16[256,512]{1,0:T(8,128)(2,1)S(1)}, bf16[256,512]{1,0:T(8,128)(2,1)S(1)}, u32[]{:S(2)}, u32[]{:S(2)}) collective-permute-start(bf16[256,512]{1,0:T(8,128)(2,1)S(1)} %shard_map.108.refs_0_), channel_id=1, source_target_pairs={{0,2},{1,3},{2,0},{3,1},{4,6},{5,7},{6,4},{7,5},{8,10},{9,11},{10,... | collective-permute-start | bytes 786440 | tf_op jit(solution)/shard_map/ppermute | solution.py:394
  106.7 9.7 %collective-permute-start.16 = (bf16[256,512]{1,0:T(8,128)(2,1)S(1)}, bf16[256,512]{1,0:T(8,128)(2,1)S(1)}, u32[]{:S(2)}, u32[]{:S(2)}) collective-permute-start(bf16[256,512]{1,0:T(8,128)(2,1)S(1)} %shard_map.108.refs_0_), channel_id=1, source_target_pairs={{0,4},{4,0},{8,12},{12,8},{16,20},{20,16},{24,28},{28,24},{1,5},{5... | collective-permute-start | bytes 786440 | tf_op jit(solution)/shard_map/ppermute | solution.py:394
  108.1 8.3 %collective-permute-start.22 = (bf16[256,512]{1,0:T(8,128)(2,1)S(1)}, bf16[256,512]{1,0:T(8,128)(2,1)S(1)}, u32[]{:S(2)}, u32[]{:S(2)}) collective-permute-start(bf16[256,512]{1,0:T(8,128)(2,1)S(1)} %shard_map.108.refs_0_), channel_id=1, source_target_pairs={{0,1},{1,0},{2,3},{3,2},{4,5},{5,4},{6,7},{7,6},{8,9},{9,8},{10,11... | collective-permute-start | bytes 786440 | tf_op jit(solution)/shard_map/ppermute | solution.py:394
  108.1 16.7 %collective-permute-start.7 = (bf16[512,512]{1,0:T(8,128)(2,1)S(1)}, bf16[512,512]{1,0:T(8,128)(2,1)S(1)}, u32[]{:S(2)}, u32[]{:S(2)}) collective-permute-start(bf16[512,512]{1,0:T(8,128)(2,1)S(1)} %shard_map.106.mine_ref), channel_id=1, source_target_pairs={{0,1},{1,0},{2,3},{3,2},{4,5},{5,4},{6,7},{7,6},{8,9},{9,8},{10,11... | collective-permute-start | bytes 1572872 | tf_op jit(solution)/shard_map/ppermute | solution.py:394
  108.6 16.2 %collective-permute-start.9 = (bf16[512,512]{1,0:T(8,128)(2,1)S(1)}, bf16[512,512]{1,0:T(8,128)(2,1)S(1)}, u32[]{:S(2)}, u32[]{:S(2)}) collective-permute-start(bf16[512,512]{1,0:T(8,128)(2,1)S(1)} %collective-permute-done.8.over_ref), channel_id=1, source_target_pairs={{0,1},{1,0},{2,3},{3,2},{4,5},{5,4},{6,7},{7,6},{8,9},{9,8},{10,11... | collective-permute-start | bytes 1572872 | tf_op jit(solution)/shard_map/ppermute | solution.py:394
  114.3 5.1 %collective-permute-start.19 = (bf16[128,512]{1,0:T(8,128)(2,1)S(1)}, bf16[128,512]{1,0:T(8,128)(2,1)S(1)}, u32[]{:S(2)}, u32[]{:S(2)}) collective-permute-start(bf16[128,512]{1,0:T(8,128)(2,1)S(1)} %shard_map.110), channel_id=1, source_target_pairs={{0,4},{4,0},{8,12},{12,8},{16,20},{20,16},{24,28},{28,24},{1,5},{5... | collective-permute-start | bytes 393224 | tf_op jit(solution)/shard_map/ppermute | solution.py:394
  116.3 6.0 %collective-permute-start.24 = (bf16[256,512]{1,0:T(8,128)(2,1)S(1)}, bf16[256,512]{1,0:T(8,128)(2,1)S(1)}, u32[]{:S(2)}, u32[]{:S(2)}) collective-permute-start(bf16[256,512]{1,0:T(8,128)(2,1)S(1)} %collective-permute-done.18.refs_0_.refs_2_), channel_id=1, source_target_pairs={{0,1},{1,0},{2,3},{3,2},{4,5},{5,4},{6,7},{7,6},{8,9},{9,8},{10,11... | collective-permute-start | bytes 786440 | tf_op jit(solution)/shard_map/ppermute | solution.py:394
  116.4 6.0 %collective-permute-start.17 = (bf16[128,512]{1,0:T(8,128)(2,1)S(1)}, bf16[128,512]{1,0:T(8,128)(2,1)S(1)}, u32[]{:S(2)}, u32[]{:S(2)}) collective-permute-start(bf16[128,512]{1,0:T(8,128)(2,1)S(1)} %shard_map.109), channel_id=1, source_target_pairs={{0,2},{1,3},{2,0},{3,1},{4,6},{5,7},{6,4},{7,5},{8,10},{9,11},{10,... | collective-permute-start | bytes 393224 | tf_op jit(solution)/shard_map/ppermute | solution.py:394
  119.4 3.5 %collective-permute-start.23 = (bf16[256,512]{1,0:T(8,128)(2,1)S(1)}, bf16[256,512]{1,0:T(8,128)(2,1)S(1)}, u32[]{:S(2)}, u32[]{:S(2)}) collective-permute-start(bf16[256,512]{1,0:T(8,128)(2,1)S(1)} %collective-permute-done.16.refs_0_.refs_1_), channel_id=1, source_target_pairs={{0,1},{1,0},{2,3},{3,2},{4,5},{5,4},{6,7},{7,6},{8,9},{9,8},{10,11... | collective-permute-start | bytes 786440 | tf_op jit(solution)/shard_map/ppermute | solution.py:394
  122.3 2.4 %collective-permute-start.21 = (bf16[128,512]{1,0:T(8,128)(2,1)S(1)}, bf16[128,512]{1,0:T(8,128)(2,1)S(1)}, u32[]{:S(2)}, u32[]{:S(2)}) collective-permute-start(bf16[128,512]{1,0:T(8,128)(2,1)S(1)} %collective-permute-done.19.refs_1_), channel_id=1, source_target_pairs={{0,1},{1,0},{2,3},{3,2},{4,5},{5,4},{6,7},{7,6},{8,9},{9,8},{10,11... | collective-permute-start | bytes 393224 | tf_op jit(solution)/shard_map/ppermute | solution.py:394
  122.3 2.4 %collective-permute-start.20 = (bf16[128,512]{1,0:T(8,128)(2,1)S(1)}, bf16[128,512]{1,0:T(8,128)(2,1)S(1)}, u32[]{:S(2)}, u32[]{:S(2)}) collective-permute-start(bf16[128,512]{1,0:T(8,128)(2,1)S(1)} %collective-permute-done.17.refs_0_), channel_id=1, source_target_pairs={{0,1},{1,0},{2,3},{3,2},{4,5},{5,4},{6,7},{7,6},{8,9},{9,8},{10,11... | collective-permute-start | bytes 393224 | tf_op jit(solution)/shard_map/ppermute | solution.py:394

commit v9 on v8

--- a/solution.py
+++ b/solution.py
@@ -328,9 +328,13 @@
     return copies
 
 
-def operator_kernel(indices, *refs):
-    sources, (out_ref, wide, sems) = refs[:-3], refs[-3:]
-    for copy in place_operators(indices, sources, out_ref, wide, sems):
+def same_kernel(in_ref, out_ref):
+    out_ref[...] = in_ref[...]
+
+
+def operator_kernel(places, *refs):
+    sources, (_, out_ref, wide, sems) = refs[:-4], refs[-4:]
+    for copy in place_operators(places, sources, out_ref, wide, sems):
         copy.wait()
 
 
@@ -368,7 +372,8 @@
     indices, mine_ref, other_ref, over_ref, far_ref, *refs
 ):
     sources, rest = refs[: len(indices)], refs[len(indices) :]
-    _, out_ref, operators_ref, wide, sems, operators_wide, operators_sems = rest
+    out_ref, operators_ref, token_ref, wide, sems, operators_wide, operators_sems = rest
+    token_ref[...] = jnp.zeros_like(token_ref)
     half = mine_ref.shape[0]
     core = lax.axis_index("rep") & 1
     copies = []
@@ -565,42 +570,41 @@
     mine += [over_y(half_of(0, x_whole)), over_x(half_of(1, y_whole))]
     places = [(0, 0), (1, 0), (2, 0), (3, 0), (3, 2)]
     places += [(4 + index, first) for index, first in places]
-    quarters = mine + [over_core(v) for v in mine]
     early, late = (0, 1, 2, 5, 6, 7), (3, 4, 8, 9)
     limit = pltpu.CompilerParams(vmem_limit_bytes=40 * 1024 * 1024)
     shape = jax.ShapeDtypeStruct((count, columns, columns), F32)
-    relation_grad = pl.pallas_call(
-        functools.partial(operator_kernel, [places[k] for k in early]),
-        out_shape=shape,
-        in_specs=[VMEM] * len(early),
-        out_specs=FAR,
+    entity_grad, relation_grad, token = pl.pallas_call(
+        functools.partial(join_kernel, [places[k] for k in early]),
+        out_shape=[
+            jax.ShapeDtypeStruct((ent_dev, columns), F32),
+            shape,
+            jax.ShapeDtypeStruct((8, 128), F32),
+        ],
+        in_specs=[VMEM] * (4 + len(early)),
+        out_specs=[FAR, FAR, VMEM],
         scratch_shapes=[
+            pltpu.VMEM((2, rows_half, columns), F32),
+            pltpu.SemaphoreType.DMA((2,)),
             pltpu.VMEM((len(early), half, columns), F32),
             pltpu.SemaphoreType.DMA((len(early), 4)),
         ],
         compiler_params=limit,
-    )(*[quarters[k] for k in early])
-    entity_grad, relation_grad = pl.pallas_call(
-        functools.partial(join_kernel, [places[k] for k in late]),
-        out_shape=[jax.ShapeDtypeStruct((ent_dev, columns), F32), shape],
-        in_specs=[VMEM] * (4 + len(late)) + [FAR],
-        out_specs=[FAR, FAR],
+    )(both, over_core(both), across, over_core(across), *(mine[:3] + [over_core(v) for v in mine[:3]]))
+    last = [
+        call(same_kernel, [(v.shape, BF)], (), (v,), (), (token,))[0] for v in mine[3:]
+    ]
+    relation_grad = pl.pallas_call(
+        functools.partial(operator_kernel, [places[k] for k in late]),
+        out_shape=shape,
+        in_specs=[VMEM] * len(late) + [FAR],
+        out_specs=FAR,
         scratch_shapes=[
-            pltpu.VMEM((2, rows_half, columns), F32),
-            pltpu.SemaphoreType.DMA((2,)),
             pltpu.VMEM((len(late), half, columns), F32),
             pltpu.SemaphoreType.DMA((len(late), 4)),
         ],
-        input_output_aliases={4 + len(late): 1},
+        input_output_aliases={len(late): 0},
         compiler_params=limit,
-    )(
-        both,
-        over_core(both),
-        across,
-        over_core(across),
-        *[quarters[k] for k in late],
-        relation_grad,
-    )
+    )(*last, *[over_core(v) for v in last], relation_grad)
     return entity_grad, relation_grad, loss.reshape(edges)
 
 

time: 127 us -> 125 us (0.984)
  waiting for transfers between devices: 62.3 us -> 60.1 us
    ppermute x25, waiting for transfers between devices: 40.3 us -> 38.1 us  [flip(): return lax.ppermute(x, axis, [(i, i ^ bit) for i in range(size)])]
    pallas_call x17 -> x19, Pallas kernels: 21.2 us -> 21.2 us  [call(): pl.pallas_call(kernel, out_shape=[jax.ShapeDtypeStruct(out[0], out[1]) fo...]
  transfers between devices with their start and end apart: 28 -> 28, of which waited for: 14 -> 17; matrix products, arithmetic and copies ran while one was open for 0% -> 0% of each run, Pallas kernels for 11% -> 12%
where the time goes in v9:
time: 125 us
  waiting for transfers between devices  60.1 us (48%)
  starting transfers between devices  37.2 us (30%)
  Pallas kernels  25 us (20%)
    ppermute x25, waiting for transfers between devices, flip(): return lax.ppermute(x, axis, [(i, i ^ bit) for i in range(size)])  38.1 us
    ppermute x25, starting transfers between devices, flip(): return lax.ppermute(x, axis, [(i, i ^ bit) for i in range(size)])  22.7 us
    all_to_all x3, waiting for transfers between devices, exchange(): return lax.all_to_all(x, 'dom', split_axis=0, concat_axis=0, tiled=True)  22 us
    pallas_call x19, Pallas kernels, call(): pl.pallas_call(kernel, out_shape=[jax.ShapeDtypeStruct(out[0], out[1]) fo...  21.2 us
    all_to_all x3, starting transfers between devices, exchange(): return lax.all_to_all(x, 'dom', split_axis=0, concat_axis=0, tiled=True)  14.6 us
    pallas_call x1, Pallas kernels, local(): pl.pallas_call(functools.partial(join_kernel, [places[k] for k in early])...  2.65 us
  transfers between devices with their start and end apart: 28, of which 17 were waited for; matrix products, arithmetic and copies ran while one was open for 0% of the time, Pallas kernels for 12%

profile of v9, /device:TPU:0, one launch (start us, length us, event | category | flops | bytes accessed | tf_op | source)
XLA Modules:
  0.0 124.5 jit_solution(10138146289240458329)
XLA Ops:
  0.6 0.0 copy-start
  0.6 2.7 %shard_map.94 = (s32[1,512]{1,0:T(1,128)}, s32[1,32]{1,0:T(1,128)}, bf16[8,8,640]{2,1,0:T(8,128)(2,1)}) custom-call(s32[1,512]{1,0:T(1,128)} %bitcast.16, s32[1,512]{1,0:T(1,128)} %bitcast.17, s32[1,32]{1,0:T(1,128)} %bitcast.18, bf16[1024,512]{1,0:T(8,128)(2,1)} %refs_1_.1), custom_call_target="tpu_custom_call" | custom-call | flops 1 | bytes 1 | tf_op jit(solution)/shard_map/pallas_call | solution.py:60
  3.3 7.3 %all-to-all-start = ((bf16[8,8,640]{2,1,0:T(8,128)(2,1)}), bf16[8,8,640]{2,1,0:T(8,128)(2,1)S(1)}, u32[]{:S(2)}, u32[]{:S(2)}) async-start(bf16[8,8,640]{2,1,0:T(8,128)(2,1)} %get-tuple-element.25), calls=%async_computation | async-start | bytes 163840 | tf_op jit(solution)/shard_map/all_to_all | solution.py:403
  10.6 4.4 %shard_map.95 = (bf16[512,512]{1,0:T(8,128)(2,1)}, bf16[512,512]{1,0:T(8,128)(2,1)}) custom-call(s32[1,512]{1,0:T(1,128)} %bitcast.13, s32[1,512]{1,0:T(1,128)} %bitcast.9, bf16[1024,512]{1,0:T(8,128)(2,1)} %refs_1_.1, bf16[4,512,512]{2,1,0:T(8,128)(2,1)} %refs_2_.3, s32[1,512]{1,0:T(1,128)} %get-tuple-element.26.refs_4_.refs_0_), custom_call_target="tpu_custom_call" | custom-call | flops 1 | bytes 1 | tf_op jit(solution)/shard_map/pallas_call | solution.py:60
  15.0 2.6 %all-to-all-done.refs_0_ = bf16[8,8,640]{2,1,0:T(8,128)(2,1)S(1)} async-done(((bf16[8,8,640]{2,1,0:T(8,128)(2,1)}), bf16[8,8,640]{2,1,0:T(8,128)(2,1)S(1)}, u32[]{:S(2)}, u32[]{:S(2)}) %all-to-all-start) | async-done | bytes 81952 | tf_op jit(solution)/shard_map/all_to_all | solution.py:403
  17.6 1.0 copy-done.2
  18.7 2.6 %shard_map.96 = (s32[1,1024]{1,0:T(1,128)S(1)}, bf16[1024,512]{1,0:T(8,128)(2,1)}, bf16[64,512]{1,0:T(8,128)(2,1)S(1)}) custom-call(bf16[8,8,640]{2,1,0:T(8,128)(2,1)S(1)} %all-to-all-done.refs_0_, bf16[1024,512]{1,0:T(8,128)(2,1)S(1)} %copy-done, bf16[512,512]{1,0:T(8,128)(2,1)S(1)} %copy-done.2), custom_call_target="tpu_custom_call" | custom-call | flops 1 | bytes 1 | tf_op jit(solution)/shard_map/pallas_call | solution.py:60
  21.3 3.6 %all-to-all-start.1 = ((bf16[8,128,512]{2,1,0:T(8,128)(2,1)}), bf16[8,128,512]{2,1,0:T(8,128)(2,1)S(1)}, u32[]{:S(2)}, u32[]{:S(2)}) async-start(bf16[8,128,512]{2,1,0:T(8,128)(2,1)} %bitcast.5), calls=%async_computation.1 | async-start | bytes 2097152 | tf_op jit(solution)/shard_map/all_to_all | solution.py:403
  24.9 0.1 collective-permute-start.2
  24.9 1.6 %collective-permute-start.1 = (bf16[64,512]{1,0:T(8,128)(2,1)S(1)}, bf16[64,512]{1,0:T(8,128)(2,1)S(1)}, u32[]{:S(2)}, u32[]{:S(2)}) collective-permute-start(bf16[64,512]{1,0:T(8,128)(2,1)S(1)} %get-tuple-element.30.refs_1_), channel_id=1, source_target_pairs={{0,2},{1,3},{2,0},{3,1},{4,6},{5,7},{6,4},{7,5},{8,10},{9,11},{10,... | collective-permute-start | bytes 196616 | tf_op jit(solution)/shard_map/ppermute | solution.py:399
  26.5 0.3 collective-permute-start
  26.8 2.4 %collective-permute-done.2.refs_4_ = bf16[64,512]{1,0:T(8,128)(2,1)S(1)} collective-permute-done((bf16[64,512]{1,0:T(8,128)(2,1)S(1)}, bf16[64,512]{1,0:T(8,128)(2,1)S(1)}, u32[]{:S(2)}, u32[]{:S(2)}) %collective-permute-start.2) | collective-permute-done | bytes 65568 | tf_op jit(solution)/shard_map/ppermute | solution.py:399
  29.2 1.5 %collective-permute-done.1.refs_3_ = bf16[64,512]{1,0:T(8,128)(2,1)S(1)} collective-permute-done((bf16[64,512]{1,0:T(8,128)(2,1)S(1)}, bf16[64,512]{1,0:T(8,128)(2,1)S(1)}, u32[]{:S(2)}, u32[]{:S(2)}) %collective-permute-start.1) | collective-permute-done | bytes 65568 | tf_op jit(solution)/shard_map/ppermute | solution.py:399
  30.7 19.5 %all-to-all-done.1 = bf16[8,128,512]{2,1,0:T(8,128)(2,1)S(1)} async-done(((bf16[8,128,512]{2,1,0:T(8,128)(2,1)}), bf16[8,128,512]{2,1,0:T(8,128)(2,1)S(1)}, u32[]{:S(2)}, u32[]{:S(2)}) %all-to-all-start.1) | async-done | bytes 1048608 | tf_op jit(solution)/shard_map/all_to_all | solution.py:403
  50.2 4.0 %shard_map.97 = (f32[1,512]{1,0:T(1,128)}, bf16[512,512]{1,0:T(8,128)(2,1)S(1)}, bf16[8,160,512]{2,1,0:T(8,128)(2,1)}) custom-call(s32[1,512]{1,0:T(1,128)S(1)} %copy-done.7, bf16[64,512]{1,0:T(8,128)(2,1)S(1)} %get-tuple-element.30.refs_1_, bf16[64,512]{1,0:T(8,128)(2,1)S(1)} %collective-permute-done.refs_2_, ...), custom_call_target="tpu_custom_call" | custom-call | flops 1 | bytes 1 | tf_op jit(solution)/shard_map/pallas_call | solution.py:60
  54.2 3.8 %all-to-all-start.2 = ((bf16[8,160,512]{2,1,0:T(8,128)(2,1)}), bf16[8,160,512]{2,1,0:T(8,128)(2,1)S(1)}, u32[]{:S(2)}, u32[]{:S(2)}) async-start(bf16[8,160,512]{2,1,0:T(8,128)(2,1)} %get-tuple-element.33.refs_3_), calls=%async_computation.2 | async-start | bytes 2621440 | tf_op jit(solution)/shard_map/all_to_all | solution.py:403
  57.9 1.1 shard_map.98.refs_3_
  59.1 0.1 collective-permute-start.3
  59.2 1.1 shard_map.99.refs_0_
  60.3 0.0 copy-start.1
  60.3 1.5 %collective-permute-done.3.refs_1_ = bf16[1024,512]{1,0:T(8,128)(2,1)S(1)} collective-permute-done((bf16[1024,512]{1,0:T(8,128)(2,1)S(1)}, bf16[1024,512]{1,0:T(8,128)(2,1)S(1)}, u32[]{:S(2)}, u32[]{:S(2)}) %collective-permute-start.3) | collective-permute-done | bytes 1048608 | tf_op jit(solution)/shard_map/ppermute | solution.py:399
  61.8 0.2 shard_map.100
  62.0 1.6 %collective-permute-start.4 = (bf16[512,512]{1,0:T(8,128)(2,1)S(1)}, bf16[512,512]{1,0:T(8,128)(2,1)S(1)}, u32[]{:S(2)}, u32[]{:S(2)}) collective-permute-start(bf16[512,512]{1,0:T(8,128)(2,1)S(1)} %get-tuple-element.36), channel_id=1, source_target_pairs={{0,2},{1,3},{2,0},{3,1},{4,6},{5,7},{6,4},{7,5},{8,10},{9,11},{10,... | collective-permute-start | bytes 1572872 | tf_op jit(solution)/shard_map/ppermute | solution.py:399
  63.6 12.5 %collective-permute-done.4.refs_1_ = bf16[512,512]{1,0:T(8,128)(2,1)S(1)} collective-permute-done((bf16[512,512]{1,0:T(8,128)(2,1)S(1)}, bf16[512,512]{1,0:T(8,128)(2,1)S(1)}, u32[]{:S(2)}, u32[]{:S(2)}) %collective-permute-start.4) | collective-permute-done | bytes 524320 | tf_op jit(solution)/shard_map/ppermute | solution.py:399
  76.1 0.1 shard_map.101
  76.2 0.0 copy-start.6
  76.2 1.8 %collective-permute-start.5 = (bf16[256,512]{1,0:T(8,128)(2,1)S(1)}, bf16[256,512]{1,0:T(8,128)(2,1)S(1)}, u32[]{:S(2)}, u32[]{:S(2)}) collective-permute-start(bf16[256,512]{1,0:T(8,128)(2,1)S(1)} %get-tuple-element.37.refs_3_), channel_id=1, source_target_pairs={{0,4},{4,0},{8,12},{12,8},{16,20},{20,16},{24,28},{28,24},{1,5},{5... | collective-permute-start | bytes 786440 | tf_op jit(solution)/shard_map/ppermute | solution.py:399
  78.0 1.6 %shard_map.102.refs_2_.refs_4_ = bf16[1024,512]{1,0:T(8,128)(2,1)S(1)} custom-call(bf16[512,512]{1,0:T(8,128)(2,1)S(1)} %get-tuple-element.34.refs_0_, s32[1,512]{1,0:T(1,128)S(1)} %bitcast.12, bf16[4,512,512]{2,1,0:T(8,128)(2,1)S(1)} %copy-done.1, bf16[256,512]{1,0:T(8,128)(2,1)S(1)} %get-tuple-element.37.refs_3_), custom_call_target="tpu_custom_call" | custom-call | flops 1 | bytes 1 | tf_op jit(solution)/shard_map/pallas_call | solution.py:60
  79.6 6.4 %collective-permute-done.5.refs_1_ = bf16[256,512]{1,0:T(8,128)(2,1)S(1)} collective-permute-done((bf16[256,512]{1,0:T(8,128)(2,1)S(1)}, bf16[256,512]{1,0:T(8,128)(2,1)S(1)}, u32[]{:S(2)}, u32[]{:S(2)}) %collective-permute-start.5) | collective-permute-done | bytes 262176 | tf_op jit(solution)/shard_map/ppermute | solution.py:399
  86.0 4.0 %collective-permute-start.11 = (bf16[64,512]{1,0:T(8,128)(2,1)S(1)}, bf16[64,512]{1,0:T(8,128)(2,1)S(1)}, u32[]{:S(2)}, u32[]{:S(2)}) collective-permute-start(bf16[64,512]{1,0:T(8,128)(2,1)S(1)} %get-tuple-element.41), channel_id=1, source_target_pairs={{0,16},{4,20},{8,24},{12,28},{16,0},{20,4},{24,8},{28,12},{1,17},{... | collective-permute-start | bytes 196616 | tf_op jit(solution)/shard_map/ppermute | solution.py:399
  90.0 0.7 collective-permute-start.12
  90.7 0.0 collective-permute-start.10
  90.8 0.0 all-to-all-done.2.refs_2_
  90.8 1.6 %shard_map.104.refs_5_ = bf16[512,512]{1,0:T(8,128)(2,1)S(1)} custom-call(s32[1,1024]{1,0:T(1,128)S(1)} %get-tuple-element.28.refs_0_, s32[1,32]{1,0:T(1,128)S(1)} %copy-done.8, bf16[8,160,512]{2,1,0:T(8,128)(2,1)S(1)} %all-to-all-done.2.refs_2_, s32[1,512]{1,0:T(1,128)S(1)} %bitcast.14, bf16[1024,512]{1,0:T(8,128)(2,1)S(1)} %shard_map.102.refs_2_.refs_4_, ...), custom_call_target="tpu_custom_call" | custom-call | flops 1 | bytes 1 | tf_op jit(solution)/shard_map/pallas_call | solution.py:60
  92.4 0.1 collective-permute-start.6
  92.4 1.6 %shard_map.105.refs_0_.refs_4_ = f32[512,512]{1,0:T(8,128)S(1)} custom-call(s32[1,1024]{1,0:T(1,128)S(1)} %get-tuple-element.28.refs_0_, s32[1,32]{1,0:T(1,128)S(1)} %copy-done.8, bf16[8,160,512]{2,1,0:T(8,128)(2,1)S(1)} %all-to-all-done.2.refs_2_, s32[1,512]{1,0:T(1,128)S(1)} %bitcast.15, bf16[1024,512]{1,0:T(8,128)(2,1)S(1)} %shard_map.102.refs_2_.refs_4_, ...), custom_call_target="tpu_custom_call" | custom-call | flops 20000000000 | bytes 1 | tf_op jit(solution)/shard_map/pallas_call | solution.py:60
  94.0 0.3 collective-permute-done.6.refs_1_
  94.3 0.1 shard_map.106.mine_ref
  94.4 1.6 %collective-permute-start.8 = (bf16[512,512]{1,0:T(8,128)(2,1)S(1)}, bf16[512,512]{1,0:T(8,128)(2,1)S(1)}, u32[]{:S(2)}, u32[]{:S(2)}) collective-permute-start(bf16[512,512]{1,0:T(8,128)(2,1)S(1)} %shard_map.106.mine_ref), channel_id=1, source_target_pairs={{0,2},{1,3},{2,0},{3,1},{4,6},{5,7},{6,4},{7,5},{8,10},{9,11},{10,... | collective-permute-start | bytes 1572872 | tf_op jit(solution)/shard_map/ppermute | solution.py:399
  96.0 0.0 collective-permute-done.11.refs_2_
  96.0 0.1 collective-permute-done.12.refs_3_
  96.1 0.0 collective-permute-done.10.refs_1_
  96.1 3.1 %collective-permute-start.15 = (bf16[64,512]{1,0:T(8,128)(2,1)S(1)}, bf16[64,512]{1,0:T(8,128)(2,1)S(1)}, u32[]{:S(2)}, u32[]{:S(2)}) collective-permute-start(bf16[64,512]{1,0:T(8,128)(2,1)S(1)} %shard_map.107.refs_0_), channel_id=1, source_target_pairs={{0,24},{4,28},{8,16},{12,20},{16,8},{20,12},{24,0},{28,4},{1,25},{... | collective-permute-start | bytes 196616 | tf_op jit(solution)/shard_map/ppermute | solution.py:399
  99.2 0.6 collective-permute-start.14
  99.9 0.7 collective-permute-start.13
  100.6 1.7 %collective-permute-done.15.refs_3_ = bf16[64,512]{1,0:T(8,128)(2,1)S(1)} collective-permute-done((bf16[64,512]{1,0:T(8,128)(2,1)S(1)}, bf16[64,512]{1,0:T(8,128)(2,1)S(1)}, u32[]{:S(2)}, u32[]{:S(2)}) %collective-permute-start.15) | collective-permute-done | bytes 65568 | tf_op jit(solution)/shard_map/ppermute | solution.py:399
  102.3 3.7 %collective-permute-done.14.refs_2_ = bf16[64,512]{1,0:T(8,128)(2,1)S(1)} collective-permute-done((bf16[64,512]{1,0:T(8,128)(2,1)S(1)}, bf16[64,512]{1,0:T(8,128)(2,1)S(1)}, u32[]{:S(2)}, u32[]{:S(2)}) %collective-permute-start.14) | collective-permute-done | bytes 65568 | tf_op jit(solution)/shard_map/ppermute | solution.py:399
  106.1 0.6 collective-permute-start.17
  106.7 1.4 %collective-permute-start.16 = (bf16[256,512]{1,0:T(8,128)(2,1)S(1)}, bf16[256,512]{1,0:T(8,128)(2,1)S(1)}, u32[]{:S(2)}, u32[]{:S(2)}) collective-permute-start(bf16[256,512]{1,0:T(8,128)(2,1)S(1)} %shard_map.108.refs_0_), channel_id=1, source_target_pairs={{0,4},{4,0},{8,12},{12,8},{16,20},{20,16},{24,28},{28,24},{1,5},{5... | collective-permute-start | bytes 786440 | tf_op jit(solution)/shard_map/ppermute | solution.py:399
  108.1 0.5 collective-permute-done.8.over_ref
  108.5 0.0 collective-permute-start.9
  108.6 0.5 collective-permute-start.18
  109.0 5.2 %collective-permute-done.17.refs_2_.refs_0_ = bf16[256,512]{1,0:T(8,128)(2,1)S(1)} collective-permute-done((bf16[256,512]{1,0:T(8,128)(2,1)S(1)}, bf16[256,512]{1,0:T(8,128)(2,1)S(1)}, u32[]{:S(2)}, u32[]{:S(2)}) %collective-permute-start.17) | collective-permute-done | bytes 262176 | tf_op jit(solution)/shard_map/ppermute | solution.py:399
  114.3 0.3 collective-permute-done.16.refs_1_.refs_0_
  114.5 0.3 collective-permute-start.19
  114.8 1.4 %collective-permute-start.21 = (bf16[128,512]{1,0:T(8,128)(2,1)S(1)}, bf16[128,512]{1,0:T(8,128)(2,1)S(1)}, u32[]{:S(2)}, u32[]{:S(2)}) collective-permute-start(bf16[128,512]{1,0:T(8,128)(2,1)S(1)} %shard_map.110), channel_id=1, source_target_pairs={{0,2},{1,3},{2,0},{3,1},{4,6},{5,7},{6,4},{7,5},{8,10},{9,11},{10,... | collective-permute-start | bytes 393224 | tf_op jit(solution)/shard_map/ppermute | solution.py:399
  116.3 2.1 %collective-permute-start.22 = (bf16[128,512]{1,0:T(8,128)(2,1)S(1)}, bf16[128,512]{1,0:T(8,128)(2,1)S(1)}, u32[]{:S(2)}, u32[]{:S(2)}) collective-permute-start(bf16[128,512]{1,0:T(8,128)(2,1)S(1)} %shard_map.112), channel_id=1, source_target_pairs={{0,4},{4,0},{8,12},{12,8},{16,20},{20,16},{24,28},{28,24},{1,5},{5... | collective-permute-start | bytes 393224 | tf_op jit(solution)/shard_map/ppermute | solution.py:399
  118.4 2.6 %shard_map.109 = (f32[1024,512]{1,0:T(8,128)}, f32[4,512,512]{2,1,0:T(8,128)}, f32[8,128]{1,0:T(8,128)S(1)}) custom-call(bf16[512,512]{1,0:T(8,128)(2,1)S(1)} %shard_map.106.mine_ref, bf16[512,512]{1,0:T(8,128)(2,1)S(1)} %collective-permute-done.7.other_ref, bf16[512,512]{1,0:T(8,128)(2,1)S(1)} %collective-permute-done.8.over_ref, ...), custom_call_target="tpu_custom_call" | custom-call | tf_op jit(solution)/shard_map/pallas_call | solution.py:576
  121.1 0.1 collective-permute-start.23
  121.2 0.6 collective-permute-done.22.refs_0_
  121.9 0.1 collective-permute-start.24
  121.9 0.6 collective-permute-done.23.refs_2_
  122.5 0.7 collective-permute-done.24.refs_3_
  123.3 1.1 shard_map.114
  (31 shorter events, 0.2 us)
Async XLA Ops:
  0.6 17.0 %copy-start = (bf16[1024,512]{1,0:T(8,128)(2,1)S(1)}, bf16[1024,512]{1,0:T(8,128)(2,1)}, u32[]{:S(2)}) copy-start(bf16[1024,512]{1,0:T(8,128)(2,1)} %refs_1_.1) | copy-start | bytes 3145732
  3.3 14.3 %all-to-all-start = ((bf16[8,8,640]{2,1,0:T(8,128)(2,1)}), bf16[8,8,640]{2,1,0:T(8,128)(2,1)S(1)}, u32[]{:S(2)}, u32[]{:S(2)}) async-start(bf16[8,8,640]{2,1,0:T(8,128)(2,1)} %get-tuple-element.25), calls=%async_computation | async-start | bytes 163840 | tf_op jit(solution)/shard_map/all_to_all | solution.py:403
  10.6 39.6 %copy-start.7 = (s32[1,512]{1,0:T(1,128)S(1)}, s32[1,512]{1,0:T(1,128)}, u32[]{:S(2)}) copy-start(s32[1,512]{1,0:T(1,128)} %get-tuple-element.26.refs_4_.refs_0_) | copy-start | bytes 6148
  17.6 1.0 copy-start.2
  18.7 31.5 %copy-start.4 = (bf16[512,512]{1,0:T(8,128)(2,1)S(1)}, bf16[512,512]{1,0:T(8,128)(2,1)}, u32[]{:S(2)}) copy-start(bf16[512,512]{1,0:T(8,128)(2,1)} %get-tuple-element.32.refs_6_) | copy-start | bytes 1572868
  21.3 28.9 %all-to-all-start.1 = ((bf16[8,128,512]{2,1,0:T(8,128)(2,1)}), bf16[8,128,512]{2,1,0:T(8,128)(2,1)S(1)}, u32[]{:S(2)}, u32[]{:S(2)}) async-start(bf16[8,128,512]{2,1,0:T(8,128)(2,1)} %bitcast.5), calls=%async_computation.1 | async-start | bytes 2097152 | tf_op jit(solution)/shard_map/all_to_all | solution.py:403
  24.9 4.4 %collective-permute-start.2 = (bf16[64,512]{1,0:T(8,128)(2,1)S(1)}, bf16[64,512]{1,0:T(8,128)(2,1)S(1)}, u32[]{:S(2)}, u32[]{:S(2)}) collective-permute-start(bf16[64,512]{1,0:T(8,128)(2,1)S(1)} %get-tuple-element.30.refs_1_), channel_id=1, source_target_pairs={{0,3},{1,2},{2,1},{3,0},{4,7},{5,6},{6,5},{7,4},{8,11},{9,10},{10,... | collective-permute-start | bytes 196616 | tf_op jit(solution)/shard_map/ppermute | solution.py:399
  24.9 5.8 %collective-permute-start.1 = (bf16[64,512]{1,0:T(8,128)(2,1)S(1)}, bf16[64,512]{1,0:T(8,128)(2,1)S(1)}, u32[]{:S(2)}, u32[]{:S(2)}) collective-permute-start(bf16[64,512]{1,0:T(8,128)(2,1)S(1)} %get-tuple-element.30.refs_1_), channel_id=1, source_target_pairs={{0,2},{1,3},{2,0},{3,1},{4,6},{5,7},{6,4},{7,5},{8,10},{9,11},{10,... | collective-permute-start | bytes 196616 | tf_op jit(solution)/shard_map/ppermute | solution.py:399
  26.5 4.2 %collective-permute-start = (bf16[64,512]{1,0:T(8,128)(2,1)S(1)}, bf16[64,512]{1,0:T(8,128)(2,1)S(1)}, u32[]{:S(2)}, u32[]{:S(2)}) collective-permute-start(bf16[64,512]{1,0:T(8,128)(2,1)S(1)} %get-tuple-element.30.refs_1_), channel_id=1, source_target_pairs={{0,1},{1,0},{2,3},{3,2},{4,5},{5,4},{6,7},{7,6},{8,9},{9,8},{10,11... | collective-permute-start | bytes 196616 | tf_op jit(solution)/shard_map/ppermute | solution.py:399
  50.2 7.7 %copy-start.3 = (bf16[512,512]{1,0:T(8,128)(2,1)S(1)}, bf16[512,512]{1,0:T(8,128)(2,1)}, u32[]{:S(2)}) copy-start(bf16[512,512]{1,0:T(8,128)(2,1)} %get-tuple-element.27.refs_2_.refs_1_) | copy-start | bytes 1572868
  50.2 7.8 %copy-start.5 = (s32[512]{0:T(512)S(1)}, s32[512]{0:T(512)}, u32[]{:S(2)}) copy-start(s32[512]{0:T(512)} %param.10) | copy-start | bytes 6148
  54.2 36.6 %all-to-all-start.2 = ((bf16[8,160,512]{2,1,0:T(8,128)(2,1)}), bf16[8,160,512]{2,1,0:T(8,128)(2,1)S(1)}, u32[]{:S(2)}, u32[]{:S(2)}) async-start(bf16[8,160,512]{2,1,0:T(8,128)(2,1)} %get-tuple-element.33.refs_3_), calls=%async_computation.2 | async-start | bytes 2621440 | tf_op jit(solution)/shard_map/all_to_all | solution.py:403
  59.1 2.7 %collective-permute-start.3 = (bf16[1024,512]{1,0:T(8,128)(2,1)S(1)}, bf16[1024,512]{1,0:T(8,128)(2,1)S(1)}, u32[]{:S(2)}, u32[]{:S(2)}) collective-permute-start(bf16[1024,512]{1,0:T(8,128)(2,1)S(1)} %shard_map.98.refs_3_), channel_id=1, source_target_pairs={{0,1},{1,0},{2,3},{3,2},{4,5},{5,4},{6,7},{7,6},{8,9},{9,8},{10,11... | collective-permute-start | bytes 3145736 | tf_op jit(solution)/shard_map/ppermute | solution.py:399
  60.3 17.7 %copy-start.1 = (bf16[4,512,512]{2,1,0:T(8,128)(2,1)S(1)}, bf16[4,512,512]{2,1,0:T(8,128)(2,1)}, u32[]{:S(2)}) copy-start(bf16[4,512,512]{2,1,0:T(8,128)(2,1)} %refs_2_.3) | copy-start | bytes 6291460
  62.0 14.0 %collective-permute-start.4 = (bf16[512,512]{1,0:T(8,128)(2,1)S(1)}, bf16[512,512]{1,0:T(8,128)(2,1)S(1)}, u32[]{:S(2)}, u32[]{:S(2)}) collective-permute-start(bf16[512,512]{1,0:T(8,128)(2,1)S(1)} %get-tuple-element.36), channel_id=1, source_target_pairs={{0,2},{1,3},{2,0},{3,1},{4,6},{5,7},{6,4},{7,5},{8,10},{9,11},{10,... | collective-permute-start | bytes 1572872 | tf_op jit(solution)/shard_map/ppermute | solution.py:399
  76.2 14.6 %copy-start.6 = (s32[512]{0:T(512)S(1)}, s32[512]{0:T(512)}, u32[]{:S(2)}) copy-start(s32[512]{0:T(512)} %param.9) | copy-start | bytes 6148
  76.2 14.6 %copy-start.8 = (s32[1,32]{1,0:T(1,128)S(1)}, s32[1,32]{1,0:T(1,128)}, u32[]{:S(2)}) copy-start(s32[1,32]{1,0:T(1,128)} %get-tuple-element.29.refs_1_) | copy-start | bytes 388
  76.2 9.8 %collective-permute-start.5 = (bf16[256,512]{1,0:T(8,128)(2,1)S(1)}, bf16[256,512]{1,0:T(8,128)(2,1)S(1)}, u32[]{:S(2)}, u32[]{:S(2)}) collective-permute-start(bf16[256,512]{1,0:T(8,128)(2,1)S(1)} %get-tuple-element.37.refs_3_), channel_id=1, source_target_pairs={{0,4},{4,0},{8,12},{12,8},{16,20},{20,16},{24,28},{28,24},{1,5},{5... | collective-permute-start | bytes 786440 | tf_op jit(solution)/shard_map/ppermute | solution.py:399
  86.0 10.0 %collective-permute-start.11 = (bf16[64,512]{1,0:T(8,128)(2,1)S(1)}, bf16[64,512]{1,0:T(8,128)(2,1)S(1)}, u32[]{:S(2)}, u32[]{:S(2)}) collective-permute-start(bf16[64,512]{1,0:T(8,128)(2,1)S(1)} %get-tuple-element.41), channel_id=1, source_target_pairs={{0,16},{4,20},{8,24},{12,28},{16,0},{20,4},{24,8},{28,12},{1,17},{... | collective-permute-start | bytes 196616 | tf_op jit(solution)/shard_map/ppermute | solution.py:399
  90.0 6.1 %collective-permute-start.12 = (bf16[64,512]{1,0:T(8,128)(2,1)S(1)}, bf16[64,512]{1,0:T(8,128)(2,1)S(1)}, u32[]{:S(2)}, u32[]{:S(2)}) collective-permute-start(bf16[64,512]{1,0:T(8,128)(2,1)S(1)} %get-tuple-element.42), channel_id=1, source_target_pairs={{0,24},{4,28},{8,16},{12,20},{16,8},{20,12},{24,0},{28,4},{1,25},{... | collective-permute-start | bytes 196616 | tf_op jit(solution)/shard_map/ppermute | solution.py:399
  90.7 5.3 %collective-permute-start.10 = (bf16[64,512]{1,0:T(8,128)(2,1)S(1)}, bf16[64,512]{1,0:T(8,128)(2,1)S(1)}, u32[]{:S(2)}, u32[]{:S(2)}) collective-permute-start(bf16[64,512]{1,0:T(8,128)(2,1)S(1)} %get-tuple-element.39.refs_5_), channel_id=1, source_target_pairs={{0,8},{4,12},{8,0},{12,4},{16,24},{20,28},{24,16},{28,20},{1,9},{5... | collective-permute-start | bytes 196616 | tf_op jit(solution)/shard_map/ppermute | solution.py:399
  92.4 2.0 %collective-permute-start.6 = (bf16[512,512]{1,0:T(8,128)(2,1)S(1)}, bf16[512,512]{1,0:T(8,128)(2,1)S(1)}, u32[]{:S(2)}, u32[]{:S(2)}) collective-permute-start(bf16[512,512]{1,0:T(8,128)(2,1)S(1)} %shard_map.104.refs_5_), channel_id=1, source_target_pairs={{0,1},{1,0},{2,3},{3,2},{4,5},{5,4},{6,7},{7,6},{8,9},{9,8},{10,11... | collective-permute-start | bytes 1572872 | tf_op jit(solution)/shard_map/ppermute | solution.py:399
  94.4 14.1 %collective-permute-start.8 = (bf16[512,512]{1,0:T(8,128)(2,1)S(1)}, bf16[512,512]{1,0:T(8,128)(2,1)S(1)}, u32[]{:S(2)}, u32[]{:S(2)}) collective-permute-start(bf16[512,512]{1,0:T(8,128)(2,1)S(1)} %shard_map.106.mine_ref), channel_id=1, source_target_pairs={{0,2},{1,3},{2,0},{3,1},{4,6},{5,7},{6,4},{7,5},{8,10},{9,11},{10,... | collective-permute-start | bytes 1572872 | tf_op jit(solution)/shard_map/ppermute | solution.py:399
  96.1 6.2 %collective-permute-start.15 = (bf16[64,512]{1,0:T(8,128)(2,1)S(1)}, bf16[64,512]{1,0:T(8,128)(2,1)S(1)}, u32[]{:S(2)}, u32[]{:S(2)}) collective-permute-start(bf16[64,512]{1,0:T(8,128)(2,1)S(1)} %shard_map.107.refs_0_), channel_id=1, source_target_pairs={{0,24},{4,28},{8,16},{12,20},{16,8},{20,12},{24,0},{28,4},{1,25},{... | collective-permute-start | bytes 196616 | tf_op jit(solution)/shard_map/ppermute | solution.py:399
  99.2 6.8 %collective-permute-start.14 = (bf16[64,512]{1,0:T(8,128)(2,1)S(1)}, bf16[64,512]{1,0:T(8,128)(2,1)S(1)}, u32[]{:S(2)}, u32[]{:S(2)}) collective-permute-start(bf16[64,512]{1,0:T(8,128)(2,1)S(1)} %shard_map.107.refs_0_), channel_id=1, source_target_pairs={{0,16},{4,20},{8,24},{12,28},{16,0},{20,4},{24,8},{28,12},{1,17},{... | collective-permute-start | bytes 196616 | tf_op jit(solution)/shard_map/ppermute | solution.py:399
  99.9 6.2 %collective-permute-start.13 = (bf16[64,512]{1,0:T(8,128)(2,1)S(1)}, bf16[64,512]{1,0:T(8,128)(2,1)S(1)}, u32[]{:S(2)}, u32[]{:S(2)}) collective-permute-start(bf16[64,512]{1,0:T(8,128)(2,1)S(1)} %shard_map.107.refs_0_), channel_id=1, source_target_pairs={{0,8},{4,12},{8,0},{12,4},{16,24},{20,28},{24,16},{28,20},{1,9},{5... | collective-permute-start | bytes 196616 | tf_op jit(solution)/shard_map/ppermute | solution.py:399
  106.1 8.2 %collective-permute-start.17 = (bf16[256,512]{1,0:T(8,128)(2,1)S(1)}, bf16[256,512]{1,0:T(8,128)(2,1)S(1)}, u32[]{:S(2)}, u32[]{:S(2)}) collective-permute-start(bf16[256,512]{1,0:T(8,128)(2,1)S(1)} %shard_map.108.refs_0_), channel_id=1, source_target_pairs={{0,2},{1,3},{2,0},{3,1},{4,6},{5,7},{6,4},{7,5},{8,10},{9,11},{10,... | collective-permute-start | bytes 786440 | tf_op jit(solution)/shard_map/ppermute | solution.py:399
  106.7 7.9 %collective-permute-start.16 = (bf16[256,512]{1,0:T(8,128)(2,1)S(1)}, bf16[256,512]{1,0:T(8,128)(2,1)S(1)}, u32[]{:S(2)}, u32[]{:S(2)}) collective-permute-start(bf16[256,512]{1,0:T(8,128)(2,1)S(1)} %shard_map.108.refs_0_), channel_id=1, source_target_pairs={{0,4},{4,0},{8,12},{12,8},{16,20},{20,16},{24,28},{28,24},{1,5},{5... | collective-permute-start | bytes 786440 | tf_op jit(solution)/shard_map/ppermute | solution.py:399
  108.1 10.4 %collective-permute-start.7 = (bf16[512,512]{1,0:T(8,128)(2,1)S(1)}, bf16[512,512]{1,0:T(8,128)(2,1)S(1)}, u32[]{:S(2)}, u32[]{:S(2)}) collective-permute-start(bf16[512,512]{1,0:T(8,128)(2,1)S(1)} %shard_map.106.mine_ref), channel_id=1, source_target_pairs={{0,1},{1,0},{2,3},{3,2},{4,5},{5,4},{6,7},{7,6},{8,9},{9,8},{10,11... | collective-permute-start | bytes 1572872 | tf_op jit(solution)/shard_map/ppermute | solution.py:399
  108.5 9.9 %collective-permute-start.9 = (bf16[512,512]{1,0:T(8,128)(2,1)S(1)}, bf16[512,512]{1,0:T(8,128)(2,1)S(1)}, u32[]{:S(2)}, u32[]{:S(2)}) collective-permute-start(bf16[512,512]{1,0:T(8,128)(2,1)S(1)} %collective-permute-done.8.over_ref), channel_id=1, source_target_pairs={{0,1},{1,0},{2,3},{3,2},{4,5},{5,4},{6,7},{7,6},{8,9},{9,8},{10,11... | collective-permute-start | bytes 1572872 | tf_op jit(solution)/shard_map/ppermute | solution.py:399
  108.6 6.2 %collective-permute-start.18 = (bf16[256,512]{1,0:T(8,128)(2,1)S(1)}, bf16[256,512]{1,0:T(8,128)(2,1)S(1)}, u32[]{:S(2)}, u32[]{:S(2)}) collective-permute-start(bf16[256,512]{1,0:T(8,128)(2,1)S(1)} %shard_map.108.refs_0_), channel_id=1, source_target_pairs={{0,1},{1,0},{2,3},{3,2},{4,5},{5,4},{6,7},{7,6},{8,9},{9,8},{10,11... | collective-permute-start | bytes 786440 | tf_op jit(solution)/shard_map/ppermute | solution.py:399
  114.3 2.0 %collective-permute-start.20 = (bf16[256,512]{1,0:T(8,128)(2,1)S(1)}, bf16[256,512]{1,0:T(8,128)(2,1)S(1)}, u32[]{:S(2)}, u32[]{:S(2)}) collective-permute-start(bf16[256,512]{1,0:T(8,128)(2,1)S(1)} %collective-permute-done.17.refs_2_.refs_0_), channel_id=1, source_target_pairs={{0,1},{1,0},{2,3},{3,2},{4,5},{5,4},{6,7},{7,6},{8,9},{9,8},{10,11... | collective-permute-start | bytes 786440 | tf_op jit(solution)/shard_map/ppermute | solution.py:399
  114.5 3.9 %collective-permute-start.19 = (bf16[256,512]{1,0:T(8,128)(2,1)S(1)}, bf16[256,512]{1,0:T(8,128)(2,1)S(1)}, u32[]{:S(2)}, u32[]{:S(2)}) collective-permute-start(bf16[256,512]{1,0:T(8,128)(2,1)S(1)} %collective-permute-done.16.refs_1_.refs_0_), channel_id=1, source_target_pairs={{0,1},{1,0},{2,3},{3,2},{4,5},{5,4},{6,7},{7,6},{8,9},{9,8},{10,11... | collective-permute-start | bytes 786440 | tf_op jit(solution)/shard_map/ppermute | solution.py:399
  114.8 6.3 %collective-permute-start.21 = (bf16[128,512]{1,0:T(8,128)(2,1)S(1)}, bf16[128,512]{1,0:T(8,128)(2,1)S(1)}, u32[]{:S(2)}, u32[]{:S(2)}) collective-permute-start(bf16[128,512]{1,0:T(8,128)(2,1)S(1)} %shard_map.110), channel_id=1, source_target_pairs={{0,2},{1,3},{2,0},{3,1},{4,6},{5,7},{6,4},{7,5},{8,10},{9,11},{10,... | collective-permute-start | bytes 393224 | tf_op jit(solution)/shard_map/ppermute | solution.py:399
  116.3 5.5 %collective-permute-start.22 = (bf16[128,512]{1,0:T(8,128)(2,1)S(1)}, bf16[128,512]{1,0:T(8,128)(2,1)S(1)}, u32[]{:S(2)}, u32[]{:S(2)}) collective-permute-start(bf16[128,512]{1,0:T(8,128)(2,1)S(1)} %shard_map.112), channel_id=1, source_target_pairs={{0,4},{4,0},{8,12},{12,8},{16,20},{20,16},{24,28},{28,24},{1,5},{5... | collective-permute-start | bytes 393224 | tf_op jit(solution)/shard_map/ppermute | solution.py:399
  121.1 1.4 %collective-permute-start.23 = (bf16[128,512]{1,0:T(8,128)(2,1)S(1)}, bf16[128,512]{1,0:T(8,128)(2,1)S(1)}, u32[]{:S(2)}, u32[]{:S(2)}) collective-permute-start(bf16[128,512]{1,0:T(8,128)(2,1)S(1)} %shard_map.111.refs_0_), channel_id=1, source_target_pairs={{0,1},{1,0},{2,3},{3,2},{4,5},{5,4},{6,7},{7,6},{8,9},{9,8},{10,11... | collective-permute-start | bytes 393224 | tf_op jit(solution)/shard_map/ppermute | solution.py:399
  121.9 1.4 %collective-permute-start.24 = (bf16[128,512]{1,0:T(8,128)(2,1)S(1)}, bf16[128,512]{1,0:T(8,128)(2,1)S(1)}, u32[]{:S(2)}, u32[]{:S(2)}) collective-permute-start(bf16[128,512]{1,0:T(8,128)(2,1)S(1)} %shard_map.113.refs_1_), channel_id=1, source_target_pairs={{0,1},{1,0},{2,3},{3,2},{4,5},{5,4},{6,7},{7,6},{8,9},{9,8},{10,11... | collective-permute-start | bytes 393224 | tf_op jit(solution)/shard_map/ppermute | solution.py:399

commit v10 on v9

--- a/solution.py
+++ b/solution.py
@@ -273,15 +273,20 @@
     sent_ref[...] = (own_ref[half:] + got_ref[half:].astype(F32)).astype(BF)
 
 
-def head_kernel(grad_ref, rel_ref, operators, out_ref):
+def head_kernel(special, grad_ref, rel_ref, operators, head_ref, *out_refs):
     rel = as_column(rel_ref[...])
     grad = grad_ref[...]
-    edges = grad.shape[0]
     total = jnp.zeros(grad.shape, F32)
     for relation in range(operators.shape[0]):
         picked = jnp.where(rel == relation, grad, jnp.zeros_like(grad))
         total = total + dot_t1(picked, operators[relation])
-    out_ref[:edges], out_ref[edges:] = split(total)
+    high, low = split(total)
+    head = head_ref[...]
+    for turn, out_ref in enumerate(out_refs):
+        count = out_ref.shape[0]
+        base = ((lax.axis_index("rep") & 1) ^ 1 ^ turn) * count if special else 0
+        heads = hot((iota((count, head.shape[1]), 0) + base) == head)
+        out_ref[...] = (dot(heads, high) + dot(heads, low)).astype(BF)
 
 
 def spread_kernel(own_ref, got_ref, *out_refs):
@@ -338,7 +343,7 @@
         copy.wait()
 
 
-def add_kernel(halves, away, ids_ref, neg_ref, back_ref, take, *out_refs):
+def add_kernel(halves, away, ids_ref, neg_ref, back_ref, base_ref, out_ref):
     parts = back_ref.shape[0]
     cap = ids_ref.shape[1] // parts
     tails = jnp.concatenate([back_ref[index, :cap] for index in range(parts)], axis=0)
@@ -347,21 +352,15 @@
         negs = negs + back_ref[index, cap:].astype(F32)
     high, low = split(negs)
     negs = jnp.concatenate([high, low], axis=0)
-    head = take(0)[...]
-    grads = take(1)
-    for out_ref in out_refs:
-        count = out_ref.shape[0]
-        base = ((lax.axis_index("rep") & 1) ^ away) * count if halves else 0
-
-        def pick(row):
-            return hot((iota((count, row.shape[1]), 0) + base) == row)
-
-        total = dot(pick(ids_ref[...]), tails)
-        heads = pick(head)
-        total = total + dot(jnp.concatenate([heads, heads], axis=1), grads[...])
-        own = pick(neg_ref[...])
-        total = total + dot(jnp.concatenate([own, own], axis=1), negs)
-        out_ref[...] = total.astype(out_ref.dtype)
+    count = out_ref.shape[0]
+    base = ((lax.axis_index("rep") & 1) ^ away) * count if halves else 0
+
+    def pick(row):
+        return hot((iota((count, row.shape[1]), 0) + base) == row)
+
+    own = pick(neg_ref[...])
+    total = dot(pick(ids_ref[...]), tails) + dot(jnp.concatenate([own, own], axis=1), negs)
+    out_ref[...] = (total + base_ref[...].astype(F32)).astype(out_ref.dtype)
 
 
 def both_kernel(kept_ref, arrived_ref, out_ref):
@@ -479,24 +478,24 @@
     away = terms(0, (back,))
     keep = terms(4, (away,))
 
-    def head_terms(after):
+    def head_terms(count, after):
         return call(
-            head_kernel,
-            [((2 * edges, columns), BF)],
+            functools.partial(head_kernel, special),
+            [((ent_dev // count, columns), BF)] * count,
             (),
-            (grad, rel, relations),
+            (grad, rel, relations, head),
             (),
             after,
             cost=0,
-        )[0]
-
-    def add(away, outs, after, cost=0):
+        )
+
+    def add(away, base, outs, after, cost=0):
         return call(
             functools.partial(add_kernel, special, away),
             outs,
             (),
-            (asked, neg_own, returned),
-            (head, head_grads),
+            (asked, neg_own, returned, base),
+            (),
             after,
             cost=cost,
         )
@@ -504,8 +503,8 @@
     if not special:
         whole = jnp.concatenate([away, keep], axis=0)
         whole = whole.reshape(count, columns, columns)
-        head_grads = head_terms(())
-        (added,) = add(0, [((ent_dev, columns), F32)], ())
+        (base,) = head_terms(1, ())
+        (added,) = add(0, base, [((ent_dev, columns), F32)], ())
         entity_grad = lax.psum(added, "rep")
         return entity_grad, lax.psum(whole, ("dom", "rep")), loss.reshape(edges)
 
@@ -533,20 +532,20 @@
         (own, over_y(sent)),
         cost=0,
     )
-    head_grads = head_terms((sent,))
+    base_away, base_kept = head_terms(2, (sent,))
     own, *sent = call(
         spread_kernel,
         [((quarter, columns), F32)] + [((quarter, columns), BF)] * 3,
         (),
         (own, over_x(sent)),
         (),
-        (head_grads,),
+        (base_kept,),
         cost=0,
     )
     met = [flip(v, "dom", 8, 2 * (k + 1)) for k, v in enumerate(sent)]
     rows_half = ent_dev // 2
-    (leaving,) = add(1, [((rows_half, columns), BF)], (sent[0],))
-    (kept,) = add(0, [((rows_half, columns), F32)], (leaving,), 20)
+    (leaving,) = add(1, base_away, [((rows_half, columns), BF)], (sent[0],))
+    (kept,) = add(0, base_kept, [((rows_half, columns), F32)], (leaving,), 20)
     arrived = over_core(leaving)
     (own,) = call(
         sum_kernel, [((quarter, columns), BF)], (), (own, *met), (), (kept,), cost=100

time: 125 us -> 124 us (level)
  no operation moved by 1% of the time
where the time goes in v10:
time: 124 us
  waiting for transfers between devices  59.4 us (48%)
  starting transfers between devices  37.5 us (30%)
  Pallas kernels  24.8 us (20%)
    ppermute x25, waiting for transfers between devices, flip(): return lax.ppermute(x, axis, [(i, i ^ bit) for i in range(size)])  37.3 us
    ppermute x25, starting transfers between devices, flip(): return lax.ppermute(x, axis, [(i, i ^ bit) for i in range(size)])  22.9 us
    all_to_all x3, waiting for transfers between devices, exchange(): return lax.all_to_all(x, 'dom', split_axis=0, concat_axis=0, tiled=True)  22 us
    pallas_call x19, Pallas kernels, call(): pl.pallas_call(kernel, out_shape=[jax.ShapeDtypeStruct(out[0], out[1]) fo...  21 us
    all_to_all x3, starting transfers between devices, exchange(): return lax.all_to_all(x, 'dom', split_axis=0, concat_axis=0, tiled=True)  14.6 us
    pallas_call x1, Pallas kernels, local(): pl.pallas_call(functools.partial(join_kernel, [places[k] for k in early])...  2.65 us
  transfers between devices with their start and end apart: 28, of which 17 were waited for; matrix products, arithmetic and copies ran while one was open for 0% of the time, Pallas kernels for 12%

profile of v10, /device:TPU:0, one launch (start us, length us, event | category | flops | bytes accessed | tf_op | source)
XLA Modules:
  0.0 123.8 jit_solution(11965075482973043233)
XLA Ops:
  0.6 0.0 copy-start
  0.6 2.7 %shard_map.94 = (s32[1,512]{1,0:T(1,128)}, s32[1,32]{1,0:T(1,128)}, bf16[8,8,640]{2,1,0:T(8,128)(2,1)}) custom-call(s32[1,512]{1,0:T(1,128)} %bitcast.15, s32[1,512]{1,0:T(1,128)} %bitcast.16, s32[1,32]{1,0:T(1,128)} %bitcast.17, bf16[1024,512]{1,0:T(8,128)(2,1)} %refs_1_.1), custom_call_target="tpu_custom_call" | custom-call | flops 1 | bytes 1 | tf_op jit(solution)/shard_map/pallas_call | solution.py:60
  3.3 7.3 %all-to-all-start = ((bf16[8,8,640]{2,1,0:T(8,128)(2,1)}), bf16[8,8,640]{2,1,0:T(8,128)(2,1)S(1)}, u32[]{:S(2)}, u32[]{:S(2)}) async-start(bf16[8,8,640]{2,1,0:T(8,128)(2,1)} %get-tuple-element.27), calls=%async_computation | async-start | bytes 163840 | tf_op jit(solution)/shard_map/all_to_all | solution.py:402
  10.6 4.4 %shard_map.95 = (bf16[512,512]{1,0:T(8,128)(2,1)}, bf16[512,512]{1,0:T(8,128)(2,1)}) custom-call(s32[1,512]{1,0:T(1,128)} %bitcast.13, s32[1,512]{1,0:T(1,128)} %bitcast.9, bf16[1024,512]{1,0:T(8,128)(2,1)} %refs_1_.1, bf16[4,512,512]{2,1,0:T(8,128)(2,1)} %refs_2_.3, s32[1,512]{1,0:T(1,128)} %get-tuple-element.28.refs_4_.refs_0_), custom_call_target="tpu_custom_call" | custom-call | flops 1 | bytes 1 | tf_op jit(solution)/shard_map/pallas_call | solution.py:60
  15.0 2.6 %all-to-all-done.refs_0_ = bf16[8,8,640]{2,1,0:T(8,128)(2,1)S(1)} async-done(((bf16[8,8,640]{2,1,0:T(8,128)(2,1)}), bf16[8,8,640]{2,1,0:T(8,128)(2,1)S(1)}, u32[]{:S(2)}, u32[]{:S(2)}) %all-to-all-start) | async-done | bytes 81952 | tf_op jit(solution)/shard_map/all_to_all | solution.py:402
  17.6 1.0 copy-done.2
  18.7 2.6 %shard_map.96 = (s32[1,1024]{1,0:T(1,128)S(1)}, bf16[1024,512]{1,0:T(8,128)(2,1)}, bf16[64,512]{1,0:T(8,128)(2,1)S(1)}) custom-call(bf16[8,8,640]{2,1,0:T(8,128)(2,1)S(1)} %all-to-all-done.refs_0_, bf16[1024,512]{1,0:T(8,128)(2,1)S(1)} %copy-done, bf16[512,512]{1,0:T(8,128)(2,1)S(1)} %copy-done.2), custom_call_target="tpu_custom_call" | custom-call | flops 1 | bytes 1 | tf_op jit(solution)/shard_map/pallas_call | solution.py:60
  21.3 3.6 %all-to-all-start.1 = ((bf16[8,128,512]{2,1,0:T(8,128)(2,1)}), bf16[8,128,512]{2,1,0:T(8,128)(2,1)S(1)}, u32[]{:S(2)}, u32[]{:S(2)}) async-start(bf16[8,128,512]{2,1,0:T(8,128)(2,1)} %bitcast.5), calls=%async_computation.1 | async-start | bytes 2097152 | tf_op jit(solution)/shard_map/all_to_all | solution.py:402
  24.9 0.1 collective-permute-start.2
  24.9 1.6 %collective-permute-start.1 = (bf16[64,512]{1,0:T(8,128)(2,1)S(1)}, bf16[64,512]{1,0:T(8,128)(2,1)S(1)}, u32[]{:S(2)}, u32[]{:S(2)}) collective-permute-start(bf16[64,512]{1,0:T(8,128)(2,1)S(1)} %get-tuple-element.32.refs_1_), channel_id=1, source_target_pairs={{0,2},{1,3},{2,0},{3,1},{4,6},{5,7},{6,4},{7,5},{8,10},{9,11},{10,... | collective-permute-start | bytes 196616 | tf_op jit(solution)/shard_map/ppermute | solution.py:398
  26.5 0.3 collective-permute-start
  26.8 2.4 %collective-permute-done.2.refs_4_ = bf16[64,512]{1,0:T(8,128)(2,1)S(1)} collective-permute-done((bf16[64,512]{1,0:T(8,128)(2,1)S(1)}, bf16[64,512]{1,0:T(8,128)(2,1)S(1)}, u32[]{:S(2)}, u32[]{:S(2)}) %collective-permute-start.2) | collective-permute-done | bytes 65568 | tf_op jit(solution)/shard_map/ppermute | solution.py:398
  29.2 1.5 %collective-permute-done.1.refs_3_ = bf16[64,512]{1,0:T(8,128)(2,1)S(1)} collective-permute-done((bf16[64,512]{1,0:T(8,128)(2,1)S(1)}, bf16[64,512]{1,0:T(8,128)(2,1)S(1)}, u32[]{:S(2)}, u32[]{:S(2)}) %collective-permute-start.1) | collective-permute-done | bytes 65568 | tf_op jit(solution)/shard_map/ppermute | solution.py:398
  30.7 0.0 collective-permute-done.refs_2_
  30.7 19.4 %all-to-all-done.1 = bf16[8,128,512]{2,1,0:T(8,128)(2,1)S(1)} async-done(((bf16[8,128,512]{2,1,0:T(8,128)(2,1)}), bf16[8,128,512]{2,1,0:T(8,128)(2,1)S(1)}, u32[]{:S(2)}, u32[]{:S(2)}) %all-to-all-start.1) | async-done | bytes 1048608 | tf_op jit(solution)/shard_map/all_to_all | solution.py:402
  50.2 4.0 %shard_map.97 = (f32[1,512]{1,0:T(1,128)}, bf16[512,512]{1,0:T(8,128)(2,1)S(1)}, bf16[8,160,512]{2,1,0:T(8,128)(2,1)}) custom-call(s32[1,512]{1,0:T(1,128)S(1)} %copy-done.7, bf16[64,512]{1,0:T(8,128)(2,1)S(1)} %get-tuple-element.32.refs_1_, bf16[64,512]{1,0:T(8,128)(2,1)S(1)} %collective-permute-done.refs_2_, ...), custom_call_target="tpu_custom_call" | custom-call | flops 1 | bytes 1 | tf_op jit(solution)/shard_map/pallas_call | solution.py:60
  54.2 3.8 %all-to-all-start.2 = ((bf16[8,160,512]{2,1,0:T(8,128)(2,1)}), bf16[8,160,512]{2,1,0:T(8,128)(2,1)S(1)}, u32[]{:S(2)}, u32[]{:S(2)}) async-start(bf16[8,160,512]{2,1,0:T(8,128)(2,1)} %get-tuple-element.35.refs_3_), calls=%async_computation.2 | async-start | bytes 2621440 | tf_op jit(solution)/shard_map/all_to_all | solution.py:402
  57.9 1.1 shard_map.98.refs_3_
  59.1 0.1 collective-permute-start.3
  59.1 1.1 shard_map.99.refs_0_
  60.3 0.0 copy-start.1
  60.3 0.0 copy-start.6
  60.3 1.5 %collective-permute-done.3.refs_1_ = bf16[1024,512]{1,0:T(8,128)(2,1)S(1)} collective-permute-done((bf16[1024,512]{1,0:T(8,128)(2,1)S(1)}, bf16[1024,512]{1,0:T(8,128)(2,1)S(1)}, u32[]{:S(2)}, u32[]{:S(2)}) %collective-permute-start.3) | collective-permute-done | bytes 1048608 | tf_op jit(solution)/shard_map/ppermute | solution.py:398
  61.8 0.2 shard_map.100
  62.0 1.6 %collective-permute-start.4 = (bf16[512,512]{1,0:T(8,128)(2,1)S(1)}, bf16[512,512]{1,0:T(8,128)(2,1)S(1)}, u32[]{:S(2)}, u32[]{:S(2)}) collective-permute-start(bf16[512,512]{1,0:T(8,128)(2,1)S(1)} %get-tuple-element.38), channel_id=1, source_target_pairs={{0,2},{1,3},{2,0},{3,1},{4,6},{5,7},{6,4},{7,5},{8,10},{9,11},{10,... | collective-permute-start | bytes 1572872 | tf_op jit(solution)/shard_map/ppermute | solution.py:398
  63.6 12.4 %collective-permute-done.4.refs_1_ = bf16[512,512]{1,0:T(8,128)(2,1)S(1)} collective-permute-done((bf16[512,512]{1,0:T(8,128)(2,1)S(1)}, bf16[512,512]{1,0:T(8,128)(2,1)S(1)}, u32[]{:S(2)}, u32[]{:S(2)}) %collective-permute-start.4) | collective-permute-done | bytes 524320 | tf_op jit(solution)/shard_map/ppermute | solution.py:398
  76.1 0.1 shard_map.101
  76.2 1.8 %collective-permute-start.5 = (bf16[256,512]{1,0:T(8,128)(2,1)S(1)}, bf16[256,512]{1,0:T(8,128)(2,1)S(1)}, u32[]{:S(2)}, u32[]{:S(2)}) collective-permute-start(bf16[256,512]{1,0:T(8,128)(2,1)S(1)} %get-tuple-element.39.refs_4_), channel_id=1, source_target_pairs={{0,4},{4,0},{8,12},{12,8},{16,20},{20,16},{24,28},{28,24},{1,5},{5... | collective-permute-start | bytes 786440 | tf_op jit(solution)/shard_map/ppermute | solution.py:398
  77.9 2.8 %shard_map.102 = (bf16[512,512]{1,0:T(8,128)(2,1)S(1)}, bf16[512,512]{1,0:T(8,128)(2,1)S(1)}) custom-call(bf16[512,512]{1,0:T(8,128)(2,1)S(1)} %get-tuple-element.36.refs_0_, s32[1,512]{1,0:T(1,128)S(1)} %bitcast.12, bf16[4,512,512]{2,1,0:T(8,128)(2,1)S(1)} %copy-done.1, s32[1,512]{1,0:T(1,128)S(1)} %bitcast.14, bf16[256,512]{1,0:T(8,128)(2,1)S(1)} %get-tuple-element.39.refs_4_), custom_call_target="tpu_custom_call" | custom-call | flops 1 | bytes 1 | tf_op jit(solution)/shard_map/pallas_call | solution.py:60
  80.7 5.2 %collective-permute-done.5.refs_1_ = bf16[256,512]{1,0:T(8,128)(2,1)S(1)} collective-permute-done((bf16[256,512]{1,0:T(8,128)(2,1)S(1)}, bf16[256,512]{1,0:T(8,128)(2,1)S(1)}, u32[]{:S(2)}, u32[]{:S(2)}) %collective-permute-start.5) | collective-permute-done | bytes 262176 | tf_op jit(solution)/shard_map/ppermute | solution.py:398
  86.0 4.0 %collective-permute-start.11 = (bf16[64,512]{1,0:T(8,128)(2,1)S(1)}, bf16[64,512]{1,0:T(8,128)(2,1)S(1)}, u32[]{:S(2)}, u32[]{:S(2)}) collective-permute-start(bf16[64,512]{1,0:T(8,128)(2,1)S(1)} %get-tuple-element.45), channel_id=1, source_target_pairs={{0,16},{4,20},{8,24},{12,28},{16,0},{20,4},{24,8},{28,12},{1,17},{... | collective-permute-start | bytes 196616 | tf_op jit(solution)/shard_map/ppermute | solution.py:398
  90.0 0.7 collective-permute-start.12
  90.8 0.9 shard_map.104.refs_4_
  91.7 0.1 collective-permute-start.6
  91.7 0.9 shard_map.105.refs_0_.refs_4_
  92.6 1.0 collective-permute-done.6.refs_1_
  93.6 0.1 shard_map.106.mine_ref
  93.7 1.6 %collective-permute-start.8 = (bf16[512,512]{1,0:T(8,128)(2,1)S(1)}, bf16[512,512]{1,0:T(8,128)(2,1)S(1)}, u32[]{:S(2)}, u32[]{:S(2)}) collective-permute-start(bf16[512,512]{1,0:T(8,128)(2,1)S(1)} %shard_map.106.mine_ref), channel_id=1, source_target_pairs={{0,2},{1,3},{2,0},{3,1},{4,6},{5,7},{6,4},{7,5},{8,10},{9,11},{10,... | collective-permute-start | bytes 1572872 | tf_op jit(solution)/shard_map/ppermute | solution.py:398
  95.3 0.0 collective-permute-done.11.refs_2_
  95.3 0.8 collective-permute-done.12.refs_3_
  96.1 2.4 %collective-permute-start.15 = (bf16[64,512]{1,0:T(8,128)(2,1)S(1)}, bf16[64,512]{1,0:T(8,128)(2,1)S(1)}, u32[]{:S(2)}, u32[]{:S(2)}) collective-permute-start(bf16[64,512]{1,0:T(8,128)(2,1)S(1)} %shard_map.107.refs_0_), channel_id=1, source_target_pairs={{0,24},{4,28},{8,16},{12,20},{16,8},{20,12},{24,0},{28,4},{1,25},{... | collective-permute-start | bytes 196616 | tf_op jit(solution)/shard_map/ppermute | solution.py:398
  98.5 0.6 collective-permute-start.14
  99.1 1.4 %collective-permute-start.13 = (bf16[64,512]{1,0:T(8,128)(2,1)S(1)}, bf16[64,512]{1,0:T(8,128)(2,1)S(1)}, u32[]{:S(2)}, u32[]{:S(2)}) collective-permute-start(bf16[64,512]{1,0:T(8,128)(2,1)S(1)} %shard_map.107.refs_0_), channel_id=1, source_target_pairs={{0,8},{4,12},{8,0},{12,4},{16,24},{20,28},{24,16},{28,20},{1,9},{5... | collective-permute-start | bytes 196616 | tf_op jit(solution)/shard_map/ppermute | solution.py:398
  100.6 2.0 %collective-permute-done.15.refs_3_ = bf16[64,512]{1,0:T(8,128)(2,1)S(1)} collective-permute-done((bf16[64,512]{1,0:T(8,128)(2,1)S(1)}, bf16[64,512]{1,0:T(8,128)(2,1)S(1)}, u32[]{:S(2)}, u32[]{:S(2)}) %collective-permute-start.15) | collective-permute-done | bytes 65568 | tf_op jit(solution)/shard_map/ppermute | solution.py:398
  102.5 2.8 %collective-permute-done.14.refs_2_ = bf16[64,512]{1,0:T(8,128)(2,1)S(1)} collective-permute-done((bf16[64,512]{1,0:T(8,128)(2,1)S(1)}, bf16[64,512]{1,0:T(8,128)(2,1)S(1)}, u32[]{:S(2)}, u32[]{:S(2)}) %collective-permute-start.14) | collective-permute-done | bytes 65568 | tf_op jit(solution)/shard_map/ppermute | solution.py:398
  105.3 0.6 collective-permute-start.17
  105.9 1.4 %collective-permute-start.16 = (bf16[256,512]{1,0:T(8,128)(2,1)S(1)}, bf16[256,512]{1,0:T(8,128)(2,1)S(1)}, u32[]{:S(2)}, u32[]{:S(2)}) collective-permute-start(bf16[256,512]{1,0:T(8,128)(2,1)S(1)} %shard_map.108.refs_0_), channel_id=1, source_target_pairs={{0,4},{4,0},{8,12},{12,8},{16,20},{20,16},{24,28},{28,24},{1,5},{5... | collective-permute-start | bytes 786440 | tf_op jit(solution)/shard_map/ppermute | solution.py:398
  107.3 0.0 collective-permute-start.7
  107.3 0.5 collective-permute-done.8.over_ref
  107.8 0.0 collective-permute-start.9
  107.8 0.5 collective-permute-start.18
  108.3 5.2 %collective-permute-done.17.refs_2_.refs_0_ = bf16[256,512]{1,0:T(8,128)(2,1)S(1)} collective-permute-done((bf16[256,512]{1,0:T(8,128)(2,1)S(1)}, bf16[256,512]{1,0:T(8,128)(2,1)S(1)}, u32[]{:S(2)}, u32[]{:S(2)}) %collective-permute-start.17) | collective-permute-done | bytes 262176 | tf_op jit(solution)/shard_map/ppermute | solution.py:398
  113.5 0.0 collective-permute-start.20
  113.5 0.1 collective-permute-done.16.refs_1_.refs_0_
  113.6 0.4 collective-permute-start.19
  114.0 1.5 %collective-permute-start.21 = (bf16[128,512]{1,0:T(8,128)(2,1)S(1)}, bf16[128,512]{1,0:T(8,128)(2,1)S(1)}, u32[]{:S(2)}, u32[]{:S(2)}) collective-permute-start(bf16[128,512]{1,0:T(8,128)(2,1)S(1)} %shard_map.110), channel_id=1, source_target_pairs={{0,2},{1,3},{2,0},{3,1},{4,6},{5,7},{6,4},{7,5},{8,10},{9,11},{10,... | collective-permute-start | bytes 393224 | tf_op jit(solution)/shard_map/ppermute | solution.py:398
  115.5 2.1 %collective-permute-start.22 = (bf16[128,512]{1,0:T(8,128)(2,1)S(1)}, bf16[128,512]{1,0:T(8,128)(2,1)S(1)}, u32[]{:S(2)}, u32[]{:S(2)}) collective-permute-start(bf16[128,512]{1,0:T(8,128)(2,1)S(1)} %shard_map.112), channel_id=1, source_target_pairs={{0,4},{4,0},{8,12},{12,8},{16,20},{20,16},{24,28},{28,24},{1,5},{5... | collective-permute-start | bytes 393224 | tf_op jit(solution)/shard_map/ppermute | solution.py:398
  117.7 2.6 %shard_map.109 = (f32[1024,512]{1,0:T(8,128)}, f32[4,512,512]{2,1,0:T(8,128)}, f32[8,128]{1,0:T(8,128)S(1)}) custom-call(bf16[512,512]{1,0:T(8,128)(2,1)S(1)} %shard_map.106.mine_ref, bf16[512,512]{1,0:T(8,128)(2,1)S(1)} %collective-permute-done.7.other_ref, bf16[512,512]{1,0:T(8,128)(2,1)S(1)} %collective-permute-done.8.over_ref, ...), custom_call_target="tpu_custom_call" | custom-call | tf_op jit(solution)/shard_map/pallas_call | solution.py:575
  120.4 0.1 collective-permute-start.23
  120.4 0.6 collective-permute-done.22.refs_0_
  121.1 0.1 collective-permute-start.24
  121.2 0.6 collective-permute-done.23.refs_2_
  121.8 0.7 collective-permute-done.24.refs_3_
  122.5 1.1 shard_map.114
  (31 shorter events, 0.2 us)
Async XLA Ops:
  0.6 17.0 %copy-start = (bf16[1024,512]{1,0:T(8,128)(2,1)S(1)}, bf16[1024,512]{1,0:T(8,128)(2,1)}, u32[]{:S(2)}) copy-start(bf16[1024,512]{1,0:T(8,128)(2,1)} %refs_1_.1) | copy-start | bytes 3145732
  3.3 14.3 %all-to-all-start = ((bf16[8,8,640]{2,1,0:T(8,128)(2,1)}), bf16[8,8,640]{2,1,0:T(8,128)(2,1)S(1)}, u32[]{:S(2)}, u32[]{:S(2)}) async-start(bf16[8,8,640]{2,1,0:T(8,128)(2,1)} %get-tuple-element.27), calls=%async_computation | async-start | bytes 163840 | tf_op jit(solution)/shard_map/all_to_all | solution.py:402
  10.6 39.6 %copy-start.7 = (s32[1,512]{1,0:T(1,128)S(1)}, s32[1,512]{1,0:T(1,128)}, u32[]{:S(2)}) copy-start(s32[1,512]{1,0:T(1,128)} %get-tuple-element.28.refs_4_.refs_0_) | copy-start | bytes 6148
  17.6 1.0 copy-start.2
  18.7 31.5 %copy-start.4 = (bf16[512,512]{1,0:T(8,128)(2,1)S(1)}, bf16[512,512]{1,0:T(8,128)(2,1)}, u32[]{:S(2)}) copy-start(bf16[512,512]{1,0:T(8,128)(2,1)} %get-tuple-element.34.refs_6_) | copy-start | bytes 1572868
  21.3 28.9 %all-to-all-start.1 = ((bf16[8,128,512]{2,1,0:T(8,128)(2,1)}), bf16[8,128,512]{2,1,0:T(8,128)(2,1)S(1)}, u32[]{:S(2)}, u32[]{:S(2)}) async-start(bf16[8,128,512]{2,1,0:T(8,128)(2,1)} %bitcast.5), calls=%async_computation.1 | async-start | bytes 2097152 | tf_op jit(solution)/shard_map/all_to_all | solution.py:402
  24.9 4.4 %collective-permute-start.2 = (bf16[64,512]{1,0:T(8,128)(2,1)S(1)}, bf16[64,512]{1,0:T(8,128)(2,1)S(1)}, u32[]{:S(2)}, u32[]{:S(2)}) collective-permute-start(bf16[64,512]{1,0:T(8,128)(2,1)S(1)} %get-tuple-element.32.refs_1_), channel_id=1, source_target_pairs={{0,3},{1,2},{2,1},{3,0},{4,7},{5,6},{6,5},{7,4},{8,11},{9,10},{10,... | collective-permute-start | bytes 196616 | tf_op jit(solution)/shard_map/ppermute | solution.py:398
  24.9 5.8 %collective-permute-start.1 = (bf16[64,512]{1,0:T(8,128)(2,1)S(1)}, bf16[64,512]{1,0:T(8,128)(2,1)S(1)}, u32[]{:S(2)}, u32[]{:S(2)}) collective-permute-start(bf16[64,512]{1,0:T(8,128)(2,1)S(1)} %get-tuple-element.32.refs_1_), channel_id=1, source_target_pairs={{0,2},{1,3},{2,0},{3,1},{4,6},{5,7},{6,4},{7,5},{8,10},{9,11},{10,... | collective-permute-start | bytes 196616 | tf_op jit(solution)/shard_map/ppermute | solution.py:398
  26.5 4.2 %collective-permute-start = (bf16[64,512]{1,0:T(8,128)(2,1)S(1)}, bf16[64,512]{1,0:T(8,128)(2,1)S(1)}, u32[]{:S(2)}, u32[]{:S(2)}) collective-permute-start(bf16[64,512]{1,0:T(8,128)(2,1)S(1)} %get-tuple-element.32.refs_1_), channel_id=1, source_target_pairs={{0,1},{1,0},{2,3},{3,2},{4,5},{5,4},{6,7},{7,6},{8,9},{9,8},{10,11... | collective-permute-start | bytes 196616 | tf_op jit(solution)/shard_map/ppermute | solution.py:398
  50.2 7.7 %copy-start.3 = (bf16[512,512]{1,0:T(8,128)(2,1)S(1)}, bf16[512,512]{1,0:T(8,128)(2,1)}, u32[]{:S(2)}) copy-start(bf16[512,512]{1,0:T(8,128)(2,1)} %get-tuple-element.29.refs_2_.refs_1_) | copy-start | bytes 1572868
  50.2 7.8 %copy-start.5 = (s32[512]{0:T(512)S(1)}, s32[512]{0:T(512)}, u32[]{:S(2)}) copy-start(s32[512]{0:T(512)} %param.10) | copy-start | bytes 6148
  54.2 36.6 %all-to-all-start.2 = ((bf16[8,160,512]{2,1,0:T(8,128)(2,1)}), bf16[8,160,512]{2,1,0:T(8,128)(2,1)S(1)}, u32[]{:S(2)}, u32[]{:S(2)}) async-start(bf16[8,160,512]{2,1,0:T(8,128)(2,1)} %get-tuple-element.35.refs_3_), calls=%async_computation.2 | async-start | bytes 2621440 | tf_op jit(solution)/shard_map/all_to_all | solution.py:402
  59.1 2.7 %collective-permute-start.3 = (bf16[1024,512]{1,0:T(8,128)(2,1)S(1)}, bf16[1024,512]{1,0:T(8,128)(2,1)S(1)}, u32[]{:S(2)}, u32[]{:S(2)}) collective-permute-start(bf16[1024,512]{1,0:T(8,128)(2,1)S(1)} %shard_map.98.refs_3_), channel_id=1, source_target_pairs={{0,1},{1,0},{2,3},{3,2},{4,5},{5,4},{6,7},{7,6},{8,9},{9,8},{10,11... | collective-permute-start | bytes 3145736 | tf_op jit(solution)/shard_map/ppermute | solution.py:398
  60.3 17.7 %copy-start.1 = (bf16[4,512,512]{2,1,0:T(8,128)(2,1)S(1)}, bf16[4,512,512]{2,1,0:T(8,128)(2,1)}, u32[]{:S(2)}) copy-start(bf16[4,512,512]{2,1,0:T(8,128)(2,1)} %refs_2_.3) | copy-start | bytes 6291460
  60.3 17.7 %copy-start.6 = (s32[512]{0:T(512)S(1)}, s32[512]{0:T(512)}, u32[]{:S(2)}) copy-start(s32[512]{0:T(512)} %param.9) | copy-start | bytes 6148
  62.0 14.0 %collective-permute-start.4 = (bf16[512,512]{1,0:T(8,128)(2,1)S(1)}, bf16[512,512]{1,0:T(8,128)(2,1)S(1)}, u32[]{:S(2)}, u32[]{:S(2)}) collective-permute-start(bf16[512,512]{1,0:T(8,128)(2,1)S(1)} %get-tuple-element.38), channel_id=1, source_target_pairs={{0,2},{1,3},{2,0},{3,1},{4,6},{5,7},{6,4},{7,5},{8,10},{9,11},{10,... | collective-permute-start | bytes 1572872 | tf_op jit(solution)/shard_map/ppermute | solution.py:398
  76.1 14.6 %copy-start.8 = (s32[1,32]{1,0:T(1,128)S(1)}, s32[1,32]{1,0:T(1,128)}, u32[]{:S(2)}) copy-start(s32[1,32]{1,0:T(1,128)} %get-tuple-element.31.refs_1_) | copy-start | bytes 388
  76.2 9.8 %collective-permute-start.5 = (bf16[256,512]{1,0:T(8,128)(2,1)S(1)}, bf16[256,512]{1,0:T(8,128)(2,1)S(1)}, u32[]{:S(2)}, u32[]{:S(2)}) collective-permute-start(bf16[256,512]{1,0:T(8,128)(2,1)S(1)} %get-tuple-element.39.refs_4_), channel_id=1, source_target_pairs={{0,4},{4,0},{8,12},{12,8},{16,20},{20,16},{24,28},{28,24},{1,5},{5... | collective-permute-start | bytes 786440 | tf_op jit(solution)/shard_map/ppermute | solution.py:398
  86.0 9.3 %collective-permute-start.11 = (bf16[64,512]{1,0:T(8,128)(2,1)S(1)}, bf16[64,512]{1,0:T(8,128)(2,1)S(1)}, u32[]{:S(2)}, u32[]{:S(2)}) collective-permute-start(bf16[64,512]{1,0:T(8,128)(2,1)S(1)} %get-tuple-element.45), channel_id=1, source_target_pairs={{0,16},{4,20},{8,24},{12,28},{16,0},{20,4},{24,8},{28,12},{1,17},{... | collective-permute-start | bytes 196616 | tf_op jit(solution)/shard_map/ppermute | solution.py:398
  90.0 6.1 %collective-permute-start.12 = (bf16[64,512]{1,0:T(8,128)(2,1)S(1)}, bf16[64,512]{1,0:T(8,128)(2,1)S(1)}, u32[]{:S(2)}, u32[]{:S(2)}) collective-permute-start(bf16[64,512]{1,0:T(8,128)(2,1)S(1)} %get-tuple-element.46), channel_id=1, source_target_pairs={{0,24},{4,28},{8,16},{12,20},{16,8},{20,12},{24,0},{28,4},{1,25},{... | collective-permute-start | bytes 196616 | tf_op jit(solution)/shard_map/ppermute | solution.py:398
  90.7 5.3 %collective-permute-start.10 = (bf16[64,512]{1,0:T(8,128)(2,1)S(1)}, bf16[64,512]{1,0:T(8,128)(2,1)S(1)}, u32[]{:S(2)}, u32[]{:S(2)}) collective-permute-start(bf16[64,512]{1,0:T(8,128)(2,1)S(1)} %get-tuple-element.43.refs_4_), channel_id=1, source_target_pairs={{0,8},{4,12},{8,0},{12,4},{16,24},{20,28},{24,16},{28,20},{1,9},{5... | collective-permute-start | bytes 196616 | tf_op jit(solution)/shard_map/ppermute | solution.py:398
  91.7 2.0 %collective-permute-start.6 = (bf16[512,512]{1,0:T(8,128)(2,1)S(1)}, bf16[512,512]{1,0:T(8,128)(2,1)S(1)}, u32[]{:S(2)}, u32[]{:S(2)}) collective-permute-start(bf16[512,512]{1,0:T(8,128)(2,1)S(1)} %shard_map.104.refs_4_), channel_id=1, source_target_pairs={{0,1},{1,0},{2,3},{3,2},{4,5},{5,4},{6,7},{7,6},{8,9},{9,8},{10,11... | collective-permute-start | bytes 1572872 | tf_op jit(solution)/shard_map/ppermute | solution.py:398
  93.7 14.0 %collective-permute-start.8 = (bf16[512,512]{1,0:T(8,128)(2,1)S(1)}, bf16[512,512]{1,0:T(8,128)(2,1)S(1)}, u32[]{:S(2)}, u32[]{:S(2)}) collective-permute-start(bf16[512,512]{1,0:T(8,128)(2,1)S(1)} %shard_map.106.mine_ref), channel_id=1, source_target_pairs={{0,2},{1,3},{2,0},{3,1},{4,6},{5,7},{6,4},{7,5},{8,10},{9,11},{10,... | collective-permute-start | bytes 1572872 | tf_op jit(solution)/shard_map/ppermute | solution.py:398
  96.1 6.4 %collective-permute-start.15 = (bf16[64,512]{1,0:T(8,128)(2,1)S(1)}, bf16[64,512]{1,0:T(8,128)(2,1)S(1)}, u32[]{:S(2)}, u32[]{:S(2)}) collective-permute-start(bf16[64,512]{1,0:T(8,128)(2,1)S(1)} %shard_map.107.refs_0_), channel_id=1, source_target_pairs={{0,24},{4,28},{8,16},{12,20},{16,8},{20,12},{24,0},{28,4},{1,25},{... | collective-permute-start | bytes 196616 | tf_op jit(solution)/shard_map/ppermute | solution.py:398
  98.5 6.8 %collective-permute-start.14 = (bf16[64,512]{1,0:T(8,128)(2,1)S(1)}, bf16[64,512]{1,0:T(8,128)(2,1)S(1)}, u32[]{:S(2)}, u32[]{:S(2)}) collective-permute-start(bf16[64,512]{1,0:T(8,128)(2,1)S(1)} %shard_map.107.refs_0_), channel_id=1, source_target_pairs={{0,16},{4,20},{8,24},{12,28},{16,0},{20,4},{24,8},{28,12},{1,17},{... | collective-permute-start | bytes 196616 | tf_op jit(solution)/shard_map/ppermute | solution.py:398
  99.1 6.1 %collective-permute-start.13 = (bf16[64,512]{1,0:T(8,128)(2,1)S(1)}, bf16[64,512]{1,0:T(8,128)(2,1)S(1)}, u32[]{:S(2)}, u32[]{:S(2)}) collective-permute-start(bf16[64,512]{1,0:T(8,128)(2,1)S(1)} %shard_map.107.refs_0_), channel_id=1, source_target_pairs={{0,8},{4,12},{8,0},{12,4},{16,24},{20,28},{24,16},{28,20},{1,9},{5... | collective-permute-start | bytes 196616 | tf_op jit(solution)/shard_map/ppermute | solution.py:398
  105.3 8.2 %collective-permute-start.17 = (bf16[256,512]{1,0:T(8,128)(2,1)S(1)}, bf16[256,512]{1,0:T(8,128)(2,1)S(1)}, u32[]{:S(2)}, u32[]{:S(2)}) collective-permute-start(bf16[256,512]{1,0:T(8,128)(2,1)S(1)} %shard_map.108.refs_0_), channel_id=1, source_target_pairs={{0,2},{1,3},{2,0},{3,1},{4,6},{5,7},{6,4},{7,5},{8,10},{9,11},{10,... | collective-permute-start | bytes 786440 | tf_op jit(solution)/shard_map/ppermute | solution.py:398
  105.9 7.7 %collective-permute-start.16 = (bf16[256,512]{1,0:T(8,128)(2,1)S(1)}, bf16[256,512]{1,0:T(8,128)(2,1)S(1)}, u32[]{:S(2)}, u32[]{:S(2)}) collective-permute-start(bf16[256,512]{1,0:T(8,128)(2,1)S(1)} %shard_map.108.refs_0_), channel_id=1, source_target_pairs={{0,4},{4,0},{8,12},{12,8},{16,20},{20,16},{24,28},{28,24},{1,5},{5... | collective-permute-start | bytes 786440 | tf_op jit(solution)/shard_map/ppermute | solution.py:398
  107.3 10.4 %collective-permute-start.7 = (bf16[512,512]{1,0:T(8,128)(2,1)S(1)}, bf16[512,512]{1,0:T(8,128)(2,1)S(1)}, u32[]{:S(2)}, u32[]{:S(2)}) collective-permute-start(bf16[512,512]{1,0:T(8,128)(2,1)S(1)} %shard_map.106.mine_ref), channel_id=1, source_target_pairs={{0,1},{1,0},{2,3},{3,2},{4,5},{5,4},{6,7},{7,6},{8,9},{9,8},{10,11... | collective-permute-start | bytes 1572872 | tf_op jit(solution)/shard_map/ppermute | solution.py:398
  107.8 9.9 %collective-permute-start.9 = (bf16[512,512]{1,0:T(8,128)(2,1)S(1)}, bf16[512,512]{1,0:T(8,128)(2,1)S(1)}, u32[]{:S(2)}, u32[]{:S(2)}) collective-permute-start(bf16[512,512]{1,0:T(8,128)(2,1)S(1)} %collective-permute-done.8.over_ref), channel_id=1, source_target_pairs={{0,1},{1,0},{2,3},{3,2},{4,5},{5,4},{6,7},{7,6},{8,9},{9,8},{10,11... | collective-permute-start | bytes 1572872 | tf_op jit(solution)/shard_map/ppermute | solution.py:398
  107.8 6.2 %collective-permute-start.18 = (bf16[256,512]{1,0:T(8,128)(2,1)S(1)}, bf16[256,512]{1,0:T(8,128)(2,1)S(1)}, u32[]{:S(2)}, u32[]{:S(2)}) collective-permute-start(bf16[256,512]{1,0:T(8,128)(2,1)S(1)} %shard_map.108.refs_0_), channel_id=1, source_target_pairs={{0,1},{1,0},{2,3},{3,2},{4,5},{5,4},{6,7},{7,6},{8,9},{9,8},{10,11... | collective-permute-start | bytes 786440 | tf_op jit(solution)/shard_map/ppermute | solution.py:398
  113.5 2.0 %collective-permute-start.20 = (bf16[256,512]{1,0:T(8,128)(2,1)S(1)}, bf16[256,512]{1,0:T(8,128)(2,1)S(1)}, u32[]{:S(2)}, u32[]{:S(2)}) collective-permute-start(bf16[256,512]{1,0:T(8,128)(2,1)S(1)} %collective-permute-done.17.refs_2_.refs_0_), channel_id=1, source_target_pairs={{0,1},{1,0},{2,3},{3,2},{4,5},{5,4},{6,7},{7,6},{8,9},{9,8},{10,11... | collective-permute-start | bytes 786440 | tf_op jit(solution)/shard_map/ppermute | solution.py:398
  113.6 4.1 %collective-permute-start.19 = (bf16[256,512]{1,0:T(8,128)(2,1)S(1)}, bf16[256,512]{1,0:T(8,128)(2,1)S(1)}, u32[]{:S(2)}, u32[]{:S(2)}) collective-permute-start(bf16[256,512]{1,0:T(8,128)(2,1)S(1)} %collective-permute-done.16.refs_1_.refs_0_), channel_id=1, source_target_pairs={{0,1},{1,0},{2,3},{3,2},{4,5},{5,4},{6,7},{7,6},{8,9},{9,8},{10,11... | collective-permute-start | bytes 786440 | tf_op jit(solution)/shard_map/ppermute | solution.py:398
  114.0 6.3 %collective-permute-start.21 = (bf16[128,512]{1,0:T(8,128)(2,1)S(1)}, bf16[128,512]{1,0:T(8,128)(2,1)S(1)}, u32[]{:S(2)}, u32[]{:S(2)}) collective-permute-start(bf16[128,512]{1,0:T(8,128)(2,1)S(1)} %shard_map.110), channel_id=1, source_target_pairs={{0,2},{1,3},{2,0},{3,1},{4,6},{5,7},{6,4},{7,5},{8,10},{9,11},{10,... | collective-permute-start | bytes 393224 | tf_op jit(solution)/shard_map/ppermute | solution.py:398
  115.5 5.5 %collective-permute-start.22 = (bf16[128,512]{1,0:T(8,128)(2,1)S(1)}, bf16[128,512]{1,0:T(8,128)(2,1)S(1)}, u32[]{:S(2)}, u32[]{:S(2)}) collective-permute-start(bf16[128,512]{1,0:T(8,128)(2,1)S(1)} %shard_map.112), channel_id=1, source_target_pairs={{0,4},{4,0},{8,12},{12,8},{16,20},{20,16},{24,28},{28,24},{1,5},{5... | collective-permute-start | bytes 393224 | tf_op jit(solution)/shard_map/ppermute | solution.py:398
  120.4 1.4 %collective-permute-start.23 = (bf16[128,512]{1,0:T(8,128)(2,1)S(1)}, bf16[128,512]{1,0:T(8,128)(2,1)S(1)}, u32[]{:S(2)}, u32[]{:S(2)}) collective-permute-start(bf16[128,512]{1,0:T(8,128)(2,1)S(1)} %shard_map.111.refs_0_), channel_id=1, source_target_pairs={{0,1},{1,0},{2,3},{3,2},{4,5},{5,4},{6,7},{7,6},{8,9},{9,8},{10,11... | collective-permute-start | bytes 393224 | tf_op jit(solution)/shard_map/ppermute | solution.py:398
  121.1 1.4 %collective-permute-start.24 = (bf16[128,512]{1,0:T(8,128)(2,1)S(1)}, bf16[128,512]{1,0:T(8,128)(2,1)S(1)}, u32[]{:S(2)}, u32[]{:S(2)}) collective-permute-start(bf16[128,512]{1,0:T(8,128)(2,1)S(1)} %shard_map.113.refs_1_), channel_id=1, source_target_pairs={{0,1},{1,0},{2,3},{3,2},{4,5},{5,4},{6,7},{7,6},{8,9},{9,8},{10,11... | collective-permute-start | bytes 393224 | tf_op jit(solution)/shard_map/ppermute | solution.py:398

commit v11 on v10

--- a/solution.py
+++ b/solution.py
@@ -196,14 +196,24 @@
     return 2 * core + (quarter >> 1), quarter & 1
 
 
-def operator_terms(special, first, rows_ref, rel, grad, out_ref):
+def operator_terms(special, first, rows_ref, rel, grad, *out_refs):
     width = grad.shape[1] // 2
     for place in range(4):
         relation, part = quarter_of(special, first + place)
         at = part * width if isinstance(part, int) else pl.multiple_of(part * width, width)
         picked = jnp.where(rel == relation, grad, jnp.zeros_like(grad))
         term = dot_t0(rows_ref[:, pl.ds(at, width)], picked)
-        out_ref[place * width : (place + 1) * width] = term.astype(out_ref.dtype)
+        out_ref = out_refs[place // 2]
+        out_ref[place % 2 * width : (place % 2 + 1) * width] = term.astype(out_ref.dtype)
+
+
+def score_kernel(
+    factor, near_ref, core_ref, across_ref, both_ref, query_ref, score_ref
+):
+    negatives = jnp.concatenate(
+        [near_ref[...], core_ref[...], across_ref[...], both_ref[...]], axis=0
+    )
+    score_ref[...] = dot_t1(query_ref[...], negatives) * factor
 
 
 def edge_kernel(
@@ -214,6 +224,7 @@
     across_ref,
     both_ref,
     got_ref,
+    score_ref,
     take,
     loss_ref,
     grad_ref,
@@ -226,7 +237,7 @@
     slots = got_ref.shape[0]
     tails = dot(hot(as_column(slot_ref[...]) == iota((edges, slots), 1)), got_ref[...])
     queries = take(0)[...]
-    scores = dot_t1(queries, negatives) * factor
+    scores = score_ref[...]
     positive = jnp.sum(queries.astype(F32) * tails, axis=1, keepdims=True) * factor
     row_max = jnp.maximum(positive, jnp.max(scores, axis=1, keepdims=True))
     exp_pos = jnp.exp(positive - row_max)
@@ -252,19 +263,12 @@
         back_ref[index, cap:] = jnp.concatenate(pieces, axis=0).astype(BF)
 
 
-def terms_kernel(special, first, grad_ref, rows_ref, rel_ref, out_ref):
-    operator_terms(special, first, rows_ref, as_column(rel_ref[...]), grad_ref[...], out_ref)
-
-
-def pair_kernel(keep_ref, got_ref, own_ref, sent_ref):
-    half = own_ref.shape[0] // 2
-    for place in range(4):
-        at = slice(place * half, (place + 1) * half)
-        term = keep_ref[at].astype(F32) + got_ref[at].astype(F32)
-        if place < 2:
-            own_ref[place * half : (place + 1) * half] = term
-        else:
-            sent_ref[(place - 2) * half : (place - 1) * half] = term.astype(BF)
+def terms_kernel(special, first, grad_ref, rows_ref, rel_ref, *out_refs):
+    operator_terms(special, first, rows_ref, as_column(rel_ref[...]), grad_ref[...], *out_refs)
+
+
+def pair_kernel(keep_ref, got_ref, out_ref):
+    out_ref[...] = (keep_ref[...].astype(F32) + got_ref[...].astype(F32)).astype(out_ref.dtype)
 
 
 def middle_kernel(own_ref, got_ref, keep_ref, sent_ref):
@@ -451,6 +455,12 @@
     got = exchange(found.reshape(parts, cap, columns)).reshape(slots, columns)
     neg_core, neg_across, neg_both = [flip(neg_near, "rep", reps, k) for k in (1, 2, 3)]
 
+    (scores,) = call(
+        functools.partial(score_kernel, factor),
+        [((edges, negs), F32)],
+        (),
+        (neg_near, neg_core, neg_across, neg_both, queries),
+    )
     loss, grad, back = call(
         functools.partial(edge_kernel, factor),
         [
@@ -459,7 +469,7 @@
             ((parts, cap + neg_dev, columns), BF),
         ],
         (),
-        (slot, neg_near, neg_core, neg_across, neg_both, got),
+        (slot, neg_near, neg_core, neg_across, neg_both, got, scores),
         (queries,),
     )
     returned = exchange(back)
@@ -468,15 +478,15 @@
     def terms(first, after):
         return call(
             functools.partial(terms_kernel, special, first),
-            [((2 * columns, columns), kind)],
+            [((columns, columns), kind)] * 2,
             (),
             (grad, rows, rel),
             (),
             after,
-        )[0]
+        )
 
     away = terms(0, (back,))
-    keep = terms(4, (away,))
+    keep = terms(4, (away[0],))
 
     def head_terms(count, after):
         return call(
@@ -501,7 +511,7 @@
         )
 
     if not special:
-        whole = jnp.concatenate([away, keep], axis=0)
+        whole = jnp.concatenate([*away, *keep], axis=0)
         whole = whole.reshape(count, columns, columns)
         (base,) = head_terms(1, ())
         (added,) = add(0, base, [((ent_dev, columns), F32)], ())
@@ -519,12 +529,9 @@
     def over_core(v):
         return flip(v, "rep", 4, 1)
 
-    own, sent = call(
-        pair_kernel,
-        [((columns, columns), F32), ((columns, columns), BF)],
-        (),
-        (keep, over_core(away)),
-    )
+    shape = (columns, columns)
+    (sent,) = call(pair_kernel, [(shape, BF)], (), (keep[1], over_core(away[1])))
+    (own,) = call(pair_kernel, [(shape, F32)], (), (keep[0], over_core(away[0])), (), (sent,))
     own, sent = call(
         middle_kernel,
         [((half, columns), F32), ((half, columns), BF)],

time: 124 us -> 124 us (level)
    ppermute x25 -> x26, waiting for transfers between devices: 37.3 us -> 36 us  [flip(): return lax.ppermute(x, axis, [(i, i ^ bit) for i in range(size)])]
    ppermute x25 -> x26, starting transfers between devices: 22.9 us -> 23.8 us  [flip(): return lax.ppermute(x, axis, [(i, i ^ bit) for i in range(size)])]
    pallas_call x19 -> x21, Pallas kernels: 21 us -> 20.9 us  [call(): pl.pallas_call(kernel, out_shape=[jax.ShapeDtypeStruct(out[0], out[1]) fo...]
  transfers between devices with their start and end apart: 28 -> 29, of which waited for: 17 -> 16; matrix products, arithmetic and copies ran while one was open for 0% -> 0% of each run, Pallas kernels for 12% -> 12%
where the time goes in v11:
time: 124 us
  waiting for transfers between devices  58.3 us (47%)
  starting transfers between devices  38.5 us (31%)
  Pallas kernels  24.6 us (20%)
    ppermute x26, waiting for transfers between devices, flip(): return lax.ppermute(x, axis, [(i, i ^ bit) for i in range(size)])  36 us
    ppermute x26, starting transfers between devices, flip(): return lax.ppermute(x, axis, [(i, i ^ bit) for i in range(size)])  23.8 us
    all_to_all x3, waiting for transfers between devices, exchange(): return lax.all_to_all(x, 'dom', split_axis=0, concat_axis=0, tiled=True)  22.3 us
    pallas_call x21, Pallas kernels, call(): pl.pallas_call(kernel, out_shape=[jax.ShapeDtypeStruct(out[0], out[1]) fo...  20.9 us
    all_to_all x3, starting transfers between devices, exchange(): return lax.all_to_all(x, 'dom', split_axis=0, concat_axis=0, tiled=True)  14.7 us
    pallas_call x1, Pallas kernels, local(): pl.pallas_call(functools.partial(join_kernel, [places[k] for k in early])...  2.65 us
  transfers between devices with their start and end apart: 29, of which 16 were waited for; matrix products, arithmetic and copies ran while one was open for 0% of the time, Pallas kernels for 12%

profile of v11, /device:TPU:0, one launch (start us, length us, event | category | flops | bytes accessed | tf_op | source)
XLA Modules:
  0.0 123.6 jit_solution(5415155308051082809)
XLA Ops:
  0.6 0.0 copy-start
  0.6 2.7 %shard_map.94 = (s32[1,512]{1,0:T(1,128)}, s32[1,32]{1,0:T(1,128)}, bf16[8,8,640]{2,1,0:T(8,128)(2,1)}) custom-call(s32[1,512]{1,0:T(1,128)} %bitcast.15, s32[1,512]{1,0:T(1,128)} %bitcast.16, s32[1,32]{1,0:T(1,128)} %bitcast.17, bf16[1024,512]{1,0:T(8,128)(2,1)} %refs_1_.1), custom_call_target="tpu_custom_call" | custom-call | flops 1 | bytes 1 | tf_op jit(solution)/shard_map/pallas_call | solution.py:60
  3.3 7.3 %all-to-all-start = ((bf16[8,8,640]{2,1,0:T(8,128)(2,1)}), bf16[8,8,640]{2,1,0:T(8,128)(2,1)S(1)}, u32[]{:S(2)}, u32[]{:S(2)}) async-start(bf16[8,8,640]{2,1,0:T(8,128)(2,1)} %get-tuple-element.29), calls=%async_computation | async-start | bytes 163840 | tf_op jit(solution)/shard_map/all_to_all | solution.py:406
  10.6 4.4 %shard_map.95 = (bf16[512,512]{1,0:T(8,128)(2,1)}, bf16[512,512]{1,0:T(8,128)(2,1)}) custom-call(s32[1,512]{1,0:T(1,128)} %bitcast.13, s32[1,512]{1,0:T(1,128)} %bitcast.9, bf16[1024,512]{1,0:T(8,128)(2,1)} %refs_1_.1, bf16[4,512,512]{2,1,0:T(8,128)(2,1)} %refs_2_.3, s32[1,512]{1,0:T(1,128)} %get-tuple-element.30.refs_4_.refs_0_), custom_call_target="tpu_custom_call" | custom-call | flops 1 | bytes 1 | tf_op jit(solution)/shard_map/pallas_call | solution.py:60
  15.0 2.6 %all-to-all-done.refs_0_ = bf16[8,8,640]{2,1,0:T(8,128)(2,1)S(1)} async-done(((bf16[8,8,640]{2,1,0:T(8,128)(2,1)}), bf16[8,8,640]{2,1,0:T(8,128)(2,1)S(1)}, u32[]{:S(2)}, u32[]{:S(2)}) %all-to-all-start) | async-done | bytes 81952 | tf_op jit(solution)/shard_map/all_to_all | solution.py:406
  17.6 1.0 copy-done.2
  18.7 2.6 %shard_map.96 = (s32[1,1024]{1,0:T(1,128)S(1)}, bf16[1024,512]{1,0:T(8,128)(2,1)}, bf16[64,512]{1,0:T(8,128)(2,1)S(1)}) custom-call(bf16[8,8,640]{2,1,0:T(8,128)(2,1)S(1)} %all-to-all-done.refs_0_, bf16[1024,512]{1,0:T(8,128)(2,1)S(1)} %copy-done, bf16[512,512]{1,0:T(8,128)(2,1)S(1)} %copy-done.2), custom_call_target="tpu_custom_call" | custom-call | flops 1 | bytes 1 | tf_op jit(solution)/shard_map/pallas_call | solution.py:60
  21.3 3.7 %all-to-all-start.1 = ((bf16[8,128,512]{2,1,0:T(8,128)(2,1)}), bf16[8,128,512]{2,1,0:T(8,128)(2,1)S(1)}, u32[]{:S(2)}, u32[]{:S(2)}) async-start(bf16[8,128,512]{2,1,0:T(8,128)(2,1)} %bitcast.5), calls=%async_computation.1 | async-start | bytes 2097152 | tf_op jit(solution)/shard_map/all_to_all | solution.py:406
  25.0 0.1 collective-permute-start.2
  25.1 1.6 %collective-permute-start.1 = (bf16[64,512]{1,0:T(8,128)(2,1)S(1)}, bf16[64,512]{1,0:T(8,128)(2,1)S(1)}, u32[]{:S(2)}, u32[]{:S(2)}) collective-permute-start(bf16[64,512]{1,0:T(8,128)(2,1)S(1)} %get-tuple-element.34.refs_0_.refs_1_), channel_id=1, source_target_pairs={{0,2},{1,3},{2,0},{3,1},{4,6},{5,7},{6,4},{7,5},{8,10},{9,11},{10,... | collective-permute-start | bytes 196616 | tf_op jit(solution)/shard_map/ppermute | solution.py:402
  26.7 0.3 collective-permute-start
  26.9 2.4 %collective-permute-done.2.refs_3_.refs_4_ = bf16[64,512]{1,0:T(8,128)(2,1)S(1)} collective-permute-done((bf16[64,512]{1,0:T(8,128)(2,1)S(1)}, bf16[64,512]{1,0:T(8,128)(2,1)S(1)}, u32[]{:S(2)}, u32[]{:S(2)}) %collective-permute-start.2) | collective-permute-done | bytes 65568 | tf_op jit(solution)/shard_map/ppermute | solution.py:402
  29.4 1.5 %collective-permute-done.1.refs_2_.refs_3_ = bf16[64,512]{1,0:T(8,128)(2,1)S(1)} collective-permute-done((bf16[64,512]{1,0:T(8,128)(2,1)S(1)}, bf16[64,512]{1,0:T(8,128)(2,1)S(1)}, u32[]{:S(2)}, u32[]{:S(2)}) %collective-permute-start.1) | collective-permute-done | bytes 65568 | tf_op jit(solution)/shard_map/ppermute | solution.py:402
  30.9 0.3 shard_map.97.refs_6_
  31.2 19.1 %all-to-all-done.1 = bf16[8,128,512]{2,1,0:T(8,128)(2,1)S(1)} async-done(((bf16[8,128,512]{2,1,0:T(8,128)(2,1)}), bf16[8,128,512]{2,1,0:T(8,128)(2,1)S(1)}, u32[]{:S(2)}, u32[]{:S(2)}) %all-to-all-start.1) | async-done | bytes 1048608 | tf_op jit(solution)/shard_map/all_to_all | solution.py:406
  50.3 3.5 %shard_map.98 = (f32[1,512]{1,0:T(1,128)}, bf16[512,512]{1,0:T(8,128)(2,1)S(1)}, bf16[8,160,512]{2,1,0:T(8,128)(2,1)}) custom-call(s32[1,512]{1,0:T(1,128)S(1)} %copy-done.7, bf16[64,512]{1,0:T(8,128)(2,1)S(1)} %get-tuple-element.34.refs_0_.refs_1_, bf16[64,512]{1,0:T(8,128)(2,1)S(1)} %collective-permute-done.refs_1_.refs_2_, ...), custom_call_target="tpu_custom_call" | custom-call | flops 1 | bytes 1 | tf_op jit(solution)/shard_map/pallas_call | solution.py:60
  53.8 3.8 %all-to-all-start.2 = ((bf16[8,160,512]{2,1,0:T(8,128)(2,1)}), bf16[8,160,512]{2,1,0:T(8,128)(2,1)S(1)}, u32[]{:S(2)}, u32[]{:S(2)}) async-start(bf16[8,160,512]{2,1,0:T(8,128)(2,1)} %get-tuple-element.37.refs_3_), calls=%async_computation.2 | async-start | bytes 2621440 | tf_op jit(solution)/shard_map/all_to_all | solution.py:406
  57.6 1.1 shard_map.99
  58.7 0.1 collective-permute-start.4
  58.8 1.1 shard_map.100
  59.9 0.6 collective-permute-start.3
  60.5 0.2 collective-permute-done.4.refs_1_
  60.7 0.1 shard_map.101.refs_2_
  60.8 1.6 %collective-permute-start.5 = (bf16[512,512]{1,0:T(8,128)(2,1)S(1)}, bf16[512,512]{1,0:T(8,128)(2,1)S(1)}, u32[]{:S(2)}, u32[]{:S(2)}) collective-permute-start(bf16[512,512]{1,0:T(8,128)(2,1)S(1)} %shard_map.101.refs_2_), channel_id=1, source_target_pairs={{0,2},{1,3},{2,0},{3,1},{4,6},{5,7},{6,4},{7,5},{8,10},{9,11},{10,... | collective-permute-start | bytes 1572872 | tf_op jit(solution)/shard_map/ppermute | solution.py:402
  62.4 0.1 shard_map.102.refs_0_
  62.5 12.3 %collective-permute-done.5.refs_1_ = bf16[512,512]{1,0:T(8,128)(2,1)S(1)} collective-permute-done((bf16[512,512]{1,0:T(8,128)(2,1)S(1)}, bf16[512,512]{1,0:T(8,128)(2,1)S(1)}, u32[]{:S(2)}, u32[]{:S(2)}) %collective-permute-start.5) | collective-permute-done | bytes 524320 | tf_op jit(solution)/shard_map/ppermute | solution.py:402
  74.8 0.1 shard_map.103
  74.9 1.8 %collective-permute-start.6 = (bf16[256,512]{1,0:T(8,128)(2,1)S(1)}, bf16[256,512]{1,0:T(8,128)(2,1)S(1)}, u32[]{:S(2)}, u32[]{:S(2)}) collective-permute-start(bf16[256,512]{1,0:T(8,128)(2,1)S(1)} %get-tuple-element.43.refs_4_), channel_id=1, source_target_pairs={{0,4},{4,0},{8,12},{12,8},{16,20},{20,16},{24,28},{28,24},{1,5},{5... | collective-permute-start | bytes 786440 | tf_op jit(solution)/shard_map/ppermute | solution.py:402
  76.7 2.7 %shard_map.104 = (bf16[512,512]{1,0:T(8,128)(2,1)S(1)}, bf16[512,512]{1,0:T(8,128)(2,1)S(1)}) custom-call(bf16[512,512]{1,0:T(8,128)(2,1)S(1)} %get-tuple-element.38.refs_0_, s32[1,512]{1,0:T(1,128)S(1)} %bitcast.12, bf16[4,512,512]{2,1,0:T(8,128)(2,1)S(1)} %copy-done.1, s32[1,512]{1,0:T(1,128)S(1)} %bitcast.14, bf16[256,512]{1,0:T(8,128)(2,1)S(1)} %get-tuple-element.43.refs_4_), custom_call_target="tpu_custom_call" | custom-call | flops 1 | bytes 1 | tf_op jit(solution)/shard_map/pallas_call | solution.py:60
  79.5 5.7 %collective-permute-done.6.refs_1_ = bf16[256,512]{1,0:T(8,128)(2,1)S(1)} collective-permute-done((bf16[256,512]{1,0:T(8,128)(2,1)S(1)}, bf16[256,512]{1,0:T(8,128)(2,1)S(1)}, u32[]{:S(2)}, u32[]{:S(2)}) %collective-permute-start.6) | collective-permute-done | bytes 262176 | tf_op jit(solution)/shard_map/ppermute | solution.py:402
  85.1 0.1 shard_map.105
  85.2 3.6 %collective-permute-start.12 = (bf16[64,512]{1,0:T(8,128)(2,1)S(1)}, bf16[64,512]{1,0:T(8,128)(2,1)S(1)}, u32[]{:S(2)}, u32[]{:S(2)}) collective-permute-start(bf16[64,512]{1,0:T(8,128)(2,1)S(1)} %get-tuple-element.49), channel_id=1, source_target_pairs={{0,16},{4,20},{8,24},{12,28},{16,0},{20,4},{24,8},{28,12},{1,17},{... | collective-permute-start | bytes 196616 | tf_op jit(solution)/shard_map/ppermute | solution.py:402
  88.8 0.9 collective-permute-start.13
  89.7 0.6 all-to-all-done.2.refs_2_
  90.3 0.9 shard_map.106.refs_4_
  91.2 0.1 collective-permute-start.7
  91.3 0.9 shard_map.107.refs_0_.refs_4_
  92.2 1.0 collective-permute-done.7.refs_1_
  93.2 0.1 shard_map.108.mine_ref
  93.3 1.6 %collective-permute-start.9 = (bf16[512,512]{1,0:T(8,128)(2,1)S(1)}, bf16[512,512]{1,0:T(8,128)(2,1)S(1)}, u32[]{:S(2)}, u32[]{:S(2)}) collective-permute-start(bf16[512,512]{1,0:T(8,128)(2,1)S(1)} %shard_map.108.mine_ref), channel_id=1, source_target_pairs={{0,2},{1,3},{2,0},{3,1},{4,6},{5,7},{6,4},{7,5},{8,10},{9,11},{10,... | collective-permute-start | bytes 1572872 | tf_op jit(solution)/shard_map/ppermute | solution.py:402
  94.9 0.0 collective-permute-done.12.refs_2_
  94.9 0.0 collective-permute-done.13.refs_3_
  94.9 0.0 collective-permute-done.11.refs_1_
  95.0 2.4 %collective-permute-start.16 = (bf16[64,512]{1,0:T(8,128)(2,1)S(1)}, bf16[64,512]{1,0:T(8,128)(2,1)S(1)}, u32[]{:S(2)}, u32[]{:S(2)}) collective-permute-start(bf16[64,512]{1,0:T(8,128)(2,1)S(1)} %shard_map.109.refs_0_), channel_id=1, source_target_pairs={{0,24},{4,28},{8,16},{12,20},{16,8},{20,12},{24,0},{28,4},{1,25},{... | collective-permute-start | bytes 196616 | tf_op jit(solution)/shard_map/ppermute | solution.py:402
  97.3 0.6 collective-permute-start.15
  98.0 1.4 %collective-permute-start.14 = (bf16[64,512]{1,0:T(8,128)(2,1)S(1)}, bf16[64,512]{1,0:T(8,128)(2,1)S(1)}, u32[]{:S(2)}, u32[]{:S(2)}) collective-permute-start(bf16[64,512]{1,0:T(8,128)(2,1)S(1)} %shard_map.109.refs_0_), channel_id=1, source_target_pairs={{0,8},{4,12},{8,0},{12,4},{16,24},{20,28},{24,16},{28,20},{1,9},{5... | collective-permute-start | bytes 196616 | tf_op jit(solution)/shard_map/ppermute | solution.py:402
  99.4 1.9 %collective-permute-done.16.refs_3_ = bf16[64,512]{1,0:T(8,128)(2,1)S(1)} collective-permute-done((bf16[64,512]{1,0:T(8,128)(2,1)S(1)}, bf16[64,512]{1,0:T(8,128)(2,1)S(1)}, u32[]{:S(2)}, u32[]{:S(2)}) %collective-permute-start.16) | collective-permute-done | bytes 65568 | tf_op jit(solution)/shard_map/ppermute | solution.py:402
  101.3 2.9 %collective-permute-done.15.refs_2_ = bf16[64,512]{1,0:T(8,128)(2,1)S(1)} collective-permute-done((bf16[64,512]{1,0:T(8,128)(2,1)S(1)}, bf16[64,512]{1,0:T(8,128)(2,1)S(1)}, u32[]{:S(2)}, u32[]{:S(2)}) %collective-permute-start.15) | collective-permute-done | bytes 65568 | tf_op jit(solution)/shard_map/ppermute | solution.py:402
  104.2 0.6 collective-permute-start.18
  104.8 1.6 %collective-permute-start.17 = (bf16[256,512]{1,0:T(8,128)(2,1)S(1)}, bf16[256,512]{1,0:T(8,128)(2,1)S(1)}, u32[]{:S(2)}, u32[]{:S(2)}) collective-permute-start(bf16[256,512]{1,0:T(8,128)(2,1)S(1)} %shard_map.110.refs_0_), channel_id=1, source_target_pairs={{0,4},{4,0},{8,12},{12,8},{16,20},{20,16},{24,28},{28,24},{1,5},{5... | collective-permute-start | bytes 786440 | tf_op jit(solution)/shard_map/ppermute | solution.py:402
  106.4 1.6 %collective-permute-done.9.over_ref = bf16[512,512]{1,0:T(8,128)(2,1)S(1)} collective-permute-done((bf16[512,512]{1,0:T(8,128)(2,1)S(1)}, bf16[512,512]{1,0:T(8,128)(2,1)S(1)}, u32[]{:S(2)}, u32[]{:S(2)}) %collective-permute-start.9) | collective-permute-done | bytes 524320 | tf_op jit(solution)/shard_map/ppermute | solution.py:402
  108.0 0.0 collective-permute-start.10
  108.0 0.5 collective-permute-start.19
  108.5 4.5 %collective-permute-done.18.refs_2_.refs_0_ = bf16[256,512]{1,0:T(8,128)(2,1)S(1)} collective-permute-done((bf16[256,512]{1,0:T(8,128)(2,1)S(1)}, bf16[256,512]{1,0:T(8,128)(2,1)S(1)}, u32[]{:S(2)}, u32[]{:S(2)}) %collective-permute-start.18) | collective-permute-done | bytes 262176 | tf_op jit(solution)/shard_map/ppermute | solution.py:402
  113.0 0.5 collective-permute-start.20
  113.5 1.6 %collective-permute-start.22 = (bf16[128,512]{1,0:T(8,128)(2,1)S(1)}, bf16[128,512]{1,0:T(8,128)(2,1)S(1)}, u32[]{:S(2)}, u32[]{:S(2)}) collective-permute-start(bf16[128,512]{1,0:T(8,128)(2,1)S(1)} %shard_map.112), channel_id=1, source_target_pairs={{0,2},{1,3},{2,0},{3,1},{4,6},{5,7},{6,4},{7,5},{8,10},{9,11},{10,... | collective-permute-start | bytes 393224 | tf_op jit(solution)/shard_map/ppermute | solution.py:402
  115.1 2.4 %collective-permute-start.23 = (bf16[128,512]{1,0:T(8,128)(2,1)S(1)}, bf16[128,512]{1,0:T(8,128)(2,1)S(1)}, u32[]{:S(2)}, u32[]{:S(2)}) collective-permute-start(bf16[128,512]{1,0:T(8,128)(2,1)S(1)} %shard_map.114), channel_id=1, source_target_pairs={{0,4},{4,0},{8,12},{12,8},{16,20},{20,16},{24,28},{28,24},{1,5},{5... | collective-permute-start | bytes 393224 | tf_op jit(solution)/shard_map/ppermute | solution.py:402
  117.5 2.6 %shard_map.111 = (f32[1024,512]{1,0:T(8,128)}, f32[4,512,512]{2,1,0:T(8,128)}, f32[8,128]{1,0:T(8,128)S(1)}) custom-call(bf16[512,512]{1,0:T(8,128)(2,1)S(1)} %shard_map.108.mine_ref, bf16[512,512]{1,0:T(8,128)(2,1)S(1)} %collective-permute-done.8.other_ref, bf16[512,512]{1,0:T(8,128)(2,1)S(1)} %collective-permute-done.9.over_ref, ...), custom_call_target="tpu_custom_call" | custom-call | tf_op jit(solution)/shard_map/pallas_call | solution.py:582
  120.2 0.1 collective-permute-start.24
  120.3 0.6 collective-permute-done.23.refs_0_
  120.9 0.1 collective-permute-start.25
  121.0 0.6 collective-permute-done.24.refs_2_
  121.6 0.7 collective-permute-done.25.refs_3_
  122.3 1.1 shard_map.116
  (35 shorter events, 0.2 us)
Async XLA Ops:
  0.6 17.0 %copy-start = (bf16[1024,512]{1,0:T(8,128)(2,1)S(1)}, bf16[1024,512]{1,0:T(8,128)(2,1)}, u32[]{:S(2)}) copy-start(bf16[1024,512]{1,0:T(8,128)(2,1)} %refs_1_.1) | copy-start | bytes 3145732
  3.3 14.3 %all-to-all-start = ((bf16[8,8,640]{2,1,0:T(8,128)(2,1)}), bf16[8,8,640]{2,1,0:T(8,128)(2,1)S(1)}, u32[]{:S(2)}, u32[]{:S(2)}) async-start(bf16[8,8,640]{2,1,0:T(8,128)(2,1)} %get-tuple-element.29), calls=%async_computation | async-start | bytes 163840 | tf_op jit(solution)/shard_map/all_to_all | solution.py:406
  17.6 1.0 copy-start.2
  18.7 12.2 %copy-start.4 = (bf16[512,512]{1,0:T(8,128)(2,1)S(1)}, bf16[512,512]{1,0:T(8,128)(2,1)}, u32[]{:S(2)}) copy-start(bf16[512,512]{1,0:T(8,128)(2,1)} %get-tuple-element.36.refs_4_.refs_7_) | copy-start | bytes 1572868
  21.3 29.0 %copy-start.7 = (s32[1,512]{1,0:T(1,128)S(1)}, s32[1,512]{1,0:T(1,128)}, u32[]{:S(2)}) copy-start(s32[1,512]{1,0:T(1,128)} %get-tuple-element.30.refs_4_.refs_0_) | copy-start | bytes 6148
  21.3 29.0 %all-to-all-start.1 = ((bf16[8,128,512]{2,1,0:T(8,128)(2,1)}), bf16[8,128,512]{2,1,0:T(8,128)(2,1)S(1)}, u32[]{:S(2)}, u32[]{:S(2)}) async-start(bf16[8,128,512]{2,1,0:T(8,128)(2,1)} %bitcast.5), calls=%async_computation.1 | async-start | bytes 2097152 | tf_op jit(solution)/shard_map/all_to_all | solution.py:406
  25.0 4.4 %collective-permute-start.2 = (bf16[64,512]{1,0:T(8,128)(2,1)S(1)}, bf16[64,512]{1,0:T(8,128)(2,1)S(1)}, u32[]{:S(2)}, u32[]{:S(2)}) collective-permute-start(bf16[64,512]{1,0:T(8,128)(2,1)S(1)} %get-tuple-element.34.refs_0_.refs_1_), channel_id=1, source_target_pairs={{0,3},{1,2},{2,1},{3,0},{4,7},{5,6},{6,5},{7,4},{8,11},{9,10},{10,... | collective-permute-start | bytes 196616 | tf_op jit(solution)/shard_map/ppermute | solution.py:402
  25.1 5.8 %collective-permute-start.1 = (bf16[64,512]{1,0:T(8,128)(2,1)S(1)}, bf16[64,512]{1,0:T(8,128)(2,1)S(1)}, u32[]{:S(2)}, u32[]{:S(2)}) collective-permute-start(bf16[64,512]{1,0:T(8,128)(2,1)S(1)} %get-tuple-element.34.refs_0_.refs_1_), channel_id=1, source_target_pairs={{0,2},{1,3},{2,0},{3,1},{4,6},{5,7},{6,4},{7,5},{8,10},{9,11},{10,... | collective-permute-start | bytes 196616 | tf_op jit(solution)/shard_map/ppermute | solution.py:402
  26.7 4.2 %collective-permute-start = (bf16[64,512]{1,0:T(8,128)(2,1)S(1)}, bf16[64,512]{1,0:T(8,128)(2,1)S(1)}, u32[]{:S(2)}, u32[]{:S(2)}) collective-permute-start(bf16[64,512]{1,0:T(8,128)(2,1)S(1)} %get-tuple-element.34.refs_0_.refs_1_), channel_id=1, source_target_pairs={{0,1},{1,0},{2,3},{3,2},{4,5},{5,4},{6,7},{7,6},{8,9},{9,8},{10,11... | collective-permute-start | bytes 196616 | tf_op jit(solution)/shard_map/ppermute | solution.py:402
  50.3 7.3 %copy-start.3 = (bf16[512,512]{1,0:T(8,128)(2,1)S(1)}, bf16[512,512]{1,0:T(8,128)(2,1)}, u32[]{:S(2)}) copy-start(bf16[512,512]{1,0:T(8,128)(2,1)} %get-tuple-element.31.refs_2_.refs_1_) | copy-start | bytes 1572868
  50.3 7.3 %copy-start.5 = (s32[512]{0:T(512)S(1)}, s32[512]{0:T(512)}, u32[]{:S(2)}) copy-start(s32[512]{0:T(512)} %param.10) | copy-start | bytes 6148
  53.8 36.6 %all-to-all-start.2 = ((bf16[8,160,512]{2,1,0:T(8,128)(2,1)}), bf16[8,160,512]{2,1,0:T(8,128)(2,1)S(1)}, u32[]{:S(2)}, u32[]{:S(2)}) async-start(bf16[8,160,512]{2,1,0:T(8,128)(2,1)} %get-tuple-element.37.refs_3_), calls=%async_computation.2 | async-start | bytes 2621440 | tf_op jit(solution)/shard_map/all_to_all | solution.py:406
  58.7 2.0 %collective-permute-start.4 = (bf16[512,512]{1,0:T(8,128)(2,1)S(1)}, bf16[512,512]{1,0:T(8,128)(2,1)S(1)}, u32[]{:S(2)}, u32[]{:S(2)}) collective-permute-start(bf16[512,512]{1,0:T(8,128)(2,1)S(1)} %get-tuple-element.42), channel_id=1, source_target_pairs={{0,1},{1,0},{2,3},{3,2},{4,5},{5,4},{6,7},{7,6},{8,9},{9,8},{10,11... | collective-permute-start | bytes 1572872 | tf_op jit(solution)/shard_map/ppermute | solution.py:402
  59.9 2.5 %collective-permute-start.3 = (bf16[512,512]{1,0:T(8,128)(2,1)S(1)}, bf16[512,512]{1,0:T(8,128)(2,1)S(1)}, u32[]{:S(2)}, u32[]{:S(2)}) collective-permute-start(bf16[512,512]{1,0:T(8,128)(2,1)S(1)} %get-tuple-element.39.refs_3_), channel_id=1, source_target_pairs={{0,1},{1,0},{2,3},{3,2},{4,5},{5,4},{6,7},{7,6},{8,9},{9,8},{10,11... | collective-permute-start | bytes 1572872 | tf_op jit(solution)/shard_map/ppermute | solution.py:402
  60.8 14.0 %collective-permute-start.5 = (bf16[512,512]{1,0:T(8,128)(2,1)S(1)}, bf16[512,512]{1,0:T(8,128)(2,1)S(1)}, u32[]{:S(2)}, u32[]{:S(2)}) collective-permute-start(bf16[512,512]{1,0:T(8,128)(2,1)S(1)} %shard_map.101.refs_2_), channel_id=1, source_target_pairs={{0,2},{1,3},{2,0},{3,1},{4,6},{5,7},{6,4},{7,5},{8,10},{9,11},{10,... | collective-permute-start | bytes 1572872 | tf_op jit(solution)/shard_map/ppermute | solution.py:402
  62.4 14.3 %copy-start.1 = (bf16[4,512,512]{2,1,0:T(8,128)(2,1)S(1)}, bf16[4,512,512]{2,1,0:T(8,128)(2,1)}, u32[]{:S(2)}) copy-start(bf16[4,512,512]{2,1,0:T(8,128)(2,1)} %refs_2_.3) | copy-start | bytes 6291460
  62.4 14.3 %copy-start.6 = (s32[512]{0:T(512)S(1)}, s32[512]{0:T(512)}, u32[]{:S(2)}) copy-start(s32[512]{0:T(512)} %param.9) | copy-start | bytes 6148
  74.9 15.4 %copy-start.8 = (s32[1,32]{1,0:T(1,128)S(1)}, s32[1,32]{1,0:T(1,128)}, u32[]{:S(2)}) copy-start(s32[1,32]{1,0:T(1,128)} %get-tuple-element.33.refs_1_) | copy-start | bytes 388
  74.9 10.2 %collective-permute-start.6 = (bf16[256,512]{1,0:T(8,128)(2,1)S(1)}, bf16[256,512]{1,0:T(8,128)(2,1)S(1)}, u32[]{:S(2)}, u32[]{:S(2)}) collective-permute-start(bf16[256,512]{1,0:T(8,128)(2,1)S(1)} %get-tuple-element.43.refs_4_), channel_id=1, source_target_pairs={{0,4},{4,0},{8,12},{12,8},{16,20},{20,16},{24,28},{28,24},{1,5},{5... | collective-permute-start | bytes 786440 | tf_op jit(solution)/shard_map/ppermute | solution.py:402
  85.2 9.7 %collective-permute-start.12 = (bf16[64,512]{1,0:T(8,128)(2,1)S(1)}, bf16[64,512]{1,0:T(8,128)(2,1)S(1)}, u32[]{:S(2)}, u32[]{:S(2)}) collective-permute-start(bf16[64,512]{1,0:T(8,128)(2,1)S(1)} %get-tuple-element.49), channel_id=1, source_target_pairs={{0,16},{4,20},{8,24},{12,28},{16,0},{20,4},{24,8},{28,12},{1,17},{... | collective-permute-start | bytes 196616 | tf_op jit(solution)/shard_map/ppermute | solution.py:402
  88.8 6.1 %collective-permute-start.13 = (bf16[64,512]{1,0:T(8,128)(2,1)S(1)}, bf16[64,512]{1,0:T(8,128)(2,1)S(1)}, u32[]{:S(2)}, u32[]{:S(2)}) collective-permute-start(bf16[64,512]{1,0:T(8,128)(2,1)S(1)} %get-tuple-element.50), channel_id=1, source_target_pairs={{0,24},{4,28},{8,16},{12,20},{16,8},{20,12},{24,0},{28,4},{1,25},{... | collective-permute-start | bytes 196616 | tf_op jit(solution)/shard_map/ppermute | solution.py:402
  89.7 5.2 %collective-permute-start.11 = (bf16[64,512]{1,0:T(8,128)(2,1)S(1)}, bf16[64,512]{1,0:T(8,128)(2,1)S(1)}, u32[]{:S(2)}, u32[]{:S(2)}) collective-permute-start(bf16[64,512]{1,0:T(8,128)(2,1)S(1)} %get-tuple-element.47.refs_4_), channel_id=1, source_target_pairs={{0,8},{4,12},{8,0},{12,4},{16,24},{20,28},{24,16},{28,20},{1,9},{5... | collective-permute-start | bytes 196616 | tf_op jit(solution)/shard_map/ppermute | solution.py:402
  91.2 2.0 %collective-permute-start.7 = (bf16[512,512]{1,0:T(8,128)(2,1)S(1)}, bf16[512,512]{1,0:T(8,128)(2,1)S(1)}, u32[]{:S(2)}, u32[]{:S(2)}) collective-permute-start(bf16[512,512]{1,0:T(8,128)(2,1)S(1)} %shard_map.106.refs_4_), channel_id=1, source_target_pairs={{0,1},{1,0},{2,3},{3,2},{4,5},{5,4},{6,7},{7,6},{8,9},{9,8},{10,11... | collective-permute-start | bytes 1572872 | tf_op jit(solution)/shard_map/ppermute | solution.py:402
  93.3 14.6 %collective-permute-start.9 = (bf16[512,512]{1,0:T(8,128)(2,1)S(1)}, bf16[512,512]{1,0:T(8,128)(2,1)S(1)}, u32[]{:S(2)}, u32[]{:S(2)}) collective-permute-start(bf16[512,512]{1,0:T(8,128)(2,1)S(1)} %shard_map.108.mine_ref), channel_id=1, source_target_pairs={{0,2},{1,3},{2,0},{3,1},{4,6},{5,7},{6,4},{7,5},{8,10},{9,11},{10,... | collective-permute-start | bytes 1572872 | tf_op jit(solution)/shard_map/ppermute | solution.py:402
  95.0 6.3 %collective-permute-start.16 = (bf16[64,512]{1,0:T(8,128)(2,1)S(1)}, bf16[64,512]{1,0:T(8,128)(2,1)S(1)}, u32[]{:S(2)}, u32[]{:S(2)}) collective-permute-start(bf16[64,512]{1,0:T(8,128)(2,1)S(1)} %shard_map.109.refs_0_), channel_id=1, source_target_pairs={{0,24},{4,28},{8,16},{12,20},{16,8},{20,12},{24,0},{28,4},{1,25},{... | collective-permute-start | bytes 196616 | tf_op jit(solution)/shard_map/ppermute | solution.py:402
  97.3 6.9 %collective-permute-start.15 = (bf16[64,512]{1,0:T(8,128)(2,1)S(1)}, bf16[64,512]{1,0:T(8,128)(2,1)S(1)}, u32[]{:S(2)}, u32[]{:S(2)}) collective-permute-start(bf16[64,512]{1,0:T(8,128)(2,1)S(1)} %shard_map.109.refs_0_), channel_id=1, source_target_pairs={{0,16},{4,20},{8,24},{12,28},{16,0},{20,4},{24,8},{28,12},{1,17},{... | collective-permute-start | bytes 196616 | tf_op jit(solution)/shard_map/ppermute | solution.py:402
  98.0 6.3 %collective-permute-start.14 = (bf16[64,512]{1,0:T(8,128)(2,1)S(1)}, bf16[64,512]{1,0:T(8,128)(2,1)S(1)}, u32[]{:S(2)}, u32[]{:S(2)}) collective-permute-start(bf16[64,512]{1,0:T(8,128)(2,1)S(1)} %shard_map.109.refs_0_), channel_id=1, source_target_pairs={{0,8},{4,12},{8,0},{12,4},{16,24},{20,28},{24,16},{28,20},{1,9},{5... | collective-permute-start | bytes 196616 | tf_op jit(solution)/shard_map/ppermute | solution.py:402
  104.2 8.7 %collective-permute-start.18 = (bf16[256,512]{1,0:T(8,128)(2,1)S(1)}, bf16[256,512]{1,0:T(8,128)(2,1)S(1)}, u32[]{:S(2)}, u32[]{:S(2)}) collective-permute-start(bf16[256,512]{1,0:T(8,128)(2,1)S(1)} %shard_map.110.refs_0_), channel_id=1, source_target_pairs={{0,2},{1,3},{2,0},{3,1},{4,6},{5,7},{6,4},{7,5},{8,10},{9,11},{10,... | collective-permute-start | bytes 786440 | tf_op jit(solution)/shard_map/ppermute | solution.py:402
  104.8 8.2 %collective-permute-start.17 = (bf16[256,512]{1,0:T(8,128)(2,1)S(1)}, bf16[256,512]{1,0:T(8,128)(2,1)S(1)}, u32[]{:S(2)}, u32[]{:S(2)}) collective-permute-start(bf16[256,512]{1,0:T(8,128)(2,1)S(1)} %shard_map.110.refs_0_), channel_id=1, source_target_pairs={{0,4},{4,0},{8,12},{12,8},{16,20},{20,16},{24,28},{28,24},{1,5},{5... | collective-permute-start | bytes 786440 | tf_op jit(solution)/shard_map/ppermute | solution.py:402
  106.4 11.1 %collective-permute-start.8 = (bf16[512,512]{1,0:T(8,128)(2,1)S(1)}, bf16[512,512]{1,0:T(8,128)(2,1)S(1)}, u32[]{:S(2)}, u32[]{:S(2)}) collective-permute-start(bf16[512,512]{1,0:T(8,128)(2,1)S(1)} %shard_map.108.mine_ref), channel_id=1, source_target_pairs={{0,1},{1,0},{2,3},{3,2},{4,5},{5,4},{6,7},{7,6},{8,9},{9,8},{10,11... | collective-permute-start | bytes 1572872 | tf_op jit(solution)/shard_map/ppermute | solution.py:402
  108.0 9.5 %collective-permute-start.10 = (bf16[512,512]{1,0:T(8,128)(2,1)S(1)}, bf16[512,512]{1,0:T(8,128)(2,1)S(1)}, u32[]{:S(2)}, u32[]{:S(2)}) collective-permute-start(bf16[512,512]{1,0:T(8,128)(2,1)S(1)} %collective-permute-done.9.over_ref), channel_id=1, source_target_pairs={{0,1},{1,0},{2,3},{3,2},{4,5},{5,4},{6,7},{7,6},{8,9},{9,8},{10,11... | collective-permute-start | bytes 1572872 | tf_op jit(solution)/shard_map/ppermute | solution.py:402
  108.0 5.5 %collective-permute-start.19 = (bf16[256,512]{1,0:T(8,128)(2,1)S(1)}, bf16[256,512]{1,0:T(8,128)(2,1)S(1)}, u32[]{:S(2)}, u32[]{:S(2)}) collective-permute-start(bf16[256,512]{1,0:T(8,128)(2,1)S(1)} %shard_map.110.refs_0_), channel_id=1, source_target_pairs={{0,1},{1,0},{2,3},{3,2},{4,5},{5,4},{6,7},{7,6},{8,9},{9,8},{10,11... | collective-permute-start | bytes 786440 | tf_op jit(solution)/shard_map/ppermute | solution.py:402
  113.0 2.1 %collective-permute-start.21 = (bf16[256,512]{1,0:T(8,128)(2,1)S(1)}, bf16[256,512]{1,0:T(8,128)(2,1)S(1)}, u32[]{:S(2)}, u32[]{:S(2)}) collective-permute-start(bf16[256,512]{1,0:T(8,128)(2,1)S(1)} %collective-permute-done.18.refs_2_.refs_0_), channel_id=1, source_target_pairs={{0,1},{1,0},{2,3},{3,2},{4,5},{5,4},{6,7},{7,6},{8,9},{9,8},{10,11... | collective-permute-start | bytes 786440 | tf_op jit(solution)/shard_map/ppermute | solution.py:402
  113.0 4.5 %collective-permute-start.20 = (bf16[256,512]{1,0:T(8,128)(2,1)S(1)}, bf16[256,512]{1,0:T(8,128)(2,1)S(1)}, u32[]{:S(2)}, u32[]{:S(2)}) collective-permute-start(bf16[256,512]{1,0:T(8,128)(2,1)S(1)} %collective-permute-done.17.refs_1_.refs_0_), channel_id=1, source_target_pairs={{0,1},{1,0},{2,3},{3,2},{4,5},{5,4},{6,7},{7,6},{8,9},{9,8},{10,11... | collective-permute-start | bytes 786440 | tf_op jit(solution)/shard_map/ppermute | solution.py:402
  113.5 6.7 %collective-permute-start.22 = (bf16[128,512]{1,0:T(8,128)(2,1)S(1)}, bf16[128,512]{1,0:T(8,128)(2,1)S(1)}, u32[]{:S(2)}, u32[]{:S(2)}) collective-permute-start(bf16[128,512]{1,0:T(8,128)(2,1)S(1)} %shard_map.112), channel_id=1, source_target_pairs={{0,2},{1,3},{2,0},{3,1},{4,6},{5,7},{6,4},{7,5},{8,10},{9,11},{10,... | collective-permute-start | bytes 393224 | tf_op jit(solution)/shard_map/ppermute | solution.py:402
  115.1 5.8 %collective-permute-start.23 = (bf16[128,512]{1,0:T(8,128)(2,1)S(1)}, bf16[128,512]{1,0:T(8,128)(2,1)S(1)}, u32[]{:S(2)}, u32[]{:S(2)}) collective-permute-start(bf16[128,512]{1,0:T(8,128)(2,1)S(1)} %shard_map.114), channel_id=1, source_target_pairs={{0,4},{4,0},{8,12},{12,8},{16,20},{20,16},{24,28},{28,24},{1,5},{5... | collective-permute-start | bytes 393224 | tf_op jit(solution)/shard_map/ppermute | solution.py:402
  120.2 1.4 %collective-permute-start.24 = (bf16[128,512]{1,0:T(8,128)(2,1)S(1)}, bf16[128,512]{1,0:T(8,128)(2,1)S(1)}, u32[]{:S(2)}, u32[]{:S(2)}) collective-permute-start(bf16[128,512]{1,0:T(8,128)(2,1)S(1)} %shard_map.113.refs_0_), channel_id=1, source_target_pairs={{0,1},{1,0},{2,3},{3,2},{4,5},{5,4},{6,7},{7,6},{8,9},{9,8},{10,11... | collective-permute-start | bytes 393224 | tf_op jit(solution)/shard_map/ppermute | solution.py:402
  120.9 1.4 %collective-permute-start.25 = (bf16[128,512]{1,0:T(8,128)(2,1)S(1)}, bf16[128,512]{1,0:T(8,128)(2,1)S(1)}, u32[]{:S(2)}, u32[]{:S(2)}) collective-permute-start(bf16[128,512]{1,0:T(8,128)(2,1)S(1)} %shard_map.115.refs_1_), channel_id=1, source_target_pairs={{0,1},{1,0},{2,3},{3,2},{4,5},{5,4},{6,7},{7,6},{8,9},{9,8},{10,11... | collective-permute-start | bytes 393224 | tf_op jit(solution)/shard_map/ppermute | solution.py:402

commit v12 on v11

--- a/solution.py
+++ b/solution.py
@@ -172,7 +172,7 @@
     query_ref[...] = total.astype(BF)
 
 
-def lookup_kernel(cap, request_ref, entities, ids_ref, rows_ref, negs_ref):
+def lookup_kernel(cap, request_ref, entities, ids_ref, rows_ref):
     parts, share, width = request_ref.shape
     columns = rows_ref.shape[1]
     pieces = []
@@ -182,6 +182,10 @@
     ids = jnp.concatenate(pieces, axis=1).astype(I32)
     ids_ref[...] = ids
     rows_ref[...] = dot(hot_rows(ids, entities.shape[0]), entities[...]).astype(BF)
+
+
+def negatives_kernel(request_ref, negs_ref):
+    parts, columns = request_ref.shape[0], negs_ref.shape[1]
     negs_ref[...] = jnp.concatenate(
         [request_ref[index, :, :columns].astype(F32) for index in range(parts)], axis=0
     ).astype(BF)
@@ -444,13 +448,16 @@
         (slot,),
         room=60,
     )
-    asked, found, neg_near = call(
+    asked, found = call(
         functools.partial(lookup_kernel, cap),
-        [((1, slots), I32), ((slots, columns), BF), ((parts * share, columns), BF)],
+        [((1, slots), I32), ((slots, columns), BF)],
         (),
         (requests, entities),
         (),
         (rows,),
+    )
+    (neg_near,) = call(
+        negatives_kernel, [((parts * share, columns), BF)], (), (requests,), (), (found,)
     )
     got = exchange(found.reshape(parts, cap, columns)).reshape(slots, columns)
     neg_core, neg_across, neg_both = [flip(neg_near, "rep", reps, k) for k in (1, 2, 3)]

time: 124 us -> 124 us (level)
    pallas_call x21 -> x22, Pallas kernels: 20.9 us -> 20.9 us  [call(): pl.pallas_call(kernel, out_shape=[jax.ShapeDtypeStruct(out[0], out[1]) fo...]
where the time goes in v12:
time: 124 us
  waiting for transfers between devices  58.3 us (47%)
  starting transfers between devices  38.5 us (31%)
  Pallas kernels  24.6 us (20%)
    ppermute x26, waiting for transfers between devices, flip(): return lax.ppermute(x, axis, [(i, i ^ bit) for i in range(size)])  36 us
    ppermute x26, starting transfers between devices, flip(): return lax.ppermute(x, axis, [(i, i ^ bit) for i in range(size)])  23.8 us
    all_to_all x3, waiting for transfers between devices, exchange(): return lax.all_to_all(x, 'dom', split_axis=0, concat_axis=0, tiled=True)  22.3 us
    pallas_call x22, Pallas kernels, call(): pl.pallas_call(kernel, out_shape=[jax.ShapeDtypeStruct(out[0], out[1]) fo...  20.9 us
    all_to_all x3, starting transfers between devices, exchange(): return lax.all_to_all(x, 'dom', split_axis=0, concat_axis=0, tiled=True)  14.7 us
    pallas_call x1, Pallas kernels, local(): pl.pallas_call(functools.partial(join_kernel, [places[k] for k in early])...  2.65 us
  transfers between devices with their start and end apart: 29, of which 16 were waited for; matrix products, arithmetic and copies ran while one was open for 0% of the time, Pallas kernels for 12%

profile of v12, /device:TPU:0, one launch (start us, length us, event | category | flops | bytes accessed | tf_op | source)
XLA Modules:
  0.0 123.6 jit_solution(14064791324073441264)
XLA Ops:
  0.6 0.0 copy-start
  0.6 2.7 %shard_map.94 = (s32[1,512]{1,0:T(1,128)}, s32[1,32]{1,0:T(1,128)}, bf16[8,8,640]{2,1,0:T(8,128)(2,1)}) custom-call(s32[1,512]{1,0:T(1,128)} %bitcast.15, s32[1,512]{1,0:T(1,128)} %bitcast.16, s32[1,32]{1,0:T(1,128)} %bitcast.17, bf16[1024,512]{1,0:T(8,128)(2,1)} %refs_1_.1), custom_call_target="tpu_custom_call" | custom-call | flops 1 | bytes 1 | tf_op jit(solution)/shard_map/pallas_call | solution.py:60
  3.3 7.3 %all-to-all-start = ((bf16[8,8,640]{2,1,0:T(8,128)(2,1)}), bf16[8,8,640]{2,1,0:T(8,128)(2,1)S(1)}, u32[]{:S(2)}, u32[]{:S(2)}) async-start(bf16[8,8,640]{2,1,0:T(8,128)(2,1)} %get-tuple-element.28), calls=%async_computation | async-start | bytes 163840 | tf_op jit(solution)/shard_map/all_to_all | solution.py:410
  10.6 4.4 %shard_map.95 = (bf16[512,512]{1,0:T(8,128)(2,1)}, bf16[512,512]{1,0:T(8,128)(2,1)}) custom-call(s32[1,512]{1,0:T(1,128)} %bitcast.13, s32[1,512]{1,0:T(1,128)} %bitcast.9, bf16[1024,512]{1,0:T(8,128)(2,1)} %refs_1_.1, bf16[4,512,512]{2,1,0:T(8,128)(2,1)} %refs_2_.3, s32[1,512]{1,0:T(1,128)} %get-tuple-element.29.refs_4_.refs_0_), custom_call_target="tpu_custom_call" | custom-call | flops 1 | bytes 1 | tf_op jit(solution)/shard_map/pallas_call | solution.py:60
  15.0 2.6 %all-to-all-done.refs_0_ = bf16[8,8,640]{2,1,0:T(8,128)(2,1)S(1)} async-done(((bf16[8,8,640]{2,1,0:T(8,128)(2,1)}), bf16[8,8,640]{2,1,0:T(8,128)(2,1)S(1)}, u32[]{:S(2)}, u32[]{:S(2)}) %all-to-all-start) | async-done | bytes 81952 | tf_op jit(solution)/shard_map/all_to_all | solution.py:410
  17.6 1.0 copy-done.2
  18.7 2.6 %shard_map.96 = (s32[1,1024]{1,0:T(1,128)S(1)}, bf16[1024,512]{1,0:T(8,128)(2,1)}) custom-call(bf16[8,8,640]{2,1,0:T(8,128)(2,1)S(1)} %all-to-all-done.refs_0_, bf16[1024,512]{1,0:T(8,128)(2,1)S(1)} %copy-done, bf16[512,512]{1,0:T(8,128)(2,1)S(1)} %copy-done.2), custom_call_target="tpu_custom_call" | custom-call | flops 1 | bytes 1 | tf_op jit(solution)/shard_map/pallas_call | solution.py:60
  21.3 3.7 %all-to-all-start.1 = ((bf16[8,128,512]{2,1,0:T(8,128)(2,1)}), bf16[8,128,512]{2,1,0:T(8,128)(2,1)S(1)}, u32[]{:S(2)}, u32[]{:S(2)}) async-start(bf16[8,128,512]{2,1,0:T(8,128)(2,1)} %bitcast.5), calls=%async_computation.1 | async-start | bytes 2097152 | tf_op jit(solution)/shard_map/all_to_all | solution.py:410
  25.0 0.1 collective-permute-start.2
  25.1 1.6 %collective-permute-start.1 = (bf16[64,512]{1,0:T(8,128)(2,1)S(1)}, bf16[64,512]{1,0:T(8,128)(2,1)S(1)}, u32[]{:S(2)}, u32[]{:S(2)}) collective-permute-start(bf16[64,512]{1,0:T(8,128)(2,1)S(1)} %shard_map.97.refs_0_.refs_1_), channel_id=1, source_target_pairs={{0,2},{1,3},{2,0},{3,1},{4,6},{5,7},{6,4},{7,5},{8,10},{9,11},{10,... | collective-permute-start | bytes 196616 | tf_op jit(solution)/shard_map/ppermute | solution.py:406
  26.7 0.3 collective-permute-start
  26.9 2.4 %collective-permute-done.2.refs_3_.refs_4_ = bf16[64,512]{1,0:T(8,128)(2,1)S(1)} collective-permute-done((bf16[64,512]{1,0:T(8,128)(2,1)S(1)}, bf16[64,512]{1,0:T(8,128)(2,1)S(1)}, u32[]{:S(2)}, u32[]{:S(2)}) %collective-permute-start.2) | collective-permute-done | bytes 65568 | tf_op jit(solution)/shard_map/ppermute | solution.py:406
  29.4 1.5 %collective-permute-done.1.refs_2_.refs_3_ = bf16[64,512]{1,0:T(8,128)(2,1)S(1)} collective-permute-done((bf16[64,512]{1,0:T(8,128)(2,1)S(1)}, bf16[64,512]{1,0:T(8,128)(2,1)S(1)}, u32[]{:S(2)}, u32[]{:S(2)}) %collective-permute-start.1) | collective-permute-done | bytes 65568 | tf_op jit(solution)/shard_map/ppermute | solution.py:406
  30.9 0.0 collective-permute-done.refs_1_.refs_2_
  30.9 0.3 shard_map.98.refs_6_
  31.2 19.1 %all-to-all-done.1 = bf16[8,128,512]{2,1,0:T(8,128)(2,1)S(1)} async-done(((bf16[8,128,512]{2,1,0:T(8,128)(2,1)}), bf16[8,128,512]{2,1,0:T(8,128)(2,1)S(1)}, u32[]{:S(2)}, u32[]{:S(2)}) %all-to-all-start.1) | async-done | bytes 1048608 | tf_op jit(solution)/shard_map/all_to_all | solution.py:410
  50.3 3.5 %shard_map.99 = (f32[1,512]{1,0:T(1,128)}, bf16[512,512]{1,0:T(8,128)(2,1)S(1)}, bf16[8,160,512]{2,1,0:T(8,128)(2,1)}) custom-call(s32[1,512]{1,0:T(1,128)S(1)} %copy-done.7, bf16[64,512]{1,0:T(8,128)(2,1)S(1)} %shard_map.97.refs_0_.refs_1_, bf16[64,512]{1,0:T(8,128)(2,1)S(1)} %collective-permute-done.refs_1_.refs_2_, ...), custom_call_target="tpu_custom_call" | custom-call | flops 1 | bytes 1 | tf_op jit(solution)/shard_map/pallas_call | solution.py:60
  53.8 3.8 %all-to-all-start.2 = ((bf16[8,160,512]{2,1,0:T(8,128)(2,1)}), bf16[8,160,512]{2,1,0:T(8,128)(2,1)S(1)}, u32[]{:S(2)}, u32[]{:S(2)}) async-start(bf16[8,160,512]{2,1,0:T(8,128)(2,1)} %get-tuple-element.35.refs_3_), calls=%async_computation.2 | async-start | bytes 2621440 | tf_op jit(solution)/shard_map/all_to_all | solution.py:410
  57.6 1.1 shard_map.100
  58.7 0.1 collective-permute-start.4
  58.8 1.1 shard_map.101
  59.9 0.6 collective-permute-start.3
  60.5 0.2 collective-permute-done.4.refs_1_
  60.7 0.1 shard_map.102.refs_2_
  60.8 1.6 %collective-permute-start.5 = (bf16[512,512]{1,0:T(8,128)(2,1)S(1)}, bf16[512,512]{1,0:T(8,128)(2,1)S(1)}, u32[]{:S(2)}, u32[]{:S(2)}) collective-permute-start(bf16[512,512]{1,0:T(8,128)(2,1)S(1)} %shard_map.102.refs_2_), channel_id=1, source_target_pairs={{0,2},{1,3},{2,0},{3,1},{4,6},{5,7},{6,4},{7,5},{8,10},{9,11},{10,... | collective-permute-start | bytes 1572872 | tf_op jit(solution)/shard_map/ppermute | solution.py:406
  62.4 0.1 shard_map.103.refs_0_
  62.5 12.3 %collective-permute-done.5.refs_1_ = bf16[512,512]{1,0:T(8,128)(2,1)S(1)} collective-permute-done((bf16[512,512]{1,0:T(8,128)(2,1)S(1)}, bf16[512,512]{1,0:T(8,128)(2,1)S(1)}, u32[]{:S(2)}, u32[]{:S(2)}) %collective-permute-start.5) | collective-permute-done | bytes 524320 | tf_op jit(solution)/shard_map/ppermute | solution.py:406
  74.8 0.1 shard_map.104
  74.9 1.8 %collective-permute-start.6 = (bf16[256,512]{1,0:T(8,128)(2,1)S(1)}, bf16[256,512]{1,0:T(8,128)(2,1)S(1)}, u32[]{:S(2)}, u32[]{:S(2)}) collective-permute-start(bf16[256,512]{1,0:T(8,128)(2,1)S(1)} %get-tuple-element.41.refs_4_), channel_id=1, source_target_pairs={{0,4},{4,0},{8,12},{12,8},{16,20},{20,16},{24,28},{28,24},{1,5},{5... | collective-permute-start | bytes 786440 | tf_op jit(solution)/shard_map/ppermute | solution.py:406
  76.7 2.7 %shard_map.105 = (bf16[512,512]{1,0:T(8,128)(2,1)S(1)}, bf16[512,512]{1,0:T(8,128)(2,1)S(1)}) custom-call(bf16[512,512]{1,0:T(8,128)(2,1)S(1)} %get-tuple-element.36.refs_0_, s32[1,512]{1,0:T(1,128)S(1)} %bitcast.12, bf16[4,512,512]{2,1,0:T(8,128)(2,1)S(1)} %copy-done.1, s32[1,512]{1,0:T(1,128)S(1)} %bitcast.14, bf16[256,512]{1,0:T(8,128)(2,1)S(1)} %get-tuple-element.41.refs_4_), custom_call_target="tpu_custom_call" | custom-call | flops 1 | bytes 1 | tf_op jit(solution)/shard_map/pallas_call | solution.py:60
  79.5 5.7 %collective-permute-done.6.refs_1_ = bf16[256,512]{1,0:T(8,128)(2,1)S(1)} collective-permute-done((bf16[256,512]{1,0:T(8,128)(2,1)S(1)}, bf16[256,512]{1,0:T(8,128)(2,1)S(1)}, u32[]{:S(2)}, u32[]{:S(2)}) %collective-permute-start.6) | collective-permute-done | bytes 262176 | tf_op jit(solution)/shard_map/ppermute | solution.py:406
  85.1 0.1 shard_map.106
  85.2 3.6 %collective-permute-start.12 = (bf16[64,512]{1,0:T(8,128)(2,1)S(1)}, bf16[64,512]{1,0:T(8,128)(2,1)S(1)}, u32[]{:S(2)}, u32[]{:S(2)}) collective-permute-start(bf16[64,512]{1,0:T(8,128)(2,1)S(1)} %get-tuple-element.47), channel_id=1, source_target_pairs={{0,16},{4,20},{8,24},{12,28},{16,0},{20,4},{24,8},{28,12},{1,17},{... | collective-permute-start | bytes 196616 | tf_op jit(solution)/shard_map/ppermute | solution.py:406
  88.8 0.9 collective-permute-start.13
  89.7 0.6 all-to-all-done.2.refs_2_
  90.3 0.9 shard_map.107.refs_4_
  91.2 0.1 collective-permute-start.7
  91.3 0.9 shard_map.108.refs_0_.refs_4_
  92.2 1.0 collective-permute-done.7.refs_1_
  93.2 0.1 shard_map.109.mine_ref
  93.3 1.6 %collective-permute-start.9 = (bf16[512,512]{1,0:T(8,128)(2,1)S(1)}, bf16[512,512]{1,0:T(8,128)(2,1)S(1)}, u32[]{:S(2)}, u32[]{:S(2)}) collective-permute-start(bf16[512,512]{1,0:T(8,128)(2,1)S(1)} %shard_map.109.mine_ref), channel_id=1, source_target_pairs={{0,2},{1,3},{2,0},{3,1},{4,6},{5,7},{6,4},{7,5},{8,10},{9,11},{10,... | collective-permute-start | bytes 1572872 | tf_op jit(solution)/shard_map/ppermute | solution.py:406
  94.9 0.0 collective-permute-done.12.refs_2_
  94.9 0.0 collective-permute-done.13.refs_3_
  94.9 0.0 collective-permute-done.11.refs_1_
  95.0 2.4 %collective-permute-start.16 = (bf16[64,512]{1,0:T(8,128)(2,1)S(1)}, bf16[64,512]{1,0:T(8,128)(2,1)S(1)}, u32[]{:S(2)}, u32[]{:S(2)}) collective-permute-start(bf16[64,512]{1,0:T(8,128)(2,1)S(1)} %shard_map.110.refs_0_), channel_id=1, source_target_pairs={{0,24},{4,28},{8,16},{12,20},{16,8},{20,12},{24,0},{28,4},{1,25},{... | collective-permute-start | bytes 196616 | tf_op jit(solution)/shard_map/ppermute | solution.py:406
  97.3 0.6 collective-permute-start.15
  98.0 1.4 %collective-permute-start.14 = (bf16[64,512]{1,0:T(8,128)(2,1)S(1)}, bf16[64,512]{1,0:T(8,128)(2,1)S(1)}, u32[]{:S(2)}, u32[]{:S(2)}) collective-permute-start(bf16[64,512]{1,0:T(8,128)(2,1)S(1)} %shard_map.110.refs_0_), channel_id=1, source_target_pairs={{0,8},{4,12},{8,0},{12,4},{16,24},{20,28},{24,16},{28,20},{1,9},{5... | collective-permute-start | bytes 196616 | tf_op jit(solution)/shard_map/ppermute | solution.py:406
  99.4 1.9 %collective-permute-done.16.refs_3_ = bf16[64,512]{1,0:T(8,128)(2,1)S(1)} collective-permute-done((bf16[64,512]{1,0:T(8,128)(2,1)S(1)}, bf16[64,512]{1,0:T(8,128)(2,1)S(1)}, u32[]{:S(2)}, u32[]{:S(2)}) %collective-permute-start.16) | collective-permute-done | bytes 65568 | tf_op jit(solution)/shard_map/ppermute | solution.py:406
  101.3 2.9 %collective-permute-done.15.refs_2_ = bf16[64,512]{1,0:T(8,128)(2,1)S(1)} collective-permute-done((bf16[64,512]{1,0:T(8,128)(2,1)S(1)}, bf16[64,512]{1,0:T(8,128)(2,1)S(1)}, u32[]{:S(2)}, u32[]{:S(2)}) %collective-permute-start.15) | collective-permute-done | bytes 65568 | tf_op jit(solution)/shard_map/ppermute | solution.py:406
  104.2 0.6 collective-permute-start.18
  104.8 1.6 %collective-permute-start.17 = (bf16[256,512]{1,0:T(8,128)(2,1)S(1)}, bf16[256,512]{1,0:T(8,128)(2,1)S(1)}, u32[]{:S(2)}, u32[]{:S(2)}) collective-permute-start(bf16[256,512]{1,0:T(8,128)(2,1)S(1)} %shard_map.111.refs_0_), channel_id=1, source_target_pairs={{0,4},{4,0},{8,12},{12,8},{16,20},{20,16},{24,28},{28,24},{1,5},{5... | collective-permute-start | bytes 786440 | tf_op jit(solution)/shard_map/ppermute | solution.py:406
  106.4 1.6 %collective-permute-done.9.over_ref = bf16[512,512]{1,0:T(8,128)(2,1)S(1)} collective-permute-done((bf16[512,512]{1,0:T(8,128)(2,1)S(1)}, bf16[512,512]{1,0:T(8,128)(2,1)S(1)}, u32[]{:S(2)}, u32[]{:S(2)}) %collective-permute-start.9) | collective-permute-done | bytes 524320 | tf_op jit(solution)/shard_map/ppermute | solution.py:406
  108.0 0.5 collective-permute-start.19
  108.5 4.5 %collective-permute-done.18.refs_2_.refs_0_ = bf16[256,512]{1,0:T(8,128)(2,1)S(1)} collective-permute-done((bf16[256,512]{1,0:T(8,128)(2,1)S(1)}, bf16[256,512]{1,0:T(8,128)(2,1)S(1)}, u32[]{:S(2)}, u32[]{:S(2)}) %collective-permute-start.18) | collective-permute-done | bytes 262176 | tf_op jit(solution)/shard_map/ppermute | solution.py:406
  113.0 0.5 collective-permute-start.20
  113.5 1.6 %collective-permute-start.22 = (bf16[128,512]{1,0:T(8,128)(2,1)S(1)}, bf16[128,512]{1,0:T(8,128)(2,1)S(1)}, u32[]{:S(2)}, u32[]{:S(2)}) collective-permute-start(bf16[128,512]{1,0:T(8,128)(2,1)S(1)} %shard_map.113), channel_id=1, source_target_pairs={{0,2},{1,3},{2,0},{3,1},{4,6},{5,7},{6,4},{7,5},{8,10},{9,11},{10,... | collective-permute-start | bytes 393224 | tf_op jit(solution)/shard_map/ppermute | solution.py:406
  115.1 2.4 %collective-permute-start.23 = (bf16[128,512]{1,0:T(8,128)(2,1)S(1)}, bf16[128,512]{1,0:T(8,128)(2,1)S(1)}, u32[]{:S(2)}, u32[]{:S(2)}) collective-permute-start(bf16[128,512]{1,0:T(8,128)(2,1)S(1)} %shard_map.115), channel_id=1, source_target_pairs={{0,4},{4,0},{8,12},{12,8},{16,20},{20,16},{24,28},{28,24},{1,5},{5... | collective-permute-start | bytes 393224 | tf_op jit(solution)/shard_map/ppermute | solution.py:406
  117.5 2.6 %shard_map.112 = (f32[1024,512]{1,0:T(8,128)}, f32[4,512,512]{2,1,0:T(8,128)}, f32[8,128]{1,0:T(8,128)S(1)}) custom-call(bf16[512,512]{1,0:T(8,128)(2,1)S(1)} %shard_map.109.mine_ref, bf16[512,512]{1,0:T(8,128)(2,1)S(1)} %collective-permute-done.8.other_ref, bf16[512,512]{1,0:T(8,128)(2,1)S(1)} %collective-permute-done.9.over_ref, ...), custom_call_target="tpu_custom_call" | custom-call | tf_op jit(solution)/shard_map/pallas_call | solution.py:589
  120.2 0.1 collective-permute-start.24
  120.3 0.6 collective-permute-done.23.refs_0_
  120.9 0.1 collective-permute-start.25
  121.0 0.6 collective-permute-done.24.refs_2_
  121.6 0.7 collective-permute-done.25.refs_3_
  122.3 1.1 shard_map.117
  (36 shorter events, 0.2 us)
Async XLA Ops:
  0.6 17.0 %copy-start = (bf16[1024,512]{1,0:T(8,128)(2,1)S(1)}, bf16[1024,512]{1,0:T(8,128)(2,1)}, u32[]{:S(2)}) copy-start(bf16[1024,512]{1,0:T(8,128)(2,1)} %refs_1_.1) | copy-start | bytes 3145732
  3.3 14.3 %all-to-all-start = ((bf16[8,8,640]{2,1,0:T(8,128)(2,1)}), bf16[8,8,640]{2,1,0:T(8,128)(2,1)S(1)}, u32[]{:S(2)}, u32[]{:S(2)}) async-start(bf16[8,8,640]{2,1,0:T(8,128)(2,1)} %get-tuple-element.28), calls=%async_computation | async-start | bytes 163840 | tf_op jit(solution)/shard_map/all_to_all | solution.py:410
  17.6 1.0 copy-start.2
  18.7 12.2 %copy-start.4 = (bf16[512,512]{1,0:T(8,128)(2,1)S(1)}, bf16[512,512]{1,0:T(8,128)(2,1)}, u32[]{:S(2)}) copy-start(bf16[512,512]{1,0:T(8,128)(2,1)} %get-tuple-element.34.refs_4_.refs_7_) | copy-start | bytes 1572868
  21.3 29.0 %copy-start.7 = (s32[1,512]{1,0:T(1,128)S(1)}, s32[1,512]{1,0:T(1,128)}, u32[]{:S(2)}) copy-start(s32[1,512]{1,0:T(1,128)} %get-tuple-element.29.refs_4_.refs_0_) | copy-start | bytes 6148
  21.3 29.0 %all-to-all-start.1 = ((bf16[8,128,512]{2,1,0:T(8,128)(2,1)}), bf16[8,128,512]{2,1,0:T(8,128)(2,1)S(1)}, u32[]{:S(2)}, u32[]{:S(2)}) async-start(bf16[8,128,512]{2,1,0:T(8,128)(2,1)} %bitcast.5), calls=%async_computation.1 | async-start | bytes 2097152 | tf_op jit(solution)/shard_map/all_to_all | solution.py:410
  25.0 4.4 %collective-permute-start.2 = (bf16[64,512]{1,0:T(8,128)(2,1)S(1)}, bf16[64,512]{1,0:T(8,128)(2,1)S(1)}, u32[]{:S(2)}, u32[]{:S(2)}) collective-permute-start(bf16[64,512]{1,0:T(8,128)(2,1)S(1)} %shard_map.97.refs_0_.refs_1_), channel_id=1, source_target_pairs={{0,3},{1,2},{2,1},{3,0},{4,7},{5,6},{6,5},{7,4},{8,11},{9,10},{10,... | collective-permute-start | bytes 196616 | tf_op jit(solution)/shard_map/ppermute | solution.py:406
  25.1 5.8 %collective-permute-start.1 = (bf16[64,512]{1,0:T(8,128)(2,1)S(1)}, bf16[64,512]{1,0:T(8,128)(2,1)S(1)}, u32[]{:S(2)}, u32[]{:S(2)}) collective-permute-start(bf16[64,512]{1,0:T(8,128)(2,1)S(1)} %shard_map.97.refs_0_.refs_1_), channel_id=1, source_target_pairs={{0,2},{1,3},{2,0},{3,1},{4,6},{5,7},{6,4},{7,5},{8,10},{9,11},{10,... | collective-permute-start | bytes 196616 | tf_op jit(solution)/shard_map/ppermute | solution.py:406
  26.7 4.2 %collective-permute-start = (bf16[64,512]{1,0:T(8,128)(2,1)S(1)}, bf16[64,512]{1,0:T(8,128)(2,1)S(1)}, u32[]{:S(2)}, u32[]{:S(2)}) collective-permute-start(bf16[64,512]{1,0:T(8,128)(2,1)S(1)} %shard_map.97.refs_0_.refs_1_), channel_id=1, source_target_pairs={{0,1},{1,0},{2,3},{3,2},{4,5},{5,4},{6,7},{7,6},{8,9},{9,8},{10,11... | collective-permute-start | bytes 196616 | tf_op jit(solution)/shard_map/ppermute | solution.py:406
  50.3 7.3 %copy-start.3 = (bf16[512,512]{1,0:T(8,128)(2,1)S(1)}, bf16[512,512]{1,0:T(8,128)(2,1)}, u32[]{:S(2)}) copy-start(bf16[512,512]{1,0:T(8,128)(2,1)} %get-tuple-element.30.refs_2_.refs_1_) | copy-start | bytes 1572868
  50.3 7.3 %copy-start.5 = (s32[512]{0:T(512)S(1)}, s32[512]{0:T(512)}, u32[]{:S(2)}) copy-start(s32[512]{0:T(512)} %param.10) | copy-start | bytes 6148
  53.8 36.6 %all-to-all-start.2 = ((bf16[8,160,512]{2,1,0:T(8,128)(2,1)}), bf16[8,160,512]{2,1,0:T(8,128)(2,1)S(1)}, u32[]{:S(2)}, u32[]{:S(2)}) async-start(bf16[8,160,512]{2,1,0:T(8,128)(2,1)} %get-tuple-element.35.refs_3_), calls=%async_computation.2 | async-start | bytes 2621440 | tf_op jit(solution)/shard_map/all_to_all | solution.py:410
  58.7 2.0 %collective-permute-start.4 = (bf16[512,512]{1,0:T(8,128)(2,1)S(1)}, bf16[512,512]{1,0:T(8,128)(2,1)S(1)}, u32[]{:S(2)}, u32[]{:S(2)}) collective-permute-start(bf16[512,512]{1,0:T(8,128)(2,1)S(1)} %get-tuple-element.40), channel_id=1, source_target_pairs={{0,1},{1,0},{2,3},{3,2},{4,5},{5,4},{6,7},{7,6},{8,9},{9,8},{10,11... | collective-permute-start | bytes 1572872 | tf_op jit(solution)/shard_map/ppermute | solution.py:406
  59.9 2.5 %collective-permute-start.3 = (bf16[512,512]{1,0:T(8,128)(2,1)S(1)}, bf16[512,512]{1,0:T(8,128)(2,1)S(1)}, u32[]{:S(2)}, u32[]{:S(2)}) collective-permute-start(bf16[512,512]{1,0:T(8,128)(2,1)S(1)} %get-tuple-element.37.refs_3_), channel_id=1, source_target_pairs={{0,1},{1,0},{2,3},{3,2},{4,5},{5,4},{6,7},{7,6},{8,9},{9,8},{10,11... | collective-permute-start | bytes 1572872 | tf_op jit(solution)/shard_map/ppermute | solution.py:406
  60.8 14.0 %collective-permute-start.5 = (bf16[512,512]{1,0:T(8,128)(2,1)S(1)}, bf16[512,512]{1,0:T(8,128)(2,1)S(1)}, u32[]{:S(2)}, u32[]{:S(2)}) collective-permute-start(bf16[512,512]{1,0:T(8,128)(2,1)S(1)} %shard_map.102.refs_2_), channel_id=1, source_target_pairs={{0,2},{1,3},{2,0},{3,1},{4,6},{5,7},{6,4},{7,5},{8,10},{9,11},{10,... | collective-permute-start | bytes 1572872 | tf_op jit(solution)/shard_map/ppermute | solution.py:406
  62.4 14.3 %copy-start.1 = (bf16[4,512,512]{2,1,0:T(8,128)(2,1)S(1)}, bf16[4,512,512]{2,1,0:T(8,128)(2,1)}, u32[]{:S(2)}) copy-start(bf16[4,512,512]{2,1,0:T(8,128)(2,1)} %refs_2_.3) | copy-start | bytes 6291460
  62.4 14.3 %copy-start.6 = (s32[512]{0:T(512)S(1)}, s32[512]{0:T(512)}, u32[]{:S(2)}) copy-start(s32[512]{0:T(512)} %param.9) | copy-start | bytes 6148
  74.9 15.4 %copy-start.8 = (s32[1,32]{1,0:T(1,128)S(1)}, s32[1,32]{1,0:T(1,128)}, u32[]{:S(2)}) copy-start(s32[1,32]{1,0:T(1,128)} %get-tuple-element.32.refs_1_) | copy-start | bytes 388
  74.9 10.2 %collective-permute-start.6 = (bf16[256,512]{1,0:T(8,128)(2,1)S(1)}, bf16[256,512]{1,0:T(8,128)(2,1)S(1)}, u32[]{:S(2)}, u32[]{:S(2)}) collective-permute-start(bf16[256,512]{1,0:T(8,128)(2,1)S(1)} %get-tuple-element.41.refs_4_), channel_id=1, source_target_pairs={{0,4},{4,0},{8,12},{12,8},{16,20},{20,16},{24,28},{28,24},{1,5},{5... | collective-permute-start | bytes 786440 | tf_op jit(solution)/shard_map/ppermute | solution.py:406
  85.2 9.7 %collective-permute-start.12 = (bf16[64,512]{1,0:T(8,128)(2,1)S(1)}, bf16[64,512]{1,0:T(8,128)(2,1)S(1)}, u32[]{:S(2)}, u32[]{:S(2)}) collective-permute-start(bf16[64,512]{1,0:T(8,128)(2,1)S(1)} %get-tuple-element.47), channel_id=1, source_target_pairs={{0,16},{4,20},{8,24},{12,28},{16,0},{20,4},{24,8},{28,12},{1,17},{... | collective-permute-start | bytes 196616 | tf_op jit(solution)/shard_map/ppermute | solution.py:406
  88.8 6.1 %collective-permute-start.13 = (bf16[64,512]{1,0:T(8,128)(2,1)S(1)}, bf16[64,512]{1,0:T(8,128)(2,1)S(1)}, u32[]{:S(2)}, u32[]{:S(2)}) collective-permute-start(bf16[64,512]{1,0:T(8,128)(2,1)S(1)} %get-tuple-element.48), channel_id=1, source_target_pairs={{0,24},{4,28},{8,16},{12,20},{16,8},{20,12},{24,0},{28,4},{1,25},{... | collective-permute-start | bytes 196616 | tf_op jit(solution)/shard_map/ppermute | solution.py:406
  89.7 5.2 %collective-permute-start.11 = (bf16[64,512]{1,0:T(8,128)(2,1)S(1)}, bf16[64,512]{1,0:T(8,128)(2,1)S(1)}, u32[]{:S(2)}, u32[]{:S(2)}) collective-permute-start(bf16[64,512]{1,0:T(8,128)(2,1)S(1)} %get-tuple-element.45.refs_4_), channel_id=1, source_target_pairs={{0,8},{4,12},{8,0},{12,4},{16,24},{20,28},{24,16},{28,20},{1,9},{5... | collective-permute-start | bytes 196616 | tf_op jit(solution)/shard_map/ppermute | solution.py:406
  91.2 2.0 %collective-permute-start.7 = (bf16[512,512]{1,0:T(8,128)(2,1)S(1)}, bf16[512,512]{1,0:T(8,128)(2,1)S(1)}, u32[]{:S(2)}, u32[]{:S(2)}) collective-permute-start(bf16[512,512]{1,0:T(8,128)(2,1)S(1)} %shard_map.107.refs_4_), channel_id=1, source_target_pairs={{0,1},{1,0},{2,3},{3,2},{4,5},{5,4},{6,7},{7,6},{8,9},{9,8},{10,11... | collective-permute-start | bytes 1572872 | tf_op jit(solution)/shard_map/ppermute | solution.py:406
  93.3 14.6 %collective-permute-start.9 = (bf16[512,512]{1,0:T(8,128)(2,1)S(1)}, bf16[512,512]{1,0:T(8,128)(2,1)S(1)}, u32[]{:S(2)}, u32[]{:S(2)}) collective-permute-start(bf16[512,512]{1,0:T(8,128)(2,1)S(1)} %shard_map.109.mine_ref), channel_id=1, source_target_pairs={{0,2},{1,3},{2,0},{3,1},{4,6},{5,7},{6,4},{7,5},{8,10},{9,11},{10,... | collective-permute-start | bytes 1572872 | tf_op jit(solution)/shard_map/ppermute | solution.py:406
  95.0 6.3 %collective-permute-start.16 = (bf16[64,512]{1,0:T(8,128)(2,1)S(1)}, bf16[64,512]{1,0:T(8,128)(2,1)S(1)}, u32[]{:S(2)}, u32[]{:S(2)}) collective-permute-start(bf16[64,512]{1,0:T(8,128)(2,1)S(1)} %shard_map.110.refs_0_), channel_id=1, source_target_pairs={{0,24},{4,28},{8,16},{12,20},{16,8},{20,12},{24,0},{28,4},{1,25},{... | collective-permute-start | bytes 196616 | tf_op jit(solution)/shard_map/ppermute | solution.py:406
  97.3 6.9 %collective-permute-start.15 = (bf16[64,512]{1,0:T(8,128)(2,1)S(1)}, bf16[64,512]{1,0:T(8,128)(2,1)S(1)}, u32[]{:S(2)}, u32[]{:S(2)}) collective-permute-start(bf16[64,512]{1,0:T(8,128)(2,1)S(1)} %shard_map.110.refs_0_), channel_id=1, source_target_pairs={{0,16},{4,20},{8,24},{12,28},{16,0},{20,4},{24,8},{28,12},{1,17},{... | collective-permute-start | bytes 196616 | tf_op jit(solution)/shard_map/ppermute | solution.py:406
  98.0 6.3 %collective-permute-start.14 = (bf16[64,512]{1,0:T(8,128)(2,1)S(1)}, bf16[64,512]{1,0:T(8,128)(2,1)S(1)}, u32[]{:S(2)}, u32[]{:S(2)}) collective-permute-start(bf16[64,512]{1,0:T(8,128)(2,1)S(1)} %shard_map.110.refs_0_), channel_id=1, source_target_pairs={{0,8},{4,12},{8,0},{12,4},{16,24},{20,28},{24,16},{28,20},{1,9},{5... | collective-permute-start | bytes 196616 | tf_op jit(solution)/shard_map/ppermute | solution.py:406
  104.2 8.7 %collective-permute-start.18 = (bf16[256,512]{1,0:T(8,128)(2,1)S(1)}, bf16[256,512]{1,0:T(8,128)(2,1)S(1)}, u32[]{:S(2)}, u32[]{:S(2)}) collective-permute-start(bf16[256,512]{1,0:T(8,128)(2,1)S(1)} %shard_map.111.refs_0_), channel_id=1, source_target_pairs={{0,2},{1,3},{2,0},{3,1},{4,6},{5,7},{6,4},{7,5},{8,10},{9,11},{10,... | collective-permute-start | bytes 786440 | tf_op jit(solution)/shard_map/ppermute | solution.py:406
  104.8 8.2 %collective-permute-start.17 = (bf16[256,512]{1,0:T(8,128)(2,1)S(1)}, bf16[256,512]{1,0:T(8,128)(2,1)S(1)}, u32[]{:S(2)}, u32[]{:S(2)}) collective-permute-start(bf16[256,512]{1,0:T(8,128)(2,1)S(1)} %shard_map.111.refs_0_), channel_id=1, source_target_pairs={{0,4},{4,0},{8,12},{12,8},{16,20},{20,16},{24,28},{28,24},{1,5},{5... | collective-permute-start | bytes 786440 | tf_op jit(solution)/shard_map/ppermute | solution.py:406
  106.4 11.1 %collective-permute-start.8 = (bf16[512,512]{1,0:T(8,128)(2,1)S(1)}, bf16[512,512]{1,0:T(8,128)(2,1)S(1)}, u32[]{:S(2)}, u32[]{:S(2)}) collective-permute-start(bf16[512,512]{1,0:T(8,128)(2,1)S(1)} %shard_map.109.mine_ref), channel_id=1, source_target_pairs={{0,1},{1,0},{2,3},{3,2},{4,5},{5,4},{6,7},{7,6},{8,9},{9,8},{10,11... | collective-permute-start | bytes 1572872 | tf_op jit(solution)/shard_map/ppermute | solution.py:406
  108.0 9.5 %collective-permute-start.10 = (bf16[512,512]{1,0:T(8,128)(2,1)S(1)}, bf16[512,512]{1,0:T(8,128)(2,1)S(1)}, u32[]{:S(2)}, u32[]{:S(2)}) collective-permute-start(bf16[512,512]{1,0:T(8,128)(2,1)S(1)} %collective-permute-done.9.over_ref), channel_id=1, source_target_pairs={{0,1},{1,0},{2,3},{3,2},{4,5},{5,4},{6,7},{7,6},{8,9},{9,8},{10,11... | collective-permute-start | bytes 1572872 | tf_op jit(solution)/shard_map/ppermute | solution.py:406
  108.0 5.5 %collective-permute-start.19 = (bf16[256,512]{1,0:T(8,128)(2,1)S(1)}, bf16[256,512]{1,0:T(8,128)(2,1)S(1)}, u32[]{:S(2)}, u32[]{:S(2)}) collective-permute-start(bf16[256,512]{1,0:T(8,128)(2,1)S(1)} %shard_map.111.refs_0_), channel_id=1, source_target_pairs={{0,1},{1,0},{2,3},{3,2},{4,5},{5,4},{6,7},{7,6},{8,9},{9,8},{10,11... | collective-permute-start | bytes 786440 | tf_op jit(solution)/shard_map/ppermute | solution.py:406
  113.0 2.1 %collective-permute-start.21 = (bf16[256,512]{1,0:T(8,128)(2,1)S(1)}, bf16[256,512]{1,0:T(8,128)(2,1)S(1)}, u32[]{:S(2)}, u32[]{:S(2)}) collective-permute-start(bf16[256,512]{1,0:T(8,128)(2,1)S(1)} %collective-permute-done.18.refs_2_.refs_0_), channel_id=1, source_target_pairs={{0,1},{1,0},{2,3},{3,2},{4,5},{5,4},{6,7},{7,6},{8,9},{9,8},{10,11... | collective-permute-start | bytes 786440 | tf_op jit(solution)/shard_map/ppermute | solution.py:406
  113.0 4.5 %collective-permute-start.20 = (bf16[256,512]{1,0:T(8,128)(2,1)S(1)}, bf16[256,512]{1,0:T(8,128)(2,1)S(1)}, u32[]{:S(2)}, u32[]{:S(2)}) collective-permute-start(bf16[256,512]{1,0:T(8,128)(2,1)S(1)} %collective-permute-done.17.refs_1_.refs_0_), channel_id=1, source_target_pairs={{0,1},{1,0},{2,3},{3,2},{4,5},{5,4},{6,7},{7,6},{8,9},{9,8},{10,11... | collective-permute-start | bytes 786440 | tf_op jit(solution)/shard_map/ppermute | solution.py:406
  113.5 6.7 %collective-permute-start.22 = (bf16[128,512]{1,0:T(8,128)(2,1)S(1)}, bf16[128,512]{1,0:T(8,128)(2,1)S(1)}, u32[]{:S(2)}, u32[]{:S(2)}) collective-permute-start(bf16[128,512]{1,0:T(8,128)(2,1)S(1)} %shard_map.113), channel_id=1, source_target_pairs={{0,2},{1,3},{2,0},{3,1},{4,6},{5,7},{6,4},{7,5},{8,10},{9,11},{10,... | collective-permute-start | bytes 393224 | tf_op jit(solution)/shard_map/ppermute | solution.py:406
  115.1 5.8 %collective-permute-start.23 = (bf16[128,512]{1,0:T(8,128)(2,1)S(1)}, bf16[128,512]{1,0:T(8,128)(2,1)S(1)}, u32[]{:S(2)}, u32[]{:S(2)}) collective-permute-start(bf16[128,512]{1,0:T(8,128)(2,1)S(1)} %shard_map.115), channel_id=1, source_target_pairs={{0,4},{4,0},{8,12},{12,8},{16,20},{20,16},{24,28},{28,24},{1,5},{5... | collective-permute-start | bytes 393224 | tf_op jit(solution)/shard_map/ppermute | solution.py:406
  120.2 1.4 %collective-permute-start.24 = (bf16[128,512]{1,0:T(8,128)(2,1)S(1)}, bf16[128,512]{1,0:T(8,128)(2,1)S(1)}, u32[]{:S(2)}, u32[]{:S(2)}) collective-permute-start(bf16[128,512]{1,0:T(8,128)(2,1)S(1)} %shard_map.114.refs_0_), channel_id=1, source_target_pairs={{0,1},{1,0},{2,3},{3,2},{4,5},{5,4},{6,7},{7,6},{8,9},{9,8},{10,11... | collective-permute-start | bytes 393224 | tf_op jit(solution)/shard_map/ppermute | solution.py:406
  120.9 1.4 %collective-permute-start.25 = (bf16[128,512]{1,0:T(8,128)(2,1)S(1)}, bf16[128,512]{1,0:T(8,128)(2,1)S(1)}, u32[]{:S(2)}, u32[]{:S(2)}) collective-permute-start(bf16[128,512]{1,0:T(8,128)(2,1)S(1)} %shard_map.116.refs_1_), channel_id=1, source_target_pairs={{0,1},{1,0},{2,3},{3,2},{4,5},{5,4},{6,7},{7,6},{8,9},{9,8},{10,11... | collective-permute-start | bytes 393224 | tf_op jit(solution)/shard_map/ppermute | solution.py:406
